TPU v7x, 32 devices: a whole 2x2x4 slice. The times are simulated.
32 devices in a mesh: groups: 2 (over y), expert: 4 (over z), dp: 4 (over x, core).
Axes of the slice: x: 2, y: 2, z: 4, core: 2. Of those that a mesh axis runs over, the one named last changes fastest.
Arguments:
- tokens: bfloat16 [4096, 2048], P(('groups', 'expert', 'dp')), parts along dimension 0, may hold values from -6 to 6
- routes: int32 [4096, 8], P(('groups', 'expert', 'dp')), parts along dimension 0, may hold values from 0 to 127, all different within a row; in each aligned block of 128 rows (0 to 127, 128 to 255, ...) at most 16 rows name the same one
- route_weight: float32 [4096, 8], P(('groups', 'expert', 'dp')), parts along dimension 0, may hold values from 0.1 to 1
- norm_gain: float32 [2048], replicated, may hold values from 0.25 to 1.75
- w_gate: bfloat16 [128, 2048, 768], P(('expert', 'dp')), may hold values from -0.125 to 0.125
- w_up: bfloat16 [128, 2048, 768], P(('expert', 'dp')), may hold values from -0.125 to 0.125
- w_down: bfloat16 [128, 768, 2048], P(('expert', 'dp')), may hold values from -0.21875 to 0.21875
Outputs:
- mixed: bfloat16 [4096, 2048], P(('groups', 'expert', 'dp')), parts along dimension 0
There are 2 independent parts, one for each index of `groups`. A program takes and returns all parts, laid end to end along the dimension named above; an argument that names none is the same for every part. Nothing has to cross between parts.
Inputs may be any that keep to these rules, and one draw needn't show every extreme that they name: `routes`: each row names 8 different experts. In the 128 rows of one device (aligned blocks), no expert is named by more than 16 rows, and in every draw some expert is named by exactly 16 rows of some device; every expert is named somewhere.
All inputs are finite; a program needn't handle non-finite values.
Results may differ from a plain program's by a relative error of at most 0.007.
Values may be sent and summed in bfloat16 or wider, within the bound.
No kernel may reach another device: no remote copies, remote signals or barrier semaphores. Data moves between devices by JAX's collectives and lax.ppermute only.
A program may use at most 256 MiB of HBM per device.

v0:
```python
import jax
import jax.numpy as jnp
from jax import lax
from jax.sharding import PartitionSpec as P

block_rows = 256


def expert_block(row_block, gate_weight, up_weight, down_weight):
    gate_part = jnp.dot(row_block, gate_weight, preferred_element_type=jnp.float32)
    up_part = jnp.dot(row_block, up_weight, preferred_element_type=jnp.float32)
    hidden = (jax.nn.silu(gate_part) * up_part).astype(jnp.bfloat16)
    return jnp.dot(hidden, down_weight, preferred_element_type=jnp.float32).astype(jnp.bfloat16)


def expert_rows(row_table, live, gate_weight, up_weight, down_weight):
    row_count = row_table.shape[0]
    feature_dim = row_table.shape[1]
    span = -(-row_count // block_rows) * block_rows
    live_count = live.astype(jnp.int32)
    place = jnp.cumsum(live_count) - 1
    total_live = jnp.sum(live_count)
    target = jnp.where(live, place, span)
    picker = (
        jnp.zeros((span,), jnp.int32)
        .at[target]
        .set(jnp.arange(row_count, dtype=jnp.int32), mode="drop")
    )
    packed = row_table[picker]
    used_blocks = (total_live + block_rows - 1) // block_rows

    def block_step(block_index, result):
        first_row = block_index * block_rows
        row_block = lax.dynamic_slice_in_dim(packed, first_row, block_rows, 0)
        produced = expert_block(row_block, gate_weight, up_weight, down_weight)
        return lax.dynamic_update_slice_in_dim(result, produced, first_row, 0)

    result = lax.fori_loop(0, used_blocks, block_step, jnp.zeros((span, feature_dim), jnp.bfloat16))
    unpacked = result[jnp.maximum(place, 0)]
    return jnp.where(live[:, None], unpacked, jnp.zeros_like(unpacked))


def run_experts(incoming, live_table, w_gate, w_up, w_down):
    source_count, local_total, slot_count, width_dim = incoming.shape

    def one_expert(expert_index, result):
        table = lax.dynamic_index_in_dim(incoming, expert_index, 1, keepdims=False)
        table = table.reshape(source_count * slot_count, width_dim)
        live = lax.dynamic_index_in_dim(live_table, expert_index, 1, keepdims=False).reshape(-1)
        produced = expert_rows(
            table, live, w_gate[expert_index], w_up[expert_index], w_down[expert_index]
        )
        produced = produced.reshape(source_count, 1, slot_count, width_dim)
        return lax.dynamic_update_slice_in_dim(result, produced, expert_index, 1)

    return lax.fori_loop(0, local_total, one_expert, jnp.zeros_like(incoming))


def nonzero_rows(incoming):
    return jnp.any(incoming != 0, axis=3)


def shards(tokens, routes, route_weight, norm_gain, w_gate, w_up, w_down):
    token_count = routes.shape[0]
    top_count = routes.shape[1]
    feature_dim = tokens.shape[1]
    expert_size = lax.axis_size("expert")
    dp_size = lax.axis_size("dp")
    device_count = expert_size * dp_size
    local_count = w_gate.shape[0]
    expert_count = local_count * device_count
    capacity = 2 * token_count * top_count // expert_count
    as_float = tokens.astype(jnp.float32)
    normed = (
        as_float
        * lax.rsqrt(jnp.mean(as_float * as_float, axis=-1, keepdims=True) + 1e-06)
        * norm_gain
    ).astype(jnp.bfloat16)
    flat_routes = routes.reshape(-1)
    one_hot = (flat_routes[:, None] == jnp.arange(expert_count, dtype=jnp.int32)[None, :]).astype(
        jnp.int32
    )
    ranks = jnp.cumsum(one_hot, axis=0)
    slot_index = jnp.sum(one_hot * ranks, axis=1) - 1
    destination = flat_routes * capacity + slot_index
    source_token = jnp.arange(token_count * top_count, dtype=jnp.int32) // top_count
    outgoing = (
        jnp.zeros((expert_count * capacity, feature_dim), jnp.bfloat16)
        .at[destination]
        .set(normed[source_token])
    )
    outgoing = outgoing.reshape(device_count, local_count, capacity, feature_dim)
    incoming = lax.all_to_all(outgoing, ("expert", "dp"), split_axis=0, concat_axis=0, tiled=True)
    returned = run_experts(incoming, nonzero_rows(incoming), w_gate, w_up, w_down)
    arrived = lax.all_to_all(returned, ("expert", "dp"), split_axis=0, concat_axis=0, tiled=True)
    arrived = arrived.reshape(expert_count * capacity, feature_dim)
    picked = arrived[destination].reshape(token_count, top_count, feature_dim)
    mixed = jnp.sum(route_weight[:, :, None] * picked.astype(jnp.float32), axis=1)
    return mixed.astype(jnp.bfloat16)


def solution(mesh):
    return jax.shard_map(
        shards,
        mesh=mesh,
        in_specs=(
            P(("groups", "expert", "dp"), None),
            P(("groups", "expert", "dp"), None),
            P(("groups", "expert", "dp"), None),
            P(),
            P(("expert", "dp"), None, None),
            P(("expert", "dp"), None, None),
            P(("expert", "dp"), None, None),
        ),
        out_specs=P(("groups", "expert", "dp"), None),
        check_vma=False,
    )
```

profile of v0, /device:TPU:8, one launch (start us, length us, event | category | flops | bytes accessed | tf_op | source)
XLA Modules:
  0.0 599.5 jit_solution(11547712035600352199)
XLA Ops:
  5.3 24.9 %scatter_custom_fusion.1 = bf16[2048,2048]{1,0:T(8,128)(2,1)} fusion(s32[1024]{0:T(1024)S(1)} %bitcast.92, bf16[128,2048]{1,0:T(8,128)(2,1)S(1)} %fusion.33, s32[1024]{0:T(1024)S(1)} %broadcast_clamp_fusion.1, bf16[]{:T(256)} %constant.179.clone.1), kind=kCustom, calls=%fused_computation.38 | custom fusion | bytes 8388610 | tf_op jit(solution)/shard_map/scatter | solution.py:90
  30.2 6.3 %all-to-all-start = ((bf16[16,8,16,2048]{3,2,1,0:T(8,128)(2,1)}), bf16[16,8,16,2048]{3,2,1,0:T(8,128)(2,1)}, u32[]{:S(2)}, u32[]{:S(2)}) async-start(bf16[16,8,16,2048]{3,2,1,0:T(8,128)(2,1)} %bitcast.87), calls=%async_computation | async-start | bytes 16777216 | tf_op jit(solution)/shard_map/all_to_all | solution.py:93
  36.4 180.7 %all-to-all-done = bf16[16,8,16,2048]{3,2,1,0:T(8,128)(2,1)} async-done(((bf16[16,8,16,2048]{3,2,1,0:T(8,128)(2,1)}), bf16[16,8,16,2048]{3,2,1,0:T(8,128)(2,1)}, u32[]{:S(2)}, u32[]{:S(2)}) %all-to-all-start) | async-done | bytes 8388640 | tf_op jit(solution)/shard_map/all_to_all | solution.py:93
  217.1 5.7 compare_reduce_fusion
  222.8 168.6 %while.62 = (s32[]{:T(128)}, bf16[16,8,16,2048]{3,2,1,0:T(8,128)(2,1)}, pred[16,8,16]{2,0,1:T(8,128)(4,1)S(1)}, bf16[16,8,16,2048]{3,2,1,0:T(8,128)(2,1)}, bf16[...) while((s32[]{:T(128)}, ...), condition=%wide.region_13.14_spmd.clone, body=%wide.region_6.13_spmd.sunk.clone | while | flops 2418185216 | bytes 25721056 | solution.py:56
  230.6 5.0 fusion.67
  239.0 3.7 gather_fusion.1
  251.7 5.0 fusion.67
  260.0 3.7 gather_fusion.1
  272.8 5.0 fusion.67
  281.1 3.7 gather_fusion.1
  293.8 5.0 fusion.67
  302.2 3.7 gather_fusion.1
  314.9 5.0 fusion.67
  323.2 3.7 gather_fusion.1
  336.0 5.0 fusion.67
  344.3 3.7 gather_fusion.1
  357.1 5.0 fusion.67
  378.2 5.0 fusion.67
  386.5 3.7 gather_fusion.1
  391.5 6.7 %all-to-all-start.1 = ((bf16[16,8,16,2048]{3,2,1,0:T(8,128)(2,1)}), bf16[16,8,16,2048]{3,2,1,0:T(8,128)(2,1)}, u32[]{:S(2)}, u32[]{:S(2)}) async-start(bf16[16,8,16,2048]{3,2,1,0:T(8,128)(2,1)} %get-tuple-element.448), calls=%async_computation.1 | async-start | bytes 16777216 | tf_op jit(solution)/shard_map/all_to_all | solution.py:95
  398.3 180.6 %all-to-all-done.1 = bf16[16,8,16,2048]{3,2,1,0:T(8,128)(2,1)} async-done(((bf16[16,8,16,2048]{3,2,1,0:T(8,128)(2,1)}), bf16[16,8,16,2048]{3,2,1,0:T(8,128)(2,1)}, u32[]{:S(2)}, u32[]{:S(2)}) %all-to-all-start.1) | async-done | bytes 8388640 | tf_op jit(solution)/shard_map/all_to_all | solution.py:95
  578.9 13.3 %gather_fusion.2 = bf16[1024,2048]{1,0:T(8,128)(2,1)} fusion(bf16[2048,2048]{1,0:T(8,128)(2,1)} %bitcast.16, s32[1024]{0:T(1024)S(1)} %broadcast_clamp_fusion), kind=kCustom, calls=%fused_computation.3 | custom fusion | bytes 8392704 | tf_op jit(solution)/shard_map/gather | solution.py:97
  592.1 7.3 %fusion.27 = bf16[128,2048]{1,0:T(8,128)(2,1)} fusion(bf16[1024,2048]{1,0:T(8,128)(2,1)} %gather_fusion.2, f32[128,8]{1,0:T(8,128)S(1)} %copy.19), kind=kLoop, calls=%fused_computation.37 | loop fusion | flops 6029312 | bytes 4722688 | tf_op jit(solution)/shard_map/reduce_sum | solution.py:98
  (204 shorter events, 110.5 us)
Async XLA Ops:
  30.2 187.0 %all-to-all-start = ((bf16[16,8,16,2048]{3,2,1,0:T(8,128)(2,1)}), bf16[16,8,16,2048]{3,2,1,0:T(8,128)(2,1)}, u32[]{:S(2)}, u32[]{:S(2)}) async-start(bf16[16,8,16,2048]{3,2,1,0:T(8,128)(2,1)} %bitcast.87), calls=%async_computation | async-start | bytes 16777216 | tf_op jit(solution)/shard_map/all_to_all | solution.py:93
  391.5 6.7 %copy-start = (f32[128,8]{0,1:T(8,128)S(1)}, f32[128,8]{0,1:T(8,128)}, u32[]{:S(2)}) copy-start(f32[128,8]{0,1:T(8,128)} %param.13) | copy-start | bytes 12292
  391.5 187.4 %all-to-all-start.1 = ((bf16[16,8,16,2048]{3,2,1,0:T(8,128)(2,1)}), bf16[16,8,16,2048]{3,2,1,0:T(8,128)(2,1)}, u32[]{:S(2)}, u32[]{:S(2)}) async-start(bf16[16,8,16,2048]{3,2,1,0:T(8,128)(2,1)} %get-tuple-element.448), calls=%async_computation.1 | async-start | bytes 16777216 | tf_op jit(solution)/shard_map/all_to_all | solution.py:95
where the time goes:
time: 603 us; the launch traced here: 599 us
  waiting for transfers between devices  361 us (60%)
  local copies, waits for them, and re-layouts  122 us (20%)
  matrix products  63 us (10%)
  other arithmetic  35.1 us (6%)
  starting transfers between devices  13 us (2%)
    all_to_all x1, waiting for transfers between devices, shards(): lax.all_to_all(outgoing, ('expert', 'dp'), split_axis=0, concat_axis=0, t...  181 us
    all_to_all x1, waiting for transfers between devices, shards(): lax.all_to_all(returned, ('expert', 'dp'), split_axis=0, concat_axis=0, t...  181 us
    dot_general x8, matrix products, expert_block(): jnp.dot(hidden, down_weight, preferred_element_type=jnp.float32)  40 us
    gather x8, local copies, waits for them, and re-layouts, expert_rows(): unpacked = result[jnp.maximum(place, 0)]  29.8 us
    scatter x1, local copies, waits for them, and re-layouts, shards(): outgoing = jnp.zeros((expert_count * capacity, feature_dim), jnp.bfloat16...  24.9 us
    dot_general x8, matrix products, expert_block(): jnp.dot(row_block, gate_weight, preferred_element_type=jnp.float32)  23 us
    gather x1, local copies, waits for them, and re-layouts, shards(): picked = arrived[destination].reshape(token_count, top_count, feature_dim)  13.3 us
  transfers between devices with their start and end apart: 2, of which 2 were waited for; matrix products, arithmetic and copies ran while one was open for 0% of the time, Pallas kernels for 0%

commit v1 on v0

v1 whole, which is shorter than its diff:
```python
import functools

import jax
import jax.numpy as jnp
from jax import lax
from jax.experimental import pallas as pl
from jax.experimental.pallas import tpu as pltpu
from jax.sharding import PartitionSpec as P

slots = 16
gather_chunks = 2
return_chunks = 4
grant = 56 * 1024 * 1024


def rounded_sum(first, *others):
    total = first.astype(jnp.float32)
    for other in others:
        total = total + other.astype(jnp.float32)
    return total.astype(jnp.bfloat16)


def pick_kernel(picker_ref, tokens_ref, rows_ref):
    sources = tokens_ref.shape[0]
    experts = rows_ref.shape[0]
    for source in range(sources):
        picked = jnp.dot(
            picker_ref[source], tokens_ref[source], preferred_element_type=jnp.float32
        ).astype(jnp.bfloat16)
        for expert in range(experts):
            rows_ref[expert, source] = picked[expert * slots : (expert + 1) * slots]


def pick_rows(picker, tokens, experts):
    sources, token_count, width = tokens.shape
    block = min(sources, 8)
    return pl.pallas_call(
        pick_kernel,
        grid=(sources // block,),
        in_specs=[
            pl.BlockSpec((block, experts * slots, token_count), lambda i: (i, 0, 0)),
            pl.BlockSpec((block, token_count, width), lambda i: (i, 0, 0)),
        ],
        out_specs=pl.BlockSpec((experts, block, slots, width), lambda i: (0, i, 0, 0)),
        out_shape=jax.ShapeDtypeStruct((experts, sources, slots, width), jnp.bfloat16),
        compiler_params=pltpu.CompilerParams(vmem_limit_bytes=grant),
        cost_estimate=pl.CostEstimate(
            flops=2 * sources * experts * slots * token_count * width,
            bytes_accessed=2 * sources * width * (token_count + experts * slots),
            transcendentals=0,
        ),
    )(picker, tokens)


def hidden_kernel(chunks, *refs):
    row_refs = refs[: 2 * chunks]
    scale_ref, gate_ref, up_ref, hidden_ref = refs[2 * chunks :]
    gate_part = None
    width = row_refs[0].shape[-1]
    for chunk in range(chunks):
        rows = jnp.concatenate([row_refs[2 * chunk][0], row_refs[2 * chunk + 1][0]], axis=0)
        depth = pl.ds(chunk * width, width)
        gate_add = jnp.dot(rows, gate_ref[0, depth, :], preferred_element_type=jnp.float32)
        up_add = jnp.dot(rows, up_ref[0, depth, :], preferred_element_type=jnp.float32)
        if gate_part is None:
            gate_part, up_part = gate_add, up_add
        else:
            gate_part, up_part = gate_part + gate_add, up_part + up_add
    hidden = gate_part / (1.0 + jnp.exp(-gate_part)) * up_part * scale_ref[0]
    hidden_ref[0] = hidden.astype(jnp.bfloat16)


def hidden_rows(row_chunks, scale, w_gate, w_up):
    experts, feature_dim, hidden_dim = w_gate.shape
    half = row_chunks[0].shape[1]
    chunks = len(row_chunks) // 2
    width = row_chunks[0].shape[2]
    whole = 2 * half
    return pl.pallas_call(
        functools.partial(hidden_kernel, chunks),
        grid=(experts,),
        in_specs=[pl.BlockSpec((1, half, width), lambda e: (e, 0, 0))] * (2 * chunks)
        + [
            pl.BlockSpec((1, whole, 1), lambda e: (e, 0, 0)),
            pl.BlockSpec((1, feature_dim, hidden_dim), lambda e: (e, 0, 0)),
            pl.BlockSpec((1, feature_dim, hidden_dim), lambda e: (e, 0, 0)),
        ],
        out_specs=pl.BlockSpec((1, whole, hidden_dim), lambda e: (e, 0, 0)),
        out_shape=jax.ShapeDtypeStruct((experts, whole, hidden_dim), jnp.bfloat16),
        compiler_params=pltpu.CompilerParams(vmem_limit_bytes=grant),
        cost_estimate=pl.CostEstimate(
            flops=4 * experts * whole * feature_dim * hidden_dim,
            bytes_accessed=4 * experts * feature_dim * hidden_dim,
            transcendentals=experts * whole * hidden_dim,
        ),
    )(*row_chunks, scale, w_gate, w_up)


def mix_kernel(hidden_ref, down_ref, spread_ref, first_ref, second_ref, made):
    expert = pl.program_id(0)
    experts = pl.num_programs(0)
    sources = spread_ref.shape[0]
    width = down_ref.shape[2]
    made[expert] = (
        jnp.dot(hidden_ref[0], down_ref[0], preferred_element_type=jnp.float32)
        .astype(jnp.bfloat16)
        .reshape(sources, slots, width)
    )

    @pl.when(expert == experts - 1)
    def _():
        for source in range(sources):
            rows = made[:, source].reshape(spread_ref.shape[2], width)
            mixed = jnp.dot(
                spread_ref[source], rows, preferred_element_type=jnp.float32
            ).astype(jnp.bfloat16)
            if source < sources // 2:
                first_ref[source] = mixed
            else:
                second_ref[source - sources // 2] = mixed


def mix_rows(hidden, w_down, spread, chunk, chunks):
    experts, whole, hidden_dim = hidden.shape
    width = w_down.shape[2] // chunks
    sources, token_count, local_rows = spread.shape
    half = jax.ShapeDtypeStruct((sources // 2, token_count, width), jnp.bfloat16)
    return pl.pallas_call(
        mix_kernel,
        grid=(experts,),
        in_specs=[
            pl.BlockSpec((1, whole, hidden_dim), lambda e: (e, 0, 0)),
            pl.BlockSpec((1, hidden_dim, width), lambda e: (e, 0, chunk)),
            pl.BlockSpec(memory_space=pltpu.VMEM),
        ],
        out_specs=[pl.BlockSpec(memory_space=pltpu.VMEM)] * 2,
        out_shape=[half, half],
        scratch_shapes=[pltpu.VMEM((experts, sources, slots, width), jnp.bfloat16)],
        compiler_params=pltpu.CompilerParams(vmem_limit_bytes=grant),
        cost_estimate=pl.CostEstimate(
            flops=2 * experts * whole * hidden_dim * width
            + 2 * sources * token_count * local_rows * width,
            bytes_accessed=2 * experts * hidden_dim * (width + whole)
            + 2 * sources * token_count * width,
            transcendentals=0,
        ),
    )(hidden, w_down, spread)


axes = ("expert", "dp")


def pairs_of(expert_pairs, dp_pairs, dp_size):
    return [
        (e_from * dp_size + d_from, e_to * dp_size + d_to)
        for e_from, e_to in expert_pairs
        for d_from, d_to in dp_pairs
    ]


stay_z = [(i, i) for i in range(4)]
stay_dp = [(i, i) for i in range(4)]
swap_z = pairs_of([(0, 1), (1, 0), (2, 3), (3, 2)], stay_dp, 4)
middle_z = pairs_of([(1, 2), (2, 1)], stay_dp, 4)
outward_z = pairs_of([(1, 0), (2, 3)], stay_dp, 4)
inward_z = pairs_of([(0, 1), (3, 2)], stay_dp, 4)
swap_x = pairs_of(stay_z, [(0, 2), (2, 0), (1, 3), (3, 1)], 4)
swap_core = pairs_of(stay_z, [(0, 1), (1, 0), (2, 3), (3, 2)], 4)


def send(value, pairs):
    return lax.ppermute(value, axes, pairs)


def tree_gather(own, edge):
    near = send(own, swap_z)
    middle = send(own, middle_z)
    cross = send(near, middle_z)
    outer = send(middle, outward_z)
    far = send(cross, outward_z)
    third = jnp.where(edge, outer, middle)
    fourth = jnp.where(edge, far, cross)
    column = [own, near, third, fourth]
    other = [send(value, swap_x) for value in column]
    return jnp.stack(column + other)


def tree_return(mine, theirs):
    chip = rounded_sum(mine, send(theirs, swap_core))
    arrived = [send(chip[4 + i], swap_x) for i in (3, 2, 1, 0)]
    fourth, third, near, own = [
        rounded_sum(chip[i], value) for i, value in zip((3, 2, 1, 0), arrived)
    ]
    cross = rounded_sum(fourth, send(fourth, inward_z))
    middle = rounded_sum(third, send(third, inward_z))
    near = rounded_sum(near, send(cross, middle_z))
    return rounded_sum(own, send(middle, middle_z), send(near, swap_z))


def slot_sources():
    z = lax.axis_index("expert")
    dp = lax.axis_index("dp")
    x, core = dp // 2, dp % 2
    low = z < 2
    column = jnp.stack([z, z ^ 1, jnp.where(low, 2, 1), jnp.where(low, 3, 0)])
    core_of = core ^ jnp.arange(2)[:, None, None]
    x_of = x ^ jnp.arange(2)[None, :, None]
    return (column[None, None, :] * 4 + x_of * 2 + core_of).reshape(-1)


def shards(tokens, routes, route_weight, norm_gain, w_gate, w_up, w_down):
    token_count, top_count = routes.shape
    feature_dim = tokens.shape[1]
    expert_size = lax.axis_size("expert")
    dp_size = lax.axis_size("dp")
    device_count = expert_size * dp_size
    local_count = w_gate.shape[0]
    as_tree = expert_size == 4 and dp_size == 4
    edge = (lax.axis_index("expert") % 3) == 0

    as_float = tokens.astype(jnp.float32)
    normed = (
        as_float
        * lax.rsqrt(jnp.mean(as_float * as_float, axis=-1, keepdims=True) + 1e-06)
        * norm_gain
    ).astype(jnp.bfloat16)

    choice = jnp.concatenate([routes.astype(jnp.float32).T, route_weight.T], axis=0)
    choices = lax.all_gather(choice, axes)
    if as_tree:
        choices = choices[slot_sources()]
    chosen, weight = choices[:, :top_count], choices[:, top_count:]
    first_expert = (lax.axis_index("expert") * dp_size + lax.axis_index("dp")) * local_count
    local = (first_expert + jnp.arange(local_count)).astype(jnp.float32)
    same = chosen[:, None] == local[None, :, None, None]
    named = jnp.any(same, axis=2)
    named_weight = jnp.sum(jnp.where(same, weight[:, None], 0.0), axis=2)
    before = (jnp.arange(token_count)[:, None] < jnp.arange(token_count)[None, :]).astype(
        jnp.bfloat16
    )
    rank = jnp.dot(named.astype(jnp.bfloat16), before, preferred_element_type=jnp.float32)
    rank = jnp.where(named, rank, -1.0)
    match = rank[:, :, None, :] == jnp.arange(slots, dtype=jnp.float32)[None, None, :, None]
    picker = match.astype(jnp.bfloat16).reshape(device_count, local_count * slots, token_count)
    spread = picker.transpose(0, 2, 1)
    scale = jnp.sum(jnp.where(match, named_weight[:, :, None, :], 0.0), axis=3)
    scale = scale.transpose(1, 0, 2).reshape(local_count, device_count * slots, 1)

    width = feature_dim // gather_chunks
    half = device_count // 2
    row_chunks = []
    for chunk in range(gather_chunks):
        part = normed[:, chunk * width : (chunk + 1) * width]
        if as_tree:
            mine = tree_gather(part, edge)
            theirs = send(mine, swap_core)
        else:
            gathered = lax.all_gather(part, axes)
            mine, theirs = gathered[:half], gathered[half:]
        for value, which in ((mine, picker[:half]), (theirs, picker[half:])):
            rows = pick_rows(which, value, local_count)
            row_chunks.append(rows.reshape(local_count, half * slots, width))
    hidden = hidden_rows(row_chunks, scale, w_gate, w_up)

    results = []
    for chunk in range(return_chunks):
        mine, theirs = mix_rows(hidden, w_down, spread, chunk, return_chunks)
        if as_tree:
            results.append(tree_return(mine, theirs))
        else:
            whole = jnp.concatenate([mine, theirs], axis=0).astype(jnp.float32)
            total = lax.psum_scatter(whole, axes, scatter_dimension=0)
            results.append(total.astype(jnp.bfloat16))
    return jnp.concatenate(results, axis=1)


def solution(mesh):
    split = P(("groups", "expert", "dp"), None)
    by_expert = P(("expert", "dp"), None, None)
    return jax.shard_map(
        shards,
        mesh=mesh,
        in_specs=(split, split, split, P(), by_expert, by_expert, by_expert),
        out_specs=split,
        check_vma=False,
    )
```

time: 603 us -> 314 us (0.52)
  waiting for transfers between devices: 361 us -> 114 us
  local copies, waits for them, and re-layouts: 122 us -> 11.9 us
  Pallas kernels: 0 us -> 76.3 us
  starting transfers between devices: 13 us -> 79.5 us
  matrix products: 63 us -> 0.14 us
  other arithmetic: 35.1 us -> 10.9 us
  blocking collectives: 0 us -> 17.3 us
    all_to_all x2 -> x0, waiting for transfers between devices: 361 us -> none  [the longest x1 181 us: shards(): lax.all_to_all(outgoing, ('expert', 'dp'), split_axis=0, concat_axis=0, t...]
    ppermute x0 -> x60, waiting for transfers between devices: none -> 114 us  [send(): return lax.ppermute(value, axes, pairs)]
    ppermute x0 -> x60, starting transfers between devices: none -> 79.5 us  [send(): return lax.ppermute(value, axes, pairs)]
    pallas_call x0 -> x9, Pallas kernels: none -> 76.3 us  [the longest x4 37.5 us: mix_rows(): pl.pallas_call(mix_kernel, grid=(experts,), in_specs=[pl.BlockSpec((1, wh...]
    dot_general x16 -> x1, matrix products: 63 us -> 0.14 us  [shards(): jnp.dot(named.astype(jnp.bfloat16), before, preferred_element_type=jnp.fl...]
    gather x17 -> x1, local copies, waits for them, and re-layouts: 53.9 us -> 0.56 us  [shards(): choices = choices[slot_sources()]]
    scatter x9 -> x0, local copies, waits for them, and re-layouts: 36.1 us -> none  [the longest x1 24.9 us: shards(): outgoing = jnp.zeros((expert_count * capacity, feature_dim), jnp.bfloat16...]
    all_gather x0 -> x1, blocking collectives: none -> 17.3 us  [shards(): choices = lax.all_gather(choice, axes)]
  transfers between devices with their start and end apart: 2 -> 60, of which waited for: 2 -> 31; matrix products, arithmetic and copies ran while one was open for 0% -> 6% of each run, Pallas kernels for 0% -> 13%
where the time goes in v1:
time: 314 us; the launch traced here: 310 us
  waiting for transfers between devices  114 us (36%)
  starting transfers between devices  79.5 us (25%)
  Pallas kernels  76.3 us (24%)
  blocking collectives  17.3 us (6%)
  local copies, waits for them, and re-layouts  11.9 us (4%)
  other arithmetic  10.9 us (3%)
    ppermute x60, waiting for transfers between devices, send(): return lax.ppermute(value, axes, pairs)  114 us
    ppermute x60, starting transfers between devices, send(): return lax.ppermute(value, axes, pairs)  79.5 us
    pallas_call x4, Pallas kernels, mix_rows(): pl.pallas_call(mix_kernel, grid=(experts,), in_specs=[pl.BlockSpec((1, wh...  37.5 us
    pallas_call x1, Pallas kernels, hidden_rows(): pl.pallas_call(functools.partial(hidden_kernel, chunks), grid=(experts,),...  23.9 us
    all_gather x1, blocking collectives, shards(): choices = lax.all_gather(choice, axes)  17.3 us
    pallas_call x4, Pallas kernels, pick_rows(): pl.pallas_call(pick_kernel, grid=(sources // block,), in_specs=[pl.BlockS...  14.9 us
    unnamed x21, local copies, waits for them, and re-layouts  6.65 us
  transfers between devices with their start and end apart: 60, of which 31 were waited for; matrix products, arithmetic and copies ran while one was open for 6% of the time, Pallas kernels for 13%

profile of v1, /device:TPU:8, one launch (start us, length us, event | category | flops | bytes accessed | tf_op | source)
XLA Modules:
  0.0 310.4 jit_solution(879377354567641283)
XLA Ops:
  2.6 5.0 %collective-permute-start.11 = (bf16[128,1024]{1,0:T(8,128)(2,1)S(1)}, bf16[128,1024]{1,0:T(8,128)(2,1)S(1)}, u32[]{:S(2)}, u32[]{:S(2)}) collective-permute-start(bf16[128,1024]{1,0:T(8,128)(2,1)S(1)} %get-tuple-element.53), channel_id=1, source_target_pairs={{4,8},{5,9},{6,10},{7,11},{8,4},{9,5},{10,6},{11,7},{20,24},{21,25... | collective-permute-start | bytes 786440 | tf_op jit(solution)/shard_map/ppermute | solution.py:172
  12.3 17.3 %all-gather = f32[256,128]{1,0:T(8,128)S(1)} all-gather(f32[16,128]{1,0:T(8,128)S(1)} %pad_maximum_fusion.1), channel_id=2, replica_groups=mesh['groups'=2,'expert'=4,'dp'=4] {'expert','dp'}, dimensions={0}, use_global_device_ids=true | all-gather | bytes 139264 | tf_op jit(solution)/shard_map/all_gather | solution.py:229
  29.7 4.2 %collective-permute-start.12 = (bf16[128,1024]{1,0:T(8,128)(2,1)S(1)}, bf16[128,1024]{1,0:T(8,128)(2,1)S(1)}, u32[]{:S(2)}, u32[]{:S(2)}) collective-permute-start(bf16[128,1024]{1,0:T(8,128)(2,1)S(1)} %collective-permute-done.11), channel_id=1, source_target_pairs={{4,0},{5,1},{6,2},{7,3},{8,12},{9,13},{10,14},{11,15},{20,16},{21,... | collective-permute-start | bytes 786440 | tf_op jit(solution)/shard_map/ppermute | solution.py:172
  37.9 3.9 %collective-permute-start.3 = (bf16[128,1024]{1,0:T(8,128)(2,1)S(1)}, bf16[128,1024]{1,0:T(8,128)(2,1)S(1)}, u32[]{:S(2)}, u32[]{:S(2)}) collective-permute-start(bf16[128,1024]{1,0:T(8,128)(2,1)S(1)} %collective-permute-done), channel_id=1, source_target_pairs={{4,8},{5,9},{6,10},{7,11},{8,4},{9,5},{10,6},{11,7},{20,24},{21,25... | collective-permute-start | bytes 786440 | tf_op jit(solution)/shard_map/ppermute | solution.py:172
  61.7 6.9 %collective-permute-done.17 = bf16[128,1024]{1,0:T(8,128)(2,1)S(1)} collective-permute-done((bf16[128,1024]{1,0:T(8,128)(2,1)S(1)}, bf16[128,1024]{1,0:T(8,128)(2,1)S(1)}, u32[]{:S(2)}, u32[]{:S(2)}) %collective-permute-start.17) | collective-permute-done | bytes 262176 | tf_op jit(solution)/shard_map/ppermute | solution.py:172
  75.0 4.9 %collective-permute-done.18 = bf16[128,1024]{1,0:T(8,128)(2,1)S(1)} collective-permute-done((bf16[128,1024]{1,0:T(8,128)(2,1)S(1)}, bf16[128,1024]{1,0:T(8,128)(2,1)S(1)}, u32[]{:S(2)}, u32[]{:S(2)}) %collective-permute-start.18) | collective-permute-done | bytes 262176 | tf_op jit(solution)/shard_map/ppermute | solution.py:172
  105.2 23.9 %shard_map.77.hidden_ref = bf16[8,256,768]{2,1,0:T(8,128)(2,1)} custom-call(bf16[8,128,1024]{2,1,0:T(8,128)(2,1)} %bitcast.169, bf16[8,128,1024]{2,1,0:T(8,128)(2,1)} %bitcast.171, bf16[8,128,1024]{2,1,0:T(8,128)(2,1)} %bitcast.168, bf16[8,128,1024]{2,1,0:T(8,128)(2,1)} %bitcast.170, f32[8,256,1]{2,1,0:T(8,128)} %reshape.209.refs_4_, ...), custom_call_target="tpu_custom_call" | custom-call | flops 12884901888 | bytes 50331648 | tf_op jit(solution)/shard_map/pallas_call | solution.py:79
  129.1 9.4 %shard_map.78 = (bf16[8,128,512]{2,1,0:T(8,128)(2,1)}, bf16[8,128,512]{2,1,0:T(8,128)(2,1)}) custom-call(bf16[8,256,768]{2,1,0:T(8,128)(2,1)} %shard_map.77.hidden_ref, bf16[8,768,2048]{2,1,0:T(8,128)(2,1)} %down_ref.7, bf16[16,128,128]{2,1,0:T(8,128)(2,1)} %fusion.5.spread_ref), custom_call_target="tpu_custom_call" | custom-call | flops 1879048192 | bytes 11534336 | tf_op jit(solution)/shard_map/pallas_call | solution.py:128
  139.0 9.4 %shard_map.79 = (bf16[8,128,512]{2,1,0:T(8,128)(2,1)}, bf16[8,128,512]{2,1,0:T(8,128)(2,1)}) custom-call(bf16[8,256,768]{2,1,0:T(8,128)(2,1)} %shard_map.77.hidden_ref, bf16[8,768,2048]{2,1,0:T(8,128)(2,1)} %down_ref.7, bf16[16,128,128]{2,1,0:T(8,128)(2,1)} %fusion.5.spread_ref), custom_call_target="tpu_custom_call" | custom-call | flops 1879048192 | bytes 11534336 | tf_op jit(solution)/shard_map/pallas_call | solution.py:128
  148.4 9.4 %shard_map.80 = (bf16[8,128,512]{2,1,0:T(8,128)(2,1)}, bf16[8,128,512]{2,1,0:T(8,128)(2,1)}) custom-call(bf16[8,256,768]{2,1,0:T(8,128)(2,1)} %shard_map.77.hidden_ref, bf16[8,768,2048]{2,1,0:T(8,128)(2,1)} %down_ref.7, bf16[16,128,128]{2,1,0:T(8,128)(2,1)} %fusion.5.spread_ref), custom_call_target="tpu_custom_call" | custom-call | flops 1879048192 | bytes 11534336 | tf_op jit(solution)/shard_map/pallas_call | solution.py:128
  158.3 9.4 %shard_map.81 = (bf16[8,128,512]{2,1,0:T(8,128)(2,1)}, bf16[8,128,512]{2,1,0:T(8,128)(2,1)}) custom-call(bf16[8,256,768]{2,1,0:T(8,128)(2,1)} %shard_map.77.hidden_ref, bf16[8,768,2048]{2,1,0:T(8,128)(2,1)} %down_ref.7, bf16[16,128,128]{2,1,0:T(8,128)(2,1)} %fusion.5.spread_ref), custom_call_target="tpu_custom_call" | custom-call | flops 1879048192 | bytes 11534336 | tf_op jit(solution)/shard_map/pallas_call | solution.py:128
  178.1 7.6 %collective-permute-done.32 = bf16[128,512]{1,0:T(8,128)(2,1)S(1)} collective-permute-done((bf16[128,512]{1,0:T(8,128)(2,1)S(1)}, bf16[128,512]{1,0:T(8,128)(2,1)S(1)}, u32[]{:S(2)}, u32[]{:S(2)}) %collective-permute-start.32) | collective-permute-done | bytes 131104 | tf_op jit(solution)/shard_map/ppermute | solution.py:172
  189.3 4.8 %collective-permute-done.42 = bf16[128,512]{1,0:T(8,128)(2,1)S(1)} collective-permute-done((bf16[128,512]{1,0:T(8,128)(2,1)S(1)}, bf16[128,512]{1,0:T(8,128)(2,1)S(1)}, u32[]{:S(2)}, u32[]{:S(2)}) %collective-permute-start.42) | collective-permute-done | bytes 131104 | tf_op jit(solution)/shard_map/ppermute | solution.py:172
  204.7 5.5 %collective-permute-done.23 = bf16[128,512]{1,0:T(8,128)(2,1)S(1)} collective-permute-done((bf16[128,512]{1,0:T(8,128)(2,1)S(1)}, bf16[128,512]{1,0:T(8,128)(2,1)S(1)}, u32[]{:S(2)}, u32[]{:S(2)}) %collective-permute-start.23) | collective-permute-done | bytes 131104 | tf_op jit(solution)/shard_map/ppermute | solution.py:172
  211.6 5.8 %collective-permute-done.27 = bf16[128,512]{1,0:T(8,128)(2,1)S(1)} collective-permute-done((bf16[128,512]{1,0:T(8,128)(2,1)S(1)}, bf16[128,512]{1,0:T(8,128)(2,1)S(1)}, u32[]{:S(2)}, u32[]{:S(2)}) %collective-permute-start.27) | collective-permute-done | bytes 131104 | tf_op jit(solution)/shard_map/ppermute | solution.py:172
  218.7 6.9 %collective-permute-done.33 = bf16[128,512]{1,0:T(8,128)(2,1)S(1)} collective-permute-done((bf16[128,512]{1,0:T(8,128)(2,1)S(1)}, bf16[128,512]{1,0:T(8,128)(2,1)S(1)}, u32[]{:S(2)}, u32[]{:S(2)}) %collective-permute-start.33) | collective-permute-done | bytes 131104 | tf_op jit(solution)/shard_map/ppermute | solution.py:172
  226.9 6.0 %collective-permute-done.37 = bf16[128,512]{1,0:T(8,128)(2,1)S(1)} collective-permute-done((bf16[128,512]{1,0:T(8,128)(2,1)S(1)}, bf16[128,512]{1,0:T(8,128)(2,1)S(1)}, u32[]{:S(2)}, u32[]{:S(2)}) %collective-permute-start.37) | collective-permute-done | bytes 131104 | tf_op jit(solution)/shard_map/ppermute | solution.py:172
  234.3 5.5 %collective-permute-done.43 = bf16[128,512]{1,0:T(8,128)(2,1)S(1)} collective-permute-done((bf16[128,512]{1,0:T(8,128)(2,1)S(1)}, bf16[128,512]{1,0:T(8,128)(2,1)S(1)}, u32[]{:S(2)}, u32[]{:S(2)}) %collective-permute-start.43) | collective-permute-done | bytes 131104 | tf_op jit(solution)/shard_map/ppermute | solution.py:172
  241.1 5.5 %collective-permute-done.47 = bf16[128,512]{1,0:T(8,128)(2,1)S(1)} collective-permute-done((bf16[128,512]{1,0:T(8,128)(2,1)S(1)}, bf16[128,512]{1,0:T(8,128)(2,1)S(1)}, u32[]{:S(2)}, u32[]{:S(2)}) %collective-permute-start.47) | collective-permute-done | bytes 131104 | tf_op jit(solution)/shard_map/ppermute | solution.py:172
  248.0 5.5 %collective-permute-done.53 = bf16[128,512]{1,0:T(8,128)(2,1)S(1)} collective-permute-done((bf16[128,512]{1,0:T(8,128)(2,1)S(1)}, bf16[128,512]{1,0:T(8,128)(2,1)S(1)}, u32[]{:S(2)}, u32[]{:S(2)}) %collective-permute-start.53) | collective-permute-done | bytes 131104 | tf_op jit(solution)/shard_map/ppermute | solution.py:172
  254.8 5.5 %collective-permute-done.57 = bf16[128,512]{1,0:T(8,128)(2,1)S(1)} collective-permute-done((bf16[128,512]{1,0:T(8,128)(2,1)S(1)}, bf16[128,512]{1,0:T(8,128)(2,1)S(1)}, u32[]{:S(2)}, u32[]{:S(2)}) %collective-permute-start.57) | collective-permute-done | bytes 131104 | tf_op jit(solution)/shard_map/ppermute | solution.py:172
  264.0 4.1 %collective-permute-done.28 = bf16[128,512]{1,0:T(8,128)(2,1)S(1)} collective-permute-done((bf16[128,512]{1,0:T(8,128)(2,1)S(1)}, bf16[128,512]{1,0:T(8,128)(2,1)S(1)}, u32[]{:S(2)}, u32[]{:S(2)}) %collective-permute-start.28) | collective-permute-done | bytes 131104 | tf_op jit(solution)/shard_map/ppermute | solution.py:172
  271.6 4.1 %collective-permute-done.38 = bf16[128,512]{1,0:T(8,128)(2,1)S(1)} collective-permute-done((bf16[128,512]{1,0:T(8,128)(2,1)S(1)}, bf16[128,512]{1,0:T(8,128)(2,1)S(1)}, u32[]{:S(2)}, u32[]{:S(2)}) %collective-permute-start.38) | collective-permute-done | bytes 131104 | tf_op jit(solution)/shard_map/ppermute | solution.py:172
  278.5 4.9 %collective-permute-done.48 = bf16[128,512]{1,0:T(8,128)(2,1)S(1)} collective-permute-done((bf16[128,512]{1,0:T(8,128)(2,1)S(1)}, bf16[128,512]{1,0:T(8,128)(2,1)S(1)}, u32[]{:S(2)}, u32[]{:S(2)}) %collective-permute-start.48) | collective-permute-done | bytes 131104 | tf_op jit(solution)/shard_map/ppermute | solution.py:172
  (192 shorter events, 134.1 us)
Async XLA Ops:
  2.6 31.3 %collective-permute-start.10 = (bf16[128,1024]{1,0:T(8,128)(2,1)S(1)}, bf16[128,1024]{1,0:T(8,128)(2,1)S(1)}, u32[]{:S(2)}, u32[]{:S(2)}) collective-permute-start(bf16[128,1024]{1,0:T(8,128)(2,1)S(1)} %get-tuple-element.53), channel_id=1, source_target_pairs={{0,4},{1,5},{2,6},{3,7},{4,0},{5,1},{6,2},{7,3},{8,12},{9,13},{10,... | collective-permute-start | bytes 786440 | tf_op jit(solution)/shard_map/ppermute | solution.py:172
  2.6 27.0 %collective-permute-start.11 = (bf16[128,1024]{1,0:T(8,128)(2,1)S(1)}, bf16[128,1024]{1,0:T(8,128)(2,1)S(1)}, u32[]{:S(2)}, u32[]{:S(2)}) collective-permute-start(bf16[128,1024]{1,0:T(8,128)(2,1)S(1)} %get-tuple-element.53), channel_id=1, source_target_pairs={{4,8},{5,9},{6,10},{7,11},{8,4},{9,5},{10,6},{11,7},{20,24},{21,25... | collective-permute-start | bytes 786440 | tf_op jit(solution)/shard_map/ppermute | solution.py:172
  7.7 50.6 %collective-permute-start.15 = (bf16[128,1024]{1,0:T(8,128)(2,1)S(1)}, bf16[128,1024]{1,0:T(8,128)(2,1)S(1)}, u32[]{:S(2)}, u32[]{:S(2)}) collective-permute-start(bf16[128,1024]{1,0:T(8,128)(2,1)S(1)} %get-tuple-element.53), channel_id=1, source_target_pairs={{0,2},{2,0},{1,3},{3,1},{4,6},{6,4},{5,7},{7,5},{8,10},{10,8},{9,1... | collective-permute-start | bytes 786440 | tf_op jit(solution)/shard_map/ppermute | solution.py:172
  9.2 28.6 %collective-permute-start = (bf16[128,1024]{1,0:T(8,128)(2,1)S(1)}, bf16[128,1024]{1,0:T(8,128)(2,1)S(1)}, u32[]{:S(2)}, u32[]{:S(2)}) collective-permute-start(bf16[128,1024]{1,0:T(8,128)(2,1)S(1)} %get-tuple-element.54), channel_id=1, source_target_pairs={{0,4},{1,5},{2,6},{3,7},{4,0},{5,1},{6,2},{7,3},{8,12},{9,13},{10,... | collective-permute-start | bytes 786440 | tf_op jit(solution)/shard_map/ppermute | solution.py:172
  9.2 27.3 %collective-permute-start.1 = (bf16[128,1024]{1,0:T(8,128)(2,1)S(1)}, bf16[128,1024]{1,0:T(8,128)(2,1)S(1)}, u32[]{:S(2)}, u32[]{:S(2)}) collective-permute-start(bf16[128,1024]{1,0:T(8,128)(2,1)S(1)} %get-tuple-element.54), channel_id=1, source_target_pairs={{4,8},{5,9},{6,10},{7,11},{8,4},{9,5},{10,6},{11,7},{20,24},{21,25... | collective-permute-start | bytes 786440 | tf_op jit(solution)/shard_map/ppermute | solution.py:172
  42.5 27.5 %collective-permute-start.5 = (bf16[128,1024]{1,0:T(8,128)(2,1)S(1)}, bf16[128,1024]{1,0:T(8,128)(2,1)S(1)}, u32[]{:S(2)}, u32[]{:S(2)}) collective-permute-start(bf16[128,1024]{1,0:T(8,128)(2,1)S(1)} %get-tuple-element.54), channel_id=1, source_target_pairs={{0,2},{2,0},{1,3},{3,1},{4,6},{6,4},{5,7},{7,5},{8,10},{10,8},{9,1... | collective-permute-start | bytes 786440 | tf_op jit(solution)/shard_map/ppermute | solution.py:172
  47.1 13.2 %collective-permute-start.16 = (bf16[128,1024]{1,0:T(8,128)(2,1)S(1)}, bf16[128,1024]{1,0:T(8,128)(2,1)S(1)}, u32[]{:S(2)}, u32[]{:S(2)}) collective-permute-start(bf16[128,1024]{1,0:T(8,128)(2,1)S(1)} %collective-permute-done.10), channel_id=1, source_target_pairs={{0,2},{2,0},{1,3},{3,1},{4,6},{6,4},{5,7},{7,5},{8,10},{10,8},{9,1... | collective-permute-start | bytes 786440 | tf_op jit(solution)/shard_map/ppermute | solution.py:172
  52.0 18.8 %collective-permute-start.6 = (bf16[128,1024]{1,0:T(8,128)(2,1)S(1)}, bf16[128,1024]{1,0:T(8,128)(2,1)S(1)}, u32[]{:S(2)}, u32[]{:S(2)}) collective-permute-start(bf16[128,1024]{1,0:T(8,128)(2,1)S(1)} %collective-permute-done), channel_id=1, source_target_pairs={{0,2},{2,0},{1,3},{3,1},{4,6},{6,4},{5,7},{7,5},{8,10},{10,8},{9,1... | collective-permute-start | bytes 786440 | tf_op jit(solution)/shard_map/ppermute | solution.py:172
  58.3 16.0 %collective-permute-start.7 = (bf16[128,1024]{1,0:T(8,128)(2,1)S(1)}, bf16[128,1024]{1,0:T(8,128)(2,1)S(1)}, u32[]{:S(2)}, u32[]{:S(2)}) collective-permute-start(bf16[128,1024]{1,0:T(8,128)(2,1)S(1)} %get-tuple-element.28), channel_id=1, source_target_pairs={{0,2},{2,0},{1,3},{3,1},{4,6},{6,4},{5,7},{7,5},{8,10},{10,8},{9,1... | collective-permute-start | bytes 786440 | tf_op jit(solution)/shard_map/ppermute | solution.py:172
  60.3 19.5 %collective-permute-start.18 = (bf16[128,1024]{1,0:T(8,128)(2,1)S(1)}, bf16[128,1024]{1,0:T(8,128)(2,1)S(1)}, u32[]{:S(2)}, u32[]{:S(2)}) collective-permute-start(bf16[128,1024]{1,0:T(8,128)(2,1)S(1)} %get-tuple-element.22), channel_id=1, source_target_pairs={{0,2},{2,0},{1,3},{3,1},{4,6},{6,4},{5,7},{7,5},{8,10},{10,8},{9,1... | collective-permute-start | bytes 786440 | tf_op jit(solution)/shard_map/ppermute | solution.py:172
  68.6 15.3 %collective-permute-start.8 = (bf16[128,1024]{1,0:T(8,128)(2,1)S(1)}, bf16[128,1024]{1,0:T(8,128)(2,1)S(1)}, u32[]{:S(2)}, u32[]{:S(2)}) collective-permute-start(bf16[128,1024]{1,0:T(8,128)(2,1)S(1)} %get-tuple-element.26), channel_id=1, source_target_pairs={{0,2},{2,0},{1,3},{3,1},{4,6},{6,4},{5,7},{7,5},{8,10},{10,8},{9,1... | collective-permute-start | bytes 786440 | tf_op jit(solution)/shard_map/ppermute | solution.py:172
  80.6 17.2 %collective-permute-start.19 = (bf16[8,128,1024]{2,1,0:T(8,128)(2,1)}, bf16[8,128,1024]{2,1,0:T(8,128)(2,1)}, u32[]{:S(2)}, u32[]{:S(2)}) collective-permute-start(bf16[8,128,1024]{2,1,0:T(8,128)(2,1)} %bitcast_dynamic-update-slice_fusion.tokens_ref), channel_id=1, source_target_pairs={{0,1},{1,0},{2,3},{3,2},{4,5},{5,4},{6,7},{7,6},{8,9},{9,8},{10,11... | collective-permute-start | bytes 6291464 | tf_op jit(solution)/shard_map/ppermute | solution.py:172
  84.7 16.8 %collective-permute-start.9 = (bf16[8,128,1024]{2,1,0:T(8,128)(2,1)}, bf16[8,128,1024]{2,1,0:T(8,128)(2,1)}, u32[]{:S(2)}, u32[]{:S(2)}) collective-permute-start(bf16[8,128,1024]{2,1,0:T(8,128)(2,1)} %bitcast_dynamic-update-slice_fusion.8.tokens_ref), channel_id=1, source_target_pairs={{0,1},{1,0},{2,3},{3,2},{4,5},{5,4},{6,7},{7,6},{8,9},{9,8},{10,11... | collective-permute-start | bytes 6291464 | tf_op jit(solution)/shard_map/ppermute | solution.py:172
  138.5 29.3 %collective-permute-start.20 = (bf16[8,128,512]{2,1,0:T(8,128)(2,1)}, bf16[8,128,512]{2,1,0:T(8,128)(2,1)S(1)}, u32[]{:S(2)}, u32[]{:S(2)}) collective-permute-start(bf16[8,128,512]{2,1,0:T(8,128)(2,1)} %get-tuple-element.14), channel_id=1, source_target_pairs={{0,1},{1,0},{2,3},{3,2},{4,5},{5,4},{6,7},{7,6},{8,9},{9,8},{10,11... | collective-permute-start | bytes 3145736 | tf_op jit(solution)/shard_map/ppermute | solution.py:172
  148.4 21.8 %collective-permute-start.30 = (bf16[8,128,512]{2,1,0:T(8,128)(2,1)}, bf16[8,128,512]{2,1,0:T(8,128)(2,1)S(1)}, u32[]{:S(2)}, u32[]{:S(2)}) collective-permute-start(bf16[8,128,512]{2,1,0:T(8,128)(2,1)} %get-tuple-element.16), channel_id=1, source_target_pairs={{0,1},{1,0},{2,3},{3,2},{4,5},{5,4},{6,7},{7,6},{8,9},{9,8},{10,11... | collective-permute-start | bytes 3145736 | tf_op jit(solution)/shard_map/ppermute | solution.py:172
  157.8 13.5 %collective-permute-start.40 = (bf16[8,128,512]{2,1,0:T(8,128)(2,1)}, bf16[8,128,512]{2,1,0:T(8,128)(2,1)S(1)}, u32[]{:S(2)}, u32[]{:S(2)}) collective-permute-start(bf16[8,128,512]{2,1,0:T(8,128)(2,1)} %get-tuple-element.18), channel_id=1, source_target_pairs={{0,1},{1,0},{2,3},{3,2},{4,5},{5,4},{6,7},{7,6},{8,9},{9,8},{10,11... | collective-permute-start | bytes 3145736 | tf_op jit(solution)/shard_map/ppermute | solution.py:172
  170.2 92.4 %collective-permute-start.25 = (bf16[128,512]{1,0:T(8,128)(2,1)S(1)}, bf16[128,512]{1,0:T(8,128)(2,1)S(1)}, u32[]{:S(2)}, u32[]{:S(2)}) collective-permute-start(bf16[128,512]{1,0:T(8,128)(2,1)S(1)} %get-tuple-element.31), channel_id=1, source_target_pairs={{0,2},{2,0},{1,3},{3,1},{4,6},{6,4},{5,7},{7,5},{8,10},{10,8},{9,1... | collective-permute-start | bytes 393224 | tf_op jit(solution)/shard_map/ppermute | solution.py:172
  171.3 119.0 %collective-permute-start.21 = (bf16[128,512]{1,0:T(8,128)(2,1)S(1)}, bf16[128,512]{1,0:T(8,128)(2,1)S(1)}, u32[]{:S(2)}, u32[]{:S(2)}) collective-permute-start(bf16[128,512]{1,0:T(8,128)(2,1)S(1)} %get-tuple-element.29), channel_id=1, source_target_pairs={{0,2},{2,0},{1,3},{3,1},{4,6},{6,4},{5,7},{7,5},{8,10},{10,8},{9,1... | collective-permute-start | bytes 393224 | tf_op jit(solution)/shard_map/ppermute | solution.py:172
  174.5 14.0 %collective-permute-start.36 = (bf16[128,512]{1,0:T(8,128)(2,1)S(1)}, bf16[128,512]{1,0:T(8,128)(2,1)S(1)}, u32[]{:S(2)}, u32[]{:S(2)}) collective-permute-start(bf16[128,512]{1,0:T(8,128)(2,1)S(1)} %get-tuple-element.36), channel_id=1, source_target_pairs={{0,2},{2,0},{1,3},{3,1},{4,6},{6,4},{5,7},{7,5},{8,10},{10,8},{9,1... | collective-permute-start | bytes 393224 | tf_op jit(solution)/shard_map/ppermute | solution.py:172
  177.3 93.0 %collective-permute-start.35 = (bf16[128,512]{1,0:T(8,128)(2,1)S(1)}, bf16[128,512]{1,0:T(8,128)(2,1)S(1)}, u32[]{:S(2)}, u32[]{:S(2)}) collective-permute-start(bf16[128,512]{1,0:T(8,128)(2,1)S(1)} %get-tuple-element.37), channel_id=1, source_target_pairs={{0,2},{2,0},{1,3},{3,1},{4,6},{6,4},{5,7},{7,5},{8,10},{10,8},{9,1... | collective-permute-start | bytes 393224 | tf_op jit(solution)/shard_map/ppermute | solution.py:172
  199.9 96.4 %collective-permute-start.31 = (bf16[128,512]{1,0:T(8,128)(2,1)S(1)}, bf16[128,512]{1,0:T(8,128)(2,1)S(1)}, u32[]{:S(2)}, u32[]{:S(2)}) collective-permute-start(bf16[128,512]{1,0:T(8,128)(2,1)S(1)} %get-tuple-element.35), channel_id=1, source_target_pairs={{0,2},{2,0},{1,3},{3,1},{4,6},{6,4},{5,7},{7,5},{8,10},{10,8},{9,1... | collective-permute-start | bytes 393224 | tf_op jit(solution)/shard_map/ppermute | solution.py:172
  262.6 15.1 %collective-permute-start.45 = (bf16[128,512]{1,0:T(8,128)(2,1)S(1)}, bf16[128,512]{1,0:T(8,128)(2,1)S(1)}, u32[]{:S(2)}, u32[]{:S(2)}) collective-permute-start(bf16[128,512]{1,0:T(8,128)(2,1)S(1)} %get-tuple-element.43), channel_id=1, source_target_pairs={{0,2},{2,0},{1,3},{3,1},{4,6},{6,4},{5,7},{7,5},{8,10},{10,8},{9,1... | collective-permute-start | bytes 393224 | tf_op jit(solution)/shard_map/ppermute | solution.py:172
  270.3 32.9 %collective-permute-start.41 = (bf16[128,512]{1,0:T(8,128)(2,1)S(1)}, bf16[128,512]{1,0:T(8,128)(2,1)S(1)}, u32[]{:S(2)}, u32[]{:S(2)}) collective-permute-start(bf16[128,512]{1,0:T(8,128)(2,1)S(1)} %get-tuple-element.41), channel_id=1, source_target_pairs={{0,2},{2,0},{1,3},{3,1},{4,6},{6,4},{5,7},{7,5},{8,10},{10,8},{9,1... | collective-permute-start | bytes 393224 | tf_op jit(solution)/shard_map/ppermute | solution.py:172
  290.3 17.8 %collective-permute-start.51 = (bf16[128,512]{1,0:T(8,128)(2,1)S(1)}, bf16[128,512]{1,0:T(8,128)(2,1)S(1)}, u32[]{:S(2)}, u32[]{:S(2)}) collective-permute-start(bf16[128,512]{1,0:T(8,128)(2,1)S(1)} %get-tuple-element.47), channel_id=1, source_target_pairs={{0,2},{2,0},{1,3},{3,1},{4,6},{6,4},{5,7},{7,5},{8,10},{10,8},{9,1... | collective-permute-start | bytes 393224 | tf_op jit(solution)/shard_map/ppermute | solution.py:172
  (42 other events, 324.5 us)

commit v2 on v1

--- a/solution.py
+++ b/solution.py
@@ -9,7 +9,7 @@
 
 slots = 16
 gather_chunks = 2
-return_chunks = 4
+return_chunks = 2
 grant = 56 * 1024 * 1024
 
 
@@ -52,13 +52,14 @@
     )(picker, tokens)
 
 
-def hidden_kernel(chunks, *refs):
-    row_refs = refs[: 2 * chunks]
-    scale_ref, gate_ref, up_ref, hidden_ref = refs[2 * chunks :]
+def hidden_kernel(chunks, groups, *refs):
+    row_refs = refs[: chunks * groups]
+    scale_ref, gate_ref, up_ref, hidden_ref = refs[chunks * groups :]
     gate_part = None
     width = row_refs[0].shape[-1]
     for chunk in range(chunks):
-        rows = jnp.concatenate([row_refs[2 * chunk][0], row_refs[2 * chunk + 1][0]], axis=0)
+        pieces = [ref[0] for ref in row_refs[chunk * groups : (chunk + 1) * groups]]
+        rows = jnp.concatenate(pieces, axis=0)
         depth = pl.ds(chunk * width, width)
         gate_add = jnp.dot(rows, gate_ref[0, depth, :], preferred_element_type=jnp.float32)
         up_add = jnp.dot(rows, up_ref[0, depth, :], preferred_element_type=jnp.float32)
@@ -72,14 +73,14 @@
 
 def hidden_rows(row_chunks, scale, w_gate, w_up):
     experts, feature_dim, hidden_dim = w_gate.shape
-    half = row_chunks[0].shape[1]
-    chunks = len(row_chunks) // 2
-    width = row_chunks[0].shape[2]
-    whole = 2 * half
+    groups = len(row_chunks[0])
+    chunks = len(row_chunks)
+    pieces = [piece for row_groups in row_chunks for piece in row_groups]
+    whole = scale.shape[1]
     return pl.pallas_call(
-        functools.partial(hidden_kernel, chunks),
+        functools.partial(hidden_kernel, chunks, groups),
         grid=(experts,),
-        in_specs=[pl.BlockSpec((1, half, width), lambda e: (e, 0, 0))] * (2 * chunks)
+        in_specs=[pl.BlockSpec((1,) + piece.shape[1:], lambda e: (e, 0, 0)) for piece in pieces]
         + [
             pl.BlockSpec((1, whole, 1), lambda e: (e, 0, 0)),
             pl.BlockSpec((1, feature_dim, hidden_dim), lambda e: (e, 0, 0)),
@@ -93,7 +94,7 @@
             bytes_accessed=4 * experts * feature_dim * hidden_dim,
             transcendentals=experts * whole * hidden_dim,
         ),
-    )(*row_chunks, scale, w_gate, w_up)
+    )(*pieces, scale, w_gate, w_up)
 
 
 def mix_kernel(hidden_ref, down_ref, spread_ref, first_ref, second_ref, made):
@@ -172,29 +173,43 @@
     return lax.ppermute(value, axes, pairs)
 
 
+def together(*values):
+    return lax.optimization_barrier(values)
+
+
 def tree_gather(own, edge):
-    near = send(own, swap_z)
-    middle = send(own, middle_z)
-    cross = send(near, middle_z)
-    outer = send(middle, outward_z)
-    far = send(cross, outward_z)
+    near, middle, own_x = together(
+        send(own, swap_z), send(own, middle_z), send(own, swap_x)
+    )
+    cross, outer, near_x = together(
+        send(near, middle_z), send(middle, outward_z), send(near, swap_x)
+    )
     third = jnp.where(edge, outer, middle)
+    far, third_x = together(send(cross, outward_z), send(third, swap_x))
     fourth = jnp.where(edge, far, cross)
-    column = [own, near, third, fourth]
-    other = [send(value, swap_x) for value in column]
-    return jnp.stack(column + other)
-
-
-def tree_return(mine, theirs):
-    chip = rounded_sum(mine, send(theirs, swap_core))
-    arrived = [send(chip[4 + i], swap_x) for i in (3, 2, 1, 0)]
-    fourth, third, near, own = [
-        rounded_sum(chip[i], value) for i, value in zip((3, 2, 1, 0), arrived)
-    ]
-    cross = rounded_sum(fourth, send(fourth, inward_z))
-    middle = rounded_sum(third, send(third, inward_z))
-    near = rounded_sum(near, send(cross, middle_z))
-    return rounded_sum(own, send(middle, middle_z), send(near, swap_z))
+    early = jnp.stack([own, near, third, own_x, near_x, third_x])
+    fourth_x = send(fourth, swap_x)
+    return early, jnp.stack([fourth, fourth_x])
+
+
+def chip_sums(mine, theirs):
+    return rounded_sum(mine, send(theirs, swap_core))
+
+
+def tree_return(chip):
+    own, near, third, own_x, near_x, third_x, fourth, fourth_x = [chip[i] for i in range(8)]
+    fourth = rounded_sum(fourth, send(fourth_x, swap_x))
+    far, third_in = together(send(fourth, inward_z), send(third_x, swap_x))
+    cross = rounded_sum(fourth, far)
+    third = rounded_sum(third, third_in)
+    outer, crossed, near_in = together(
+        send(third, inward_z), send(cross, middle_z), send(near_x, swap_x)
+    )
+    middle = rounded_sum(third, outer)
+    near = rounded_sum(near, near_in, crossed)
+    return rounded_sum(
+        own, send(own_x, swap_x), send(middle, middle_z), send(near, swap_z)
+    )
 
 
 def slot_sources():
@@ -203,9 +218,10 @@
     x, core = dp // 2, dp % 2
     low = z < 2
     column = jnp.stack([z, z ^ 1, jnp.where(low, 2, 1), jnp.where(low, 3, 0)])
-    core_of = core ^ jnp.arange(2)[:, None, None]
-    x_of = x ^ jnp.arange(2)[None, :, None]
-    return (column[None, None, :] * 4 + x_of * 2 + core_of).reshape(-1)
+    slot_z = column[jnp.array([0, 1, 2, 0, 1, 2, 3, 3])]
+    slot_x = x ^ jnp.array([0, 0, 0, 1, 1, 1, 0, 1])
+    core_of = core ^ jnp.arange(2)[:, None]
+    return (slot_z * 4 + slot_x * 2 + core_of).reshape(-1)
 
 
 def shards(tokens, routes, route_weight, norm_gain, w_gate, w_up, w_down):
@@ -225,21 +241,21 @@
         * norm_gain
     ).astype(jnp.bfloat16)
 
-    choice = jnp.concatenate([routes.astype(jnp.float32).T, route_weight.T], axis=0)
-    choices = lax.all_gather(choice, axes)
+    every = jnp.arange(device_count * local_count, dtype=jnp.int32)
+    same = routes[:, :, None] == every
+    named = jnp.any(same, axis=1)
+    named_weight = jnp.sum(jnp.where(same, route_weight[:, :, None], 0.0), axis=1)
+    before = (jnp.arange(token_count)[:, None] > jnp.arange(token_count)[None, :]).astype(
+        jnp.bfloat16
+    )
+    rank = jnp.dot(before, named.astype(jnp.bfloat16), preferred_element_type=jnp.float32)
+    rank = jnp.where(named, rank, -1.0)
+    choice = jnp.stack([rank.T, named_weight.T]).reshape(2, device_count, local_count, token_count)
+    choice = choice.transpose(1, 0, 2, 3).reshape(device_count, 2 * local_count, token_count)
+    choices = lax.all_to_all(choice, axes, split_axis=0, concat_axis=0, tiled=True)
     if as_tree:
         choices = choices[slot_sources()]
-    chosen, weight = choices[:, :top_count], choices[:, top_count:]
-    first_expert = (lax.axis_index("expert") * dp_size + lax.axis_index("dp")) * local_count
-    local = (first_expert + jnp.arange(local_count)).astype(jnp.float32)
-    same = chosen[:, None] == local[None, :, None, None]
-    named = jnp.any(same, axis=2)
-    named_weight = jnp.sum(jnp.where(same, weight[:, None], 0.0), axis=2)
-    before = (jnp.arange(token_count)[:, None] < jnp.arange(token_count)[None, :]).astype(
-        jnp.bfloat16
-    )
-    rank = jnp.dot(named.astype(jnp.bfloat16), before, preferred_element_type=jnp.float32)
-    rank = jnp.where(named, rank, -1.0)
+    rank, named_weight = choices[:, :local_count], choices[:, local_count:]
     match = rank[:, :, None, :] == jnp.arange(slots, dtype=jnp.float32)[None, None, :, None]
     picker = match.astype(jnp.bfloat16).reshape(device_count, local_count * slots, token_count)
     spread = picker.transpose(0, 2, 1)
@@ -252,25 +268,30 @@
     for chunk in range(gather_chunks):
         part = normed[:, chunk * width : (chunk + 1) * width]
         if as_tree:
-            mine = tree_gather(part, edge)
-            theirs = send(mine, swap_core)
+            early, late = tree_gather(part, edge)
+            groups = [early, late, send(early, swap_core), send(late, swap_core)]
         else:
-            gathered = lax.all_gather(part, axes)
-            mine, theirs = gathered[:half], gathered[half:]
-        for value, which in ((mine, picker[:half]), (theirs, picker[half:])):
-            rows = pick_rows(which, value, local_count)
-            row_chunks.append(rows.reshape(local_count, half * slots, width))
+            groups = [lax.all_gather(part, axes)]
+        first = 0
+        row_groups = []
+        for group in groups:
+            count = group.shape[0]
+            rows = pick_rows(picker[first : first + count], group, local_count)
+            row_groups.append(rows.reshape(local_count, count * slots, width))
+            first += count
+        row_chunks.append(row_groups)
     hidden = hidden_rows(row_chunks, scale, w_gate, w_up)
 
-    results = []
+    sums = []
     for chunk in range(return_chunks):
         mine, theirs = mix_rows(hidden, w_down, spread, chunk, return_chunks)
         if as_tree:
-            results.append(tree_return(mine, theirs))
+            sums.append(chip_sums(mine, theirs))
         else:
             whole = jnp.concatenate([mine, theirs], axis=0).astype(jnp.float32)
             total = lax.psum_scatter(whole, axes, scatter_dimension=0)
-            results.append(total.astype(jnp.bfloat16))
+            sums.append(total.astype(jnp.bfloat16))
+    results = [tree_return(chip) for chip in sums] if as_tree else sums
     return jnp.concatenate(results, axis=1)
 
 

time: 314 us -> 228 us (0.73)
  waiting for transfers between devices: 114 us -> 66.8 us
  starting transfers between devices: 79.5 us -> 62.1 us
  blocking collectives: 17.3 us -> 0 us
  Pallas kernels: 76.3 us -> 71.9 us
    ppermute x60 -> x42, waiting for transfers between devices: 114 us -> 63.3 us  [send(): return lax.ppermute(value, axes, pairs)]
    ppermute x60 -> x42, starting transfers between devices: 79.5 us -> 57.3 us  [send(): return lax.ppermute(value, axes, pairs)]
    all_gather x1 -> x0, blocking collectives: 17.3 us -> none  [shards(): choices = lax.all_gather(choice, axes)]
    pallas_call x4 -> x2, Pallas kernels: 37.5 us -> 25.9 us  [mix_rows(): pl.pallas_call(mix_kernel, grid=(experts,), in_specs=[pl.BlockSpec((1, wh...]
    pallas_call x4 -> x8, Pallas kernels: 14.9 us -> 21.8 us  [pick_rows(): pl.pallas_call(pick_kernel, grid=(sources // block,), in_specs=[pl.BlockS...]
    all_to_all x0 -> x1, starting transfers between devices: none -> 4.77 us  [shards(): lax.all_to_all(choice, axes, split_axis=0, concat_axis=0, tiled=True)]
    all_to_all x0 -> x1, waiting for transfers between devices: none -> 3.5 us  [shards(): lax.all_to_all(choice, axes, split_axis=0, concat_axis=0, tiled=True)]
    unnamed x21 -> x31, local copies, waits for them, and re-layouts: 6.65 us -> 7.05 us
  transfers between devices with their start and end apart: 60 -> 43, of which waited for: 31 -> 17; matrix products, arithmetic and copies ran while one was open for 6% -> 9% of each run, Pallas kernels for 13% -> 14%
where the time goes in v2:
time: 228 us; the launch traced here: 227 us
  Pallas kernels  71.9 us (32%)
  waiting for transfers between devices  66.8 us (29%)
  starting transfers between devices  62.1 us (27%)
  local copies, waits for them, and re-layouts  13.8 us (6%)
  other arithmetic  11.1 us (5%)
    ppermute x42, waiting for transfers between devices, send(): return lax.ppermute(value, axes, pairs)  63.3 us
    ppermute x42, starting transfers between devices, send(): return lax.ppermute(value, axes, pairs)  57.3 us
    pallas_call x2, Pallas kernels, mix_rows(): pl.pallas_call(mix_kernel, grid=(experts,), in_specs=[pl.BlockSpec((1, wh...  25.9 us
    pallas_call x1, Pallas kernels, hidden_rows(): pl.pallas_call(functools.partial(hidden_kernel, chunks, groups), grid=(ex...  24.2 us
    pallas_call x8, Pallas kernels, pick_rows(): pl.pallas_call(pick_kernel, grid=(sources // block,), in_specs=[pl.BlockS...  21.8 us
    unnamed x31, local copies, waits for them, and re-layouts  7.05 us
    all_to_all x1, starting transfers between devices, shards(): lax.all_to_all(choice, axes, split_axis=0, concat_axis=0, tiled=True)  4.77 us
  transfers between devices with their start and end apart: 43, of which 17 were waited for; matrix products, arithmetic and copies ran while one was open for 9% of the time, Pallas kernels for 14%

profile of v2, /device:TPU:8, one launch (start us, length us, event | category | flops | bytes accessed | tf_op | source)
XLA Modules:
  0.0 226.5 jit_solution(5148349947640773107)
XLA Ops:
  2.7 5.0 %collective-permute-start.12 = (bf16[128,1024]{1,0:T(8,128)(2,1)S(1)}, bf16[128,1024]{1,0:T(8,128)(2,1)S(1)}, u32[]{:S(2)}, u32[]{:S(2)}) collective-permute-start(bf16[128,1024]{1,0:T(8,128)(2,1)S(1)} %get-tuple-element.77), channel_id=1, source_target_pairs={{4,8},{5,9},{6,10},{7,11},{8,4},{9,5},{10,6},{11,7},{20,24},{21,25... | collective-permute-start | bytes 786440 | tf_op jit(solution)/shard_map/ppermute | solution.py:173
  13.1 4.8 %all-to-all-start = ((f32[16,16,128]{2,1,0:T(8,128)}), f32[16,16,128]{2,1,0:T(8,128)S(1)}, u32[]{:S(2)}, u32[]{:S(2)}) async-start(f32[16,16,128]{2,1,0:T(8,128)} %copy_bitcast_fusion), calls=%async_computation | async-start | bytes 262144 | tf_op jit(solution)/shard_map/all_to_all | solution.py:255
  19.7 3.5 %all-to-all-done = f32[16,16,128]{2,1,0:T(8,128)S(1)} async-done(((f32[16,16,128]{2,1,0:T(8,128)}), f32[16,16,128]{2,1,0:T(8,128)S(1)}, u32[]{:S(2)}, u32[]{:S(2)}) %all-to-all-start) | async-done | bytes 131104 | tf_op jit(solution)/shard_map/all_to_all | solution.py:255
  29.7 3.4 %collective-permute-done.2 = bf16[128,1024]{1,0:T(8,128)(2,1)S(1)} collective-permute-done((bf16[128,1024]{1,0:T(8,128)(2,1)S(1)}, bf16[128,1024]{1,0:T(8,128)(2,1)S(1)}, u32[]{:S(2)}, u32[]{:S(2)}) %collective-permute-start.2) | collective-permute-done | bytes 262176 | tf_op jit(solution)/shard_map/ppermute | solution.py:173
  33.1 3.5 %collective-permute-start.3 = (bf16[128,1024]{1,0:T(8,128)(2,1)S(1)}, bf16[128,1024]{1,0:T(8,128)(2,1)S(1)}, u32[]{:S(2)}, u32[]{:S(2)}) collective-permute-start(bf16[128,1024]{1,0:T(8,128)(2,1)S(1)} %collective-permute-done), channel_id=1, source_target_pairs={{4,8},{5,9},{6,10},{7,11},{8,4},{9,5},{10,6},{11,7},{20,24},{21,25... | collective-permute-start | bytes 786440 | tf_op jit(solution)/shard_map/ppermute | solution.py:173
  41.2 4.0 %collective-permute-done.15 = bf16[128,1024]{1,0:T(8,128)(2,1)S(1)} collective-permute-done((bf16[128,1024]{1,0:T(8,128)(2,1)S(1)}, bf16[128,1024]{1,0:T(8,128)(2,1)S(1)}, u32[]{:S(2)}, u32[]{:S(2)}) %collective-permute-start.15) | collective-permute-done | bytes 262176 | tf_op jit(solution)/shard_map/ppermute | solution.py:173
  47.3 4.4 %collective-permute-start.17 = (bf16[128,1024]{1,0:T(8,128)(2,1)S(1)}, bf16[128,1024]{1,0:T(8,128)(2,1)S(1)}, u32[]{:S(2)}, u32[]{:S(2)}) collective-permute-start(bf16[128,1024]{1,0:T(8,128)(2,1)S(1)} %collective-permute-done.14), channel_id=1, source_target_pairs={{4,0},{5,1},{6,2},{7,3},{8,12},{9,13},{10,14},{11,15},{20,16},{21,... | collective-permute-start | bytes 786440 | tf_op jit(solution)/shard_map/ppermute | solution.py:173
  53.2 3.8 %collective-permute-start.6 = (bf16[128,1024]{1,0:T(8,128)(2,1)S(1)}, bf16[128,1024]{1,0:T(8,128)(2,1)S(1)}, u32[]{:S(2)}, u32[]{:S(2)}) collective-permute-start(bf16[128,1024]{1,0:T(8,128)(2,1)S(1)} %collective-permute-done.3), channel_id=1, source_target_pairs={{4,0},{5,1},{6,2},{7,3},{8,12},{9,13},{10,14},{11,15},{20,16},{21,... | collective-permute-start | bytes 786440 | tf_op jit(solution)/shard_map/ppermute | solution.py:173
  67.3 6.2 %collective-permute-done.19 = bf16[128,1024]{1,0:T(8,128)(2,1)S(1)} collective-permute-done((bf16[128,1024]{1,0:T(8,128)(2,1)S(1)}, bf16[128,1024]{1,0:T(8,128)(2,1)S(1)}, u32[]{:S(2)}, u32[]{:S(2)}) %collective-permute-start.19) | collective-permute-done | bytes 262176 | tf_op jit(solution)/shard_map/ppermute | solution.py:173
  73.7 4.7 %collective-permute-done.8 = bf16[128,1024]{1,0:T(8,128)(2,1)S(1)} collective-permute-done((bf16[128,1024]{1,0:T(8,128)(2,1)S(1)}, bf16[128,1024]{1,0:T(8,128)(2,1)S(1)}, u32[]{:S(2)}, u32[]{:S(2)}) %collective-permute-start.8) | collective-permute-done | bytes 262176 | tf_op jit(solution)/shard_map/ppermute | solution.py:173
  80.3 3.2 %shard_map.95 = bf16[8,6,16,1024]{3,2,1,0:T(8,128)(2,1)} custom-call(bf16[6,128,128]{2,1,0:T(8,128)(2,1)} %bitcast.128, bf16[6,128,1024]{2,1,0:T(8,128)(2,1)} %bitcast_dynamic-update-slice_fusion.tokens_ref), custom_call_target="tpu_custom_call" | custom-call | flops 201326592 | bytes 3145728 | tf_op jit(solution)/shard_map/pallas_call | solution.py:37
  83.5 3.2 %shard_map.91 = bf16[8,6,16,1024]{3,2,1,0:T(8,128)(2,1)} custom-call(bf16[6,128,128]{2,1,0:T(8,128)(2,1)} %bitcast.129, bf16[6,128,1024]{2,1,0:T(8,128)(2,1)} %bitcast_dynamic-update-slice_fusion.6.tokens_ref), custom_call_target="tpu_custom_call" | custom-call | flops 201326592 | bytes 3145728 | tf_op jit(solution)/shard_map/pallas_call | solution.py:37
  97.1 3.3 %shard_map.97 = bf16[8,6,16,1024]{3,2,1,0:T(8,128)(2,1)} custom-call(bf16[6,128,128]{2,1,0:T(8,128)(2,1)} %bitcast.126, bf16[6,128,1024]{2,1,0:T(8,128)(2,1)} %collective-permute-done.20.tokens_ref), custom_call_target="tpu_custom_call" | custom-call | flops 201326592 | bytes 3145728 | tf_op jit(solution)/shard_map/pallas_call | solution.py:37
  100.4 3.3 %shard_map.93 = bf16[8,6,16,1024]{3,2,1,0:T(8,128)(2,1)} custom-call(bf16[6,128,128]{2,1,0:T(8,128)(2,1)} %bitcast.127, bf16[6,128,1024]{2,1,0:T(8,128)(2,1)} %collective-permute-done.9.tokens_ref), custom_call_target="tpu_custom_call" | custom-call | flops 201326592 | bytes 3145728 | tf_op jit(solution)/shard_map/pallas_call | solution.py:37
  103.7 24.2 %shard_map.99.hidden_ref = bf16[8,256,768]{2,1,0:T(8,128)(2,1)} custom-call(bf16[8,96,1024]{2,1,0:T(8,128)(2,1)} %bitcast.118, bf16[8,32,1024]{2,1,0:T(8,128)(2,1)} %bitcast.123, bf16[8,96,1024]{2,1,0:T(8,128)(2,1)} %bitcast.120, bf16[8,32,1024]{2,1,0:T(8,128)(2,1)} %bitcast.125, bf16[8,96,1024]{2,1,0:T(8,128)(2,1)} %bitcast.117, ...), custom_call_target="tpu_custom_call" | custom-call | flops 12884901888 | bytes 50331648 | tf_op jit(solution)/shard_map/pallas_call | solution.py:80
  127.8 12.9 %shard_map.100 = (bf16[8,128,1024]{2,1,0:T(8,128)(2,1)}, bf16[8,128,1024]{2,1,0:T(8,128)(2,1)}) custom-call(bf16[8,256,768]{2,1,0:T(8,128)(2,1)} %shard_map.99.hidden_ref, bf16[8,768,2048]{2,1,0:T(8,128)(2,1)} %down_ref.3, bf16[16,128,128]{2,1,0:T(8,128)(2,1)} %fusion.5.spread_ref), custom_call_target="tpu_custom_call" | custom-call | flops 3758096384 | bytes 19922944 | tf_op jit(solution)/shard_map/pallas_call | solution.py:129
  141.2 13.0 %shard_map.101 = (bf16[8,128,1024]{2,1,0:T(8,128)(2,1)}, bf16[8,128,1024]{2,1,0:T(8,128)(2,1)}) custom-call(bf16[8,256,768]{2,1,0:T(8,128)(2,1)} %shard_map.99.hidden_ref, bf16[8,768,2048]{2,1,0:T(8,128)(2,1)} %down_ref.3, bf16[16,128,128]{2,1,0:T(8,128)(2,1)} %fusion.5.spread_ref), custom_call_target="tpu_custom_call" | custom-call | flops 3758096384 | bytes 19922944 | tf_op jit(solution)/shard_map/pallas_call | solution.py:129
  155.7 2.9 %collective-permute-done.32 = bf16[8,128,1024]{2,1,0:T(8,128)(2,1)S(1)} collective-permute-done((bf16[8,128,1024]{2,1,0:T(8,128)(2,1)}, bf16[8,128,1024]{2,1,0:T(8,128)(2,1)S(1)}, u32[]{:S(2)}, u32[]{:S(2)}) %collective-permute-start.32) | collective-permute-done | bytes 2097184 | tf_op jit(solution)/shard_map/ppermute | solution.py:173
  170.5 5.3 %collective-permute-done.26 = bf16[128,1024]{1,0:T(8,128)(2,1)S(1)} collective-permute-done((bf16[128,1024]{1,0:T(8,128)(2,1)S(1)}, bf16[128,1024]{1,0:T(8,128)(2,1)S(1)}, u32[]{:S(2)}, u32[]{:S(2)}) %collective-permute-start.26) | collective-permute-done | bytes 262176 | tf_op jit(solution)/shard_map/ppermute | solution.py:173
  177.5 15.1 %collective-permute-done.36 = bf16[128,1024]{1,0:T(8,128)(2,1)S(1)} collective-permute-done((bf16[128,1024]{1,0:T(8,128)(2,1)S(1)}, bf16[128,1024]{1,0:T(8,128)(2,1)S(1)}, u32[]{:S(2)}, u32[]{:S(2)}) %collective-permute-start.36) | collective-permute-done | bytes 262176 | tf_op jit(solution)/shard_map/ppermute | solution.py:173
  197.8 4.2 %collective-permute-done.28 = bf16[128,1024]{1,0:T(8,128)(2,1)S(1)} collective-permute-done((bf16[128,1024]{1,0:T(8,128)(2,1)S(1)}, bf16[128,1024]{1,0:T(8,128)(2,1)S(1)}, u32[]{:S(2)}, u32[]{:S(2)}) %collective-permute-start.28) | collective-permute-done | bytes 262176 | tf_op jit(solution)/shard_map/ppermute | solution.py:173
  206.3 3.0 %collective-permute-start.30 = (bf16[128,1024]{1,0:T(8,128)(2,1)S(1)}, bf16[128,1024]{1,0:T(8,128)(2,1)S(1)}, u32[]{:S(2)}, u32[]{:S(2)}) collective-permute-start(bf16[128,1024]{1,0:T(8,128)(2,1)S(1)} %add_convert_fusion.4), channel_id=1, source_target_pairs={{4,8},{5,9},{6,10},{7,11},{8,4},{9,5},{10,6},{11,7},{20,24},{21,25... | collective-permute-start | bytes 786440 | tf_op jit(solution)/shard_map/ppermute | solution.py:173
  212.0 3.7 %collective-permute-done.37 = bf16[128,1024]{1,0:T(8,128)(2,1)S(1)} collective-permute-done((bf16[128,1024]{1,0:T(8,128)(2,1)S(1)}, bf16[128,1024]{1,0:T(8,128)(2,1)S(1)}, u32[]{:S(2)}, u32[]{:S(2)}) %collective-permute-start.37) | collective-permute-done | bytes 262176 | tf_op jit(solution)/shard_map/ppermute | solution.py:173
  215.7 3.2 %collective-permute-start.40 = (bf16[128,1024]{1,0:T(8,128)(2,1)S(1)}, bf16[128,1024]{1,0:T(8,128)(2,1)S(1)}, u32[]{:S(2)}, u32[]{:S(2)}) collective-permute-start(bf16[128,1024]{1,0:T(8,128)(2,1)S(1)} %add_convert_fusion.2), channel_id=1, source_target_pairs={{4,8},{5,9},{6,10},{7,11},{8,4},{9,5},{10,6},{11,7},{20,24},{21,25... | collective-permute-start | bytes 786440 | tf_op jit(solution)/shard_map/ppermute | solution.py:173
  (161 shorter events, 82.0 us)
Async XLA Ops:
  2.6 21.2 %collective-permute-start.11 = (bf16[128,1024]{1,0:T(8,128)(2,1)S(1)}, bf16[128,1024]{1,0:T(8,128)(2,1)S(1)}, u32[]{:S(2)}, u32[]{:S(2)}) collective-permute-start(bf16[128,1024]{1,0:T(8,128)(2,1)S(1)} %get-tuple-element.77), channel_id=1, source_target_pairs={{0,4},{1,5},{2,6},{3,7},{4,0},{5,1},{6,2},{7,3},{8,12},{9,13},{10,... | collective-permute-start | bytes 786440 | tf_op jit(solution)/shard_map/ppermute | solution.py:173
  2.7 22.2 %collective-permute-start.12 = (bf16[128,1024]{1,0:T(8,128)(2,1)S(1)}, bf16[128,1024]{1,0:T(8,128)(2,1)S(1)}, u32[]{:S(2)}, u32[]{:S(2)}) collective-permute-start(bf16[128,1024]{1,0:T(8,128)(2,1)S(1)} %get-tuple-element.77), channel_id=1, source_target_pairs={{4,8},{5,9},{6,10},{7,11},{8,4},{9,5},{10,6},{11,7},{20,24},{21,25... | collective-permute-start | bytes 786440 | tf_op jit(solution)/shard_map/ppermute | solution.py:173
  7.7 17.1 %collective-permute-start.13 = (bf16[128,1024]{1,0:T(8,128)(2,1)S(1)}, bf16[128,1024]{1,0:T(8,128)(2,1)S(1)}, u32[]{:S(2)}, u32[]{:S(2)}) collective-permute-start(bf16[128,1024]{1,0:T(8,128)(2,1)S(1)} %get-tuple-element.77), channel_id=1, source_target_pairs={{0,2},{2,0},{1,3},{3,1},{4,6},{6,4},{5,7},{7,5},{8,10},{10,8},{9,1... | collective-permute-start | bytes 786440 | tf_op jit(solution)/shard_map/ppermute | solution.py:173
  9.3 20.5 %collective-permute-start = (bf16[128,1024]{1,0:T(8,128)(2,1)S(1)}, bf16[128,1024]{1,0:T(8,128)(2,1)S(1)}, u32[]{:S(2)}, u32[]{:S(2)}) collective-permute-start(bf16[128,1024]{1,0:T(8,128)(2,1)S(1)} %get-tuple-element.78), channel_id=1, source_target_pairs={{0,4},{1,5},{2,6},{3,7},{4,0},{5,1},{6,2},{7,3},{8,12},{9,13},{10,... | collective-permute-start | bytes 786440 | tf_op jit(solution)/shard_map/ppermute | solution.py:173
  9.3 20.5 %collective-permute-start.1 = (bf16[128,1024]{1,0:T(8,128)(2,1)S(1)}, bf16[128,1024]{1,0:T(8,128)(2,1)S(1)}, u32[]{:S(2)}, u32[]{:S(2)}) collective-permute-start(bf16[128,1024]{1,0:T(8,128)(2,1)S(1)} %get-tuple-element.78), channel_id=1, source_target_pairs={{4,8},{5,9},{6,10},{7,11},{8,4},{9,5},{10,6},{11,7},{20,24},{21,25... | collective-permute-start | bytes 786440 | tf_op jit(solution)/shard_map/ppermute | solution.py:173
  24.8 14.3 %collective-permute-start.14 = (bf16[128,1024]{1,0:T(8,128)(2,1)S(1)}, bf16[128,1024]{1,0:T(8,128)(2,1)S(1)}, u32[]{:S(2)}, u32[]{:S(2)}) collective-permute-start(bf16[128,1024]{1,0:T(8,128)(2,1)S(1)} %collective-permute-done.11), channel_id=1, source_target_pairs={{4,8},{5,9},{6,10},{7,11},{8,4},{9,5},{10,6},{11,7},{20,24},{21,25... | collective-permute-start | bytes 786440 | tf_op jit(solution)/shard_map/ppermute | solution.py:173
  27.8 13.4 %collective-permute-start.16 = (bf16[128,1024]{1,0:T(8,128)(2,1)S(1)}, bf16[128,1024]{1,0:T(8,128)(2,1)S(1)}, u32[]{:S(2)}, u32[]{:S(2)}) collective-permute-start(bf16[128,1024]{1,0:T(8,128)(2,1)S(1)} %collective-permute-done.11), channel_id=1, source_target_pairs={{0,2},{2,0},{1,3},{3,1},{4,6},{6,4},{5,7},{7,5},{8,10},{10,8},{9,1... | collective-permute-start | bytes 786440 | tf_op jit(solution)/shard_map/ppermute | solution.py:173
  33.1 18.6 %collective-permute-start.3 = (bf16[128,1024]{1,0:T(8,128)(2,1)S(1)}, bf16[128,1024]{1,0:T(8,128)(2,1)S(1)}, u32[]{:S(2)}, u32[]{:S(2)}) collective-permute-start(bf16[128,1024]{1,0:T(8,128)(2,1)S(1)} %collective-permute-done), channel_id=1, source_target_pairs={{4,8},{5,9},{6,10},{7,11},{8,4},{9,5},{10,6},{11,7},{20,24},{21,25... | collective-permute-start | bytes 786440 | tf_op jit(solution)/shard_map/ppermute | solution.py:173
  36.6 15.1 %collective-permute-start.5 = (bf16[128,1024]{1,0:T(8,128)(2,1)S(1)}, bf16[128,1024]{1,0:T(8,128)(2,1)S(1)}, u32[]{:S(2)}, u32[]{:S(2)}) collective-permute-start(bf16[128,1024]{1,0:T(8,128)(2,1)S(1)} %collective-permute-done), channel_id=1, source_target_pairs={{0,2},{2,0},{1,3},{3,1},{4,6},{6,4},{5,7},{7,5},{8,10},{10,8},{9,1... | collective-permute-start | bytes 786440 | tf_op jit(solution)/shard_map/ppermute | solution.py:173
  45.9 14.0 %collective-permute-start.18 = (bf16[128,1024]{1,0:T(8,128)(2,1)S(1)}, bf16[128,1024]{1,0:T(8,128)(2,1)S(1)}, u32[]{:S(2)}, u32[]{:S(2)}) collective-permute-start(bf16[128,1024]{1,0:T(8,128)(2,1)S(1)} %get-tuple-element.66), channel_id=1, source_target_pairs={{0,2},{2,0},{1,3},{3,1},{4,6},{6,4},{5,7},{7,5},{8,10},{10,8},{9,1... | collective-permute-start | bytes 786440 | tf_op jit(solution)/shard_map/ppermute | solution.py:173
  60.7 36.4 %collective-permute-start.20 = (bf16[6,128,1024]{2,1,0:T(8,128)(2,1)}, bf16[6,128,1024]{2,1,0:T(8,128)(2,1)}, u32[]{:S(2)}, u32[]{:S(2)}) collective-permute-start(bf16[6,128,1024]{2,1,0:T(8,128)(2,1)} %bitcast_dynamic-update-slice_fusion.tokens_ref), channel_id=1, source_target_pairs={{0,1},{1,0},{2,3},{3,2},{4,5},{5,4},{6,7},{7,6},{8,9},{9,8},{10,11... | collective-permute-start | bytes 4718600 | tf_op jit(solution)/shard_map/ppermute | solution.py:173
  61.6 38.8 %collective-permute-start.9 = (bf16[6,128,1024]{2,1,0:T(8,128)(2,1)}, bf16[6,128,1024]{2,1,0:T(8,128)(2,1)}, u32[]{:S(2)}, u32[]{:S(2)}) collective-permute-start(bf16[6,128,1024]{2,1,0:T(8,128)(2,1)} %bitcast_dynamic-update-slice_fusion.6.tokens_ref), channel_id=1, source_target_pairs={{0,1},{1,0},{2,3},{3,2},{4,5},{5,4},{6,7},{7,6},{8,9},{9,8},{10,11... | collective-permute-start | bytes 4718600 | tf_op jit(solution)/shard_map/ppermute | solution.py:173
  64.7 13.7 %collective-permute-start.8 = (bf16[128,1024]{1,0:T(8,128)(2,1)S(1)}, bf16[128,1024]{1,0:T(8,128)(2,1)S(1)}, u32[]{:S(2)}, u32[]{:S(2)}) collective-permute-start(bf16[128,1024]{1,0:T(8,128)(2,1)S(1)} %broadcast_select_fusion.2), channel_id=1, source_target_pairs={{0,2},{2,0},{1,3},{3,1},{4,6},{6,4},{5,7},{7,5},{8,10},{10,8},{9,1... | collective-permute-start | bytes 786440 | tf_op jit(solution)/shard_map/ppermute | solution.py:173
  73.6 17.5 %collective-permute-start.21 = (bf16[2,128,1024]{2,1,0:T(8,128)(2,1)S(1)}, bf16[2,128,1024]{2,1,0:T(8,128)(2,1)S(1)}, u32[]{:S(2)}, u32[]{:S(2)}) collective-permute-start(bf16[2,128,1024]{2,1,0:T(8,128)(2,1)S(1)} %pad_maximum_fusion.1.tokens_ref), channel_id=1, source_target_pairs={{0,1},{1,0},{2,3},{3,2},{4,5},{5,4},{6,7},{7,6},{8,9},{9,8},{10,11... | collective-permute-start | bytes 1572872 | tf_op jit(solution)/shard_map/ppermute | solution.py:173
  78.5 15.6 %collective-permute-start.10 = (bf16[2,128,1024]{2,1,0:T(8,128)(2,1)S(1)}, bf16[2,128,1024]{2,1,0:T(8,128)(2,1)S(1)}, u32[]{:S(2)}, u32[]{:S(2)}) collective-permute-start(bf16[2,128,1024]{2,1,0:T(8,128)(2,1)S(1)} %pad_maximum_fusion.tokens_ref), channel_id=1, source_target_pairs={{0,1},{1,0},{2,3},{3,2},{4,5},{5,4},{6,7},{7,6},{8,9},{9,8},{10,11... | collective-permute-start | bytes 1572872 | tf_op jit(solution)/shard_map/ppermute | solution.py:173
  140.7 13.5 %collective-permute-start.22 = (bf16[8,128,1024]{2,1,0:T(8,128)(2,1)}, bf16[8,128,1024]{2,1,0:T(8,128)(2,1)S(1)}, u32[]{:S(2)}, u32[]{:S(2)}) collective-permute-start(bf16[8,128,1024]{2,1,0:T(8,128)(2,1)} %get-tuple-element.52), channel_id=1, source_target_pairs={{0,1},{1,0},{2,3},{3,2},{4,5},{5,4},{6,7},{7,6},{8,9},{9,8},{10,11... | collective-permute-start | bytes 6291464 | tf_op jit(solution)/shard_map/ppermute | solution.py:173
  160.0 15.7 %collective-permute-start.26 = (bf16[128,1024]{1,0:T(8,128)(2,1)S(1)}, bf16[128,1024]{1,0:T(8,128)(2,1)S(1)}, u32[]{:S(2)}, u32[]{:S(2)}) collective-permute-start(bf16[128,1024]{1,0:T(8,128)(2,1)S(1)} %get-tuple-element.71), channel_id=1, source_target_pairs={{0,2},{2,0},{1,3},{3,1},{4,6},{6,4},{5,7},{7,5},{8,10},{10,8},{9,1... | collective-permute-start | bytes 786440 | tf_op jit(solution)/shard_map/ppermute | solution.py:173
  165.9 31.0 %collective-permute-start.29 = (bf16[128,1024]{1,0:T(8,128)(2,1)S(1)}, bf16[128,1024]{1,0:T(8,128)(2,1)S(1)}, u32[]{:S(2)}, u32[]{:S(2)}) collective-permute-start(bf16[128,1024]{1,0:T(8,128)(2,1)S(1)} %get-tuple-element.70), channel_id=1, source_target_pairs={{0,2},{2,0},{1,3},{3,1},{4,6},{6,4},{5,7},{7,5},{8,10},{10,8},{9,1... | collective-permute-start | bytes 786440 | tf_op jit(solution)/shard_map/ppermute | solution.py:173
  166.2 52.9 %collective-permute-start.23 = (bf16[128,1024]{1,0:T(8,128)(2,1)S(1)}, bf16[128,1024]{1,0:T(8,128)(2,1)S(1)}, u32[]{:S(2)}, u32[]{:S(2)}) collective-permute-start(bf16[128,1024]{1,0:T(8,128)(2,1)S(1)} %get-tuple-element.69), channel_id=1, source_target_pairs={{0,2},{2,0},{1,3},{3,1},{4,6},{6,4},{5,7},{7,5},{8,10},{10,8},{9,1... | collective-permute-start | bytes 786440 | tf_op jit(solution)/shard_map/ppermute | solution.py:173
  170.1 22.5 %collective-permute-start.36 = (bf16[128,1024]{1,0:T(8,128)(2,1)S(1)}, bf16[128,1024]{1,0:T(8,128)(2,1)S(1)}, u32[]{:S(2)}, u32[]{:S(2)}) collective-permute-start(bf16[128,1024]{1,0:T(8,128)(2,1)S(1)} %get-tuple-element.75), channel_id=1, source_target_pairs={{0,2},{2,0},{1,3},{3,1},{4,6},{6,4},{5,7},{7,5},{8,10},{10,8},{9,1... | collective-permute-start | bytes 786440 | tf_op jit(solution)/shard_map/ppermute | solution.py:173
  175.7 30.6 %collective-permute-start.39 = (bf16[128,1024]{1,0:T(8,128)(2,1)S(1)}, bf16[128,1024]{1,0:T(8,128)(2,1)S(1)}, u32[]{:S(2)}, u32[]{:S(2)}) collective-permute-start(bf16[128,1024]{1,0:T(8,128)(2,1)S(1)} %get-tuple-element.74), channel_id=1, source_target_pairs={{0,2},{2,0},{1,3},{3,1},{4,6},{6,4},{5,7},{7,5},{8,10},{10,8},{9,1... | collective-permute-start | bytes 786440 | tf_op jit(solution)/shard_map/ppermute | solution.py:173
  176.0 19.4 %collective-permute-start.35 = (bf16[128,1024]{1,0:T(8,128)(2,1)S(1)}, bf16[128,1024]{1,0:T(8,128)(2,1)S(1)}, u32[]{:S(2)}, u32[]{:S(2)}) collective-permute-start(bf16[128,1024]{1,0:T(8,128)(2,1)S(1)} %fusion.8), channel_id=1, source_target_pairs={{0,4},{1,5},{2,6},{3,7},{12,8},{13,9},{14,10},{15,11},{16,20},{17,... | collective-permute-start | bytes 786440 | tf_op jit(solution)/shard_map/ppermute | solution.py:173
  196.9 24.5 %collective-permute-start.33 = (bf16[128,1024]{1,0:T(8,128)(2,1)S(1)}, bf16[128,1024]{1,0:T(8,128)(2,1)S(1)}, u32[]{:S(2)}, u32[]{:S(2)}) collective-permute-start(bf16[128,1024]{1,0:T(8,128)(2,1)S(1)} %get-tuple-element.73), channel_id=1, source_target_pairs={{0,2},{2,0},{1,3},{3,1},{4,6},{6,4},{5,7},{7,5},{8,10},{10,8},{9,1... | collective-permute-start | bytes 786440 | tf_op jit(solution)/shard_map/ppermute | solution.py:173
  206.3 12.9 %collective-permute-start.30 = (bf16[128,1024]{1,0:T(8,128)(2,1)S(1)}, bf16[128,1024]{1,0:T(8,128)(2,1)S(1)}, u32[]{:S(2)}, u32[]{:S(2)}) collective-permute-start(bf16[128,1024]{1,0:T(8,128)(2,1)S(1)} %add_convert_fusion.4), channel_id=1, source_target_pairs={{4,8},{5,9},{6,10},{7,11},{8,4},{9,5},{10,6},{11,7},{20,24},{21,25... | collective-permute-start | bytes 786440 | tf_op jit(solution)/shard_map/ppermute | solution.py:173
  (30 other events, 267.9 us)

commit v3 on v2

--- a/solution.py
+++ b/solution.py
@@ -10,7 +10,11 @@
 slots = 16
 gather_chunks = 2
 return_chunks = 2
-grant = 56 * 1024 * 1024
+mebi = 1024 * 1024
+
+
+def grant(sources, tree_mebi):
+    return (tree_mebi if sources <= 16 else 56) * mebi
 
 
 def rounded_sum(first, *others):
@@ -43,7 +47,7 @@
         ],
         out_specs=pl.BlockSpec((experts, block, slots, width), lambda i: (0, i, 0, 0)),
         out_shape=jax.ShapeDtypeStruct((experts, sources, slots, width), jnp.bfloat16),
-        compiler_params=pltpu.CompilerParams(vmem_limit_bytes=grant),
+        compiler_params=pltpu.CompilerParams(vmem_limit_bytes=grant(sources, 16)),
         cost_estimate=pl.CostEstimate(
             flops=2 * sources * experts * slots * token_count * width,
             bytes_accessed=2 * sources * width * (token_count + experts * slots),
@@ -52,13 +56,106 @@
     )(picker, tokens)
 
 
-def hidden_kernel(chunks, groups, *refs):
+def table_kernel(source_ref, choices_ref, *refs):
+    picker_refs, spread_ref, scale_ref = refs[:3], refs[3], refs[4]
+    experts = scale_ref.shape[0]
+    token_count = choices_ref.shape[2]
+    early, late = picker_refs[0].shape[0], picker_refs[2].shape[0] // 2
+    place = lax.broadcasted_iota(jnp.int32, (experts, slots, token_count), 1).astype(jnp.float32)
+    for slot in range(2 * (early + late)):
+        choice = choices_ref[source_ref[slot]]
+        match = choice[:experts][:, None, :] == place
+        weight = jnp.where(match, choice[experts:][:, None, :], 0.0)
+        scale_ref[:, slot * slots : (slot + 1) * slots, :] = jnp.sum(weight, axis=2, keepdims=True)
+        picker = jnp.where(match, 1.0, 0.0).reshape(experts * slots, token_count)
+        if slot < 2 * early:
+            picker_refs[slot // early][slot % early] = picker.astype(jnp.bfloat16)
+        else:
+            picker_refs[2][slot - 2 * early] = picker.astype(jnp.bfloat16)
+        spread_ref[slot] = picker.T.astype(jnp.bfloat16)
+
+
+def tables(source, choices, experts):
+    count, _, token_count = choices.shape
+    rows = experts * slots
+    late = count // 8
+    early = count // 2 - late
+    shapes = [(early, rows, token_count), (early, rows, token_count), (2 * late, rows, token_count)]
+    shapes = [jax.ShapeDtypeStruct(shape, jnp.bfloat16) for shape in shapes]
+    shapes.append(jax.ShapeDtypeStruct((count, token_count, rows), jnp.bfloat16))
+    shapes.append(jax.ShapeDtypeStruct((experts, count * slots, 1), jnp.float32))
+    return pl.pallas_call(
+        table_kernel,
+        in_specs=[
+            pl.BlockSpec(memory_space=pltpu.SMEM),
+            pl.BlockSpec(memory_space=pltpu.VMEM),
+        ],
+        out_specs=[pl.BlockSpec(memory_space=pltpu.VMEM)] * 5,
+        out_shape=shapes,
+        compiler_params=pltpu.CompilerParams(vmem_limit_bytes=grant(count, 12)),
+    )(source, choices)
+
+
+def pair_kernel(count, *refs):
+    token_refs = refs[:count]
+    mine_ref, theirs_ref, mine_rows_ref, theirs_rows_ref = refs[count:]
+    experts = mine_rows_ref.shape[0]
+    for source in range(count):
+        for picker_ref, rows_ref in ((mine_ref, mine_rows_ref), (theirs_ref, theirs_rows_ref)):
+            picked = jnp.dot(
+                picker_ref[source], token_refs[source][...], preferred_element_type=jnp.float32
+            ).astype(jnp.bfloat16)
+            rows_ref[:, source] = picked.reshape(experts, slots, picked.shape[1])
+
+
+def pick_pair(blocks, mine, theirs, experts):
+    count = len(blocks)
+    token_count, width = blocks[0].shape
+    rows = jax.ShapeDtypeStruct((experts, count, slots, width), jnp.bfloat16)
+    return pl.pallas_call(
+        functools.partial(pair_kernel, count),
+        in_specs=[pl.BlockSpec(memory_space=pltpu.VMEM)] * (count + 2),
+        out_specs=[pl.BlockSpec(memory_space=pltpu.VMEM)] * 2,
+        out_shape=[rows, rows],
+        compiler_params=pltpu.CompilerParams(vmem_limit_bytes=grant(count, 16)),
+        cost_estimate=pl.CostEstimate(
+            flops=4 * count * experts * slots * token_count * width,
+            bytes_accessed=2 * count * width * (token_count + 2 * experts * slots),
+            transcendentals=0,
+        ),
+    )(*blocks, mine, theirs)
+
+
+def hidden_kernel(chunks, groups, late, *refs):
     row_refs = refs[: chunks * groups]
-    scale_ref, gate_ref, up_ref, hidden_ref = refs[chunks * groups :]
+    refs = refs[chunks * groups :]
+    late_refs = refs[: chunks * late]
+    refs = refs[chunks * late :]
+    width = row_refs[0].shape[-1]
+    if late:
+        picker_ref, scale_ref, gate_ref, up_ref, hidden_ref, late_rows = refs
+
+        @pl.when(pl.program_id(0) == 0)
+        def _():
+            for chunk in range(chunks):
+                for source in range(late):
+                    picked = jnp.dot(
+                        picker_ref[source],
+                        late_refs[chunk * late + source][...],
+                        preferred_element_type=jnp.float32,
+                    ).astype(jnp.bfloat16)
+                    late_rows[:, source, :, chunk * width : (chunk + 1) * width] = picked.reshape(
+                        late_rows.shape[0], slots, width
+                    )
+
+    else:
+        scale_ref, gate_ref, up_ref, hidden_ref = refs
     gate_part = None
-    width = row_refs[0].shape[-1]
     for chunk in range(chunks):
         pieces = [ref[0] for ref in row_refs[chunk * groups : (chunk + 1) * groups]]
+        if late:
+            extra = late_rows[pl.program_id(0), :, :, chunk * width : (chunk + 1) * width]
+            pieces.append(extra.reshape(late * slots, width))
         rows = jnp.concatenate(pieces, axis=0)
         depth = pl.ds(chunk * width, width)
         gate_add = jnp.dot(rows, gate_ref[0, depth, :], preferred_element_type=jnp.float32)
@@ -71,16 +168,21 @@
     hidden_ref[0] = hidden.astype(jnp.bfloat16)
 
 
-def hidden_rows(row_chunks, scale, w_gate, w_up):
+def hidden_rows(row_chunks, late_chunks, late_picker, scale, w_gate, w_up):
     experts, feature_dim, hidden_dim = w_gate.shape
-    groups = len(row_chunks[0])
-    chunks = len(row_chunks)
+    chunks, groups, late = len(row_chunks), len(row_chunks[0]), len(late_chunks[0])
     pieces = [piece for row_groups in row_chunks for piece in row_groups]
+    late_pieces = [piece for blocks in late_chunks for piece in blocks]
+    scratch = []
+    if late:
+        late_pieces.append(late_picker)
+        scratch = [pltpu.VMEM((experts, late, slots, feature_dim), jnp.bfloat16)]
     whole = scale.shape[1]
     return pl.pallas_call(
-        functools.partial(hidden_kernel, chunks, groups),
+        functools.partial(hidden_kernel, chunks, groups, late),
         grid=(experts,),
         in_specs=[pl.BlockSpec((1,) + piece.shape[1:], lambda e: (e, 0, 0)) for piece in pieces]
+        + [pl.BlockSpec(memory_space=pltpu.VMEM)] * len(late_pieces)
         + [
             pl.BlockSpec((1, whole, 1), lambda e: (e, 0, 0)),
             pl.BlockSpec((1, feature_dim, hidden_dim), lambda e: (e, 0, 0)),
@@ -88,56 +190,59 @@
         ],
         out_specs=pl.BlockSpec((1, whole, hidden_dim), lambda e: (e, 0, 0)),
         out_shape=jax.ShapeDtypeStruct((experts, whole, hidden_dim), jnp.bfloat16),
-        compiler_params=pltpu.CompilerParams(vmem_limit_bytes=grant),
+        scratch_shapes=scratch,
+        compiler_params=pltpu.CompilerParams(vmem_limit_bytes=grant(whole // slots, 32)),
         cost_estimate=pl.CostEstimate(
             flops=4 * experts * whole * feature_dim * hidden_dim,
             bytes_accessed=4 * experts * feature_dim * hidden_dim,
             transcendentals=experts * whole * hidden_dim,
         ),
-    )(*pieces, scale, w_gate, w_up)
-
-
-def mix_kernel(hidden_ref, down_ref, spread_ref, first_ref, second_ref, made):
-    expert = pl.program_id(0)
-    experts = pl.num_programs(0)
+    )(*pieces, *late_pieces, scale, w_gate, w_up)
+
+
+def mix_kernel(order, hidden_ref, down_ref, spread_ref, first_ref, second_ref, made):
+    step = pl.program_id(0)
+    group = hidden_ref.shape[0]
     sources = spread_ref.shape[0]
     width = down_ref.shape[2]
-    made[expert] = (
-        jnp.dot(hidden_ref[0], down_ref[0], preferred_element_type=jnp.float32)
-        .astype(jnp.bfloat16)
-        .reshape(sources, slots, width)
-    )
-
-    @pl.when(expert == experts - 1)
+    for one in range(group):
+        made[step * group + one] = (
+            jnp.dot(hidden_ref[one], down_ref[one], preferred_element_type=jnp.float32)
+            .astype(jnp.bfloat16)
+            .reshape(sources, slots, width)
+        )
+
+    @pl.when(step == pl.num_programs(0) - 1)
     def _():
         for source in range(sources):
             rows = made[:, source].reshape(spread_ref.shape[2], width)
             mixed = jnp.dot(
                 spread_ref[source], rows, preferred_element_type=jnp.float32
             ).astype(jnp.bfloat16)
-            if source < sources // 2:
-                first_ref[source] = mixed
+            if order[source] < sources // 2:
+                first_ref[order[source]] = mixed
             else:
-                second_ref[source - sources // 2] = mixed
-
-
-def mix_rows(hidden, w_down, spread, chunk, chunks):
+                second_ref[order[source] - sources // 2] = mixed
+
+
+def mix_rows(hidden, w_down, spread, order, chunk, chunks):
     experts, whole, hidden_dim = hidden.shape
     width = w_down.shape[2] // chunks
     sources, token_count, local_rows = spread.shape
+    group = 2 if experts % 2 == 0 else 1
     half = jax.ShapeDtypeStruct((sources // 2, token_count, width), jnp.bfloat16)
     return pl.pallas_call(
-        mix_kernel,
-        grid=(experts,),
+        functools.partial(mix_kernel, order),
+        grid=(experts // group,),
         in_specs=[
-            pl.BlockSpec((1, whole, hidden_dim), lambda e: (e, 0, 0)),
-            pl.BlockSpec((1, hidden_dim, width), lambda e: (e, 0, chunk)),
+            pl.BlockSpec((group, whole, hidden_dim), lambda e: (e, 0, 0)),
+            pl.BlockSpec((group, hidden_dim, width), lambda e: (e, 0, chunk)),
             pl.BlockSpec(memory_space=pltpu.VMEM),
         ],
         out_specs=[pl.BlockSpec(memory_space=pltpu.VMEM)] * 2,
         out_shape=[half, half],
         scratch_shapes=[pltpu.VMEM((experts, sources, slots, width), jnp.bfloat16)],
-        compiler_params=pltpu.CompilerParams(vmem_limit_bytes=grant),
+        compiler_params=pltpu.CompilerParams(vmem_limit_bytes=grant(sources, 28)),
         cost_estimate=pl.CostEstimate(
             flops=2 * experts * whole * hidden_dim * width
             + 2 * sources * token_count * local_rows * width,
@@ -177,19 +282,32 @@
     return lax.optimization_barrier(values)
 
 
-def tree_gather(own, edge):
+def tree_start(own):
     near, middle, own_x = together(
         send(own, swap_z), send(own, middle_z), send(own, swap_x)
     )
-    cross, outer, near_x = together(
-        send(near, middle_z), send(middle, outward_z), send(near, swap_x)
-    )
+    return near, middle, own_x
+
+
+def tree_second(near, middle, *others):
+    return together(
+        send(near, middle_z), send(middle, outward_z), send(near, swap_x), *others
+    )
+
+
+def tree_third(cross, outer, middle, edge, *others):
     third = jnp.where(edge, outer, middle)
-    far, third_x = together(send(cross, outward_z), send(third, swap_x))
-    fourth = jnp.where(edge, far, cross)
-    early = jnp.stack([own, near, third, own_x, near_x, third_x])
-    fourth_x = send(fourth, swap_x)
-    return early, jnp.stack([fourth, fourth_x])
+    far, third_x, *others = together(send(cross, outward_z), send(third, swap_x), *others)
+    return third, third_x, jnp.where(edge, far, cross), *others
+
+
+def tree_rest(early, fourth, mine, theirs, experts):
+    mine_rows, theirs_rows, fourth_x = together(
+        *pick_pair(early, mine, theirs, experts), send(fourth, swap_x)
+    )
+    late = [fourth, fourth_x]
+    rows = [mine_rows, send(theirs_rows, swap_core)]
+    return rows, late + [send(block, swap_core) for block in late]
 
 
 def chip_sums(mine, theirs):
@@ -198,12 +316,15 @@
 
 def tree_return(chip):
     own, near, third, own_x, near_x, third_x, fourth, fourth_x = [chip[i] for i in range(8)]
-    fourth = rounded_sum(fourth, send(fourth_x, swap_x))
-    far, third_in = together(send(fourth, inward_z), send(third_x, swap_x))
+    fourth_in, third_x, near_x, own_x = together(send(fourth_x, swap_x), third_x, near_x, own_x)
+    fourth = rounded_sum(fourth, fourth_in)
+    far, third_in, near_x, own_x = together(
+        send(fourth, inward_z), send(third_x, swap_x), near_x, own_x
+    )
     cross = rounded_sum(fourth, far)
     third = rounded_sum(third, third_in)
-    outer, crossed, near_in = together(
-        send(third, inward_z), send(cross, middle_z), send(near_x, swap_x)
+    outer, crossed, near_in, own_x = together(
+        send(third, inward_z), send(cross, middle_z), send(near_x, swap_x), own_x
     )
     middle = rounded_sum(third, outer)
     near = rounded_sum(near, near_in, crossed)
@@ -218,10 +339,15 @@
     x, core = dp // 2, dp % 2
     low = z < 2
     column = jnp.stack([z, z ^ 1, jnp.where(low, 2, 1), jnp.where(low, 3, 0)])
-    slot_z = column[jnp.array([0, 1, 2, 0, 1, 2, 3, 3])]
-    slot_x = x ^ jnp.array([0, 0, 0, 1, 1, 1, 0, 1])
-    core_of = core ^ jnp.arange(2)[:, None]
-    return (slot_z * 4 + slot_x * 2 + core_of).reshape(-1)
+    early = jnp.array([0, 1, 2, 0, 1, 2]), jnp.array([0, 0, 0, 1, 1, 1])
+    late = jnp.array([3, 3]), jnp.array([0, 1])
+
+    def device(which, core_of):
+        return column[which[0]] * 4 + (x ^ which[1]) * 2 + core_of
+
+    return jnp.concatenate(
+        [device(early, core), device(early, 1 - core), device(late, core), device(late, 1 - core)]
+    )
 
 
 def shards(tokens, routes, route_weight, norm_gain, w_gate, w_up, w_down):
@@ -253,38 +379,46 @@
     choice = jnp.stack([rank.T, named_weight.T]).reshape(2, device_count, local_count, token_count)
     choice = choice.transpose(1, 0, 2, 3).reshape(device_count, 2 * local_count, token_count)
     choices = lax.all_to_all(choice, axes, split_axis=0, concat_axis=0, tiled=True)
+
+    width = feature_dim // gather_chunks
+    parts = [normed[:, chunk * width : (chunk + 1) * width] for chunk in range(gather_chunks)]
     if as_tree:
-        choices = choices[slot_sources()]
-    rank, named_weight = choices[:, :local_count], choices[:, local_count:]
-    match = rank[:, :, None, :] == jnp.arange(slots, dtype=jnp.float32)[None, None, :, None]
-    picker = match.astype(jnp.bfloat16).reshape(device_count, local_count * slots, token_count)
-    spread = picker.transpose(0, 2, 1)
-    scale = jnp.sum(jnp.where(match, named_weight[:, :, None, :], 0.0), axis=3)
-    scale = scale.transpose(1, 0, 2).reshape(local_count, device_count * slots, 1)
-
-    width = feature_dim // gather_chunks
-    half = device_count // 2
-    row_chunks = []
-    for chunk in range(gather_chunks):
-        part = normed[:, chunk * width : (chunk + 1) * width]
-        if as_tree:
-            early, late = tree_gather(part, edge)
-            groups = [early, late, send(early, swap_core), send(late, swap_core)]
-        else:
-            groups = [lax.all_gather(part, axes)]
-        first = 0
-        row_groups = []
-        for group in groups:
-            count = group.shape[0]
-            rows = pick_rows(picker[first : first + count], group, local_count)
-            row_groups.append(rows.reshape(local_count, count * slots, width))
-            first += count
-        row_chunks.append(row_groups)
-    hidden = hidden_rows(row_chunks, scale, w_gate, w_up)
+        firsts = [tree_start(part) for part in parts]
+        seconds = []
+        for near, middle, own_x in firsts:
+            cross, outer, near_x, choices = tree_second(near, middle, choices)
+            seconds.append((cross, outer, near_x))
+        mine, theirs, late_picker, spread, scale = tables(slot_sources(), choices, local_count)
+        theirs = send(theirs, swap_core)
+        thirds = []
+        for (near, middle, own_x), (cross, outer, near_x) in zip(firsts, seconds):
+            third, third_x, fourth, theirs = tree_third(cross, outer, middle, edge, theirs)
+            thirds.append((third, third_x, fourth))
+        order = (0, 1, 2, 3, 4, 5, 8, 9, 10, 11, 12, 13, 6, 7, 14, 15)
+        row_chunks, late_chunks = [], []
+        for part, (near, middle, own_x), (cross, outer, near_x), (third, third_x, fourth) in zip(
+            parts, firsts, seconds, thirds
+        ):
+            early = part, near, third, own_x, near_x, third_x
+            rows, late = tree_rest(early, fourth, mine, theirs, local_count)
+            row_chunks.append([rows_of.reshape(local_count, -1, width) for rows_of in rows])
+            late_chunks.append(late)
+    else:
+        rank, named_weight = choices[:, :local_count], choices[:, local_count:]
+        match = rank[:, :, None, :] == jnp.arange(slots, dtype=jnp.float32)[None, None, :, None]
+        picker = match.astype(jnp.bfloat16).reshape(device_count, local_count * slots, token_count)
+        scale = jnp.sum(jnp.where(match, named_weight[:, :, None, :], 0.0), axis=3)
+        scale = scale.transpose(1, 0, 2).reshape(local_count, device_count * slots, 1)
+        spread = picker.transpose(0, 2, 1)
+        rows = [pick_rows(picker, lax.all_gather(part, axes), local_count) for part in parts]
+        row_chunks = [[rows_of.reshape(local_count, -1, width)] for rows_of in rows]
+        late_chunks, late_picker = [[]] * gather_chunks, None
+        order = tuple(range(device_count))
+    hidden = hidden_rows(row_chunks, late_chunks, late_picker, scale, w_gate, w_up)
 
     sums = []
     for chunk in range(return_chunks):
-        mine, theirs = mix_rows(hidden, w_down, spread, chunk, return_chunks)
+        mine, theirs = mix_rows(hidden, w_down, spread, order, chunk, return_chunks)
         if as_tree:
             sums.append(chip_sums(mine, theirs))
         else:

time: 228 us -> 172 us (0.75)
  Pallas kernels: 71.9 us -> 41.1 us
  waiting for transfers between devices: 66.8 us -> 48.6 us
  local copies, waits for them, and re-layouts: 13.8 us -> 2.44 us
  starting transfers between devices: 62.1 us -> 68.6 us
    pallas_call x11 -> x6, Pallas kernels: 71.9 us -> 41.1 us  [the longest x1 21.6 us: hidden_rows(): pl.pallas_call(functools.partial(hidden_kernel, chunks, groups, late), gr...]
    ppermute x42 -> x45, waiting for transfers between devices: 63.3 us -> 48.6 us  [send(): return lax.ppermute(value, axes, pairs)]
    unnamed x31 -> x6, local copies, waits for them, and re-layouts: 7.05 us -> 0.21 us
    ppermute x42 -> x45, starting transfers between devices: 57.3 us -> 61.9 us  [send(): return lax.ppermute(value, axes, pairs)]
    all_to_all x1, waiting for transfers between devices: 3.5 us -> 0.01 us  [shards(): lax.all_to_all(choice, axes, split_axis=0, concat_axis=0, tiled=True)]
  transfers between devices with their start and end apart: 43 -> 46, of which waited for: 17 -> 23; matrix products, arithmetic and copies ran while one was open for 9% -> 5% of each run, Pallas kernels for 14% -> 7%
where the time goes in v3:
time: 172 us; the launch traced here: 171 us
  starting transfers between devices  68.6 us (40%)
  waiting for transfers between devices  48.6 us (28%)
  Pallas kernels  41.1 us (24%)
  other arithmetic  9.39 us (5%)
  local copies, waits for them, and re-layouts  2.44 us (1%)
    ppermute x45, starting transfers between devices, send(): return lax.ppermute(value, axes, pairs)  61.9 us
    ppermute x45, waiting for transfers between devices, send(): return lax.ppermute(value, axes, pairs)  48.6 us
    pallas_call x1, Pallas kernels, hidden_rows(): pl.pallas_call(functools.partial(hidden_kernel, chunks, groups, late), gr...  21.6 us
    pallas_call x2, Pallas kernels, mix_rows(): pl.pallas_call(functools.partial(mix_kernel, order), grid=(experts // gro...  16.5 us
    all_to_all x1, starting transfers between devices, shards(): lax.all_to_all(choice, axes, split_axis=0, concat_axis=0, tiled=True)  6.7 us
  transfers between devices with their start and end apart: 46, of which 23 were waited for; matrix products, arithmetic and copies ran while one was open for 5% of the time, Pallas kernels for 7%

profile of v3, /device:TPU:8, one launch (start us, length us, event | category | flops | bytes accessed | tf_op | source)
XLA Modules:
  0.0 170.8 jit_solution(13231454944391660480)
XLA Ops:
  4.1 3.5 %collective-permute-start.9 = (bf16[128,1024]{1,0:T(8,128)(2,1)S(1)}, bf16[128,1024]{1,0:T(8,128)(2,1)S(1)}, u32[]{:S(2)}, u32[]{:S(2)}) collective-permute-start(bf16[128,1024]{1,0:T(8,128)(2,1)S(1)} %get-tuple-element.139.refs_0_), channel_id=1, source_target_pairs={{4,8},{5,9},{6,10},{7,11},{8,4},{9,5},{10,6},{11,7},{20,24},{21,25... | collective-permute-start | bytes 786440 | tf_op jit(solution)/shard_map/ppermute | solution.py:278
  8.2 2.3 %collective-permute-start.1 = (bf16[128,1024]{1,0:T(8,128)(2,1)S(1)}, bf16[128,1024]{1,0:T(8,128)(2,1)S(1)}, u32[]{:S(2)}, u32[]{:S(2)}) collective-permute-start(bf16[128,1024]{1,0:T(8,128)(2,1)S(1)} %get-tuple-element.140.refs_0_), channel_id=1, source_target_pairs={{4,8},{5,9},{6,10},{7,11},{8,4},{9,5},{10,6},{11,7},{20,24},{21,25... | collective-permute-start | bytes 786440 | tf_op jit(solution)/shard_map/ppermute | solution.py:278
  12.5 6.7 %all-to-all-start = ((f32[16,16,128]{2,1,0:T(8,128)}), f32[16,16,128]{2,1,0:T(8,128)S(1)}, u32[]{:S(2)}, u32[]{:S(2)}) async-start(f32[16,16,128]{2,1,0:T(8,128)} %copy_bitcast_fusion), calls=%async_computation | async-start | bytes 262144 | tf_op jit(solution)/shard_map/all_to_all | solution.py:381
  19.5 3.8 %collective-permute-start.4 = (bf16[128,1024]{1,0:T(8,128)(2,1)S(1)}, bf16[128,1024]{1,0:T(8,128)(2,1)S(1)}, u32[]{:S(2)}, u32[]{:S(2)}) collective-permute-start(bf16[128,1024]{1,0:T(8,128)(2,1)S(1)} %collective-permute-done.1), channel_id=1, source_target_pairs={{4,0},{5,1},{6,2},{7,3},{8,12},{9,13},{10,14},{11,15},{20,16},{21,... | collective-permute-start | bytes 786440 | tf_op jit(solution)/shard_map/ppermute | solution.py:278
  24.0 4.5 %collective-permute-done.8.refs_1_ = bf16[128,1024]{1,0:T(8,128)(2,1)S(1)} collective-permute-done((bf16[128,1024]{1,0:T(8,128)(2,1)S(1)}, bf16[128,1024]{1,0:T(8,128)(2,1)S(1)}, u32[]{:S(2)}, u32[]{:S(2)}) %collective-permute-start.8) | collective-permute-done | bytes 262176 | tf_op jit(solution)/shard_map/ppermute | solution.py:278
  30.2 4.3 %collective-permute-start.11 = (bf16[128,1024]{1,0:T(8,128)(2,1)S(1)}, bf16[128,1024]{1,0:T(8,128)(2,1)S(1)}, u32[]{:S(2)}, u32[]{:S(2)}) collective-permute-start(bf16[128,1024]{1,0:T(8,128)(2,1)S(1)} %collective-permute-done.8.refs_1_), channel_id=1, source_target_pairs={{4,8},{5,9},{6,10},{7,11},{8,4},{9,5},{10,6},{11,7},{20,24},{21,25... | collective-permute-start | bytes 786440 | tf_op jit(solution)/shard_map/ppermute | solution.py:278
  42.3 3.6 %collective-permute-done.3 = bf16[128,1024]{1,0:T(8,128)(2,1)S(1)} collective-permute-done((bf16[128,1024]{1,0:T(8,128)(2,1)S(1)}, bf16[128,1024]{1,0:T(8,128)(2,1)S(1)}, u32[]{:S(2)}, u32[]{:S(2)}) %collective-permute-start.3) | collective-permute-done | bytes 262176 | tf_op jit(solution)/shard_map/ppermute | solution.py:278
  46.6 3.5 %collective-permute-start.15 = (bf16[128,1024]{1,0:T(8,128)(2,1)S(1)}, bf16[128,1024]{1,0:T(8,128)(2,1)S(1)}, u32[]{:S(2)}, u32[]{:S(2)}) collective-permute-start(bf16[128,1024]{1,0:T(8,128)(2,1)S(1)} %collective-permute-done.11), channel_id=1, source_target_pairs={{4,0},{5,1},{6,2},{7,3},{8,12},{9,13},{10,14},{11,15},{20,16},{21,... | collective-permute-start | bytes 786440 | tf_op jit(solution)/shard_map/ppermute | solution.py:278
  54.9 3.7 %collective-permute-done.7.refs_5_ = bf16[128,1024]{1,0:T(8,128)(2,1)S(1)} collective-permute-done((bf16[128,1024]{1,0:T(8,128)(2,1)S(1)}, bf16[128,1024]{1,0:T(8,128)(2,1)S(1)}, u32[]{:S(2)}, u32[]{:S(2)}) %collective-permute-start.7) | collective-permute-done | bytes 262176 | tf_op jit(solution)/shard_map/ppermute | solution.py:278
  63.5 4.0 %collective-permute-done.19.refs_9_ = bf16[128,1024]{1,0:T(8,128)(2,1)S(1)} collective-permute-done((bf16[128,1024]{1,0:T(8,128)(2,1)S(1)}, bf16[128,1024]{1,0:T(8,128)(2,1)S(1)}, u32[]{:S(2)}, u32[]{:S(2)}) %collective-permute-start.19) | collective-permute-done | bytes 262176 | tf_op jit(solution)/shard_map/ppermute | solution.py:278
  67.6 2.8 %collective-permute-done.17.refs_5_ = bf16[128,1024]{1,0:T(8,128)(2,1)S(1)} collective-permute-done((bf16[128,1024]{1,0:T(8,128)(2,1)S(1)}, bf16[128,1024]{1,0:T(8,128)(2,1)S(1)}, u32[]{:S(2)}, u32[]{:S(2)}) %collective-permute-start.17) | collective-permute-done | bytes 262176 | tf_op jit(solution)/shard_map/ppermute | solution.py:278
  71.4 5.0 %collective-permute-done.23.refs_10_ = bf16[128,1024]{1,0:T(8,128)(2,1)S(1)} collective-permute-done((bf16[128,1024]{1,0:T(8,128)(2,1)S(1)}, bf16[128,1024]{1,0:T(8,128)(2,1)S(1)}, u32[]{:S(2)}, u32[]{:S(2)}) %collective-permute-start.23) | collective-permute-done | bytes 262176 | tf_op jit(solution)/shard_map/ppermute | solution.py:278
  78.0 21.6 %shard_map.112.hidden_ref = bf16[8,256,768]{2,1,0:T(8,128)(2,1)S(1)} custom-call(bf16[8,96,1024]{2,1,0:T(8,128)(2,1)S(1)} %bitcast.76, bf16[8,96,1024]{2,1,0:T(8,128)(2,1)S(1)} %bitcast.77, bf16[8,96,1024]{2,1,0:T(8,128)(2,1)S(1)} %bitcast.75, bf16[8,96,1024]{2,1,0:T(8,128)(2,1)S(1)} %bitcast.78, bf16[128,1024]{1,0:T(8,128)(2,1)S(1)} %broadcast_select_fusion.1.refs_4_, ...), custom_call_target="tpu_custom_call" | custom-call | flops 12884901888 | bytes 50331648 | tf_op jit(solution)/shard_map/pallas_call | solution.py:181
  99.6 8.2 %shard_map.113 = (bf16[8,128,1024]{2,1,0:T(8,128)(2,1)S(1)}, bf16[8,128,1024]{2,1,0:T(8,128)(2,1)S(1)}) custom-call(bf16[8,256,768]{2,1,0:T(8,128)(2,1)S(1)} %shard_map.112.hidden_ref, bf16[8,768,2048]{2,1,0:T(8,128)(2,1)} %down_ref.3, bf16[16,128,128]{2,1,0:T(8,128)(2,1)S(1)} %get-tuple-element.102.spread_ref), custom_call_target="tpu_custom_call" | custom-call | flops 3758096384 | bytes 19922944 | tf_op jit(solution)/shard_map/pallas_call | solution.py:234
  108.0 8.2 %shard_map.114 = (bf16[8,128,1024]{2,1,0:T(8,128)(2,1)S(1)}, bf16[8,128,1024]{2,1,0:T(8,128)(2,1)S(1)}) custom-call(bf16[8,256,768]{2,1,0:T(8,128)(2,1)S(1)} %shard_map.112.hidden_ref, bf16[8,768,2048]{2,1,0:T(8,128)(2,1)} %down_ref.3, bf16[16,128,128]{2,1,0:T(8,128)(2,1)S(1)} %get-tuple-element.102.spread_ref), custom_call_target="tpu_custom_call" | custom-call | flops 3758096384 | bytes 19922944 | tf_op jit(solution)/shard_map/pallas_call | solution.py:234
  122.6 4.4 %collective-permute-done.26 = bf16[128,1024]{1,0:T(8,128)(2,1)S(1)} collective-permute-done((bf16[128,1024]{1,0:T(8,128)(2,1)S(1)}, bf16[128,1024]{1,0:T(8,128)(2,1)S(1)}, u32[]{:S(2)}, u32[]{:S(2)}) %collective-permute-start.26) | collective-permute-done | bytes 262176 | tf_op jit(solution)/shard_map/ppermute | solution.py:278
  129.3 3.3 %collective-permute-done.36 = bf16[128,1024]{1,0:T(8,128)(2,1)S(1)} collective-permute-done((bf16[128,1024]{1,0:T(8,128)(2,1)S(1)}, bf16[128,1024]{1,0:T(8,128)(2,1)S(1)}, u32[]{:S(2)}, u32[]{:S(2)}) %collective-permute-start.36) | collective-permute-done | bytes 262176 | tf_op jit(solution)/shard_map/ppermute | solution.py:278
  135.7 2.6 %collective-permute-done.28 = bf16[128,1024]{1,0:T(8,128)(2,1)S(1)} collective-permute-done((bf16[128,1024]{1,0:T(8,128)(2,1)S(1)}, bf16[128,1024]{1,0:T(8,128)(2,1)S(1)}, u32[]{:S(2)}, u32[]{:S(2)}) %collective-permute-start.28) | collective-permute-done | bytes 262176 | tf_op jit(solution)/shard_map/ppermute | solution.py:278
  138.3 3.1 %collective-permute-start.30 = (bf16[128,1024]{1,0:T(8,128)(2,1)S(1)}, bf16[128,1024]{1,0:T(8,128)(2,1)S(1)}, u32[]{:S(2)}, u32[]{:S(2)}) collective-permute-start(bf16[128,1024]{1,0:T(8,128)(2,1)S(1)} %add_convert_fusion.5), channel_id=1, source_target_pairs={{4,8},{5,9},{6,10},{7,11},{8,4},{9,5},{10,6},{11,7},{20,24},{21,25... | collective-permute-start | bytes 786440 | tf_op jit(solution)/shard_map/ppermute | solution.py:278
  143.6 3.0 %collective-permute-start.40 = (bf16[128,1024]{1,0:T(8,128)(2,1)S(1)}, bf16[128,1024]{1,0:T(8,128)(2,1)S(1)}, u32[]{:S(2)}, u32[]{:S(2)}) collective-permute-start(bf16[128,1024]{1,0:T(8,128)(2,1)S(1)} %add_convert_fusion.3), channel_id=1, source_target_pairs={{4,8},{5,9},{6,10},{7,11},{8,4},{9,5},{10,6},{11,7},{20,24},{21,25... | collective-permute-start | bytes 786440 | tf_op jit(solution)/shard_map/ppermute | solution.py:278
  150.0 2.2 %collective-permute-start.34 = (bf16[128,1024]{1,0:T(8,128)(2,1)S(1)}, bf16[128,1024]{1,0:T(8,128)(2,1)S(1)}, u32[]{:S(2)}, u32[]{:S(2)}) collective-permute-start(bf16[128,1024]{1,0:T(8,128)(2,1)S(1)} %fusion.12), channel_id=1, source_target_pairs={{0,4},{1,5},{2,6},{3,7},{4,0},{5,1},{6,2},{7,3},{8,12},{9,13},{10,... | collective-permute-start | bytes 786440 | tf_op jit(solution)/shard_map/ppermute | solution.py:278
  152.2 3.0 %collective-permute-start.33 = (bf16[128,1024]{1,0:T(8,128)(2,1)S(1)}, bf16[128,1024]{1,0:T(8,128)(2,1)S(1)}, u32[]{:S(2)}, u32[]{:S(2)}) collective-permute-start(bf16[128,1024]{1,0:T(8,128)(2,1)S(1)} %add_convert_fusion.4), channel_id=1, source_target_pairs={{4,8},{5,9},{6,10},{7,11},{8,4},{9,5},{10,6},{11,7},{20,24},{21,25... | collective-permute-start | bytes 786440 | tf_op jit(solution)/shard_map/ppermute | solution.py:278
  157.9 2.2 %collective-permute-start.44 = (bf16[128,1024]{1,0:T(8,128)(2,1)S(1)}, bf16[128,1024]{1,0:T(8,128)(2,1)S(1)}, u32[]{:S(2)}, u32[]{:S(2)}) collective-permute-start(bf16[128,1024]{1,0:T(8,128)(2,1)S(1)} %fusion.5), channel_id=1, source_target_pairs={{0,4},{1,5},{2,6},{3,7},{4,0},{5,1},{6,2},{7,3},{8,12},{9,13},{10,... | collective-permute-start | bytes 786440 | tf_op jit(solution)/shard_map/ppermute | solution.py:278
  160.2 2.9 %collective-permute-start.43 = (bf16[128,1024]{1,0:T(8,128)(2,1)S(1)}, bf16[128,1024]{1,0:T(8,128)(2,1)S(1)}, u32[]{:S(2)}, u32[]{:S(2)}) collective-permute-start(bf16[128,1024]{1,0:T(8,128)(2,1)S(1)} %add_convert_fusion.2), channel_id=1, source_target_pairs={{4,8},{5,9},{6,10},{7,11},{8,4},{9,5},{10,6},{11,7},{20,24},{21,25... | collective-permute-start | bytes 786440 | tf_op jit(solution)/shard_map/ppermute | solution.py:278
  (120 shorter events, 58.0 us)
Async XLA Ops:
  2.6 21.5 %collective-permute-start.10 = (bf16[128,1024]{1,0:T(8,128)(2,1)S(1)}, bf16[128,1024]{1,0:T(8,128)(2,1)S(1)}, u32[]{:S(2)}, u32[]{:S(2)}) collective-permute-start(bf16[128,1024]{1,0:T(8,128)(2,1)S(1)} %get-tuple-element.139.refs_0_), channel_id=1, source_target_pairs={{0,2},{2,0},{1,3},{3,1},{4,6},{6,4},{5,7},{7,5},{8,10},{10,8},{9,1... | collective-permute-start | bytes 786440 | tf_op jit(solution)/shard_map/ppermute | solution.py:278
  4.1 19.9 %collective-permute-start.9 = (bf16[128,1024]{1,0:T(8,128)(2,1)S(1)}, bf16[128,1024]{1,0:T(8,128)(2,1)S(1)}, u32[]{:S(2)}, u32[]{:S(2)}) collective-permute-start(bf16[128,1024]{1,0:T(8,128)(2,1)S(1)} %get-tuple-element.139.refs_0_), channel_id=1, source_target_pairs={{4,8},{5,9},{6,10},{7,11},{8,4},{9,5},{10,6},{11,7},{20,24},{21,25... | collective-permute-start | bytes 786440 | tf_op jit(solution)/shard_map/ppermute | solution.py:278
  7.6 11.7 %collective-permute-start.2 = (bf16[128,1024]{1,0:T(8,128)(2,1)S(1)}, bf16[128,1024]{1,0:T(8,128)(2,1)S(1)}, u32[]{:S(2)}, u32[]{:S(2)}) collective-permute-start(bf16[128,1024]{1,0:T(8,128)(2,1)S(1)} %get-tuple-element.140.refs_0_), channel_id=1, source_target_pairs={{0,2},{2,0},{1,3},{3,1},{4,6},{6,4},{5,7},{7,5},{8,10},{10,8},{9,1... | collective-permute-start | bytes 786440 | tf_op jit(solution)/shard_map/ppermute | solution.py:278
  8.2 11.3 %collective-permute-start.1 = (bf16[128,1024]{1,0:T(8,128)(2,1)S(1)}, bf16[128,1024]{1,0:T(8,128)(2,1)S(1)}, u32[]{:S(2)}, u32[]{:S(2)}) collective-permute-start(bf16[128,1024]{1,0:T(8,128)(2,1)S(1)} %get-tuple-element.140.refs_0_), channel_id=1, source_target_pairs={{4,8},{5,9},{6,10},{7,11},{8,4},{9,5},{10,6},{11,7},{20,24},{21,25... | collective-permute-start | bytes 786440 | tf_op jit(solution)/shard_map/ppermute | solution.py:278
  12.5 29.0 %all-to-all-start = ((f32[16,16,128]{2,1,0:T(8,128)}), f32[16,16,128]{2,1,0:T(8,128)S(1)}, u32[]{:S(2)}, u32[]{:S(2)}) async-start(f32[16,16,128]{2,1,0:T(8,128)} %copy_bitcast_fusion), calls=%async_computation | async-start | bytes 262144 | tf_op jit(solution)/shard_map/all_to_all | solution.py:381
  19.3 9.3 %collective-permute-start.8 = (bf16[128,1024]{1,0:T(8,128)(2,1)S(1)}, bf16[128,1024]{1,0:T(8,128)(2,1)S(1)}, u32[]{:S(2)}, u32[]{:S(2)}) collective-permute-start(bf16[128,1024]{1,0:T(8,128)(2,1)S(1)} %get-tuple-element.139.refs_0_), channel_id=1, source_target_pairs={{0,4},{1,5},{2,6},{3,7},{4,0},{5,1},{6,2},{7,3},{8,12},{9,13},{10,... | collective-permute-start | bytes 786440 | tf_op jit(solution)/shard_map/ppermute | solution.py:278
  19.5 17.5 %collective-permute-start.4 = (bf16[128,1024]{1,0:T(8,128)(2,1)S(1)}, bf16[128,1024]{1,0:T(8,128)(2,1)S(1)}, u32[]{:S(2)}, u32[]{:S(2)}) collective-permute-start(bf16[128,1024]{1,0:T(8,128)(2,1)S(1)} %collective-permute-done.1), channel_id=1, source_target_pairs={{4,0},{5,1},{6,2},{7,3},{8,12},{9,13},{10,14},{11,15},{20,16},{21,... | collective-permute-start | bytes 786440 | tf_op jit(solution)/shard_map/ppermute | solution.py:278
  28.5 17.4 %collective-permute-start.13 = (bf16[128,1024]{1,0:T(8,128)(2,1)S(1)}, bf16[128,1024]{1,0:T(8,128)(2,1)S(1)}, u32[]{:S(2)}, u32[]{:S(2)}) collective-permute-start(bf16[128,1024]{1,0:T(8,128)(2,1)S(1)} %collective-permute-done.8.refs_1_), channel_id=1, source_target_pairs={{0,2},{2,0},{1,3},{3,1},{4,6},{6,4},{5,7},{7,5},{8,10},{10,8},{9,1... | collective-permute-start | bytes 786440 | tf_op jit(solution)/shard_map/ppermute | solution.py:278
  30.2 15.7 %collective-permute-start.11 = (bf16[128,1024]{1,0:T(8,128)(2,1)S(1)}, bf16[128,1024]{1,0:T(8,128)(2,1)S(1)}, u32[]{:S(2)}, u32[]{:S(2)}) collective-permute-start(bf16[128,1024]{1,0:T(8,128)(2,1)S(1)} %collective-permute-done.8.refs_1_), channel_id=1, source_target_pairs={{4,8},{5,9},{6,10},{7,11},{8,4},{9,5},{10,6},{11,7},{20,24},{21,25... | collective-permute-start | bytes 786440 | tf_op jit(solution)/shard_map/ppermute | solution.py:278
  35.1 10.8 %collective-permute-start.3 = (bf16[128,1024]{1,0:T(8,128)(2,1)S(1)}, bf16[128,1024]{1,0:T(8,128)(2,1)S(1)}, u32[]{:S(2)}, u32[]{:S(2)}) collective-permute-start(bf16[128,1024]{1,0:T(8,128)(2,1)S(1)} %collective-permute-done.refs_1_), channel_id=1, source_target_pairs={{4,8},{5,9},{6,10},{7,11},{8,4},{9,5},{10,6},{11,7},{20,24},{21,25... | collective-permute-start | bytes 786440 | tf_op jit(solution)/shard_map/ppermute | solution.py:278
  46.0 13.4 %collective-permute-start.16 = (bf16[128,1024]{1,0:T(8,128)(2,1)S(1)}, bf16[128,1024]{1,0:T(8,128)(2,1)S(1)}, u32[]{:S(2)}, u32[]{:S(2)}) collective-permute-start(bf16[128,1024]{1,0:T(8,128)(2,1)S(1)} %broadcast_select_fusion.2.refs_2_), channel_id=1, source_target_pairs={{0,2},{2,0},{1,3},{3,1},{4,6},{6,4},{5,7},{7,5},{8,10},{10,8},{9,1... | collective-permute-start | bytes 786440 | tf_op jit(solution)/shard_map/ppermute | solution.py:278
  46.6 12.7 %collective-permute-start.15 = (bf16[128,1024]{1,0:T(8,128)(2,1)S(1)}, bf16[128,1024]{1,0:T(8,128)(2,1)S(1)}, u32[]{:S(2)}, u32[]{:S(2)}) collective-permute-start(bf16[128,1024]{1,0:T(8,128)(2,1)S(1)} %collective-permute-done.11), channel_id=1, source_target_pairs={{4,0},{5,1},{6,2},{7,3},{8,12},{9,13},{10,14},{11,15},{20,16},{21,... | collective-permute-start | bytes 786440 | tf_op jit(solution)/shard_map/ppermute | solution.py:278
  60.0 10.3 %collective-permute-start.17 = (bf16[128,1024]{1,0:T(8,128)(2,1)S(1)}, bf16[128,1024]{1,0:T(8,128)(2,1)S(1)}, u32[]{:S(2)}, u32[]{:S(2)}) collective-permute-start(bf16[128,1024]{1,0:T(8,128)(2,1)S(1)} %broadcast_select_fusion.1.refs_4_), channel_id=1, source_target_pairs={{0,2},{2,0},{1,3},{3,1},{4,6},{6,4},{5,7},{7,5},{8,10},{10,8},{9,1... | collective-permute-start | bytes 786440 | tf_op jit(solution)/shard_map/ppermute | solution.py:278
  121.6 11.0 %collective-permute-start.36 = (bf16[128,1024]{1,0:T(8,128)(2,1)S(1)}, bf16[128,1024]{1,0:T(8,128)(2,1)S(1)}, u32[]{:S(2)}, u32[]{:S(2)}) collective-permute-start(bf16[128,1024]{1,0:T(8,128)(2,1)S(1)} %get-tuple-element.138), channel_id=1, source_target_pairs={{0,2},{2,0},{1,3},{3,1},{4,6},{6,4},{5,7},{7,5},{8,10},{10,8},{9,1... | collective-permute-start | bytes 786440 | tf_op jit(solution)/shard_map/ppermute | solution.py:278
  128.4 9.9 %collective-permute-start.28 = (bf16[128,1024]{1,0:T(8,128)(2,1)S(1)}, bf16[128,1024]{1,0:T(8,128)(2,1)S(1)}, u32[]{:S(2)}, u32[]{:S(2)}) collective-permute-start(bf16[128,1024]{1,0:T(8,128)(2,1)S(1)} %get-tuple-element.106), channel_id=1, source_target_pairs={{0,2},{2,0},{1,3},{3,1},{4,6},{6,4},{5,7},{7,5},{8,10},{10,8},{9,1... | collective-permute-start | bytes 786440 | tf_op jit(solution)/shard_map/ppermute | solution.py:278
  132.7 10.8 %collective-permute-start.37 = (bf16[128,1024]{1,0:T(8,128)(2,1)S(1)}, bf16[128,1024]{1,0:T(8,128)(2,1)S(1)}, u32[]{:S(2)}, u32[]{:S(2)}) collective-permute-start(bf16[128,1024]{1,0:T(8,128)(2,1)S(1)} %fusion.6), channel_id=1, source_target_pairs={{0,4},{1,5},{2,6},{3,7},{12,8},{13,9},{14,10},{15,11},{16,20},{17,... | collective-permute-start | bytes 786440 | tf_op jit(solution)/shard_map/ppermute | solution.py:278
  134.0 9.5 %collective-permute-start.38 = (bf16[128,1024]{1,0:T(8,128)(2,1)S(1)}, bf16[128,1024]{1,0:T(8,128)(2,1)S(1)}, u32[]{:S(2)}, u32[]{:S(2)}) collective-permute-start(bf16[128,1024]{1,0:T(8,128)(2,1)S(1)} %get-tuple-element.120), channel_id=1, source_target_pairs={{0,2},{2,0},{1,3},{3,1},{4,6},{6,4},{5,7},{7,5},{8,10},{10,8},{9,1... | collective-permute-start | bytes 786440 | tf_op jit(solution)/shard_map/ppermute | solution.py:278
  138.3 9.6 %collective-permute-start.30 = (bf16[128,1024]{1,0:T(8,128)(2,1)S(1)}, bf16[128,1024]{1,0:T(8,128)(2,1)S(1)}, u32[]{:S(2)}, u32[]{:S(2)}) collective-permute-start(bf16[128,1024]{1,0:T(8,128)(2,1)S(1)} %add_convert_fusion.5), channel_id=1, source_target_pairs={{4,8},{5,9},{6,10},{7,11},{8,4},{9,5},{10,6},{11,7},{20,24},{21,25... | collective-permute-start | bytes 786440 | tf_op jit(solution)/shard_map/ppermute | solution.py:278
  143.6 11.6 %collective-permute-start.40 = (bf16[128,1024]{1,0:T(8,128)(2,1)S(1)}, bf16[128,1024]{1,0:T(8,128)(2,1)S(1)}, u32[]{:S(2)}, u32[]{:S(2)}) collective-permute-start(bf16[128,1024]{1,0:T(8,128)(2,1)S(1)} %add_convert_fusion.3), channel_id=1, source_target_pairs={{4,8},{5,9},{6,10},{7,11},{8,4},{9,5},{10,6},{11,7},{20,24},{21,25... | collective-permute-start | bytes 786440 | tf_op jit(solution)/shard_map/ppermute | solution.py:278
  146.6 11.1 %collective-permute-start.39 = (bf16[128,1024]{1,0:T(8,128)(2,1)S(1)}, bf16[128,1024]{1,0:T(8,128)(2,1)S(1)}, u32[]{:S(2)}, u32[]{:S(2)}) collective-permute-start(bf16[128,1024]{1,0:T(8,128)(2,1)S(1)} %fusion.7), channel_id=1, source_target_pairs={{0,4},{1,5},{2,6},{3,7},{12,8},{13,9},{14,10},{15,11},{16,20},{17,... | collective-permute-start | bytes 786440 | tf_op jit(solution)/shard_map/ppermute | solution.py:278
  147.9 9.8 %collective-permute-start.41 = (bf16[128,1024]{1,0:T(8,128)(2,1)S(1)}, bf16[128,1024]{1,0:T(8,128)(2,1)S(1)}, u32[]{:S(2)}, u32[]{:S(2)}) collective-permute-start(bf16[128,1024]{1,0:T(8,128)(2,1)S(1)} %get-tuple-element.125), channel_id=1, source_target_pairs={{0,2},{2,0},{1,3},{3,1},{4,6},{6,4},{5,7},{7,5},{8,10},{10,8},{9,1... | collective-permute-start | bytes 786440 | tf_op jit(solution)/shard_map/ppermute | solution.py:278
  150.0 13.4 %collective-permute-start.34 = (bf16[128,1024]{1,0:T(8,128)(2,1)S(1)}, bf16[128,1024]{1,0:T(8,128)(2,1)S(1)}, u32[]{:S(2)}, u32[]{:S(2)}) collective-permute-start(bf16[128,1024]{1,0:T(8,128)(2,1)S(1)} %fusion.12), channel_id=1, source_target_pairs={{0,4},{1,5},{2,6},{3,7},{4,0},{5,1},{6,2},{7,3},{8,12},{9,13},{10,... | collective-permute-start | bytes 786440 | tf_op jit(solution)/shard_map/ppermute | solution.py:278
  152.2 12.3 %collective-permute-start.33 = (bf16[128,1024]{1,0:T(8,128)(2,1)S(1)}, bf16[128,1024]{1,0:T(8,128)(2,1)S(1)}, u32[]{:S(2)}, u32[]{:S(2)}) collective-permute-start(bf16[128,1024]{1,0:T(8,128)(2,1)S(1)} %add_convert_fusion.4), channel_id=1, source_target_pairs={{4,8},{5,9},{6,10},{7,11},{8,4},{9,5},{10,6},{11,7},{20,24},{21,25... | collective-permute-start | bytes 786440 | tf_op jit(solution)/shard_map/ppermute | solution.py:278
  155.2 9.3 %collective-permute-start.32 = (bf16[128,1024]{1,0:T(8,128)(2,1)S(1)}, bf16[128,1024]{1,0:T(8,128)(2,1)S(1)}, u32[]{:S(2)}, u32[]{:S(2)}) collective-permute-start(bf16[128,1024]{1,0:T(8,128)(2,1)S(1)} %get-tuple-element.113), channel_id=1, source_target_pairs={{0,2},{2,0},{1,3},{3,1},{4,6},{6,4},{5,7},{7,5},{8,10},{10,8},{9,1... | collective-permute-start | bytes 786440 | tf_op jit(solution)/shard_map/ppermute | solution.py:278
  (24 other events, 177.7 us)

commit v4 on v3

--- a/solution.py
+++ b/solution.py
@@ -54,6 +54,27 @@
             transcendentals=0,
         ),
     )(picker, tokens)
+
+
+def norm_kernel(tokens_ref, gain_ref, *part_refs):
+    as_float = tokens_ref[...].astype(jnp.float32)
+    mean = jnp.mean(as_float * as_float, axis=-1, keepdims=True)
+    normed = (as_float * lax.rsqrt(mean + 1e-06) * gain_ref[...]).astype(jnp.bfloat16)
+    width = part_refs[0].shape[1]
+    for chunk, part_ref in enumerate(part_refs):
+        part_ref[...] = normed[:, chunk * width : (chunk + 1) * width]
+
+
+def normed_parts(tokens, norm_gain, chunks):
+    token_count, feature_dim = tokens.shape
+    part = jax.ShapeDtypeStruct((token_count, feature_dim // chunks), jnp.bfloat16)
+    return pl.pallas_call(
+        norm_kernel,
+        in_specs=[pl.BlockSpec(memory_space=pltpu.VMEM)] * 2,
+        out_specs=[pl.BlockSpec(memory_space=pltpu.VMEM)] * chunks,
+        out_shape=[part] * chunks,
+        compiler_params=pltpu.CompilerParams(vmem_limit_bytes=16 * mebi),
+    )(tokens, norm_gain.reshape(1, feature_dim))
 
 
 def table_kernel(source_ref, choices_ref, *refs):
@@ -302,12 +323,10 @@
 
 
 def tree_rest(early, fourth, mine, theirs, experts):
-    mine_rows, theirs_rows, fourth_x = together(
-        *pick_pair(early, mine, theirs, experts), send(fourth, swap_x)
-    )
+    mine_rows, theirs_rows = pick_pair(early, mine, theirs, experts)
+    fourth_x, theirs_rows = together(send(fourth, swap_x), send(theirs_rows, swap_core))
     late = [fourth, fourth_x]
-    rows = [mine_rows, send(theirs_rows, swap_core)]
-    return rows, late + [send(block, swap_core) for block in late]
+    return [mine_rows, theirs_rows], late + [send(block, swap_core) for block in late]
 
 
 def chip_sums(mine, theirs):
@@ -360,13 +379,8 @@
     as_tree = expert_size == 4 and dp_size == 4
     edge = (lax.axis_index("expert") % 3) == 0
 
-    as_float = tokens.astype(jnp.float32)
-    normed = (
-        as_float
-        * lax.rsqrt(jnp.mean(as_float * as_float, axis=-1, keepdims=True) + 1e-06)
-        * norm_gain
-    ).astype(jnp.bfloat16)
-
+    width = feature_dim // gather_chunks
+    parts = normed_parts(tokens, norm_gain, gather_chunks)
     every = jnp.arange(device_count * local_count, dtype=jnp.int32)
     same = routes[:, :, None] == every
     named = jnp.any(same, axis=1)
@@ -378,21 +392,28 @@
     rank = jnp.where(named, rank, -1.0)
     choice = jnp.stack([rank.T, named_weight.T]).reshape(2, device_count, local_count, token_count)
     choice = choice.transpose(1, 0, 2, 3).reshape(device_count, 2 * local_count, token_count)
-    choices = lax.all_to_all(choice, axes, split_axis=0, concat_axis=0, tiled=True)
-
-    width = feature_dim // gather_chunks
-    parts = [normed[:, chunk * width : (chunk + 1) * width] for chunk in range(gather_chunks)]
     if as_tree:
         firsts = [tree_start(part) for part in parts]
+        near, middle, own_x = firsts[0]
+        near, middle, own_x, choice = together(near, middle, own_x, choice)
+        firsts[0] = near, middle, own_x
+    choices = lax.all_to_all(choice, axes, split_axis=0, concat_axis=0, tiled=True)
+    if as_tree:
         seconds = []
-        for near, middle, own_x in firsts:
-            cross, outer, near_x, choices = tree_second(near, middle, choices)
+        for chunk, (near, middle, own_x) in enumerate(firsts):
+            if chunk == 0:
+                cross, outer, near_x, choices = tree_second(near, middle, choices)
+            else:
+                cross, outer, near_x = tree_second(near, middle)
             seconds.append((cross, outer, near_x))
         mine, theirs, late_picker, spread, scale = tables(slot_sources(), choices, local_count)
         theirs = send(theirs, swap_core)
         thirds = []
         for (near, middle, own_x), (cross, outer, near_x) in zip(firsts, seconds):
-            third, third_x, fourth, theirs = tree_third(cross, outer, middle, edge, theirs)
+            if not thirds:
+                third, third_x, fourth, theirs = tree_third(cross, outer, middle, edge, theirs)
+            else:
+                third, third_x, fourth = tree_third(cross, outer, middle, edge)
             thirds.append((third, third_x, fourth))
         order = (0, 1, 2, 3, 4, 5, 8, 9, 10, 11, 12, 13, 6, 7, 14, 15)
         row_chunks, late_chunks = [], []

time: 172 us -> 165 us (0.959)
  waiting for transfers between devices: 48.6 us -> 40.6 us
  local copies, waits for them, and re-layouts: 2.44 us -> 5.47 us
  other arithmetic: 9.39 us -> 7.48 us
    ppermute x45, waiting for transfers between devices: 48.6 us -> 40.6 us  [send(): return lax.ppermute(value, axes, pairs)]
    unnamed x6, local copies, waits for them, and re-layouts: 0.21 us -> 3.32 us
  transfers between devices with their start and end apart: 46 -> 46, of which waited for: 23 -> 18; matrix products, arithmetic and copies ran while one was open for 5% -> 6% of each run, Pallas kernels for 7% -> 6%
where the time goes in v4:
time: 165 us; the launch traced here: 163 us
  starting transfers between devices  68 us (41%)
  Pallas kernels  41.3 us (25%)
  waiting for transfers between devices  40.6 us (25%)
  other arithmetic  7.48 us (5%)
  local copies, waits for them, and re-layouts  5.47 us (3%)
    ppermute x45, starting transfers between devices, send(): return lax.ppermute(value, axes, pairs)  62.7 us
    ppermute x45, waiting for transfers between devices, send(): return lax.ppermute(value, axes, pairs)  40.6 us
    pallas_call x1, Pallas kernels, hidden_rows(): pl.pallas_call(functools.partial(hidden_kernel, chunks, groups, late), gr...  21.6 us
    pallas_call x2, Pallas kernels, mix_rows(): pl.pallas_call(functools.partial(mix_kernel, order), grid=(experts // gro...  16.5 us
    all_to_all x1, starting transfers between devices, shards(): lax.all_to_all(choice, axes, split_axis=0, concat_axis=0, tiled=True)  5.26 us
    unnamed x6, local copies, waits for them, and re-layouts  3.32 us
  transfers between devices with their start and end apart: 46, of which 18 were waited for; matrix products, arithmetic and copies ran while one was open for 6% of the time, Pallas kernels for 6%

profile of v4, /device:TPU:8, one launch (start us, length us, event | category | flops | bytes accessed | tf_op | source)
XLA Modules:
  0.0 163.5 jit_solution(328001228250630874)
XLA Ops:
  3.5 3.5 %collective-permute-start.1 = (bf16[128,1024]{1,0:T(8,128)(2,1)S(1)}, bf16[128,1024]{1,0:T(8,128)(2,1)S(1)}, u32[]{:S(2)}, u32[]{:S(2)}) collective-permute-start(bf16[128,1024]{1,0:T(8,128)(2,1)S(1)} %get-tuple-element.70.refs_0_), channel_id=1, source_target_pairs={{4,8},{5,9},{6,10},{7,11},{8,4},{9,5},{10,6},{11,7},{20,24},{21,25... | collective-permute-start | bytes 786440 | tf_op jit(solution)/shard_map/ppermute | solution.py:299
  7.7 2.3 %collective-permute-start.12 = (bf16[128,1024]{1,0:T(8,128)(2,1)S(1)}, bf16[128,1024]{1,0:T(8,128)(2,1)S(1)}, u32[]{:S(2)}, u32[]{:S(2)}) collective-permute-start(bf16[128,1024]{1,0:T(8,128)(2,1)S(1)} %get-tuple-element.90.refs_0_), channel_id=1, source_target_pairs={{4,8},{5,9},{6,10},{7,11},{8,4},{9,5},{10,6},{11,7},{20,24},{21,25... | collective-permute-start | bytes 786440 | tf_op jit(solution)/shard_map/ppermute | solution.py:299
  15.0 3.7 %collective-permute-start.4 = (bf16[128,1024]{1,0:T(8,128)(2,1)S(1)}, bf16[128,1024]{1,0:T(8,128)(2,1)S(1)}, u32[]{:S(2)}, u32[]{:S(2)}) collective-permute-start(bf16[128,1024]{1,0:T(8,128)(2,1)S(1)} %collective-permute-done.1), channel_id=1, source_target_pairs={{4,0},{5,1},{6,2},{7,3},{8,12},{9,13},{10,14},{11,15},{20,16},{21,... | collective-permute-start | bytes 786440 | tf_op jit(solution)/shard_map/ppermute | solution.py:299
  19.4 5.3 %all-to-all-start = ((f32[16,16,128]{2,1,0:T(8,128)}), f32[16,16,128]{2,1,0:T(8,128)S(1)}, u32[]{:S(2)}, u32[]{:S(2)}) async-start(f32[16,16,128]{2,1,0:T(8,128)} %copy_bitcast_fusion), calls=%async_computation | async-start | bytes 262144 | tf_op jit(solution)/shard_map/all_to_all | solution.py:400
  26.1 3.4 %collective-permute-start.3 = (bf16[128,1024]{1,0:T(8,128)(2,1)S(1)}, bf16[128,1024]{1,0:T(8,128)(2,1)S(1)}, u32[]{:S(2)}, u32[]{:S(2)}) collective-permute-start(bf16[128,1024]{1,0:T(8,128)(2,1)S(1)} %collective-permute-done.refs_1_), channel_id=1, source_target_pairs={{4,8},{5,9},{6,10},{7,11},{8,4},{9,5},{10,6},{11,7},{20,24},{21,25... | collective-permute-start | bytes 786440 | tf_op jit(solution)/shard_map/ppermute | solution.py:299
  31.2 2.5 %collective-permute-start.14 = (bf16[128,1024]{1,0:T(8,128)(2,1)S(1)}, bf16[128,1024]{1,0:T(8,128)(2,1)S(1)}, u32[]{:S(2)}, u32[]{:S(2)}) collective-permute-start(bf16[128,1024]{1,0:T(8,128)(2,1)S(1)} %collective-permute-done.11.refs_1_), channel_id=1, source_target_pairs={{4,8},{5,9},{6,10},{7,11},{8,4},{9,5},{10,6},{11,7},{20,24},{21,25... | collective-permute-start | bytes 786440 | tf_op jit(solution)/shard_map/ppermute | solution.py:299
  39.2 2.4 %collective-permute-done.15 = bf16[128,1024]{1,0:T(8,128)(2,1)} collective-permute-done((bf16[128,1024]{1,0:T(8,128)(2,1)S(1)}, bf16[128,1024]{1,0:T(8,128)(2,1)}, u32[]{:S(2)}, u32[]{:S(2)}) %collective-permute-start.15) | collective-permute-done | bytes 262176 | tf_op jit(solution)/shard_map/ppermute | solution.py:299
  43.3 5.6 %collective-permute-start.17 = (bf16[128,1024]{1,0:T(8,128)(2,1)S(1)}, bf16[128,1024]{1,0:T(8,128)(2,1)S(1)}, u32[]{:S(2)}, u32[]{:S(2)}) collective-permute-start(bf16[128,1024]{1,0:T(8,128)(2,1)S(1)} %collective-permute-done.14), channel_id=1, source_target_pairs={{4,0},{5,1},{6,2},{7,3},{8,12},{9,13},{10,14},{11,15},{20,16},{21,... | collective-permute-start | bytes 786440 | tf_op jit(solution)/shard_map/ppermute | solution.py:299
  57.5 7.0 %collective-permute-done.19.refs_9_ = bf16[128,1024]{1,0:T(8,128)(2,1)S(1)} collective-permute-done((bf16[128,1024]{1,0:T(8,128)(2,1)S(1)}, bf16[128,1024]{1,0:T(8,128)(2,1)S(1)}, u32[]{:S(2)}, u32[]{:S(2)}) %collective-permute-start.19) | collective-permute-done | bytes 262176 | tf_op jit(solution)/shard_map/ppermute | solution.py:299
  65.0 4.2 %collective-permute-done.9.refs_5_ = bf16[128,1024]{1,0:T(8,128)(2,1)S(1)} collective-permute-done((bf16[128,1024]{1,0:T(8,128)(2,1)S(1)}, bf16[128,1024]{1,0:T(8,128)(2,1)S(1)}, u32[]{:S(2)}, u32[]{:S(2)}) %collective-permute-start.9) | collective-permute-done | bytes 262176 | tf_op jit(solution)/shard_map/ppermute | solution.py:299
  70.7 21.6 %shard_map.113.hidden_ref = bf16[8,256,768]{2,1,0:T(8,128)(2,1)S(1)} custom-call(bf16[8,96,1024]{2,1,0:T(8,128)(2,1)S(1)} %bitcast.78, bf16[8,96,1024]{2,1,0:T(8,128)(2,1)S(1)} %bitcast.79, bf16[8,96,1024]{2,1,0:T(8,128)(2,1)S(1)} %bitcast.76, bf16[8,96,1024]{2,1,0:T(8,128)(2,1)S(1)} %bitcast.77, bf16[128,1024]{1,0:T(8,128)(2,1)S(1)} %broadcast_select_fusion.2.refs_4_, ...), custom_call_target="tpu_custom_call" | custom-call | flops 12884901888 | bytes 50331648 | tf_op jit(solution)/shard_map/pallas_call | solution.py:202
  92.3 8.2 %shard_map.114 = (bf16[8,128,1024]{2,1,0:T(8,128)(2,1)S(1)}, bf16[8,128,1024]{2,1,0:T(8,128)(2,1)S(1)}) custom-call(bf16[8,256,768]{2,1,0:T(8,128)(2,1)S(1)} %shard_map.113.hidden_ref, bf16[8,768,2048]{2,1,0:T(8,128)(2,1)} %down_ref.3, bf16[16,128,128]{2,1,0:T(8,128)(2,1)S(1)} %get-tuple-element.106.spread_ref), custom_call_target="tpu_custom_call" | custom-call | flops 3758096384 | bytes 19922944 | tf_op jit(solution)/shard_map/pallas_call | solution.py:255
  100.8 8.2 %shard_map.115 = (bf16[8,128,1024]{2,1,0:T(8,128)(2,1)S(1)}, bf16[8,128,1024]{2,1,0:T(8,128)(2,1)S(1)}) custom-call(bf16[8,256,768]{2,1,0:T(8,128)(2,1)S(1)} %shard_map.113.hidden_ref, bf16[8,768,2048]{2,1,0:T(8,128)(2,1)} %down_ref.3, bf16[16,128,128]{2,1,0:T(8,128)(2,1)S(1)} %get-tuple-element.106.spread_ref), custom_call_target="tpu_custom_call" | custom-call | flops 3758096384 | bytes 19922944 | tf_op jit(solution)/shard_map/pallas_call | solution.py:255
  111.1 2.2 %collective-permute-done.35 = bf16[8,128,1024]{2,1,0:T(8,128)(2,1)S(1)} collective-permute-done((bf16[8,128,1024]{2,1,0:T(8,128)(2,1)S(1)}, bf16[8,128,1024]{2,1,0:T(8,128)(2,1)S(1)}, u32[]{:S(2)}, u32[]{:S(2)}) %collective-permute-start.35) | collective-permute-done | bytes 2097184 | tf_op jit(solution)/shard_map/ppermute | solution.py:299
  114.9 4.8 %collective-permute-done.26 = bf16[128,1024]{1,0:T(8,128)(2,1)S(1)} collective-permute-done((bf16[128,1024]{1,0:T(8,128)(2,1)S(1)}, bf16[128,1024]{1,0:T(8,128)(2,1)S(1)}, u32[]{:S(2)}, u32[]{:S(2)}) %collective-permute-start.26) | collective-permute-done | bytes 262176 | tf_op jit(solution)/shard_map/ppermute | solution.py:299
  121.6 3.7 %collective-permute-done.36 = bf16[128,1024]{1,0:T(8,128)(2,1)S(1)} collective-permute-done((bf16[128,1024]{1,0:T(8,128)(2,1)S(1)}, bf16[128,1024]{1,0:T(8,128)(2,1)S(1)}, u32[]{:S(2)}, u32[]{:S(2)}) %collective-permute-start.36) | collective-permute-done | bytes 262176 | tf_op jit(solution)/shard_map/ppermute | solution.py:299
  128.5 2.5 %collective-permute-done.28 = bf16[128,1024]{1,0:T(8,128)(2,1)S(1)} collective-permute-done((bf16[128,1024]{1,0:T(8,128)(2,1)S(1)}, bf16[128,1024]{1,0:T(8,128)(2,1)S(1)}, u32[]{:S(2)}, u32[]{:S(2)}) %collective-permute-start.28) | collective-permute-done | bytes 262176 | tf_op jit(solution)/shard_map/ppermute | solution.py:299
  131.1 3.4 %collective-permute-start.30 = (bf16[128,1024]{1,0:T(8,128)(2,1)S(1)}, bf16[128,1024]{1,0:T(8,128)(2,1)S(1)}, u32[]{:S(2)}, u32[]{:S(2)}) collective-permute-start(bf16[128,1024]{1,0:T(8,128)(2,1)S(1)} %add_convert_fusion.5), channel_id=1, source_target_pairs={{4,8},{5,9},{6,10},{7,11},{8,4},{9,5},{10,6},{11,7},{20,24},{21,25... | collective-permute-start | bytes 786440 | tf_op jit(solution)/shard_map/ppermute | solution.py:299
  136.4 2.8 %collective-permute-start.40 = (bf16[128,1024]{1,0:T(8,128)(2,1)S(1)}, bf16[128,1024]{1,0:T(8,128)(2,1)S(1)}, u32[]{:S(2)}, u32[]{:S(2)}) collective-permute-start(bf16[128,1024]{1,0:T(8,128)(2,1)S(1)} %add_convert_fusion.3), channel_id=1, source_target_pairs={{4,8},{5,9},{6,10},{7,11},{8,4},{9,5},{10,6},{11,7},{20,24},{21,25... | collective-permute-start | bytes 786440 | tf_op jit(solution)/shard_map/ppermute | solution.py:299
  142.9 2.4 %collective-permute-start.34 = (bf16[128,1024]{1,0:T(8,128)(2,1)S(1)}, bf16[128,1024]{1,0:T(8,128)(2,1)S(1)}, u32[]{:S(2)}, u32[]{:S(2)}) collective-permute-start(bf16[128,1024]{1,0:T(8,128)(2,1)S(1)} %fusion.9), channel_id=1, source_target_pairs={{0,4},{1,5},{2,6},{3,7},{4,0},{5,1},{6,2},{7,3},{8,12},{9,13},{10,... | collective-permute-start | bytes 786440 | tf_op jit(solution)/shard_map/ppermute | solution.py:299
  145.4 2.9 %collective-permute-start.33 = (bf16[128,1024]{1,0:T(8,128)(2,1)S(1)}, bf16[128,1024]{1,0:T(8,128)(2,1)S(1)}, u32[]{:S(2)}, u32[]{:S(2)}) collective-permute-start(bf16[128,1024]{1,0:T(8,128)(2,1)S(1)} %add_convert_fusion.4), channel_id=1, source_target_pairs={{4,8},{5,9},{6,10},{7,11},{8,4},{9,5},{10,6},{11,7},{20,24},{21,25... | collective-permute-start | bytes 786440 | tf_op jit(solution)/shard_map/ppermute | solution.py:299
  150.6 2.2 %collective-permute-start.44 = (bf16[128,1024]{1,0:T(8,128)(2,1)S(1)}, bf16[128,1024]{1,0:T(8,128)(2,1)S(1)}, u32[]{:S(2)}, u32[]{:S(2)}) collective-permute-start(bf16[128,1024]{1,0:T(8,128)(2,1)S(1)} %fusion.2), channel_id=1, source_target_pairs={{0,4},{1,5},{2,6},{3,7},{4,0},{5,1},{6,2},{7,3},{8,12},{9,13},{10,... | collective-permute-start | bytes 786440 | tf_op jit(solution)/shard_map/ppermute | solution.py:299
  152.9 3.0 %collective-permute-start.43 = (bf16[128,1024]{1,0:T(8,128)(2,1)S(1)}, bf16[128,1024]{1,0:T(8,128)(2,1)S(1)}, u32[]{:S(2)}, u32[]{:S(2)}) collective-permute-start(bf16[128,1024]{1,0:T(8,128)(2,1)S(1)} %add_convert_fusion.2), channel_id=1, source_target_pairs={{4,8},{5,9},{6,10},{7,11},{8,4},{9,5},{10,6},{11,7},{20,24},{21,25... | collective-permute-start | bytes 786440 | tf_op jit(solution)/shard_map/ppermute | solution.py:299
  157.5 2.2 %collective-permute-done.44 = bf16[128,1024]{1,0:T(8,128)(2,1)S(1)} collective-permute-done((bf16[128,1024]{1,0:T(8,128)(2,1)S(1)}, bf16[128,1024]{1,0:T(8,128)(2,1)S(1)}, u32[]{:S(2)}, u32[]{:S(2)}) %collective-permute-start.44) | collective-permute-done | bytes 262176 | tf_op jit(solution)/shard_map/ppermute | solution.py:299
  (117 shorter events, 53.0 us)
Async XLA Ops:
  2.0 12.7 %collective-permute-start.2 = (bf16[128,1024]{1,0:T(8,128)(2,1)S(1)}, bf16[128,1024]{1,0:T(8,128)(2,1)S(1)}, u32[]{:S(2)}, u32[]{:S(2)}) collective-permute-start(bf16[128,1024]{1,0:T(8,128)(2,1)S(1)} %get-tuple-element.70.refs_0_), channel_id=1, source_target_pairs={{0,2},{2,0},{1,3},{3,1},{4,6},{6,4},{5,7},{7,5},{8,10},{10,8},{9,1... | collective-permute-start | bytes 786440 | tf_op jit(solution)/shard_map/ppermute | solution.py:299
  3.5 11.5 %collective-permute-start.1 = (bf16[128,1024]{1,0:T(8,128)(2,1)S(1)}, bf16[128,1024]{1,0:T(8,128)(2,1)S(1)}, u32[]{:S(2)}, u32[]{:S(2)}) collective-permute-start(bf16[128,1024]{1,0:T(8,128)(2,1)S(1)} %get-tuple-element.70.refs_0_), channel_id=1, source_target_pairs={{4,8},{5,9},{6,10},{7,11},{8,4},{9,5},{10,6},{11,7},{20,24},{21,25... | collective-permute-start | bytes 786440 | tf_op jit(solution)/shard_map/ppermute | solution.py:299
  7.1 19.0 %collective-permute-start.13 = (bf16[128,1024]{1,0:T(8,128)(2,1)S(1)}, bf16[128,1024]{1,0:T(8,128)(2,1)S(1)}, u32[]{:S(2)}, u32[]{:S(2)}) collective-permute-start(bf16[128,1024]{1,0:T(8,128)(2,1)S(1)} %get-tuple-element.90.refs_0_), channel_id=1, source_target_pairs={{0,2},{2,0},{1,3},{3,1},{4,6},{6,4},{5,7},{7,5},{8,10},{10,8},{9,1... | collective-permute-start | bytes 786440 | tf_op jit(solution)/shard_map/ppermute | solution.py:299
  7.7 23.0 %collective-permute-start.12 = (bf16[128,1024]{1,0:T(8,128)(2,1)S(1)}, bf16[128,1024]{1,0:T(8,128)(2,1)S(1)}, u32[]{:S(2)}, u32[]{:S(2)}) collective-permute-start(bf16[128,1024]{1,0:T(8,128)(2,1)S(1)} %get-tuple-element.90.refs_0_), channel_id=1, source_target_pairs={{4,8},{5,9},{6,10},{7,11},{8,4},{9,5},{10,6},{11,7},{20,24},{21,25... | collective-permute-start | bytes 786440 | tf_op jit(solution)/shard_map/ppermute | solution.py:299
  14.7 16.0 %collective-permute-start.11 = (bf16[128,1024]{1,0:T(8,128)(2,1)S(1)}, bf16[128,1024]{1,0:T(8,128)(2,1)S(1)}, u32[]{:S(2)}, u32[]{:S(2)}) collective-permute-start(bf16[128,1024]{1,0:T(8,128)(2,1)S(1)} %get-tuple-element.90.refs_0_), channel_id=1, source_target_pairs={{0,4},{1,5},{2,6},{3,7},{4,0},{5,1},{6,2},{7,3},{8,12},{9,13},{10,... | collective-permute-start | bytes 786440 | tf_op jit(solution)/shard_map/ppermute | solution.py:299
  15.0 18.7 %collective-permute-start.4 = (bf16[128,1024]{1,0:T(8,128)(2,1)S(1)}, bf16[128,1024]{1,0:T(8,128)(2,1)S(1)}, u32[]{:S(2)}, u32[]{:S(2)}) collective-permute-start(bf16[128,1024]{1,0:T(8,128)(2,1)S(1)} %collective-permute-done.1), channel_id=1, source_target_pairs={{4,0},{5,1},{6,2},{7,3},{8,12},{9,13},{10,14},{11,15},{20,16},{21,... | collective-permute-start | bytes 786440 | tf_op jit(solution)/shard_map/ppermute | solution.py:299
  19.4 17.0 %all-to-all-start = ((f32[16,16,128]{2,1,0:T(8,128)}), f32[16,16,128]{2,1,0:T(8,128)S(1)}, u32[]{:S(2)}, u32[]{:S(2)}) async-start(f32[16,16,128]{2,1,0:T(8,128)} %copy_bitcast_fusion), calls=%async_computation | async-start | bytes 262144 | tf_op jit(solution)/shard_map/all_to_all | solution.py:400
  24.6 11.7 %collective-permute-start.5 = (bf16[128,1024]{1,0:T(8,128)(2,1)S(1)}, bf16[128,1024]{1,0:T(8,128)(2,1)S(1)}, u32[]{:S(2)}, u32[]{:S(2)}) collective-permute-start(bf16[128,1024]{1,0:T(8,128)(2,1)S(1)} %collective-permute-done.refs_1_), channel_id=1, source_target_pairs={{0,2},{2,0},{1,3},{3,1},{4,6},{6,4},{5,7},{7,5},{8,10},{10,8},{9,1... | collective-permute-start | bytes 786440 | tf_op jit(solution)/shard_map/ppermute | solution.py:299
  26.1 10.9 %collective-permute-start.3 = (bf16[128,1024]{1,0:T(8,128)(2,1)S(1)}, bf16[128,1024]{1,0:T(8,128)(2,1)S(1)}, u32[]{:S(2)}, u32[]{:S(2)}) collective-permute-start(bf16[128,1024]{1,0:T(8,128)(2,1)S(1)} %collective-permute-done.refs_1_), channel_id=1, source_target_pairs={{4,8},{5,9},{6,10},{7,11},{8,4},{9,5},{10,6},{11,7},{20,24},{21,25... | collective-permute-start | bytes 786440 | tf_op jit(solution)/shard_map/ppermute | solution.py:299
  30.7 11.0 %collective-permute-start.16 = (bf16[128,1024]{1,0:T(8,128)(2,1)S(1)}, bf16[128,1024]{1,0:T(8,128)(2,1)S(1)}, u32[]{:S(2)}, u32[]{:S(2)}) collective-permute-start(bf16[128,1024]{1,0:T(8,128)(2,1)S(1)} %collective-permute-done.11.refs_1_), channel_id=1, source_target_pairs={{0,2},{2,0},{1,3},{3,1},{4,6},{6,4},{5,7},{7,5},{8,10},{10,8},{9,1... | collective-permute-start | bytes 786440 | tf_op jit(solution)/shard_map/ppermute | solution.py:299
  31.2 10.4 %collective-permute-start.14 = (bf16[128,1024]{1,0:T(8,128)(2,1)S(1)}, bf16[128,1024]{1,0:T(8,128)(2,1)S(1)}, u32[]{:S(2)}, u32[]{:S(2)}) collective-permute-start(bf16[128,1024]{1,0:T(8,128)(2,1)S(1)} %collective-permute-done.11.refs_1_), channel_id=1, source_target_pairs={{4,8},{5,9},{6,10},{7,11},{8,4},{9,5},{10,6},{11,7},{20,24},{21,25... | collective-permute-start | bytes 786440 | tf_op jit(solution)/shard_map/ppermute | solution.py:299
  37.1 15.6 %collective-permute-start.7 = (bf16[128,1024]{1,0:T(8,128)(2,1)S(1)}, bf16[128,1024]{1,0:T(8,128)(2,1)S(1)}, u32[]{:S(2)}, u32[]{:S(2)}) collective-permute-start(bf16[128,1024]{1,0:T(8,128)(2,1)S(1)} %broadcast_select_fusion.3.refs_2_), channel_id=1, source_target_pairs={{0,2},{2,0},{1,3},{3,1},{4,6},{6,4},{5,7},{7,5},{8,10},{10,8},{9,1... | collective-permute-start | bytes 786440 | tf_op jit(solution)/shard_map/ppermute | solution.py:299
  37.9 14.7 %collective-permute-start.6 = (bf16[128,1024]{1,0:T(8,128)(2,1)S(1)}, bf16[128,1024]{1,0:T(8,128)(2,1)S(1)}, u32[]{:S(2)}, u32[]{:S(2)}) collective-permute-start(bf16[128,1024]{1,0:T(8,128)(2,1)S(1)} %collective-permute-done.3), channel_id=1, source_target_pairs={{4,0},{5,1},{6,2},{7,3},{8,12},{9,13},{10,14},{11,15},{20,16},{21,... | collective-permute-start | bytes 786440 | tf_op jit(solution)/shard_map/ppermute | solution.py:299
  53.6 10.9 %collective-permute-start.20 = (bf16[8,6,16,1024]{3,2,1,0:T(8,128)(2,1)S(1)}, bf16[8,6,16,1024]{3,2,1,0:T(8,128)(2,1)S(1)}, u32[]{:S(2)}, u32[]{:S(2)}) collective-permute-start(bf16[8,6,16,1024]{3,2,1,0:T(8,128)(2,1)S(1)} %get-tuple-element.100), channel_id=1, source_target_pairs={{0,1},{1,0},{2,3},{3,2},{4,5},{5,4},{6,7},{7,6},{8,9},{9,8},{10,11... | collective-permute-start | bytes 4718600 | tf_op jit(solution)/shard_map/ppermute | solution.py:299
  54.7 14.5 %collective-permute-start.10 = (bf16[8,6,16,1024]{3,2,1,0:T(8,128)(2,1)S(1)}, bf16[8,6,16,1024]{3,2,1,0:T(8,128)(2,1)S(1)}, u32[]{:S(2)}, u32[]{:S(2)}) collective-permute-start(bf16[8,6,16,1024]{3,2,1,0:T(8,128)(2,1)S(1)} %get-tuple-element.88), channel_id=1, source_target_pairs={{0,1},{1,0},{2,3},{3,2},{4,5},{5,4},{6,7},{7,6},{8,9},{9,8},{10,11... | collective-permute-start | bytes 4718600 | tf_op jit(solution)/shard_map/ppermute | solution.py:299
  55.8 13.3 %collective-permute-start.9 = (bf16[128,1024]{1,0:T(8,128)(2,1)S(1)}, bf16[128,1024]{1,0:T(8,128)(2,1)S(1)}, u32[]{:S(2)}, u32[]{:S(2)}) collective-permute-start(bf16[128,1024]{1,0:T(8,128)(2,1)S(1)} %broadcast_select_fusion.2.refs_4_), channel_id=1, source_target_pairs={{0,2},{2,0},{1,3},{3,1},{4,6},{6,4},{5,7},{7,5},{8,10},{10,8},{9,1... | collective-permute-start | bytes 786440 | tf_op jit(solution)/shard_map/ppermute | solution.py:299
  57.4 11.7 %collective-permute-start.23 = (bf16[128,1024]{1,0:T(8,128)(2,1)S(1)}, bf16[128,1024]{1,0:T(8,128)(2,1)S(1)}, u32[]{:S(2)}, u32[]{:S(2)}) collective-permute-start(bf16[128,1024]{1,0:T(8,128)(2,1)S(1)} %broadcast_select_fusion.refs_8_), channel_id=1, source_target_pairs={{0,1},{1,0},{2,3},{3,2},{4,5},{5,4},{6,7},{7,6},{8,9},{9,8},{10,11... | collective-permute-start | bytes 786440 | tf_op jit(solution)/shard_map/ppermute | solution.py:299
  114.4 11.0 %collective-permute-start.36 = (bf16[128,1024]{1,0:T(8,128)(2,1)S(1)}, bf16[128,1024]{1,0:T(8,128)(2,1)S(1)}, u32[]{:S(2)}, u32[]{:S(2)}) collective-permute-start(bf16[128,1024]{1,0:T(8,128)(2,1)S(1)} %get-tuple-element.142), channel_id=1, source_target_pairs={{0,2},{2,0},{1,3},{3,1},{4,6},{6,4},{5,7},{7,5},{8,10},{10,8},{9,1... | collective-permute-start | bytes 786440 | tf_op jit(solution)/shard_map/ppermute | solution.py:299
  121.1 9.9 %collective-permute-start.28 = (bf16[128,1024]{1,0:T(8,128)(2,1)S(1)}, bf16[128,1024]{1,0:T(8,128)(2,1)S(1)}, u32[]{:S(2)}, u32[]{:S(2)}) collective-permute-start(bf16[128,1024]{1,0:T(8,128)(2,1)S(1)} %get-tuple-element.110), channel_id=1, source_target_pairs={{0,2},{2,0},{1,3},{3,1},{4,6},{6,4},{5,7},{7,5},{8,10},{10,8},{9,1... | collective-permute-start | bytes 786440 | tf_op jit(solution)/shard_map/ppermute | solution.py:299
  125.4 10.9 %collective-permute-start.37 = (bf16[128,1024]{1,0:T(8,128)(2,1)S(1)}, bf16[128,1024]{1,0:T(8,128)(2,1)S(1)}, u32[]{:S(2)}, u32[]{:S(2)}) collective-permute-start(bf16[128,1024]{1,0:T(8,128)(2,1)S(1)} %fusion.3), channel_id=1, source_target_pairs={{0,4},{1,5},{2,6},{3,7},{12,8},{13,9},{14,10},{15,11},{16,20},{17,... | collective-permute-start | bytes 786440 | tf_op jit(solution)/shard_map/ppermute | solution.py:299
  136.4 11.8 %collective-permute-start.40 = (bf16[128,1024]{1,0:T(8,128)(2,1)S(1)}, bf16[128,1024]{1,0:T(8,128)(2,1)S(1)}, u32[]{:S(2)}, u32[]{:S(2)}) collective-permute-start(bf16[128,1024]{1,0:T(8,128)(2,1)S(1)} %add_convert_fusion.3), channel_id=1, source_target_pairs={{4,8},{5,9},{6,10},{7,11},{8,4},{9,5},{10,6},{11,7},{20,24},{21,25... | collective-permute-start | bytes 786440 | tf_op jit(solution)/shard_map/ppermute | solution.py:299
  139.3 11.1 %collective-permute-start.39 = (bf16[128,1024]{1,0:T(8,128)(2,1)S(1)}, bf16[128,1024]{1,0:T(8,128)(2,1)S(1)}, u32[]{:S(2)}, u32[]{:S(2)}) collective-permute-start(bf16[128,1024]{1,0:T(8,128)(2,1)S(1)} %fusion.4), channel_id=1, source_target_pairs={{0,4},{1,5},{2,6},{3,7},{12,8},{13,9},{14,10},{15,11},{16,20},{17,... | collective-permute-start | bytes 786440 | tf_op jit(solution)/shard_map/ppermute | solution.py:299
  142.9 13.1 %collective-permute-start.34 = (bf16[128,1024]{1,0:T(8,128)(2,1)S(1)}, bf16[128,1024]{1,0:T(8,128)(2,1)S(1)}, u32[]{:S(2)}, u32[]{:S(2)}) collective-permute-start(bf16[128,1024]{1,0:T(8,128)(2,1)S(1)} %fusion.9), channel_id=1, source_target_pairs={{0,4},{1,5},{2,6},{3,7},{4,0},{5,1},{6,2},{7,3},{8,12},{9,13},{10,... | collective-permute-start | bytes 786440 | tf_op jit(solution)/shard_map/ppermute | solution.py:299
  145.4 11.9 %collective-permute-start.33 = (bf16[128,1024]{1,0:T(8,128)(2,1)S(1)}, bf16[128,1024]{1,0:T(8,128)(2,1)S(1)}, u32[]{:S(2)}, u32[]{:S(2)}) collective-permute-start(bf16[128,1024]{1,0:T(8,128)(2,1)S(1)} %add_convert_fusion.4), channel_id=1, source_target_pairs={{4,8},{5,9},{6,10},{7,11},{8,4},{9,5},{10,6},{11,7},{20,24},{21,25... | collective-permute-start | bytes 786440 | tf_op jit(solution)/shard_map/ppermute | solution.py:299
  (24 other events, 167.2 us)

commit v5 on v4

--- a/solution.py
+++ b/solution.py
@@ -56,6 +56,36 @@
     )(picker, tokens)
 
 
+def rank_kernel(routes_ref, weight_ref, choice_ref):
+    top_count, token_count = routes_ref.shape
+    devices, experts = choice_ref.shape[0], choice_ref.shape[1] // 2
+    shape = devices * experts, token_count
+    every = lax.broadcasted_iota(jnp.int32, shape, 0)
+    named, weight = jnp.zeros(shape, jnp.float32), jnp.zeros(shape, jnp.float32)
+    for k in range(top_count):
+        same = routes_ref[k : k + 1, :] == every
+        named = jnp.where(same, 1.0, named)
+        weight = jnp.where(same, weight_ref[k : k + 1, :], weight)
+    square = token_count, token_count
+    before = lax.broadcasted_iota(jnp.int32, square, 0) < lax.broadcasted_iota(jnp.int32, square, 1)
+    before = jnp.where(before, 1.0, 0.0).astype(jnp.bfloat16)
+    rank = jnp.dot(named.astype(jnp.bfloat16), before, preferred_element_type=jnp.float32)
+    rank = jnp.where(named > 0.0, rank, -1.0)
+    choice_ref[:, :experts] = rank.reshape(devices, experts, token_count)
+    choice_ref[:, experts:] = weight.reshape(devices, experts, token_count)
+
+
+def ranked(routes, route_weight, devices, experts):
+    token_count = routes.shape[0]
+    return pl.pallas_call(
+        rank_kernel,
+        in_specs=[pl.BlockSpec(memory_space=pltpu.VMEM)] * 2,
+        out_specs=pl.BlockSpec(memory_space=pltpu.VMEM),
+        out_shape=jax.ShapeDtypeStruct((devices, 2 * experts, token_count), jnp.float32),
+        compiler_params=pltpu.CompilerParams(vmem_limit_bytes=8 * mebi),
+    )(routes.T, route_weight.T)
+
+
 def norm_kernel(tokens_ref, gain_ref, *part_refs):
     as_float = tokens_ref[...].astype(jnp.float32)
     mean = jnp.mean(as_float * as_float, axis=-1, keepdims=True)
@@ -77,14 +107,28 @@
     )(tokens, norm_gain.reshape(1, feature_dim))
 
 
-def table_kernel(source_ref, choices_ref, *refs):
+def slot_sources(z, dp):
+    low = z < 2
+    column = z, z ^ 1, jnp.where(low, 2, 1), jnp.where(low, 3, 0)
+    early = [(column[i], side) for side in (0, 2) for i in range(3)]
+    late = [(column[3], side) for side in (0, 2)]
+    return [
+        from_z * 4 + (dp ^ (side + core))
+        for group in (early, late)
+        for core in (0, 1)
+        for from_z, side in group
+    ]
+
+
+def table_kernel(place_ref, choices_ref, *refs):
     picker_refs, spread_ref, scale_ref = refs[:3], refs[3], refs[4]
     experts = scale_ref.shape[0]
     token_count = choices_ref.shape[2]
     early, late = picker_refs[0].shape[0], picker_refs[2].shape[0] // 2
     place = lax.broadcasted_iota(jnp.int32, (experts, slots, token_count), 1).astype(jnp.float32)
-    for slot in range(2 * (early + late)):
-        choice = choices_ref[source_ref[slot]]
+    sources = slot_sources(place_ref[0], place_ref[1])
+    for slot, source in enumerate(sources):
+        choice = choices_ref[source]
         match = choice[:experts][:, None, :] == place
         weight = jnp.where(match, choice[experts:][:, None, :], 0.0)
         scale_ref[:, slot * slots : (slot + 1) * slots, :] = jnp.sum(weight, axis=2, keepdims=True)
@@ -96,7 +140,7 @@
         spread_ref[slot] = picker.T.astype(jnp.bfloat16)
 
 
-def tables(source, choices, experts):
+def tables(place, choices, experts):
     count, _, token_count = choices.shape
     rows = experts * slots
     late = count // 8
@@ -114,7 +158,7 @@
         out_specs=[pl.BlockSpec(memory_space=pltpu.VMEM)] * 5,
         out_shape=shapes,
         compiler_params=pltpu.CompilerParams(vmem_limit_bytes=grant(count, 12)),
-    )(source, choices)
+    )(place, choices)
 
 
 def pair_kernel(count, *refs):
@@ -310,10 +354,12 @@
     return near, middle, own_x
 
 
-def tree_second(near, middle, *others):
-    return together(
-        send(near, middle_z), send(middle, outward_z), send(near, swap_x), *others
-    )
+def tree_second(near, middle, own_x, *others):
+    if own_x is None:
+        near_x = send(near, swap_x)
+    else:
+        near_x = send(own_x, swap_z)
+    return together(send(near, middle_z), send(middle, outward_z), near_x, *others)
 
 
 def tree_third(cross, outer, middle, edge, *others):
@@ -333,39 +379,27 @@
     return rounded_sum(mine, send(theirs, swap_core))
 
 
-def tree_return(chip):
+def tree_return(chip, near_by_z):
     own, near, third, own_x, near_x, third_x, fourth, fourth_x = [chip[i] for i in range(8)]
+    if near_by_z:
+        near_x = send(near_x, swap_z)
     fourth_in, third_x, near_x, own_x = together(send(fourth_x, swap_x), third_x, near_x, own_x)
+    if near_by_z:
+        own_x = rounded_sum(own_x, near_x)
     fourth = rounded_sum(fourth, fourth_in)
     far, third_in, near_x, own_x = together(
         send(fourth, inward_z), send(third_x, swap_x), near_x, own_x
     )
     cross = rounded_sum(fourth, far)
     third = rounded_sum(third, third_in)
-    outer, crossed, near_in, own_x = together(
-        send(third, inward_z), send(cross, middle_z), send(near_x, swap_x), own_x
-    )
+    sent = [send(third, inward_z), send(cross, middle_z)]
+    if not near_by_z:
+        sent.append(send(near_x, swap_x))
+    outer, crossed, *near_in, own_x = together(*sent, own_x)
     middle = rounded_sum(third, outer)
-    near = rounded_sum(near, near_in, crossed)
+    near = rounded_sum(near, crossed, *near_in)
     return rounded_sum(
         own, send(own_x, swap_x), send(middle, middle_z), send(near, swap_z)
-    )
-
-
-def slot_sources():
-    z = lax.axis_index("expert")
-    dp = lax.axis_index("dp")
-    x, core = dp // 2, dp % 2
-    low = z < 2
-    column = jnp.stack([z, z ^ 1, jnp.where(low, 2, 1), jnp.where(low, 3, 0)])
-    early = jnp.array([0, 1, 2, 0, 1, 2]), jnp.array([0, 0, 0, 1, 1, 1])
-    late = jnp.array([3, 3]), jnp.array([0, 1])
-
-    def device(which, core_of):
-        return column[which[0]] * 4 + (x ^ which[1]) * 2 + core_of
-
-    return jnp.concatenate(
-        [device(early, core), device(early, 1 - core), device(late, core), device(late, 1 - core)]
     )
 
 
@@ -381,43 +415,42 @@
 
     width = feature_dim // gather_chunks
     parts = normed_parts(tokens, norm_gain, gather_chunks)
-    every = jnp.arange(device_count * local_count, dtype=jnp.int32)
-    same = routes[:, :, None] == every
-    named = jnp.any(same, axis=1)
-    named_weight = jnp.sum(jnp.where(same, route_weight[:, :, None], 0.0), axis=1)
-    before = (jnp.arange(token_count)[:, None] > jnp.arange(token_count)[None, :]).astype(
-        jnp.bfloat16
-    )
-    rank = jnp.dot(before, named.astype(jnp.bfloat16), preferred_element_type=jnp.float32)
-    rank = jnp.where(named, rank, -1.0)
-    choice = jnp.stack([rank.T, named_weight.T]).reshape(2, device_count, local_count, token_count)
-    choice = choice.transpose(1, 0, 2, 3).reshape(device_count, 2 * local_count, token_count)
     if as_tree:
+        choice = ranked(routes, route_weight, device_count, local_count)
         firsts = [tree_start(part) for part in parts]
-        near, middle, own_x = firsts[0]
-        near, middle, own_x, choice = together(near, middle, own_x, choice)
-        firsts[0] = near, middle, own_x
+        seconds = [
+            tree_second(near, middle, own_x if chunk % 2 else None, choice)
+            for chunk, (near, middle, own_x) in enumerate(firsts)
+        ]
+        choice = seconds[0][3]
+    else:
+        every = jnp.arange(device_count * local_count, dtype=jnp.int32)
+        same = routes[:, :, None] == every
+        named = jnp.any(same, axis=1)
+        named_weight = jnp.sum(jnp.where(same, route_weight[:, :, None], 0.0), axis=1)
+        count = jnp.arange(token_count)
+        before = (count[:, None] > count[None, :]).astype(jnp.bfloat16)
+        rank = jnp.dot(before, named.astype(jnp.bfloat16), preferred_element_type=jnp.float32)
+        rank = jnp.where(named, rank, -1.0)
+        choice = jnp.stack([rank.T, named_weight.T])
+        choice = choice.reshape(2, device_count, local_count, token_count).transpose(1, 0, 2, 3)
+        choice = choice.reshape(device_count, 2 * local_count, token_count)
     choices = lax.all_to_all(choice, axes, split_axis=0, concat_axis=0, tiled=True)
     if as_tree:
-        seconds = []
-        for chunk, (near, middle, own_x) in enumerate(firsts):
-            if chunk == 0:
-                cross, outer, near_x, choices = tree_second(near, middle, choices)
-            else:
-                cross, outer, near_x = tree_second(near, middle)
-            seconds.append((cross, outer, near_x))
-        mine, theirs, late_picker, spread, scale = tables(slot_sources(), choices, local_count)
+        place = jnp.stack([lax.axis_index("expert"), lax.axis_index("dp")])
+        mine, theirs, late_picker, spread, scale = tables(place, choices, local_count)
         theirs = send(theirs, swap_core)
         thirds = []
-        for (near, middle, own_x), (cross, outer, near_x) in zip(firsts, seconds):
+        for cross, outer, near_x, _ in seconds:
+            middle = firsts[len(thirds)][1]
             if not thirds:
+                third, third_x, fourth = tree_third(cross, outer, middle, edge)
+            else:
                 third, third_x, fourth, theirs = tree_third(cross, outer, middle, edge, theirs)
-            else:
-                third, third_x, fourth = tree_third(cross, outer, middle, edge)
             thirds.append((third, third_x, fourth))
         order = (0, 1, 2, 3, 4, 5, 8, 9, 10, 11, 12, 13, 6, 7, 14, 15)
         row_chunks, late_chunks = [], []
-        for part, (near, middle, own_x), (cross, outer, near_x), (third, third_x, fourth) in zip(
+        for part, (near, middle, own_x), (cross, outer, near_x, _), (third, third_x, fourth) in zip(
             parts, firsts, seconds, thirds
         ):
             early = part, near, third, own_x, near_x, third_x
@@ -446,7 +479,9 @@
             whole = jnp.concatenate([mine, theirs], axis=0).astype(jnp.float32)
             total = lax.psum_scatter(whole, axes, scatter_dimension=0)
             sums.append(total.astype(jnp.bfloat16))
-    results = [tree_return(chip) for chip in sums] if as_tree else sums
+    results = sums
+    if as_tree:
+        results = [tree_return(chip, chunk % 2 == 1) for chunk, chip in enumerate(sums)]
     return jnp.concatenate(results, axis=1)
 
 

time: 165 us -> 166 us (level)
  waiting for transfers between devices: 40.6 us -> 49.1 us
  other arithmetic: 7.48 us -> 4.17 us
  starting transfers between devices: 68 us -> 65 us
    ppermute x45, waiting for transfers between devices: 40.6 us -> 49.1 us  [send(): return lax.ppermute(value, axes, pairs)]
    ppermute x45, starting transfers between devices: 62.7 us -> 59.6 us  [send(): return lax.ppermute(value, axes, pairs)]
    gather x2 -> x0, local copies, waits for them, and re-layouts: 1.81 us -> none  [device(): return column[which[0]] * 4 + (x ^ which[1]) * 2 + core_of]
    unnamed x6 -> x12, local copies, waits for them, and re-layouts: 3.32 us -> 3.81 us
  transfers between devices with their start and end apart: 46 -> 46, of which waited for: 18 -> 21; matrix products, arithmetic and copies ran while one was open for 6% -> 2% of each run, Pallas kernels for 6% -> 7%
where the time goes in v5:
time: 166 us; the launch traced here: 165 us
  starting transfers between devices  65 us (39%)
  waiting for transfers between devices  49.1 us (30%)
  Pallas kernels  42.1 us (25%)
  other arithmetic  4.17 us (3%)
  local copies, waits for them, and re-layouts  4 us (2%)
    ppermute x45, starting transfers between devices, send(): return lax.ppermute(value, axes, pairs)  59.6 us
    ppermute x45, waiting for transfers between devices, send(): return lax.ppermute(value, axes, pairs)  49.1 us
    pallas_call x1, Pallas kernels, hidden_rows(): pl.pallas_call(functools.partial(hidden_kernel, chunks, groups, late), gr...  21.6 us
    pallas_call x2, Pallas kernels, mix_rows(): pl.pallas_call(functools.partial(mix_kernel, order), grid=(experts // gro...  16.5 us
    all_to_all x1, starting transfers between devices, shards(): lax.all_to_all(choice, axes, split_axis=0, concat_axis=0, tiled=True)  5.34 us
    unnamed x12, local copies, waits for them, and re-layouts  3.81 us
  transfers between devices with their start and end apart: 46, of which 21 were waited for; matrix products, arithmetic and copies ran while one was open for 2% of the time, Pallas kernels for 7%

profile of v5, /device:TPU:8, one launch (start us, length us, event | category | flops | bytes accessed | tf_op | source)
XLA Modules:
  0.0 164.8 jit_solution(4095126242872437733)
XLA Ops:
  3.5 3.5 %collective-permute-start.1 = (bf16[128,1024]{1,0:T(8,128)(2,1)S(1)}, bf16[128,1024]{1,0:T(8,128)(2,1)S(1)}, u32[]{:S(2)}, u32[]{:S(2)}) collective-permute-start(bf16[128,1024]{1,0:T(8,128)(2,1)S(1)} %get-tuple-element.64.refs_0_), channel_id=1, source_target_pairs={{4,8},{5,9},{6,10},{7,11},{8,4},{9,5},{10,6},{11,7},{20,24},{21,25... | collective-permute-start | bytes 786440 | tf_op jit(solution)/shard_map/ppermute | solution.py:343
  7.7 2.3 %collective-permute-start.9 = (bf16[128,1024]{1,0:T(8,128)(2,1)S(1)}, bf16[128,1024]{1,0:T(8,128)(2,1)S(1)}, u32[]{:S(2)}, u32[]{:S(2)}) collective-permute-start(bf16[128,1024]{1,0:T(8,128)(2,1)S(1)} %get-tuple-element.74.refs_0_), channel_id=1, source_target_pairs={{4,8},{5,9},{6,10},{7,11},{8,4},{9,5},{10,6},{11,7},{20,24},{21,25... | collective-permute-start | bytes 786440 | tf_op jit(solution)/shard_map/ppermute | solution.py:343
  11.1 3.6 %collective-permute-done.1 = bf16[128,1024]{1,0:T(8,128)(2,1)S(1)} collective-permute-done((bf16[128,1024]{1,0:T(8,128)(2,1)S(1)}, bf16[128,1024]{1,0:T(8,128)(2,1)S(1)}, u32[]{:S(2)}, u32[]{:S(2)}) %collective-permute-start.1) | collective-permute-done | bytes 262176 | tf_op jit(solution)/shard_map/ppermute | solution.py:343
  16.3 2.6 %collective-permute-start.4 = (bf16[128,1024]{1,0:T(8,128)(2,1)S(1)}, bf16[128,1024]{1,0:T(8,128)(2,1)}, u32[]{:S(2)}, u32[]{:S(2)}) collective-permute-start(bf16[128,1024]{1,0:T(8,128)(2,1)S(1)} %collective-permute-done.1), channel_id=1, source_target_pairs={{4,0},{5,1},{6,2},{7,3},{8,12},{9,13},{10,14},{11,15},{20,16},{21,... | collective-permute-start | bytes 786440 | tf_op jit(solution)/shard_map/ppermute | solution.py:343
  21.4 3.9 %collective-permute-start.11 = (bf16[128,1024]{1,0:T(8,128)(2,1)S(1)}, bf16[128,1024]{1,0:T(8,128)(2,1)S(1)}, u32[]{:S(2)}, u32[]{:S(2)}) collective-permute-start(bf16[128,1024]{1,0:T(8,128)(2,1)S(1)} %collective-permute-done.8.refs_1_), channel_id=1, source_target_pairs={{4,8},{5,9},{6,10},{7,11},{8,4},{9,5},{10,6},{11,7},{20,24},{21,25... | collective-permute-start | bytes 786440 | tf_op jit(solution)/shard_map/ppermute | solution.py:343
  29.6 5.3 %all-to-all-start = ((f32[16,16,128]{2,1,0:T(8,128)}), f32[16,16,128]{2,1,0:T(8,128)S(1)}, u32[]{:S(2)}, u32[]{:S(2)}) async-start(f32[16,16,128]{2,1,0:T(8,128)} %shard_map.74), calls=%async_computation | async-start | bytes 262144 | tf_op jit(solution)/shard_map/all_to_all | solution.py:438
  36.5 4.1 %collective-permute-start.6 = (bf16[128,1024]{1,0:T(8,128)(2,1)S(1)}, bf16[128,1024]{1,0:T(8,128)(2,1)}, u32[]{:S(2)}, u32[]{:S(2)}) collective-permute-start(bf16[128,1024]{1,0:T(8,128)(2,1)S(1)} %collective-permute-done.3), channel_id=1, source_target_pairs={{4,0},{5,1},{6,2},{7,3},{8,12},{9,13},{10,14},{11,15},{20,16},{21,... | collective-permute-start | bytes 786440 | tf_op jit(solution)/shard_map/ppermute | solution.py:343
  41.6 2.2 %collective-permute-start.14 = (bf16[128,1024]{1,0:T(8,128)(2,1)}, bf16[128,1024]{1,0:T(8,128)(2,1)}, u32[]{:S(2)}, u32[]{:S(2)}) collective-permute-start(bf16[128,1024]{1,0:T(8,128)(2,1)} %copy-done.4), channel_id=1, source_target_pairs={{4,0},{5,1},{6,2},{7,3},{8,12},{9,13},{10,14},{11,15},{20,16},{21,... | collective-permute-start | bytes 786440 | tf_op jit(solution)/shard_map/ppermute | solution.py:343
  46.6 3.7 %collective-permute-done.15.refs_5_ = bf16[128,1024]{1,0:T(8,128)(2,1)S(1)} collective-permute-done((bf16[128,1024]{1,0:T(8,128)(2,1)S(1)}, bf16[128,1024]{1,0:T(8,128)(2,1)S(1)}, u32[]{:S(2)}, u32[]{:S(2)}) %collective-permute-start.15) | collective-permute-done | bytes 262176 | tf_op jit(solution)/shard_map/ppermute | solution.py:343
  56.0 7.0 %collective-permute-done.17.refs_5_ = bf16[128,1024]{1,0:T(8,128)(2,1)S(1)} collective-permute-done((bf16[128,1024]{1,0:T(8,128)(2,1)S(1)}, bf16[128,1024]{1,0:T(8,128)(2,1)S(1)}, u32[]{:S(2)}, u32[]{:S(2)}) %collective-permute-start.17) | collective-permute-done | bytes 262176 | tf_op jit(solution)/shard_map/ppermute | solution.py:343
  63.5 4.2 %collective-permute-done.19.refs_9_ = bf16[128,1024]{1,0:T(8,128)(2,1)S(1)} collective-permute-done((bf16[128,1024]{1,0:T(8,128)(2,1)S(1)}, bf16[128,1024]{1,0:T(8,128)(2,1)S(1)}, u32[]{:S(2)}, u32[]{:S(2)}) %collective-permute-start.19) | collective-permute-done | bytes 262176 | tf_op jit(solution)/shard_map/ppermute | solution.py:343
  69.3 21.6 %shard_map.78.hidden_ref = bf16[8,256,768]{2,1,0:T(8,128)(2,1)S(1)} custom-call(bf16[8,96,1024]{2,1,0:T(8,128)(2,1)S(1)} %bitcast.65, bf16[8,96,1024]{2,1,0:T(8,128)(2,1)S(1)} %bitcast.66, bf16[8,96,1024]{2,1,0:T(8,128)(2,1)S(1)} %bitcast.67, bf16[8,96,1024]{2,1,0:T(8,128)(2,1)S(1)} %bitcast.68, bf16[128,1024]{1,0:T(8,128)(2,1)S(1)} %broadcast_select_fusion.1.refs_4_, ...), custom_call_target="tpu_custom_call" | custom-call | flops 12884901888 | bytes 50331648 | tf_op jit(solution)/shard_map/pallas_call | solution.py:246
  90.9 8.2 %shard_map.79 = (bf16[8,128,1024]{2,1,0:T(8,128)(2,1)S(1)}, bf16[8,128,1024]{2,1,0:T(8,128)(2,1)S(1)}) custom-call(bf16[8,256,768]{2,1,0:T(8,128)(2,1)S(1)} %shard_map.78.hidden_ref, bf16[8,768,2048]{2,1,0:T(8,128)(2,1)} %down_ref.3, bf16[16,128,128]{2,1,0:T(8,128)(2,1)S(1)} %get-tuple-element.96.spread_ref), custom_call_target="tpu_custom_call" | custom-call | flops 3758096384 | bytes 19922944 | tf_op jit(solution)/shard_map/pallas_call | solution.py:299
  99.3 8.2 %shard_map.80 = (bf16[8,128,1024]{2,1,0:T(8,128)(2,1)S(1)}, bf16[8,128,1024]{2,1,0:T(8,128)(2,1)S(1)}) custom-call(bf16[8,256,768]{2,1,0:T(8,128)(2,1)S(1)} %shard_map.78.hidden_ref, bf16[8,768,2048]{2,1,0:T(8,128)(2,1)} %down_ref.3, bf16[16,128,128]{2,1,0:T(8,128)(2,1)S(1)} %get-tuple-element.96.spread_ref), custom_call_target="tpu_custom_call" | custom-call | flops 3758096384 | bytes 19922944 | tf_op jit(solution)/shard_map/pallas_call | solution.py:299
  112.9 3.5 %collective-permute-start.37 = (bf16[128,1024]{1,0:T(8,128)(2,1)S(1)}, bf16[128,1024]{1,0:T(8,128)(2,1)S(1)}, u32[]{:S(2)}, u32[]{:S(2)}) collective-permute-start(bf16[128,1024]{1,0:T(8,128)(2,1)S(1)} %get-tuple-element.128), channel_id=1, source_target_pairs={{0,4},{1,5},{2,6},{3,7},{4,0},{5,1},{6,2},{7,3},{8,12},{9,13},{10,... | collective-permute-start | bytes 786440 | tf_op jit(solution)/shard_map/ppermute | solution.py:343
  119.8 3.7 %collective-permute-done.37 = bf16[128,1024]{1,0:T(8,128)(2,1)S(1)} collective-permute-done((bf16[128,1024]{1,0:T(8,128)(2,1)S(1)}, bf16[128,1024]{1,0:T(8,128)(2,1)S(1)}, u32[]{:S(2)}, u32[]{:S(2)}) %collective-permute-start.37) | collective-permute-done | bytes 262176 | tf_op jit(solution)/shard_map/ppermute | solution.py:343
  131.2 4.3 %collective-permute-start.30 = (bf16[128,1024]{1,0:T(8,128)(2,1)S(1)}, bf16[128,1024]{1,0:T(8,128)(2,1)S(1)}, u32[]{:S(2)}, u32[]{:S(2)}) collective-permute-start(bf16[128,1024]{1,0:T(8,128)(2,1)S(1)} %add_convert_fusion.6), channel_id=1, source_target_pairs={{4,8},{5,9},{6,10},{7,11},{8,4},{9,5},{10,6},{11,7},{20,24},{21,25... | collective-permute-start | bytes 786440 | tf_op jit(solution)/shard_map/ppermute | solution.py:343
  137.6 2.9 %collective-permute-start.41 = (bf16[128,1024]{1,0:T(8,128)(2,1)S(1)}, bf16[128,1024]{1,0:T(8,128)(2,1)S(1)}, u32[]{:S(2)}, u32[]{:S(2)}) collective-permute-start(bf16[128,1024]{1,0:T(8,128)(2,1)S(1)} %add_convert_fusion.3), channel_id=1, source_target_pairs={{4,8},{5,9},{6,10},{7,11},{8,4},{9,5},{10,6},{11,7},{20,24},{21,25... | collective-permute-start | bytes 786440 | tf_op jit(solution)/shard_map/ppermute | solution.py:343
  144.1 2.2 %collective-permute-start.34 = (bf16[128,1024]{1,0:T(8,128)(2,1)S(1)}, bf16[128,1024]{1,0:T(8,128)(2,1)S(1)}, u32[]{:S(2)}, u32[]{:S(2)}) collective-permute-start(bf16[128,1024]{1,0:T(8,128)(2,1)S(1)} %fusion.7), channel_id=1, source_target_pairs={{0,4},{1,5},{2,6},{3,7},{4,0},{5,1},{6,2},{7,3},{8,12},{9,13},{10,... | collective-permute-start | bytes 786440 | tf_op jit(solution)/shard_map/ppermute | solution.py:343
  149.4 2.4 %collective-permute-done.40 = bf16[128,1024]{1,0:T(8,128)(2,1)S(1)} collective-permute-done((bf16[128,1024]{1,0:T(8,128)(2,1)S(1)}, bf16[128,1024]{1,0:T(8,128)(2,1)S(1)}, u32[]{:S(2)}, u32[]{:S(2)}) %collective-permute-start.40) | collective-permute-done | bytes 262176 | tf_op jit(solution)/shard_map/ppermute | solution.py:343
  152.0 2.9 %collective-permute-start.43 = (bf16[128,1024]{1,0:T(8,128)(2,1)S(1)}, bf16[128,1024]{1,0:T(8,128)(2,1)S(1)}, u32[]{:S(2)}, u32[]{:S(2)}) collective-permute-start(bf16[128,1024]{1,0:T(8,128)(2,1)S(1)} %add_convert_fusion.2), channel_id=1, source_target_pairs={{4,8},{5,9},{6,10},{7,11},{8,4},{9,5},{10,6},{11,7},{20,24},{21,25... | collective-permute-start | bytes 786440 | tf_op jit(solution)/shard_map/ppermute | solution.py:343
  154.9 2.5 %collective-permute-done.34 = bf16[128,1024]{1,0:T(8,128)(2,1)S(1)} collective-permute-done((bf16[128,1024]{1,0:T(8,128)(2,1)S(1)}, bf16[128,1024]{1,0:T(8,128)(2,1)S(1)}, u32[]{:S(2)}, u32[]{:S(2)}) %collective-permute-start.34) | collective-permute-done | bytes 262176 | tf_op jit(solution)/shard_map/ppermute | solution.py:343
  158.2 2.6 %collective-permute-done.44 = bf16[128,1024]{1,0:T(8,128)(2,1)S(1)} collective-permute-done((bf16[128,1024]{1,0:T(8,128)(2,1)S(1)}, bf16[128,1024]{1,0:T(8,128)(2,1)S(1)}, u32[]{:S(2)}, u32[]{:S(2)}) %collective-permute-start.44) | collective-permute-done | bytes 262176 | tf_op jit(solution)/shard_map/ppermute | solution.py:343
  160.8 3.0 %collective-permute-done.42 = bf16[128,1024]{1,0:T(8,128)(2,1)S(1)} collective-permute-done((bf16[128,1024]{1,0:T(8,128)(2,1)S(1)}, bf16[128,1024]{1,0:T(8,128)(2,1)S(1)}, u32[]{:S(2)}, u32[]{:S(2)}) %collective-permute-start.42) | collective-permute-done | bytes 262176 | tf_op jit(solution)/shard_map/ppermute | solution.py:343
  (111 shorter events, 53.8 us)
Async XLA Ops:
  3.5 11.1 %collective-permute-start.1 = (bf16[128,1024]{1,0:T(8,128)(2,1)S(1)}, bf16[128,1024]{1,0:T(8,128)(2,1)S(1)}, u32[]{:S(2)}, u32[]{:S(2)}) collective-permute-start(bf16[128,1024]{1,0:T(8,128)(2,1)S(1)} %get-tuple-element.64.refs_0_), channel_id=1, source_target_pairs={{4,8},{5,9},{6,10},{7,11},{8,4},{9,5},{10,6},{11,7},{20,24},{21,25... | collective-permute-start | bytes 786440 | tf_op jit(solution)/shard_map/ppermute | solution.py:343
  7.1 12.4 %collective-permute-start.10 = (bf16[128,1024]{1,0:T(8,128)(2,1)S(1)}, bf16[128,1024]{1,0:T(8,128)(2,1)S(1)}, u32[]{:S(2)}, u32[]{:S(2)}) collective-permute-start(bf16[128,1024]{1,0:T(8,128)(2,1)S(1)} %get-tuple-element.74.refs_0_), channel_id=1, source_target_pairs={{0,2},{2,0},{1,3},{3,1},{4,6},{6,4},{5,7},{7,5},{8,10},{10,8},{9,1... | collective-permute-start | bytes 786440 | tf_op jit(solution)/shard_map/ppermute | solution.py:343
  7.7 13.7 %collective-permute-start.9 = (bf16[128,1024]{1,0:T(8,128)(2,1)S(1)}, bf16[128,1024]{1,0:T(8,128)(2,1)S(1)}, u32[]{:S(2)}, u32[]{:S(2)}) collective-permute-start(bf16[128,1024]{1,0:T(8,128)(2,1)S(1)} %get-tuple-element.74.refs_0_), channel_id=1, source_target_pairs={{4,8},{5,9},{6,10},{7,11},{8,4},{9,5},{10,6},{11,7},{20,24},{21,25... | collective-permute-start | bytes 786440 | tf_op jit(solution)/shard_map/ppermute | solution.py:343
  11.1 10.3 %collective-permute-start.8 = (bf16[128,1024]{1,0:T(8,128)(2,1)S(1)}, bf16[128,1024]{1,0:T(8,128)(2,1)S(1)}, u32[]{:S(2)}, u32[]{:S(2)}) collective-permute-start(bf16[128,1024]{1,0:T(8,128)(2,1)S(1)} %get-tuple-element.74.refs_0_), channel_id=1, source_target_pairs={{0,4},{1,5},{2,6},{3,7},{4,0},{5,1},{6,2},{7,3},{8,12},{9,13},{10,... | collective-permute-start | bytes 786440 | tf_op jit(solution)/shard_map/ppermute | solution.py:343
  16.3 11.0 %collective-permute-start.4 = (bf16[128,1024]{1,0:T(8,128)(2,1)S(1)}, bf16[128,1024]{1,0:T(8,128)(2,1)}, u32[]{:S(2)}, u32[]{:S(2)}) collective-permute-start(bf16[128,1024]{1,0:T(8,128)(2,1)S(1)} %collective-permute-done.1), channel_id=1, source_target_pairs={{4,0},{5,1},{6,2},{7,3},{8,12},{9,13},{10,14},{11,15},{20,16},{21,... | collective-permute-start | bytes 786440 | tf_op jit(solution)/shard_map/ppermute | solution.py:343
  18.9 10.6 %collective-permute-start.5 = (bf16[128,1024]{1,0:T(8,128)(2,1)S(1)}, bf16[128,1024]{1,0:T(8,128)(2,1)S(1)}, u32[]{:S(2)}, u32[]{:S(2)}) collective-permute-start(bf16[128,1024]{1,0:T(8,128)(2,1)S(1)} %collective-permute-done.refs_1_), channel_id=1, source_target_pairs={{0,2},{2,0},{1,3},{3,1},{4,6},{6,4},{5,7},{7,5},{8,10},{10,8},{9,1... | collective-permute-start | bytes 786440 | tf_op jit(solution)/shard_map/ppermute | solution.py:343
  21.4 19.2 %collective-permute-start.11 = (bf16[128,1024]{1,0:T(8,128)(2,1)S(1)}, bf16[128,1024]{1,0:T(8,128)(2,1)S(1)}, u32[]{:S(2)}, u32[]{:S(2)}) collective-permute-start(bf16[128,1024]{1,0:T(8,128)(2,1)S(1)} %collective-permute-done.8.refs_1_), channel_id=1, source_target_pairs={{4,8},{5,9},{6,10},{7,11},{8,4},{9,5},{10,6},{11,7},{20,24},{21,25... | collective-permute-start | bytes 786440 | tf_op jit(solution)/shard_map/ppermute | solution.py:343
  25.3 15.3 %collective-permute-start.12 = (bf16[128,1024]{1,0:T(8,128)(2,1)S(1)}, bf16[128,1024]{1,0:T(8,128)(2,1)}, u32[]{:S(2)}, u32[]{:S(2)}) collective-permute-start(bf16[128,1024]{1,0:T(8,128)(2,1)S(1)} %collective-permute-done.9), channel_id=1, source_target_pairs={{4,0},{5,1},{6,2},{7,3},{8,12},{9,13},{10,14},{11,15},{20,16},{21,... | collective-permute-start | bytes 786440 | tf_op jit(solution)/shard_map/ppermute | solution.py:343
  27.4 13.9 %collective-permute-start.13 = (bf16[128,1024]{1,0:T(8,128)(2,1)S(1)}, bf16[128,1024]{1,0:T(8,128)(2,1)S(1)}, u32[]{:S(2)}, u32[]{:S(2)}) collective-permute-start(bf16[128,1024]{1,0:T(8,128)(2,1)S(1)} %collective-permute-done.10.refs_3_), channel_id=1, source_target_pairs={{0,4},{1,5},{2,6},{3,7},{4,0},{5,1},{6,2},{7,3},{8,12},{9,13},{10,... | collective-permute-start | bytes 786440 | tf_op jit(solution)/shard_map/ppermute | solution.py:343
  29.6 14.4 %all-to-all-start = ((f32[16,16,128]{2,1,0:T(8,128)}), f32[16,16,128]{2,1,0:T(8,128)S(1)}, u32[]{:S(2)}, u32[]{:S(2)}) async-start(f32[16,16,128]{2,1,0:T(8,128)} %shard_map.74), calls=%async_computation | async-start | bytes 262144 | tf_op jit(solution)/shard_map/all_to_all | solution.py:438
  52.1 10.9 %collective-permute-start.18 = (bf16[8,6,16,1024]{3,2,1,0:T(8,128)(2,1)S(1)}, bf16[8,6,16,1024]{3,2,1,0:T(8,128)(2,1)S(1)}, u32[]{:S(2)}, u32[]{:S(2)}) collective-permute-start(bf16[8,6,16,1024]{3,2,1,0:T(8,128)(2,1)S(1)} %get-tuple-element.84), channel_id=1, source_target_pairs={{0,1},{1,0},{2,3},{3,2},{4,5},{5,4},{6,7},{7,6},{8,9},{9,8},{10,11... | collective-permute-start | bytes 4718600 | tf_op jit(solution)/shard_map/ppermute | solution.py:343
  53.2 14.5 %collective-permute-start.20 = (bf16[8,6,16,1024]{3,2,1,0:T(8,128)(2,1)S(1)}, bf16[8,6,16,1024]{3,2,1,0:T(8,128)(2,1)S(1)}, u32[]{:S(2)}, u32[]{:S(2)}) collective-permute-start(bf16[8,6,16,1024]{3,2,1,0:T(8,128)(2,1)S(1)} %get-tuple-element.90), channel_id=1, source_target_pairs={{0,1},{1,0},{2,3},{3,2},{4,5},{5,4},{6,7},{7,6},{8,9},{9,8},{10,11... | collective-permute-start | bytes 4718600 | tf_op jit(solution)/shard_map/ppermute | solution.py:343
  54.6 13.1 %collective-permute-start.19 = (bf16[128,1024]{1,0:T(8,128)(2,1)S(1)}, bf16[128,1024]{1,0:T(8,128)(2,1)S(1)}, u32[]{:S(2)}, u32[]{:S(2)}) collective-permute-start(bf16[128,1024]{1,0:T(8,128)(2,1)S(1)} %broadcast_select_fusion.refs_8_), channel_id=1, source_target_pairs={{0,2},{2,0},{1,3},{3,1},{4,6},{6,4},{5,7},{7,5},{8,10},{10,8},{9,1... | collective-permute-start | bytes 786440 | tf_op jit(solution)/shard_map/ppermute | solution.py:343
  56.0 11.7 %collective-permute-start.21 = (bf16[128,1024]{1,0:T(8,128)(2,1)S(1)}, bf16[128,1024]{1,0:T(8,128)(2,1)S(1)}, u32[]{:S(2)}, u32[]{:S(2)}) collective-permute-start(bf16[128,1024]{1,0:T(8,128)(2,1)S(1)} %broadcast_select_fusion.1.refs_4_), channel_id=1, source_target_pairs={{0,1},{1,0},{2,3},{3,2},{4,5},{5,4},{6,7},{7,6},{8,9},{9,8},{10,11... | collective-permute-start | bytes 786440 | tf_op jit(solution)/shard_map/ppermute | solution.py:343
  112.9 10.6 %collective-permute-start.37 = (bf16[128,1024]{1,0:T(8,128)(2,1)S(1)}, bf16[128,1024]{1,0:T(8,128)(2,1)S(1)}, u32[]{:S(2)}, u32[]{:S(2)}) collective-permute-start(bf16[128,1024]{1,0:T(8,128)(2,1)S(1)} %get-tuple-element.128), channel_id=1, source_target_pairs={{0,4},{1,5},{2,6},{3,7},{4,0},{5,1},{6,2},{7,3},{8,12},{9,13},{10,... | collective-permute-start | bytes 786440 | tf_op jit(solution)/shard_map/ppermute | solution.py:343
  117.6 11.5 %collective-permute-start.27 = (bf16[128,1024]{1,0:T(8,128)(2,1)S(1)}, bf16[128,1024]{1,0:T(8,128)(2,1)S(1)}, u32[]{:S(2)}, u32[]{:S(2)}) collective-permute-start(bf16[128,1024]{1,0:T(8,128)(2,1)S(1)} %fusion.8), channel_id=1, source_target_pairs={{0,4},{1,5},{2,6},{3,7},{12,8},{13,9},{14,10},{15,11},{16,20},{17,... | collective-permute-start | bytes 786440 | tf_op jit(solution)/shard_map/ppermute | solution.py:343
  118.9 12.2 %collective-permute-start.28 = (bf16[128,1024]{1,0:T(8,128)(2,1)S(1)}, bf16[128,1024]{1,0:T(8,128)(2,1)S(1)}, u32[]{:S(2)}, u32[]{:S(2)}) collective-permute-start(bf16[128,1024]{1,0:T(8,128)(2,1)S(1)} %get-tuple-element.100), channel_id=1, source_target_pairs={{0,2},{2,0},{1,3},{3,1},{4,6},{6,4},{5,7},{7,5},{8,10},{10,8},{9,1... | collective-permute-start | bytes 786440 | tf_op jit(solution)/shard_map/ppermute | solution.py:343
  125.6 12.0 %collective-permute-start.38 = (bf16[128,1024]{1,0:T(8,128)(2,1)S(1)}, bf16[128,1024]{1,0:T(8,128)(2,1)S(1)}, u32[]{:S(2)}, u32[]{:S(2)}) collective-permute-start(bf16[128,1024]{1,0:T(8,128)(2,1)S(1)} %fusion.1), channel_id=1, source_target_pairs={{0,4},{1,5},{2,6},{3,7},{12,8},{13,9},{14,10},{15,11},{16,20},{17,... | collective-permute-start | bytes 786440 | tf_op jit(solution)/shard_map/ppermute | solution.py:343
  126.9 10.7 %collective-permute-start.39 = (bf16[128,1024]{1,0:T(8,128)(2,1)S(1)}, bf16[128,1024]{1,0:T(8,128)(2,1)S(1)}, u32[]{:S(2)}, u32[]{:S(2)}) collective-permute-start(bf16[128,1024]{1,0:T(8,128)(2,1)S(1)} %get-tuple-element.114), channel_id=1, source_target_pairs={{0,2},{2,0},{1,3},{3,1},{4,6},{6,4},{5,7},{7,5},{8,10},{10,8},{9,1... | collective-permute-start | bytes 786440 | tf_op jit(solution)/shard_map/ppermute | solution.py:343
  131.2 10.7 %collective-permute-start.30 = (bf16[128,1024]{1,0:T(8,128)(2,1)S(1)}, bf16[128,1024]{1,0:T(8,128)(2,1)S(1)}, u32[]{:S(2)}, u32[]{:S(2)}) collective-permute-start(bf16[128,1024]{1,0:T(8,128)(2,1)S(1)} %add_convert_fusion.6), channel_id=1, source_target_pairs={{4,8},{5,9},{6,10},{7,11},{8,4},{9,5},{10,6},{11,7},{20,24},{21,25... | collective-permute-start | bytes 786440 | tf_op jit(solution)/shard_map/ppermute | solution.py:343
  137.6 11.7 %collective-permute-start.41 = (bf16[128,1024]{1,0:T(8,128)(2,1)S(1)}, bf16[128,1024]{1,0:T(8,128)(2,1)S(1)}, u32[]{:S(2)}, u32[]{:S(2)}) collective-permute-start(bf16[128,1024]{1,0:T(8,128)(2,1)S(1)} %add_convert_fusion.3), channel_id=1, source_target_pairs={{4,8},{5,9},{6,10},{7,11},{8,4},{9,5},{10,6},{11,7},{20,24},{21,25... | collective-permute-start | bytes 786440 | tf_op jit(solution)/shard_map/ppermute | solution.py:343
  140.7 11.1 %collective-permute-start.40 = (bf16[128,1024]{1,0:T(8,128)(2,1)S(1)}, bf16[128,1024]{1,0:T(8,128)(2,1)S(1)}, u32[]{:S(2)}, u32[]{:S(2)}) collective-permute-start(bf16[128,1024]{1,0:T(8,128)(2,1)S(1)} %fusion.2), channel_id=1, source_target_pairs={{0,4},{1,5},{2,6},{3,7},{12,8},{13,9},{14,10},{15,11},{16,20},{17,... | collective-permute-start | bytes 786440 | tf_op jit(solution)/shard_map/ppermute | solution.py:343
  144.1 13.4 %collective-permute-start.34 = (bf16[128,1024]{1,0:T(8,128)(2,1)S(1)}, bf16[128,1024]{1,0:T(8,128)(2,1)S(1)}, u32[]{:S(2)}, u32[]{:S(2)}) collective-permute-start(bf16[128,1024]{1,0:T(8,128)(2,1)S(1)} %fusion.7), channel_id=1, source_target_pairs={{0,4},{1,5},{2,6},{3,7},{4,0},{5,1},{6,2},{7,3},{8,12},{9,13},{10,... | collective-permute-start | bytes 786440 | tf_op jit(solution)/shard_map/ppermute | solution.py:343
  146.3 11.7 %collective-permute-start.33 = (bf16[128,1024]{1,0:T(8,128)(2,1)S(1)}, bf16[128,1024]{1,0:T(8,128)(2,1)S(1)}, u32[]{:S(2)}, u32[]{:S(2)}) collective-permute-start(bf16[128,1024]{1,0:T(8,128)(2,1)S(1)} %add_convert_fusion.5), channel_id=1, source_target_pairs={{4,8},{5,9},{6,10},{7,11},{8,4},{9,5},{10,6},{11,7},{20,24},{21,25... | collective-permute-start | bytes 786440 | tf_op jit(solution)/shard_map/ppermute | solution.py:343
  (28 other events, 180.5 us)

commit v6 on v5

--- a/solution.py
+++ b/solution.py
@@ -110,8 +110,8 @@
 def slot_sources(z, dp):
     low = z < 2
     column = z, z ^ 1, jnp.where(low, 2, 1), jnp.where(low, 3, 0)
-    early = [(column[i], side) for side in (0, 2) for i in range(3)]
-    late = [(column[3], side) for side in (0, 2)]
+    early = [(column[i], side) for side in (0, 2) for i in (0, 1)]
+    late = [(column[i], side) for side in (0, 2) for i in (2, 3)]
     return [
         from_z * 4 + (dp ^ (side + core))
         for group in (early, late)
@@ -143,7 +143,7 @@
 def tables(place, choices, experts):
     count, _, token_count = choices.shape
     rows = experts * slots
-    late = count // 8
+    late = count // 4
     early = count // 2 - late
     shapes = [(early, rows, token_count), (early, rows, token_count), (2 * late, rows, token_count)]
     shapes = [jax.ShapeDtypeStruct(shape, jnp.bfloat16) for shape in shapes]
@@ -335,6 +335,8 @@
 middle_z = pairs_of([(1, 2), (2, 1)], stay_dp, 4)
 outward_z = pairs_of([(1, 0), (2, 3)], stay_dp, 4)
 inward_z = pairs_of([(0, 1), (3, 2)], stay_dp, 4)
+leap_out = pairs_of([(3, 1), (0, 2)], stay_dp, 4)
+leap_back = pairs_of([(1, 3), (2, 0)], stay_dp, 4)
 swap_x = pairs_of(stay_z, [(0, 2), (2, 0), (1, 3), (3, 1)], 4)
 swap_core = pairs_of(stay_z, [(0, 1), (1, 0), (2, 3), (3, 2)], 4)
 
@@ -347,31 +349,27 @@
     return lax.optimization_barrier(values)
 
 
-def tree_start(own):
-    near, middle, own_x = together(
-        send(own, swap_z), send(own, middle_z), send(own, swap_x)
+def tree_start(own, *others):
+    return together(
+        send(own, swap_z),
+        send(own, middle_z),
+        send(own, leap_out),
+        send(own, swap_x),
+        *others,
     )
-    return near, middle, own_x
-
-
-def tree_second(near, middle, own_x, *others):
-    if own_x is None:
-        near_x = send(near, swap_x)
-    else:
-        near_x = send(own_x, swap_z)
-    return together(send(near, middle_z), send(middle, outward_z), near_x, *others)
-
-
-def tree_third(cross, outer, middle, edge, *others):
-    third = jnp.where(edge, outer, middle)
-    far, third_x, *others = together(send(cross, outward_z), send(third, swap_x), *others)
-    return third, third_x, jnp.where(edge, far, cross), *others
-
-
-def tree_rest(early, fourth, mine, theirs, experts):
+
+
+def tree_second(near, middle, cross, edge, *others):
+    outer, far, near_x, *others = together(
+        send(middle, outward_z), send(cross, outward_z), send(near, swap_x), *others
+    )
+    return jnp.where(edge, outer, middle), jnp.where(edge, far, cross), near_x, *others
+
+
+def tree_rest(early, third, fourth, third_x, mine, theirs, experts):
     mine_rows, theirs_rows = pick_pair(early, mine, theirs, experts)
     fourth_x, theirs_rows = together(send(fourth, swap_x), send(theirs_rows, swap_core))
-    late = [fourth, fourth_x]
+    late = [third, fourth, third_x, fourth_x]
     return [mine_rows, theirs_rows], late + [send(block, swap_core) for block in late]
 
 
@@ -379,27 +377,21 @@
     return rounded_sum(mine, send(theirs, swap_core))
 
 
-def tree_return(chip, near_by_z):
-    own, near, third, own_x, near_x, third_x, fourth, fourth_x = [chip[i] for i in range(8)]
-    if near_by_z:
-        near_x = send(near_x, swap_z)
-    fourth_in, third_x, near_x, own_x = together(send(fourth_x, swap_x), third_x, near_x, own_x)
-    if near_by_z:
-        own_x = rounded_sum(own_x, near_x)
+def tree_return(chip):
+    own, near, own_x, near_x, third, fourth, third_x, fourth_x = [chip[i] for i in range(8)]
+    third_in = send(third_x, swap_x)
+    fourth_in, near_x, own_x = together(send(fourth_x, swap_x), near_x, own_x)
     fourth = rounded_sum(fourth, fourth_in)
-    far, third_in, near_x, own_x = together(
-        send(fourth, inward_z), send(third_x, swap_x), near_x, own_x
+    third = rounded_sum(third, third_in)
+    far, outer, near_in, own_x = together(
+        send(fourth, inward_z), send(third, inward_z), send(near_x, swap_x), own_x
     )
-    cross = rounded_sum(fourth, far)
-    third = rounded_sum(third, third_in)
-    sent = [send(third, inward_z), send(cross, middle_z)]
-    if not near_by_z:
-        sent.append(send(near_x, swap_x))
-    outer, crossed, *near_in, own_x = together(*sent, own_x)
-    middle = rounded_sum(third, outer)
-    near = rounded_sum(near, crossed, *near_in)
     return rounded_sum(
-        own, send(own_x, swap_x), send(middle, middle_z), send(near, swap_z)
+        own,
+        send(own_x, swap_x),
+        send(rounded_sum(fourth, far), leap_back),
+        send(rounded_sum(third, outer), middle_z),
+        send(rounded_sum(near, near_in), swap_z),
     )
 
 
@@ -417,12 +409,13 @@
     parts = normed_parts(tokens, norm_gain, gather_chunks)
     if as_tree:
         choice = ranked(routes, route_weight, device_count, local_count)
-        firsts = [tree_start(part) for part in parts]
-        seconds = [
-            tree_second(near, middle, own_x if chunk % 2 else None, choice)
-            for chunk, (near, middle, own_x) in enumerate(firsts)
-        ]
-        choice = seconds[0][3]
+        firsts = []
+        for part in parts:
+            if not firsts:
+                near, middle, cross, own_x, choice = tree_start(part, choice)
+            else:
+                near, middle, cross, own_x = tree_start(part)
+            firsts.append((near, middle, cross, own_x))
     else:
         every = jnp.arange(device_count * local_count, dtype=jnp.int32)
         same = routes[:, :, None] == every
@@ -438,23 +431,27 @@
     choices = lax.all_to_all(choice, axes, split_axis=0, concat_axis=0, tiled=True)
     if as_tree:
         place = jnp.stack([lax.axis_index("expert"), lax.axis_index("dp")])
+        seconds = []
+        for near, middle, cross, own_x in firsts:
+            if not seconds:
+                third, fourth, near_x, choices = tree_second(near, middle, cross, edge, choices)
+            else:
+                third, fourth, near_x, third_x = tree_second(
+                    near, middle, cross, edge, seconds[-1][3]
+                )
+                seconds[-1] = (*seconds[-1][:3], third_x)
+            seconds.append((third, fourth, near_x, send(third, swap_x)))
         mine, theirs, late_picker, spread, scale = tables(place, choices, local_count)
         theirs = send(theirs, swap_core)
-        thirds = []
-        for cross, outer, near_x, _ in seconds:
-            middle = firsts[len(thirds)][1]
-            if not thirds:
-                third, third_x, fourth = tree_third(cross, outer, middle, edge)
-            else:
-                third, third_x, fourth, theirs = tree_third(cross, outer, middle, edge, theirs)
-            thirds.append((third, third_x, fourth))
-        order = (0, 1, 2, 3, 4, 5, 8, 9, 10, 11, 12, 13, 6, 7, 14, 15)
+        order = (0, 1, 2, 3, 8, 9, 10, 11, 4, 5, 6, 7, 12, 13, 14, 15)
         row_chunks, late_chunks = [], []
-        for part, (near, middle, own_x), (cross, outer, near_x, _), (third, third_x, fourth) in zip(
-            parts, firsts, seconds, thirds
+        for part, (near, middle, cross, own_x), (third, fourth, near_x, third_x) in zip(
+            parts, firsts, seconds
         ):
-            early = part, near, third, own_x, near_x, third_x
-            rows, late = tree_rest(early, fourth, mine, theirs, local_count)
+            early = part, near, own_x, near_x
+            rows, late = tree_rest(
+                early, third, fourth, third_x, mine, theirs, local_count
+            )
             row_chunks.append([rows_of.reshape(local_count, -1, width) for rows_of in rows])
             late_chunks.append(late)
     else:
@@ -481,7 +478,7 @@
             sums.append(total.astype(jnp.bfloat16))
     results = sums
     if as_tree:
-        results = [tree_return(chip, chunk % 2 == 1) for chunk, chip in enumerate(sums)]
+        results = [tree_return(chip) for chip in sums]
     return jnp.concatenate(results, axis=1)
 
 

time: 166 us -> 181 us (1.090)
  waiting for transfers between devices: 49.1 us -> 59.2 us
  starting transfers between devices: 65 us -> 71.1 us
    ppermute x45 -> x49, waiting for transfers between devices: 49.1 us -> 59.1 us  [send(): return lax.ppermute(value, axes, pairs)]
    ppermute x45 -> x49, starting transfers between devices: 59.6 us -> 65.8 us  [send(): return lax.ppermute(value, axes, pairs)]
    unnamed x12 -> x8, local copies, waits for them, and re-layouts: 3.81 us -> 3.11 us
  transfers between devices with their start and end apart: 46 -> 50, of which waited for: 21 -> 23; matrix products, arithmetic and copies ran while one was open for 2% -> 2% of each run, Pallas kernels for 7% -> 6%
where the time goes in v6:
time: 181 us; the launch traced here: 180 us
  starting transfers between devices  71.1 us (39%)
  waiting for transfers between devices  59.2 us (33%)
  Pallas kernels  42.1 us (23%)
  other arithmetic  4.37 us (2%)
  local copies, waits for them, and re-layouts  3.25 us (2%)
    ppermute x49, starting transfers between devices, send(): return lax.ppermute(value, axes, pairs)  65.8 us
    ppermute x49, waiting for transfers between devices, send(): return lax.ppermute(value, axes, pairs)  59.1 us
    pallas_call x1, Pallas kernels, hidden_rows(): pl.pallas_call(functools.partial(hidden_kernel, chunks, groups, late), gr...  22.2 us
    pallas_call x2, Pallas kernels, mix_rows(): pl.pallas_call(functools.partial(mix_kernel, order), grid=(experts // gro...  16.5 us
    all_to_all x1, starting transfers between devices, shards(): lax.all_to_all(choice, axes, split_axis=0, concat_axis=0, tiled=True)  5.27 us
  transfers between devices with their start and end apart: 50, of which 23 were waited for; matrix products, arithmetic and copies ran while one was open for 2% of the time, Pallas kernels for 6%

profile of v6, /device:TPU:8, one launch (start us, length us, event | category | flops | bytes accessed | tf_op | source)
XLA Modules:
  0.0 180.4 jit_solution(1571131519395505671)
XLA Ops:
  4.8 3.5 %collective-permute-start.1 = (bf16[128,1024]{1,0:T(8,128)(2,1)S(1)}, bf16[128,1024]{1,0:T(8,128)(2,1)S(1)}, u32[]{:S(2)}, u32[]{:S(2)}) collective-permute-start(bf16[128,1024]{1,0:T(8,128)(2,1)S(1)} %get-tuple-element.55.refs_0_), channel_id=1, source_target_pairs={{4,8},{5,9},{6,10},{7,11},{8,4},{9,5},{10,6},{11,7},{20,24},{21,25... | collective-permute-start | bytes 786440 | tf_op jit(solution)/shard_map/ppermute | solution.py:345
  11.4 4.2 %collective-permute-done.2 = bf16[128,1024]{1,0:T(8,128)(2,1)S(1)} collective-permute-done((bf16[128,1024]{1,0:T(8,128)(2,1)S(1)}, bf16[128,1024]{1,0:T(8,128)(2,1)S(1)}, u32[]{:S(2)}, u32[]{:S(2)}) %collective-permute-start.2) | collective-permute-done | bytes 262176 | tf_op jit(solution)/shard_map/ppermute | solution.py:345
  15.6 3.5 %collective-permute-start.11 = (bf16[128,1024]{1,0:T(8,128)(2,1)S(1)}, bf16[128,1024]{1,0:T(8,128)(2,1)S(1)}, u32[]{:S(2)}, u32[]{:S(2)}) collective-permute-start(bf16[128,1024]{1,0:T(8,128)(2,1)S(1)} %get-tuple-element.69.refs_0_), channel_id=1, source_target_pairs={{4,8},{5,9},{6,10},{7,11},{8,4},{9,5},{10,6},{11,7},{20,24},{21,25... | collective-permute-start | bytes 786440 | tf_op jit(solution)/shard_map/ppermute | solution.py:345
  19.1 2.2 %collective-permute-done.1 = bf16[128,1024]{1,0:T(8,128)(2,1)S(1)} collective-permute-done((bf16[128,1024]{1,0:T(8,128)(2,1)S(1)}, bf16[128,1024]{1,0:T(8,128)(2,1)S(1)}, u32[]{:S(2)}, u32[]{:S(2)}) %collective-permute-start.1) | collective-permute-done | bytes 262176 | tf_op jit(solution)/shard_map/ppermute | solution.py:345
  24.0 4.6 %collective-permute-start.4 = (bf16[128,1024]{1,0:T(8,128)(2,1)S(1)}, bf16[128,1024]{1,0:T(8,128)(2,1)}, u32[]{:S(2)}, u32[]{:S(2)}) collective-permute-start(bf16[128,1024]{1,0:T(8,128)(2,1)S(1)} %collective-permute-done.1), channel_id=1, source_target_pairs={{4,0},{5,1},{6,2},{7,3},{8,12},{9,13},{10,14},{11,15},{20,16},{21,... | collective-permute-start | bytes 786440 | tf_op jit(solution)/shard_map/ppermute | solution.py:345
  29.9 5.3 %all-to-all-start = ((f32[16,16,128]{2,1,0:T(8,128)}), f32[16,16,128]{2,1,0:T(8,128)S(1)}, u32[]{:S(2)}, u32[]{:S(2)}) async-start(f32[16,16,128]{2,1,0:T(8,128)} %shard_map.74), calls=%async_computation | async-start | bytes 262144 | tf_op jit(solution)/shard_map/all_to_all | solution.py:431
  36.8 3.2 %collective-permute-start.14 = (bf16[128,1024]{1,0:T(8,128)(2,1)S(1)}, bf16[128,1024]{1,0:T(8,128)(2,1)}, u32[]{:S(2)}, u32[]{:S(2)}) collective-permute-start(bf16[128,1024]{1,0:T(8,128)(2,1)S(1)} %collective-permute-done.11), channel_id=1, source_target_pairs={{4,0},{5,1},{6,2},{7,3},{8,12},{9,13},{10,14},{11,15},{20,16},{21,... | collective-permute-start | bytes 786440 | tf_op jit(solution)/shard_map/ppermute | solution.py:345
  40.0 2.0 %collective-permute-start.15 = (bf16[128,1024]{1,0:T(8,128)(2,1)S(1)}, bf16[128,1024]{1,0:T(8,128)(2,1)}, u32[]{:S(2)}, u32[]{:S(2)}) collective-permute-start(bf16[128,1024]{1,0:T(8,128)(2,1)S(1)} %collective-permute-done.12), channel_id=1, source_target_pairs={{4,0},{5,1},{6,2},{7,3},{8,12},{9,13},{10,14},{11,15},{20,16},{21,... | collective-permute-start | bytes 786440 | tf_op jit(solution)/shard_map/ppermute | solution.py:345
  47.3 4.5 %collective-permute-done.15 = bf16[128,1024]{1,0:T(8,128)(2,1)} collective-permute-done((bf16[128,1024]{1,0:T(8,128)(2,1)S(1)}, bf16[128,1024]{1,0:T(8,128)(2,1)}, u32[]{:S(2)}, u32[]{:S(2)}) %collective-permute-start.15) | collective-permute-done | bytes 262176 | tf_op jit(solution)/shard_map/ppermute | solution.py:345
  55.0 6.9 %collective-permute-done.8.refs_7_ = bf16[128,1024]{1,0:T(8,128)(2,1)S(1)} collective-permute-done((bf16[128,1024]{1,0:T(8,128)(2,1)S(1)}, bf16[128,1024]{1,0:T(8,128)(2,1)S(1)}, u32[]{:S(2)}, u32[]{:S(2)}) %collective-permute-start.8) | collective-permute-done | bytes 262176 | tf_op jit(solution)/shard_map/ppermute | solution.py:345
  63.7 3.9 %collective-permute-done.18.refs_15_ = bf16[128,1024]{1,0:T(8,128)(2,1)S(1)} collective-permute-done((bf16[128,1024]{1,0:T(8,128)(2,1)S(1)}, bf16[128,1024]{1,0:T(8,128)(2,1)S(1)}, u32[]{:S(2)}, u32[]{:S(2)}) %collective-permute-start.18) | collective-permute-done | bytes 262176 | tf_op jit(solution)/shard_map/ppermute | solution.py:345
  68.6 4.2 %collective-permute-done.24.refs_14_ = bf16[128,1024]{1,0:T(8,128)(2,1)S(1)} collective-permute-done((bf16[128,1024]{1,0:T(8,128)(2,1)S(1)}, bf16[128,1024]{1,0:T(8,128)(2,1)S(1)}, u32[]{:S(2)}, u32[]{:S(2)}) %collective-permute-start.24) | collective-permute-done | bytes 262176 | tf_op jit(solution)/shard_map/ppermute | solution.py:345
  75.1 22.2 %shard_map.78.hidden_ref = bf16[8,256,768]{2,1,0:T(8,128)(2,1)S(1)} custom-call(bf16[8,64,1024]{2,1,0:T(8,128)(2,1)S(1)} %bitcast.65, bf16[8,64,1024]{2,1,0:T(8,128)(2,1)S(1)} %bitcast.66, bf16[8,64,1024]{2,1,0:T(8,128)(2,1)S(1)} %bitcast.67, bf16[8,64,1024]{2,1,0:T(8,128)(2,1)S(1)} %bitcast.68, bf16[128,1024]{1,0:T(8,128)(2,1)S(1)} %broadcast_select_fusion.2.refs_4_, ...), custom_call_target="tpu_custom_call" | custom-call | flops 12884901888 | bytes 50331648 | tf_op jit(solution)/shard_map/pallas_call | solution.py:246
  97.2 8.2 %shard_map.79 = (bf16[8,128,1024]{2,1,0:T(8,128)(2,1)S(1)}, bf16[8,128,1024]{2,1,0:T(8,128)(2,1)S(1)}) custom-call(bf16[8,256,768]{2,1,0:T(8,128)(2,1)S(1)} %shard_map.78.hidden_ref, bf16[8,768,2048]{2,1,0:T(8,128)(2,1)} %down_ref.3, bf16[16,128,128]{2,1,0:T(8,128)(2,1)S(1)} %get-tuple-element.86.spread_ref), custom_call_target="tpu_custom_call" | custom-call | flops 3758096384 | bytes 19922944 | tf_op jit(solution)/shard_map/pallas_call | solution.py:299
  105.7 8.2 %shard_map.80 = (bf16[8,128,1024]{2,1,0:T(8,128)(2,1)S(1)}, bf16[8,128,1024]{2,1,0:T(8,128)(2,1)S(1)}) custom-call(bf16[8,256,768]{2,1,0:T(8,128)(2,1)S(1)} %shard_map.78.hidden_ref, bf16[8,768,2048]{2,1,0:T(8,128)(2,1)} %down_ref.3, bf16[16,128,128]{2,1,0:T(8,128)(2,1)S(1)} %get-tuple-element.86.spread_ref), custom_call_target="tpu_custom_call" | custom-call | flops 3758096384 | bytes 19922944 | tf_op jit(solution)/shard_map/pallas_call | solution.py:299
  121.4 9.0 %collective-permute-done.30 = bf16[128,1024]{1,0:T(8,128)(2,1)S(1)} collective-permute-done((bf16[128,1024]{1,0:T(8,128)(2,1)S(1)}, bf16[128,1024]{1,0:T(8,128)(2,1)S(1)}, u32[]{:S(2)}, u32[]{:S(2)}) %collective-permute-start.30) | collective-permute-done | bytes 262176 | tf_op jit(solution)/shard_map/ppermute | solution.py:345
  135.9 5.6 %collective-permute-done.42 = bf16[128,1024]{1,0:T(8,128)(2,1)S(1)} collective-permute-done((bf16[128,1024]{1,0:T(8,128)(2,1)S(1)}, bf16[128,1024]{1,0:T(8,128)(2,1)S(1)}, u32[]{:S(2)}, u32[]{:S(2)}) %collective-permute-start.42) | collective-permute-done | bytes 262176 | tf_op jit(solution)/shard_map/ppermute | solution.py:345
  147.3 4.1 %collective-permute-start.38 = (bf16[128,1024]{1,0:T(8,128)(2,1)S(1)}, bf16[128,1024]{1,0:T(8,128)(2,1)S(1)}, u32[]{:S(2)}, u32[]{:S(2)}) collective-permute-start(bf16[128,1024]{1,0:T(8,128)(2,1)S(1)} %fusion.7), channel_id=1, source_target_pairs={{0,4},{1,5},{2,6},{3,7},{4,0},{5,1},{6,2},{7,3},{8,12},{9,13},{10,... | collective-permute-start | bytes 786440 | tf_op jit(solution)/shard_map/ppermute | solution.py:345
  151.5 3.3 %collective-permute-start.36 = (bf16[128,1024]{1,0:T(8,128)(2,1)S(1)}, bf16[128,1024]{1,0:T(8,128)(2,1)S(1)}, u32[]{:S(2)}, u32[]{:S(2)}) collective-permute-start(bf16[128,1024]{1,0:T(8,128)(2,1)S(1)} %add_convert_fusion.5), channel_id=1, source_target_pairs={{4,12},{5,13},{6,14},{7,15},{8,0},{9,1},{10,2},{11,3},{20,28},{21,... | collective-permute-start | bytes 786440 | tf_op jit(solution)/shard_map/ppermute | solution.py:345
  155.2 4.8 %collective-permute-done.41 = bf16[128,1024]{1,0:T(8,128)(2,1)S(1)} collective-permute-done((bf16[128,1024]{1,0:T(8,128)(2,1)S(1)}, bf16[128,1024]{1,0:T(8,128)(2,1)S(1)}, u32[]{:S(2)}, u32[]{:S(2)}) %collective-permute-start.41) | collective-permute-done | bytes 262176 | tf_op jit(solution)/shard_map/ppermute | solution.py:345
  159.9 3.8 %collective-permute-start.37 = (bf16[128,1024]{1,0:T(8,128)(2,1)S(1)}, bf16[128,1024]{1,0:T(8,128)(2,1)S(1)}, u32[]{:S(2)}, u32[]{:S(2)}) collective-permute-start(bf16[128,1024]{1,0:T(8,128)(2,1)S(1)} %add_convert_fusion.4), channel_id=1, source_target_pairs={{4,8},{5,9},{6,10},{7,11},{8,4},{9,5},{10,6},{11,7},{20,24},{21,25... | collective-permute-start | bytes 786440 | tf_op jit(solution)/shard_map/ppermute | solution.py:345
  164.6 4.9 %collective-permute-start.46 = (bf16[128,1024]{1,0:T(8,128)(2,1)S(1)}, bf16[128,1024]{1,0:T(8,128)(2,1)S(1)}, u32[]{:S(2)}, u32[]{:S(2)}) collective-permute-start(bf16[128,1024]{1,0:T(8,128)(2,1)S(1)} %add_convert_fusion.3), channel_id=1, source_target_pairs={{4,12},{5,13},{6,14},{7,15},{8,0},{9,1},{10,2},{11,3},{20,28},{21,... | collective-permute-start | bytes 786440 | tf_op jit(solution)/shard_map/ppermute | solution.py:345
  172.1 3.8 %collective-permute-done.46 = bf16[128,1024]{1,0:T(8,128)(2,1)S(1)} collective-permute-done((bf16[128,1024]{1,0:T(8,128)(2,1)S(1)}, bf16[128,1024]{1,0:T(8,128)(2,1)S(1)}, u32[]{:S(2)}, u32[]{:S(2)}) %collective-permute-start.46) | collective-permute-done | bytes 262176 | tf_op jit(solution)/shard_map/ppermute | solution.py:345
  176.0 3.3 %collective-permute-done.47 = bf16[128,1024]{1,0:T(8,128)(2,1)S(1)} collective-permute-done((bf16[128,1024]{1,0:T(8,128)(2,1)S(1)}, bf16[128,1024]{1,0:T(8,128)(2,1)S(1)}, u32[]{:S(2)}, u32[]{:S(2)}) %collective-permute-start.47) | collective-permute-done | bytes 262176 | tf_op jit(solution)/shard_map/ppermute | solution.py:345
  (112 shorter events, 50.8 us)
Async XLA Ops:
  4.8 16.4 %collective-permute-start.1 = (bf16[128,1024]{1,0:T(8,128)(2,1)S(1)}, bf16[128,1024]{1,0:T(8,128)(2,1)S(1)}, u32[]{:S(2)}, u32[]{:S(2)}) collective-permute-start(bf16[128,1024]{1,0:T(8,128)(2,1)S(1)} %get-tuple-element.55.refs_0_), channel_id=1, source_target_pairs={{4,8},{5,9},{6,10},{7,11},{8,4},{9,5},{10,6},{11,7},{20,24},{21,25... | collective-permute-start | bytes 786440 | tf_op jit(solution)/shard_map/ppermute | solution.py:345
  8.3 15.2 %collective-permute-start = (bf16[128,1024]{1,0:T(8,128)(2,1)S(1)}, bf16[128,1024]{1,0:T(8,128)(2,1)S(1)}, u32[]{:S(2)}, u32[]{:S(2)}) collective-permute-start(bf16[128,1024]{1,0:T(8,128)(2,1)S(1)} %get-tuple-element.55.refs_0_), channel_id=1, source_target_pairs={{0,4},{1,5},{2,6},{3,7},{4,0},{5,1},{6,2},{7,3},{8,12},{9,13},{10,... | collective-permute-start | bytes 786440 | tf_op jit(solution)/shard_map/ppermute | solution.py:345
  9.2 14.8 %collective-permute-start.13 = (bf16[128,1024]{1,0:T(8,128)(2,1)S(1)}, bf16[128,1024]{1,0:T(8,128)(2,1)S(1)}, u32[]{:S(2)}, u32[]{:S(2)}) collective-permute-start(bf16[128,1024]{1,0:T(8,128)(2,1)S(1)} %get-tuple-element.69.refs_0_), channel_id=1, source_target_pairs={{0,2},{2,0},{1,3},{3,1},{4,6},{6,4},{5,7},{7,5},{8,10},{10,8},{9,1... | collective-permute-start | bytes 786440 | tf_op jit(solution)/shard_map/ppermute | solution.py:345
  10.1 18.6 %collective-permute-start.12 = (bf16[128,1024]{1,0:T(8,128)(2,1)S(1)}, bf16[128,1024]{1,0:T(8,128)(2,1)S(1)}, u32[]{:S(2)}, u32[]{:S(2)}) collective-permute-start(bf16[128,1024]{1,0:T(8,128)(2,1)S(1)} %get-tuple-element.69.refs_0_), channel_id=1, source_target_pairs={{12,4},{13,5},{14,6},{15,7},{0,8},{1,9},{2,10},{3,11},{28,20},{29,... | collective-permute-start | bytes 786440 | tf_op jit(solution)/shard_map/ppermute | solution.py:345
  15.6 19.7 %collective-permute-start.11 = (bf16[128,1024]{1,0:T(8,128)(2,1)S(1)}, bf16[128,1024]{1,0:T(8,128)(2,1)S(1)}, u32[]{:S(2)}, u32[]{:S(2)}) collective-permute-start(bf16[128,1024]{1,0:T(8,128)(2,1)S(1)} %get-tuple-element.69.refs_0_), channel_id=1, source_target_pairs={{4,8},{5,9},{6,10},{7,11},{8,4},{9,5},{10,6},{11,7},{20,24},{21,25... | collective-permute-start | bytes 786440 | tf_op jit(solution)/shard_map/ppermute | solution.py:345
  21.3 14.0 %collective-permute-start.10 = (bf16[128,1024]{1,0:T(8,128)(2,1)S(1)}, bf16[128,1024]{1,0:T(8,128)(2,1)S(1)}, u32[]{:S(2)}, u32[]{:S(2)}) collective-permute-start(bf16[128,1024]{1,0:T(8,128)(2,1)S(1)} %get-tuple-element.69.refs_0_), channel_id=1, source_target_pairs={{0,4},{1,5},{2,6},{3,7},{4,0},{5,1},{6,2},{7,3},{8,12},{9,13},{10,... | collective-permute-start | bytes 786440 | tf_op jit(solution)/shard_map/ppermute | solution.py:345
  23.5 16.5 %collective-permute-start.6 = (bf16[128,1024]{1,0:T(8,128)(2,1)S(1)}, bf16[128,1024]{1,0:T(8,128)(2,1)S(1)}, u32[]{:S(2)}, u32[]{:S(2)}) collective-permute-start(bf16[128,1024]{1,0:T(8,128)(2,1)S(1)} %collective-permute-done.refs_1_), channel_id=1, source_target_pairs={{0,2},{2,0},{1,3},{3,1},{4,6},{6,4},{5,7},{7,5},{8,10},{10,8},{9,1... | collective-permute-start | bytes 786440 | tf_op jit(solution)/shard_map/ppermute | solution.py:345
  24.0 18.0 %collective-permute-start.4 = (bf16[128,1024]{1,0:T(8,128)(2,1)S(1)}, bf16[128,1024]{1,0:T(8,128)(2,1)}, u32[]{:S(2)}, u32[]{:S(2)}) collective-permute-start(bf16[128,1024]{1,0:T(8,128)(2,1)S(1)} %collective-permute-done.1), channel_id=1, source_target_pairs={{4,0},{5,1},{6,2},{7,3},{8,12},{9,13},{10,14},{11,15},{20,16},{21,... | collective-permute-start | bytes 786440 | tf_op jit(solution)/shard_map/ppermute | solution.py:345
  28.6 13.3 %collective-permute-start.5 = (bf16[128,1024]{1,0:T(8,128)(2,1)S(1)}, bf16[128,1024]{1,0:T(8,128)(2,1)S(1)}, u32[]{:S(2)}, u32[]{:S(2)}) collective-permute-start(bf16[128,1024]{1,0:T(8,128)(2,1)S(1)} %collective-permute-done.2), channel_id=1, source_target_pairs={{4,0},{5,1},{6,2},{7,3},{8,12},{9,13},{10,14},{11,15},{20,16},{21,... | collective-permute-start | bytes 786440 | tf_op jit(solution)/shard_map/ppermute | solution.py:345
  45.7 21.9 %collective-permute-start.9 = (bf16[8,4,16,1024]{3,2,1,0:T(8,128)(2,1)S(1)}, bf16[8,4,16,1024]{3,2,1,0:T(8,128)(2,1)S(1)}, u32[]{:S(2)}, u32[]{:S(2)}) collective-permute-start(bf16[8,4,16,1024]{3,2,1,0:T(8,128)(2,1)S(1)} %get-tuple-element.67), channel_id=1, source_target_pairs={{0,1},{1,0},{2,3},{3,2},{4,5},{5,4},{6,7},{7,6},{8,9},{9,8},{10,11... | collective-permute-start | bytes 3145736 | tf_op jit(solution)/shard_map/ppermute | solution.py:345
  52.6 15.4 %collective-permute-start.19 = (bf16[8,4,16,1024]{3,2,1,0:T(8,128)(2,1)S(1)}, bf16[8,4,16,1024]{3,2,1,0:T(8,128)(2,1)S(1)}, u32[]{:S(2)}, u32[]{:S(2)}) collective-permute-start(bf16[8,4,16,1024]{3,2,1,0:T(8,128)(2,1)S(1)} %get-tuple-element.78), channel_id=1, source_target_pairs={{0,1},{1,0},{2,3},{3,2},{4,5},{5,4},{6,7},{7,6},{8,9},{9,8},{10,11... | collective-permute-start | bytes 3145736 | tf_op jit(solution)/shard_map/ppermute | solution.py:345
  55.0 13.2 %collective-permute-start.21 = (bf16[128,1024]{1,0:T(8,128)(2,1)S(1)}, bf16[128,1024]{1,0:T(8,128)(2,1)S(1)}, u32[]{:S(2)}, u32[]{:S(2)}) collective-permute-start(bf16[128,1024]{1,0:T(8,128)(2,1)S(1)} %broadcast_select_fusion.3.refs_5_), channel_id=1, source_target_pairs={{0,1},{1,0},{2,3},{3,2},{4,5},{5,4},{6,7},{7,6},{8,9},{9,8},{10,11... | collective-permute-start | bytes 786440 | tf_op jit(solution)/shard_map/ppermute | solution.py:345
  115.5 14.8 %collective-permute-start.32 = (bf16[128,1024]{1,0:T(8,128)(2,1)S(1)}, bf16[128,1024]{1,0:T(8,128)(2,1)S(1)}, u32[]{:S(2)}, u32[]{:S(2)}) collective-permute-start(bf16[128,1024]{1,0:T(8,128)(2,1)S(1)} %get-tuple-element.107), channel_id=1, source_target_pairs={{0,2},{2,0},{1,3},{3,1},{4,6},{6,4},{5,7},{7,5},{8,10},{10,8},{9,1... | collective-permute-start | bytes 786440 | tf_op jit(solution)/shard_map/ppermute | solution.py:345
  119.2 16.7 %collective-permute-start.40 = (bf16[128,1024]{1,0:T(8,128)(2,1)S(1)}, bf16[128,1024]{1,0:T(8,128)(2,1)S(1)}, u32[]{:S(2)}, u32[]{:S(2)}) collective-permute-start(bf16[128,1024]{1,0:T(8,128)(2,1)S(1)} %get-tuple-element.116), channel_id=1, source_target_pairs={{0,2},{2,0},{1,3},{3,1},{4,6},{6,4},{5,7},{7,5},{8,10},{10,8},{9,1... | collective-permute-start | bytes 786440 | tf_op jit(solution)/shard_map/ppermute | solution.py:345
  121.1 20.5 %collective-permute-start.42 = (bf16[128,1024]{1,0:T(8,128)(2,1)S(1)}, bf16[128,1024]{1,0:T(8,128)(2,1)S(1)}, u32[]{:S(2)}, u32[]{:S(2)}) collective-permute-start(bf16[128,1024]{1,0:T(8,128)(2,1)S(1)} %get-tuple-element.113), channel_id=1, source_target_pairs={{0,2},{2,0},{1,3},{3,1},{4,6},{6,4},{5,7},{7,5},{8,10},{10,8},{9,1... | collective-permute-start | bytes 786440 | tf_op jit(solution)/shard_map/ppermute | solution.py:345
  130.5 13.8 %collective-permute-start.33 = (bf16[128,1024]{1,0:T(8,128)(2,1)S(1)}, bf16[128,1024]{1,0:T(8,128)(2,1)S(1)}, u32[]{:S(2)}, u32[]{:S(2)}) collective-permute-start(bf16[128,1024]{1,0:T(8,128)(2,1)S(1)} %get-tuple-element.105), channel_id=1, source_target_pairs={{0,4},{1,5},{2,6},{3,7},{12,8},{13,9},{14,10},{15,11},{16,20},{17,... | collective-permute-start | bytes 786440 | tf_op jit(solution)/shard_map/ppermute | solution.py:345
  131.8 14.6 %collective-permute-start.31 = (bf16[128,1024]{1,0:T(8,128)(2,1)S(1)}, bf16[128,1024]{1,0:T(8,128)(2,1)S(1)}, u32[]{:S(2)}, u32[]{:S(2)}) collective-permute-start(bf16[128,1024]{1,0:T(8,128)(2,1)S(1)} %get-tuple-element.106), channel_id=1, source_target_pairs={{0,4},{1,5},{2,6},{3,7},{12,8},{13,9},{14,10},{15,11},{16,20},{17,... | collective-permute-start | bytes 786440 | tf_op jit(solution)/shard_map/ppermute | solution.py:345
  133.1 14.1 %collective-permute-start.34 = (bf16[128,1024]{1,0:T(8,128)(2,1)S(1)}, bf16[128,1024]{1,0:T(8,128)(2,1)S(1)}, u32[]{:S(2)}, u32[]{:S(2)}) collective-permute-start(bf16[128,1024]{1,0:T(8,128)(2,1)S(1)} %get-tuple-element.90), channel_id=1, source_target_pairs={{0,2},{2,0},{1,3},{3,1},{4,6},{6,4},{5,7},{7,5},{8,10},{10,8},{9,1... | collective-permute-start | bytes 786440 | tf_op jit(solution)/shard_map/ppermute | solution.py:345
  141.8 13.1 %collective-permute-start.43 = (bf16[128,1024]{1,0:T(8,128)(2,1)S(1)}, bf16[128,1024]{1,0:T(8,128)(2,1)S(1)}, u32[]{:S(2)}, u32[]{:S(2)}) collective-permute-start(bf16[128,1024]{1,0:T(8,128)(2,1)S(1)} %get-tuple-element.111), channel_id=1, source_target_pairs={{0,4},{1,5},{2,6},{3,7},{12,8},{13,9},{14,10},{15,11},{16,20},{17,... | collective-permute-start | bytes 786440 | tf_op jit(solution)/shard_map/ppermute | solution.py:345
  143.1 16.9 %collective-permute-start.41 = (bf16[128,1024]{1,0:T(8,128)(2,1)S(1)}, bf16[128,1024]{1,0:T(8,128)(2,1)S(1)}, u32[]{:S(2)}, u32[]{:S(2)}) collective-permute-start(bf16[128,1024]{1,0:T(8,128)(2,1)S(1)} %get-tuple-element.112), channel_id=1, source_target_pairs={{0,4},{1,5},{2,6},{3,7},{12,8},{13,9},{14,10},{15,11},{16,20},{17,... | collective-permute-start | bytes 786440 | tf_op jit(solution)/shard_map/ppermute | solution.py:345
  144.4 19.4 %collective-permute-start.44 = (bf16[128,1024]{1,0:T(8,128)(2,1)S(1)}, bf16[128,1024]{1,0:T(8,128)(2,1)S(1)}, u32[]{:S(2)}, u32[]{:S(2)}) collective-permute-start(bf16[128,1024]{1,0:T(8,128)(2,1)S(1)} %get-tuple-element.99), channel_id=1, source_target_pairs={{0,2},{2,0},{1,3},{3,1},{4,6},{6,4},{5,7},{7,5},{8,10},{10,8},{9,1... | collective-permute-start | bytes 786440 | tf_op jit(solution)/shard_map/ppermute | solution.py:345
  147.3 17.3 %collective-permute-start.38 = (bf16[128,1024]{1,0:T(8,128)(2,1)S(1)}, bf16[128,1024]{1,0:T(8,128)(2,1)S(1)}, u32[]{:S(2)}, u32[]{:S(2)}) collective-permute-start(bf16[128,1024]{1,0:T(8,128)(2,1)S(1)} %fusion.7), channel_id=1, source_target_pairs={{0,4},{1,5},{2,6},{3,7},{4,0},{5,1},{6,2},{7,3},{8,12},{9,13},{10,... | collective-permute-start | bytes 786440 | tf_op jit(solution)/shard_map/ppermute | solution.py:345
  151.5 18.1 %collective-permute-start.36 = (bf16[128,1024]{1,0:T(8,128)(2,1)S(1)}, bf16[128,1024]{1,0:T(8,128)(2,1)S(1)}, u32[]{:S(2)}, u32[]{:S(2)}) collective-permute-start(bf16[128,1024]{1,0:T(8,128)(2,1)S(1)} %add_convert_fusion.5), channel_id=1, source_target_pairs={{4,12},{5,13},{6,14},{7,15},{8,0},{9,1},{10,2},{11,3},{20,28},{21,... | collective-permute-start | bytes 786440 | tf_op jit(solution)/shard_map/ppermute | solution.py:345
  154.8 15.1 %collective-permute-start.35 = (bf16[128,1024]{1,0:T(8,128)(2,1)S(1)}, bf16[128,1024]{1,0:T(8,128)(2,1)S(1)}, u32[]{:S(2)}, u32[]{:S(2)}) collective-permute-start(bf16[128,1024]{1,0:T(8,128)(2,1)S(1)} %get-tuple-element.92), channel_id=1, source_target_pairs={{0,2},{2,0},{1,3},{3,1},{4,6},{6,4},{5,7},{7,5},{8,10},{10,8},{9,1... | collective-permute-start | bytes 786440 | tf_op jit(solution)/shard_map/ppermute | solution.py:345
  (30 other events, 212.1 us)

commit v7 on v5

--- a/solution.py
+++ b/solution.py
@@ -347,19 +347,14 @@
     return lax.optimization_barrier(values)
 
 
-def tree_start(own):
-    near, middle, own_x = together(
-        send(own, swap_z), send(own, middle_z), send(own, swap_x)
+def tree_start(own, *others):
+    return together(send(own, swap_z), send(own, middle_z), send(own, swap_x), *others)
+
+
+def tree_second(near, middle, *others):
+    return together(
+        send(near, middle_z), send(middle, outward_z), send(near, swap_x), *others
     )
-    return near, middle, own_x
-
-
-def tree_second(near, middle, own_x, *others):
-    if own_x is None:
-        near_x = send(near, swap_x)
-    else:
-        near_x = send(own_x, swap_z)
-    return together(send(near, middle_z), send(middle, outward_z), near_x, *others)
 
 
 def tree_third(cross, outer, middle, edge, *others):
@@ -379,25 +374,20 @@
     return rounded_sum(mine, send(theirs, swap_core))
 
 
-def tree_return(chip, near_by_z):
+def tree_return(chip):
     own, near, third, own_x, near_x, third_x, fourth, fourth_x = [chip[i] for i in range(8)]
-    if near_by_z:
-        near_x = send(near_x, swap_z)
     fourth_in, third_x, near_x, own_x = together(send(fourth_x, swap_x), third_x, near_x, own_x)
-    if near_by_z:
-        own_x = rounded_sum(own_x, near_x)
     fourth = rounded_sum(fourth, fourth_in)
     far, third_in, near_x, own_x = together(
         send(fourth, inward_z), send(third_x, swap_x), near_x, own_x
     )
     cross = rounded_sum(fourth, far)
     third = rounded_sum(third, third_in)
-    sent = [send(third, inward_z), send(cross, middle_z)]
-    if not near_by_z:
-        sent.append(send(near_x, swap_x))
-    outer, crossed, *near_in, own_x = together(*sent, own_x)
+    outer, crossed, near_in, own_x = together(
+        send(third, inward_z), send(cross, middle_z), send(near_x, swap_x), own_x
+    )
     middle = rounded_sum(third, outer)
-    near = rounded_sum(near, crossed, *near_in)
+    near = rounded_sum(near, near_in, crossed)
     return rounded_sum(
         own, send(own_x, swap_x), send(middle, middle_z), send(near, swap_z)
     )
@@ -417,12 +407,13 @@
     parts = normed_parts(tokens, norm_gain, gather_chunks)
     if as_tree:
         choice = ranked(routes, route_weight, device_count, local_count)
-        firsts = [tree_start(part) for part in parts]
-        seconds = [
-            tree_second(near, middle, own_x if chunk % 2 else None, choice)
-            for chunk, (near, middle, own_x) in enumerate(firsts)
-        ]
-        choice = seconds[0][3]
+        firsts = []
+        for part in parts:
+            if not firsts:
+                near, middle, own_x, choice = tree_start(part, choice)
+            else:
+                near, middle, own_x = tree_start(part)
+            firsts.append((near, middle, own_x))
     else:
         every = jnp.arange(device_count * local_count, dtype=jnp.int32)
         same = routes[:, :, None] == every
@@ -438,19 +429,25 @@
     choices = lax.all_to_all(choice, axes, split_axis=0, concat_axis=0, tiled=True)
     if as_tree:
         place = jnp.stack([lax.axis_index("expert"), lax.axis_index("dp")])
+        seconds = []
+        for near, middle, own_x in firsts:
+            if not seconds:
+                cross, outer, near_x, choices = tree_second(near, middle, choices)
+            else:
+                cross, outer, near_x = tree_second(near, middle)
+            seconds.append((cross, outer, near_x))
         mine, theirs, late_picker, spread, scale = tables(place, choices, local_count)
         theirs = send(theirs, swap_core)
         thirds = []
-        for cross, outer, near_x, _ in seconds:
-            middle = firsts[len(thirds)][1]
+        for (near, middle, own_x), (cross, outer, near_x) in zip(firsts, seconds):
             if not thirds:
+                third, third_x, fourth, theirs = tree_third(cross, outer, middle, edge, theirs)
+            else:
                 third, third_x, fourth = tree_third(cross, outer, middle, edge)
-            else:
-                third, third_x, fourth, theirs = tree_third(cross, outer, middle, edge, theirs)
             thirds.append((third, third_x, fourth))
         order = (0, 1, 2, 3, 4, 5, 8, 9, 10, 11, 12, 13, 6, 7, 14, 15)
         row_chunks, late_chunks = [], []
-        for part, (near, middle, own_x), (cross, outer, near_x, _), (third, third_x, fourth) in zip(
+        for part, (near, middle, own_x), (cross, outer, near_x), (third, third_x, fourth) in zip(
             parts, firsts, seconds, thirds
         ):
             early = part, near, third, own_x, near_x, third_x
@@ -481,7 +478,7 @@
             sums.append(total.astype(jnp.bfloat16))
     results = sums
     if as_tree:
-        results = [tree_return(chip, chunk % 2 == 1) for chunk, chip in enumerate(sums)]
+        results = [tree_return(chip) for chip in sums]
     return jnp.concatenate(results, axis=1)
 
 

time: 166 us -> 162 us (0.976)
  waiting for transfers between devices: 49.1 us -> 41.8 us
  starting transfers between devices: 65 us -> 69.1 us
    ppermute x45, waiting for transfers between devices: 49.1 us -> 41.8 us  [send(): return lax.ppermute(value, axes, pairs)]
    ppermute x45, starting transfers between devices: 59.6 us -> 65.1 us  [send(): return lax.ppermute(value, axes, pairs)]
    unnamed x12 -> x8, local copies, waits for them, and re-layouts: 3.81 us -> 3.11 us
  transfers between devices with their start and end apart: 46 -> 46, of which waited for: 21 -> 20; matrix products, arithmetic and copies ran while one was open for 2% -> 2% of each run, Pallas kernels for 7% -> 7%
where the time goes in v7:
time: 162 us; the launch traced here: 161 us
  starting transfers between devices  69.1 us (43%)
  Pallas kernels  42.1 us (26%)
  waiting for transfers between devices  41.8 us (26%)
  other arithmetic  4.22 us (3%)
  local copies, waits for them, and re-layouts  3.28 us (2%)
    ppermute x45, starting transfers between devices, send(): return lax.ppermute(value, axes, pairs)  65.1 us
    ppermute x45, waiting for transfers between devices, send(): return lax.ppermute(value, axes, pairs)  41.8 us
    pallas_call x1, Pallas kernels, hidden_rows(): pl.pallas_call(functools.partial(hidden_kernel, chunks, groups, late), gr...  21.6 us
    pallas_call x2, Pallas kernels, mix_rows(): pl.pallas_call(functools.partial(mix_kernel, order), grid=(experts // gro...  16.5 us
    all_to_all x1, starting transfers between devices, shards(): lax.all_to_all(choice, axes, split_axis=0, concat_axis=0, tiled=True)  4.03 us
  transfers between devices with their start and end apart: 46, of which 20 were waited for; matrix products, arithmetic and copies ran while one was open for 2% of the time, Pallas kernels for 7%

profile of v7, /device:TPU:8, one launch (start us, length us, event | category | flops | bytes accessed | tf_op | source)
XLA Modules:
  0.0 161.0 jit_solution(11568793779864660520)
XLA Ops:
  3.5 3.5 %collective-permute-start.1 = (bf16[128,1024]{1,0:T(8,128)(2,1)S(1)}, bf16[128,1024]{1,0:T(8,128)(2,1)S(1)}, u32[]{:S(2)}, u32[]{:S(2)}) collective-permute-start(bf16[128,1024]{1,0:T(8,128)(2,1)S(1)} %get-tuple-element.67.refs_0_), channel_id=1, source_target_pairs={{4,8},{5,9},{6,10},{7,11},{8,4},{9,5},{10,6},{11,7},{20,24},{21,25... | collective-permute-start | bytes 786440 | tf_op jit(solution)/shard_map/ppermute | solution.py:343
  7.7 2.3 %collective-permute-start.12 = (bf16[128,1024]{1,0:T(8,128)(2,1)S(1)}, bf16[128,1024]{1,0:T(8,128)(2,1)S(1)}, u32[]{:S(2)}, u32[]{:S(2)}) collective-permute-start(bf16[128,1024]{1,0:T(8,128)(2,1)S(1)} %get-tuple-element.84.refs_0_), channel_id=1, source_target_pairs={{4,8},{5,9},{6,10},{7,11},{8,4},{9,5},{10,6},{11,7},{20,24},{21,25... | collective-permute-start | bytes 786440 | tf_op jit(solution)/shard_map/ppermute | solution.py:343
  16.3 1.9 %collective-permute-start.4 = (bf16[128,1024]{1,0:T(8,128)(2,1)S(1)}, bf16[128,1024]{1,0:T(8,128)(2,1)S(1)}, u32[]{:S(2)}, u32[]{:S(2)}) collective-permute-start(bf16[128,1024]{1,0:T(8,128)(2,1)S(1)} %collective-permute-done.1), channel_id=1, source_target_pairs={{4,0},{5,1},{6,2},{7,3},{8,12},{9,13},{10,14},{11,15},{20,16},{21,... | collective-permute-start | bytes 786440 | tf_op jit(solution)/shard_map/ppermute | solution.py:343
  18.9 3.5 %collective-permute-start.3 = (bf16[128,1024]{1,0:T(8,128)(2,1)S(1)}, bf16[128,1024]{1,0:T(8,128)(2,1)S(1)}, u32[]{:S(2)}, u32[]{:S(2)}) collective-permute-start(bf16[128,1024]{1,0:T(8,128)(2,1)S(1)} %collective-permute-done.refs_1_), channel_id=1, source_target_pairs={{4,8},{5,9},{6,10},{7,11},{8,4},{9,5},{10,6},{11,7},{20,24},{21,25... | collective-permute-start | bytes 786440 | tf_op jit(solution)/shard_map/ppermute | solution.py:343
  22.4 4.0 %all-to-all-start = ((f32[16,16,128]{2,1,0:T(8,128)}), f32[16,16,128]{2,1,0:T(8,128)S(1)}, u32[]{:S(2)}, u32[]{:S(2)}) async-start(f32[16,16,128]{2,1,0:T(8,128)} %shard_map.74), calls=%async_computation | async-start | bytes 262144 | tf_op jit(solution)/shard_map/all_to_all | solution.py:429
  26.5 2.7 %collective-permute-start.15 = (bf16[128,1024]{1,0:T(8,128)(2,1)S(1)}, bf16[128,1024]{1,0:T(8,128)(2,1)}, u32[]{:S(2)}, u32[]{:S(2)}) collective-permute-start(bf16[128,1024]{1,0:T(8,128)(2,1)S(1)} %collective-permute-done.12), channel_id=1, source_target_pairs={{4,0},{5,1},{6,2},{7,3},{8,12},{9,13},{10,14},{11,15},{20,16},{21,... | collective-permute-start | bytes 786440 | tf_op jit(solution)/shard_map/ppermute | solution.py:343
  29.2 1.9 %collective-permute-start.16 = (bf16[128,1024]{1,0:T(8,128)(2,1)S(1)}, bf16[128,1024]{1,0:T(8,128)(2,1)S(1)}, u32[]{:S(2)}, u32[]{:S(2)}) collective-permute-start(bf16[128,1024]{1,0:T(8,128)(2,1)S(1)} %collective-permute-done.11.refs_1_), channel_id=1, source_target_pairs={{0,2},{2,0},{1,3},{3,1},{4,6},{6,4},{5,7},{7,5},{8,10},{10,8},{9,1... | collective-permute-start | bytes 786440 | tf_op jit(solution)/shard_map/ppermute | solution.py:343
  31.1 4.3 %collective-permute-start.14 = (bf16[128,1024]{1,0:T(8,128)(2,1)S(1)}, bf16[128,1024]{1,0:T(8,128)(2,1)S(1)}, u32[]{:S(2)}, u32[]{:S(2)}) collective-permute-start(bf16[128,1024]{1,0:T(8,128)(2,1)S(1)} %collective-permute-done.11.refs_1_), channel_id=1, source_target_pairs={{4,8},{5,9},{6,10},{7,11},{8,4},{9,5},{10,6},{11,7},{20,24},{21,25... | collective-permute-start | bytes 786440 | tf_op jit(solution)/shard_map/ppermute | solution.py:343
  37.9 3.5 %collective-permute-done.14 = bf16[128,1024]{1,0:T(8,128)(2,1)S(1)} collective-permute-done((bf16[128,1024]{1,0:T(8,128)(2,1)S(1)}, bf16[128,1024]{1,0:T(8,128)(2,1)S(1)}, u32[]{:S(2)}, u32[]{:S(2)}) %collective-permute-start.14) | collective-permute-done | bytes 262176 | tf_op jit(solution)/shard_map/ppermute | solution.py:343
  44.6 4.3 %collective-permute-done.18.refs_5_ = bf16[128,1024]{1,0:T(8,128)(2,1)S(1)} collective-permute-done((bf16[128,1024]{1,0:T(8,128)(2,1)S(1)}, bf16[128,1024]{1,0:T(8,128)(2,1)S(1)}, u32[]{:S(2)}, u32[]{:S(2)}) %collective-permute-start.18) | collective-permute-done | bytes 262176 | tf_op jit(solution)/shard_map/ppermute | solution.py:343
  53.8 7.0 %collective-permute-done.19.refs_9_ = bf16[128,1024]{1,0:T(8,128)(2,1)S(1)} collective-permute-done((bf16[128,1024]{1,0:T(8,128)(2,1)S(1)}, bf16[128,1024]{1,0:T(8,128)(2,1)S(1)}, u32[]{:S(2)}, u32[]{:S(2)}) %collective-permute-start.19) | collective-permute-done | bytes 262176 | tf_op jit(solution)/shard_map/ppermute | solution.py:343
  61.3 4.2 %collective-permute-done.9.refs_5_ = bf16[128,1024]{1,0:T(8,128)(2,1)S(1)} collective-permute-done((bf16[128,1024]{1,0:T(8,128)(2,1)S(1)}, bf16[128,1024]{1,0:T(8,128)(2,1)S(1)}, u32[]{:S(2)}, u32[]{:S(2)}) %collective-permute-start.9) | collective-permute-done | bytes 262176 | tf_op jit(solution)/shard_map/ppermute | solution.py:343
  67.0 21.6 %shard_map.78.hidden_ref = bf16[8,256,768]{2,1,0:T(8,128)(2,1)S(1)} custom-call(bf16[8,96,1024]{2,1,0:T(8,128)(2,1)S(1)} %bitcast.67, bf16[8,96,1024]{2,1,0:T(8,128)(2,1)S(1)} %bitcast.68, bf16[8,96,1024]{2,1,0:T(8,128)(2,1)S(1)} %bitcast.65, bf16[8,96,1024]{2,1,0:T(8,128)(2,1)S(1)} %bitcast.66, bf16[128,1024]{1,0:T(8,128)(2,1)S(1)} %broadcast_select_fusion.2.refs_4_, ...), custom_call_target="tpu_custom_call" | custom-call | flops 12884901888 | bytes 50331648 | tf_op jit(solution)/shard_map/pallas_call | solution.py:246
  88.7 8.2 %shard_map.79 = (bf16[8,128,1024]{2,1,0:T(8,128)(2,1)S(1)}, bf16[8,128,1024]{2,1,0:T(8,128)(2,1)S(1)}) custom-call(bf16[8,256,768]{2,1,0:T(8,128)(2,1)S(1)} %shard_map.78.hidden_ref, bf16[8,768,2048]{2,1,0:T(8,128)(2,1)} %down_ref.3, bf16[16,128,128]{2,1,0:T(8,128)(2,1)S(1)} %get-tuple-element.100.spread_ref), custom_call_target="tpu_custom_call" | custom-call | flops 3758096384 | bytes 19922944 | tf_op jit(solution)/shard_map/pallas_call | solution.py:299
  97.1 8.2 %shard_map.80 = (bf16[8,128,1024]{2,1,0:T(8,128)(2,1)S(1)}, bf16[8,128,1024]{2,1,0:T(8,128)(2,1)S(1)}) custom-call(bf16[8,256,768]{2,1,0:T(8,128)(2,1)S(1)} %shard_map.78.hidden_ref, bf16[8,768,2048]{2,1,0:T(8,128)(2,1)} %down_ref.3, bf16[16,128,128]{2,1,0:T(8,128)(2,1)S(1)} %get-tuple-element.100.spread_ref), custom_call_target="tpu_custom_call" | custom-call | flops 3758096384 | bytes 19922944 | tf_op jit(solution)/shard_map/pallas_call | solution.py:299
  112.3 3.8 %collective-permute-done.26 = bf16[128,1024]{1,0:T(8,128)(2,1)S(1)} collective-permute-done((bf16[128,1024]{1,0:T(8,128)(2,1)S(1)}, bf16[128,1024]{1,0:T(8,128)(2,1)S(1)}, u32[]{:S(2)}, u32[]{:S(2)}) %collective-permute-start.26) | collective-permute-done | bytes 262176 | tf_op jit(solution)/shard_map/ppermute | solution.py:343
  119.0 2.7 %collective-permute-done.36 = bf16[128,1024]{1,0:T(8,128)(2,1)S(1)} collective-permute-done((bf16[128,1024]{1,0:T(8,128)(2,1)S(1)}, bf16[128,1024]{1,0:T(8,128)(2,1)S(1)}, u32[]{:S(2)}, u32[]{:S(2)}) %collective-permute-start.36) | collective-permute-done | bytes 262176 | tf_op jit(solution)/shard_map/ppermute | solution.py:343
  124.8 2.6 %collective-permute-done.28 = bf16[128,1024]{1,0:T(8,128)(2,1)S(1)} collective-permute-done((bf16[128,1024]{1,0:T(8,128)(2,1)S(1)}, bf16[128,1024]{1,0:T(8,128)(2,1)S(1)}, u32[]{:S(2)}, u32[]{:S(2)}) %collective-permute-start.28) | collective-permute-done | bytes 262176 | tf_op jit(solution)/shard_map/ppermute | solution.py:343
  127.4 4.3 %collective-permute-start.30 = (bf16[128,1024]{1,0:T(8,128)(2,1)S(1)}, bf16[128,1024]{1,0:T(8,128)(2,1)S(1)}, u32[]{:S(2)}, u32[]{:S(2)}) collective-permute-start(bf16[128,1024]{1,0:T(8,128)(2,1)S(1)} %add_convert_fusion.5), channel_id=1, source_target_pairs={{4,8},{5,9},{6,10},{7,11},{8,4},{9,5},{10,6},{11,7},{20,24},{21,25... | collective-permute-start | bytes 786440 | tf_op jit(solution)/shard_map/ppermute | solution.py:343
  134.7 2.0 %collective-permute-start.40 = (bf16[128,1024]{1,0:T(8,128)(2,1)S(1)}, bf16[128,1024]{1,0:T(8,128)(2,1)S(1)}, u32[]{:S(2)}, u32[]{:S(2)}) collective-permute-start(bf16[128,1024]{1,0:T(8,128)(2,1)S(1)} %add_convert_fusion.3), channel_id=1, source_target_pairs={{4,8},{5,9},{6,10},{7,11},{8,4},{9,5},{10,6},{11,7},{20,24},{21,25... | collective-permute-start | bytes 786440 | tf_op jit(solution)/shard_map/ppermute | solution.py:343
  140.2 2.4 %collective-permute-start.34 = (bf16[128,1024]{1,0:T(8,128)(2,1)S(1)}, bf16[128,1024]{1,0:T(8,128)(2,1)S(1)}, u32[]{:S(2)}, u32[]{:S(2)}) collective-permute-start(bf16[128,1024]{1,0:T(8,128)(2,1)S(1)} %fusion.8), channel_id=1, source_target_pairs={{0,4},{1,5},{2,6},{3,7},{4,0},{5,1},{6,2},{7,3},{8,12},{9,13},{10,... | collective-permute-start | bytes 786440 | tf_op jit(solution)/shard_map/ppermute | solution.py:343
  142.7 2.9 %collective-permute-start.33 = (bf16[128,1024]{1,0:T(8,128)(2,1)S(1)}, bf16[128,1024]{1,0:T(8,128)(2,1)S(1)}, u32[]{:S(2)}, u32[]{:S(2)}) collective-permute-start(bf16[128,1024]{1,0:T(8,128)(2,1)S(1)} %add_convert_fusion.4), channel_id=1, source_target_pairs={{4,8},{5,9},{6,10},{7,11},{8,4},{9,5},{10,6},{11,7},{20,24},{21,25... | collective-permute-start | bytes 786440 | tf_op jit(solution)/shard_map/ppermute | solution.py:343
  148.1 2.2 %collective-permute-start.44 = (bf16[128,1024]{1,0:T(8,128)(2,1)S(1)}, bf16[128,1024]{1,0:T(8,128)(2,1)S(1)}, u32[]{:S(2)}, u32[]{:S(2)}) collective-permute-start(bf16[128,1024]{1,0:T(8,128)(2,1)S(1)} %fusion.1), channel_id=1, source_target_pairs={{0,4},{1,5},{2,6},{3,7},{4,0},{5,1},{6,2},{7,3},{8,12},{9,13},{10,... | collective-permute-start | bytes 786440 | tf_op jit(solution)/shard_map/ppermute | solution.py:343
  150.4 3.1 %collective-permute-start.43 = (bf16[128,1024]{1,0:T(8,128)(2,1)S(1)}, bf16[128,1024]{1,0:T(8,128)(2,1)S(1)}, u32[]{:S(2)}, u32[]{:S(2)}) collective-permute-start(bf16[128,1024]{1,0:T(8,128)(2,1)S(1)} %add_convert_fusion.2), channel_id=1, source_target_pairs={{4,8},{5,9},{6,10},{7,11},{8,4},{9,5},{10,6},{11,7},{20,24},{21,25... | collective-permute-start | bytes 786440 | tf_op jit(solution)/shard_map/ppermute | solution.py:343
  (106 shorter events, 53.4 us)
Async XLA Ops:
  3.5 11.1 %collective-permute-start.1 = (bf16[128,1024]{1,0:T(8,128)(2,1)S(1)}, bf16[128,1024]{1,0:T(8,128)(2,1)S(1)}, u32[]{:S(2)}, u32[]{:S(2)}) collective-permute-start(bf16[128,1024]{1,0:T(8,128)(2,1)S(1)} %get-tuple-element.67.refs_0_), channel_id=1, source_target_pairs={{4,8},{5,9},{6,10},{7,11},{8,4},{9,5},{10,6},{11,7},{20,24},{21,25... | collective-permute-start | bytes 786440 | tf_op jit(solution)/shard_map/ppermute | solution.py:343
  7.1 11.9 %collective-permute-start.13 = (bf16[128,1024]{1,0:T(8,128)(2,1)S(1)}, bf16[128,1024]{1,0:T(8,128)(2,1)S(1)}, u32[]{:S(2)}, u32[]{:S(2)}) collective-permute-start(bf16[128,1024]{1,0:T(8,128)(2,1)S(1)} %get-tuple-element.84.refs_0_), channel_id=1, source_target_pairs={{0,2},{2,0},{1,3},{3,1},{4,6},{6,4},{5,7},{7,5},{8,10},{10,8},{9,1... | collective-permute-start | bytes 786440 | tf_op jit(solution)/shard_map/ppermute | solution.py:343
  7.7 18.8 %collective-permute-start.12 = (bf16[128,1024]{1,0:T(8,128)(2,1)S(1)}, bf16[128,1024]{1,0:T(8,128)(2,1)S(1)}, u32[]{:S(2)}, u32[]{:S(2)}) collective-permute-start(bf16[128,1024]{1,0:T(8,128)(2,1)S(1)} %get-tuple-element.84.refs_0_), channel_id=1, source_target_pairs={{4,8},{5,9},{6,10},{7,11},{8,4},{9,5},{10,6},{11,7},{20,24},{21,25... | collective-permute-start | bytes 786440 | tf_op jit(solution)/shard_map/ppermute | solution.py:343
  11.1 15.4 %collective-permute-start.11 = (bf16[128,1024]{1,0:T(8,128)(2,1)S(1)}, bf16[128,1024]{1,0:T(8,128)(2,1)S(1)}, u32[]{:S(2)}, u32[]{:S(2)}) collective-permute-start(bf16[128,1024]{1,0:T(8,128)(2,1)S(1)} %get-tuple-element.84.refs_0_), channel_id=1, source_target_pairs={{0,4},{1,5},{2,6},{3,7},{4,0},{5,1},{6,2},{7,3},{8,12},{9,13},{10,... | collective-permute-start | bytes 786440 | tf_op jit(solution)/shard_map/ppermute | solution.py:343
  16.3 14.8 %collective-permute-start.4 = (bf16[128,1024]{1,0:T(8,128)(2,1)S(1)}, bf16[128,1024]{1,0:T(8,128)(2,1)S(1)}, u32[]{:S(2)}, u32[]{:S(2)}) collective-permute-start(bf16[128,1024]{1,0:T(8,128)(2,1)S(1)} %collective-permute-done.1), channel_id=1, source_target_pairs={{4,0},{5,1},{6,2},{7,3},{8,12},{9,13},{10,14},{11,15},{20,16},{21,... | collective-permute-start | bytes 786440 | tf_op jit(solution)/shard_map/ppermute | solution.py:343
  18.2 17.2 %collective-permute-start.5 = (bf16[128,1024]{1,0:T(8,128)(2,1)S(1)}, bf16[128,1024]{1,0:T(8,128)(2,1)S(1)}, u32[]{:S(2)}, u32[]{:S(2)}) collective-permute-start(bf16[128,1024]{1,0:T(8,128)(2,1)S(1)} %collective-permute-done.refs_1_), channel_id=1, source_target_pairs={{0,2},{2,0},{1,3},{3,1},{4,6},{6,4},{5,7},{7,5},{8,10},{10,8},{9,1... | collective-permute-start | bytes 786440 | tf_op jit(solution)/shard_map/ppermute | solution.py:343
  18.9 16.5 %collective-permute-start.3 = (bf16[128,1024]{1,0:T(8,128)(2,1)S(1)}, bf16[128,1024]{1,0:T(8,128)(2,1)S(1)}, u32[]{:S(2)}, u32[]{:S(2)}) collective-permute-start(bf16[128,1024]{1,0:T(8,128)(2,1)S(1)} %collective-permute-done.refs_1_), channel_id=1, source_target_pairs={{4,8},{5,9},{6,10},{7,11},{8,4},{9,5},{10,6},{11,7},{20,24},{21,25... | collective-permute-start | bytes 786440 | tf_op jit(solution)/shard_map/ppermute | solution.py:343
  22.4 13.0 %all-to-all-start = ((f32[16,16,128]{2,1,0:T(8,128)}), f32[16,16,128]{2,1,0:T(8,128)S(1)}, u32[]{:S(2)}, u32[]{:S(2)}) async-start(f32[16,16,128]{2,1,0:T(8,128)} %shard_map.74), calls=%async_computation | async-start | bytes 262144 | tf_op jit(solution)/shard_map/all_to_all | solution.py:429
  26.5 10.9 %collective-permute-start.15 = (bf16[128,1024]{1,0:T(8,128)(2,1)S(1)}, bf16[128,1024]{1,0:T(8,128)(2,1)}, u32[]{:S(2)}, u32[]{:S(2)}) collective-permute-start(bf16[128,1024]{1,0:T(8,128)(2,1)S(1)} %collective-permute-done.12), channel_id=1, source_target_pairs={{4,0},{5,1},{6,2},{7,3},{8,12},{9,13},{10,14},{11,15},{20,16},{21,... | collective-permute-start | bytes 786440 | tf_op jit(solution)/shard_map/ppermute | solution.py:343
  31.1 10.3 %collective-permute-start.14 = (bf16[128,1024]{1,0:T(8,128)(2,1)S(1)}, bf16[128,1024]{1,0:T(8,128)(2,1)S(1)}, u32[]{:S(2)}, u32[]{:S(2)}) collective-permute-start(bf16[128,1024]{1,0:T(8,128)(2,1)S(1)} %collective-permute-done.11.refs_1_), channel_id=1, source_target_pairs={{4,8},{5,9},{6,10},{7,11},{8,4},{9,5},{10,6},{11,7},{20,24},{21,25... | collective-permute-start | bytes 786440 | tf_op jit(solution)/shard_map/ppermute | solution.py:343
  35.5 13.5 %collective-permute-start.7 = (bf16[128,1024]{1,0:T(8,128)(2,1)S(1)}, bf16[128,1024]{1,0:T(8,128)(2,1)S(1)}, u32[]{:S(2)}, u32[]{:S(2)}) collective-permute-start(bf16[128,1024]{1,0:T(8,128)(2,1)S(1)} %broadcast_select_fusion.3.refs_2_), channel_id=1, source_target_pairs={{0,2},{2,0},{1,3},{3,1},{4,6},{6,4},{5,7},{7,5},{8,10},{10,8},{9,1... | collective-permute-start | bytes 786440 | tf_op jit(solution)/shard_map/ppermute | solution.py:343
  36.1 12.9 %collective-permute-start.6 = (bf16[128,1024]{1,0:T(8,128)(2,1)S(1)}, bf16[128,1024]{1,0:T(8,128)(2,1)S(1)}, u32[]{:S(2)}, u32[]{:S(2)}) collective-permute-start(bf16[128,1024]{1,0:T(8,128)(2,1)S(1)} %collective-permute-done.3), channel_id=1, source_target_pairs={{4,0},{5,1},{6,2},{7,3},{8,12},{9,13},{10,14},{11,15},{20,16},{21,... | collective-permute-start | bytes 786440 | tf_op jit(solution)/shard_map/ppermute | solution.py:343
  49.9 10.9 %collective-permute-start.20 = (bf16[8,6,16,1024]{3,2,1,0:T(8,128)(2,1)S(1)}, bf16[8,6,16,1024]{3,2,1,0:T(8,128)(2,1)S(1)}, u32[]{:S(2)}, u32[]{:S(2)}) collective-permute-start(bf16[8,6,16,1024]{3,2,1,0:T(8,128)(2,1)S(1)} %get-tuple-element.94), channel_id=1, source_target_pairs={{0,1},{1,0},{2,3},{3,2},{4,5},{5,4},{6,7},{7,6},{8,9},{9,8},{10,11... | collective-permute-start | bytes 4718600 | tf_op jit(solution)/shard_map/ppermute | solution.py:343
  51.0 14.5 %collective-permute-start.10 = (bf16[8,6,16,1024]{3,2,1,0:T(8,128)(2,1)S(1)}, bf16[8,6,16,1024]{3,2,1,0:T(8,128)(2,1)S(1)}, u32[]{:S(2)}, u32[]{:S(2)}) collective-permute-start(bf16[8,6,16,1024]{3,2,1,0:T(8,128)(2,1)S(1)} %get-tuple-element.82), channel_id=1, source_target_pairs={{0,1},{1,0},{2,3},{3,2},{4,5},{5,4},{6,7},{7,6},{8,9},{9,8},{10,11... | collective-permute-start | bytes 4718600 | tf_op jit(solution)/shard_map/ppermute | solution.py:343
  53.2 12.4 %collective-permute-start.9 = (bf16[128,1024]{1,0:T(8,128)(2,1)S(1)}, bf16[128,1024]{1,0:T(8,128)(2,1)S(1)}, u32[]{:S(2)}, u32[]{:S(2)}) collective-permute-start(bf16[128,1024]{1,0:T(8,128)(2,1)S(1)} %broadcast_select_fusion.2.refs_4_), channel_id=1, source_target_pairs={{0,2},{2,0},{1,3},{3,1},{4,6},{6,4},{5,7},{7,5},{8,10},{10,8},{9,1... | collective-permute-start | bytes 786440 | tf_op jit(solution)/shard_map/ppermute | solution.py:343
  53.8 11.7 %collective-permute-start.23 = (bf16[128,1024]{1,0:T(8,128)(2,1)S(1)}, bf16[128,1024]{1,0:T(8,128)(2,1)S(1)}, u32[]{:S(2)}, u32[]{:S(2)}) collective-permute-start(bf16[128,1024]{1,0:T(8,128)(2,1)S(1)} %broadcast_select_fusion.refs_8_), channel_id=1, source_target_pairs={{0,1},{1,0},{2,3},{3,2},{4,5},{5,4},{6,7},{7,6},{8,9},{9,8},{10,11... | collective-permute-start | bytes 786440 | tf_op jit(solution)/shard_map/ppermute | solution.py:343
  110.7 11.0 %collective-permute-start.36 = (bf16[128,1024]{1,0:T(8,128)(2,1)S(1)}, bf16[128,1024]{1,0:T(8,128)(2,1)S(1)}, u32[]{:S(2)}, u32[]{:S(2)}) collective-permute-start(bf16[128,1024]{1,0:T(8,128)(2,1)S(1)} %get-tuple-element.136), channel_id=1, source_target_pairs={{0,2},{2,0},{1,3},{3,1},{4,6},{6,4},{5,7},{7,5},{8,10},{10,8},{9,1... | collective-permute-start | bytes 786440 | tf_op jit(solution)/shard_map/ppermute | solution.py:343
  121.8 12.8 %collective-permute-start.37 = (bf16[128,1024]{1,0:T(8,128)(2,1)S(1)}, bf16[128,1024]{1,0:T(8,128)(2,1)S(1)}, u32[]{:S(2)}, u32[]{:S(2)}) collective-permute-start(bf16[128,1024]{1,0:T(8,128)(2,1)S(1)} %fusion.2), channel_id=1, source_target_pairs={{0,4},{1,5},{2,6},{3,7},{12,8},{13,9},{14,10},{15,11},{16,20},{17,... | collective-permute-start | bytes 786440 | tf_op jit(solution)/shard_map/ppermute | solution.py:343
  123.1 11.5 %collective-permute-start.38 = (bf16[128,1024]{1,0:T(8,128)(2,1)S(1)}, bf16[128,1024]{1,0:T(8,128)(2,1)S(1)}, u32[]{:S(2)}, u32[]{:S(2)}) collective-permute-start(bf16[128,1024]{1,0:T(8,128)(2,1)S(1)} %get-tuple-element.118), channel_id=1, source_target_pairs={{0,2},{2,0},{1,3},{3,1},{4,6},{6,4},{5,7},{7,5},{8,10},{10,8},{9,1... | collective-permute-start | bytes 786440 | tf_op jit(solution)/shard_map/ppermute | solution.py:343
  127.4 10.7 %collective-permute-start.30 = (bf16[128,1024]{1,0:T(8,128)(2,1)S(1)}, bf16[128,1024]{1,0:T(8,128)(2,1)S(1)}, u32[]{:S(2)}, u32[]{:S(2)}) collective-permute-start(bf16[128,1024]{1,0:T(8,128)(2,1)S(1)} %add_convert_fusion.5), channel_id=1, source_target_pairs={{4,8},{5,9},{6,10},{7,11},{8,4},{9,5},{10,6},{11,7},{20,24},{21,25... | collective-permute-start | bytes 786440 | tf_op jit(solution)/shard_map/ppermute | solution.py:343
  134.7 10.8 %collective-permute-start.40 = (bf16[128,1024]{1,0:T(8,128)(2,1)S(1)}, bf16[128,1024]{1,0:T(8,128)(2,1)S(1)}, u32[]{:S(2)}, u32[]{:S(2)}) collective-permute-start(bf16[128,1024]{1,0:T(8,128)(2,1)S(1)} %add_convert_fusion.3), channel_id=1, source_target_pairs={{4,8},{5,9},{6,10},{7,11},{8,4},{9,5},{10,6},{11,7},{20,24},{21,25... | collective-permute-start | bytes 786440 | tf_op jit(solution)/shard_map/ppermute | solution.py:343
  136.8 11.1 %collective-permute-start.39 = (bf16[128,1024]{1,0:T(8,128)(2,1)S(1)}, bf16[128,1024]{1,0:T(8,128)(2,1)S(1)}, u32[]{:S(2)}, u32[]{:S(2)}) collective-permute-start(bf16[128,1024]{1,0:T(8,128)(2,1)S(1)} %fusion.3), channel_id=1, source_target_pairs={{0,4},{1,5},{2,6},{3,7},{12,8},{13,9},{14,10},{15,11},{16,20},{17,... | collective-permute-start | bytes 786440 | tf_op jit(solution)/shard_map/ppermute | solution.py:343
  140.2 13.4 %collective-permute-start.34 = (bf16[128,1024]{1,0:T(8,128)(2,1)S(1)}, bf16[128,1024]{1,0:T(8,128)(2,1)S(1)}, u32[]{:S(2)}, u32[]{:S(2)}) collective-permute-start(bf16[128,1024]{1,0:T(8,128)(2,1)S(1)} %fusion.8), channel_id=1, source_target_pairs={{0,4},{1,5},{2,6},{3,7},{4,0},{5,1},{6,2},{7,3},{8,12},{9,13},{10,... | collective-permute-start | bytes 786440 | tf_op jit(solution)/shard_map/ppermute | solution.py:343
  142.7 12.4 %collective-permute-start.33 = (bf16[128,1024]{1,0:T(8,128)(2,1)S(1)}, bf16[128,1024]{1,0:T(8,128)(2,1)S(1)}, u32[]{:S(2)}, u32[]{:S(2)}) collective-permute-start(bf16[128,1024]{1,0:T(8,128)(2,1)S(1)} %add_convert_fusion.4), channel_id=1, source_target_pairs={{4,8},{5,9},{6,10},{7,11},{8,4},{9,5},{10,6},{11,7},{20,24},{21,25... | collective-permute-start | bytes 786440 | tf_op jit(solution)/shard_map/ppermute | solution.py:343
  (26 other events, 168.1 us)

commit v8 on v7

--- a/solution.py
+++ b/solution.py
@@ -374,23 +374,33 @@
     return rounded_sum(mine, send(theirs, swap_core))
 
 
-def tree_return(chip):
+def tree_return(chip, near_by_z):
     own, near, third, own_x, near_x, third_x, fourth, fourth_x = [chip[i] for i in range(8)]
+    if near_by_z:
+        near_x = send(near_x, swap_z)
     fourth_in, third_x, near_x, own_x = together(send(fourth_x, swap_x), third_x, near_x, own_x)
+    if near_by_z:
+        own_x = rounded_sum(own_x, near_x)
     fourth = rounded_sum(fourth, fourth_in)
     far, third_in, near_x, own_x = together(
         send(fourth, inward_z), send(third_x, swap_x), near_x, own_x
     )
     cross = rounded_sum(fourth, far)
     third = rounded_sum(third, third_in)
-    outer, crossed, near_in, own_x = together(
-        send(third, inward_z), send(cross, middle_z), send(near_x, swap_x), own_x
+    outer, crossed, by_x, own_x = together(
+        send(third, inward_z),
+        send(cross, middle_z),
+        send(own_x if near_by_z else near_x, swap_x),
+        own_x,
     )
     middle = rounded_sum(third, outer)
-    near = rounded_sum(near, near_in, crossed)
-    return rounded_sum(
-        own, send(own_x, swap_x), send(middle, middle_z), send(near, swap_z)
-    )
+    if near_by_z:
+        near = rounded_sum(near, crossed)
+        own_in = by_x
+    else:
+        near = rounded_sum(near, by_x, crossed)
+        own_in = send(own_x, swap_x)
+    return rounded_sum(own, own_in, send(middle, middle_z), send(near, swap_z))
 
 
 def shards(tokens, routes, route_weight, norm_gain, w_gate, w_up, w_down):
@@ -478,7 +488,7 @@
             sums.append(total.astype(jnp.bfloat16))
     results = sums
     if as_tree:
-        results = [tree_return(chip) for chip in sums]
+        results = [tree_return(chip, chunk % 2 == 1) for chunk, chip in enumerate(sums)]
     return jnp.concatenate(results, axis=1)
 
 

time: 162 us -> 160 us (0.988)
  no operation moved by 1% of the time
where the time goes in v8:
time: 160 us
  starting transfers between devices  69.2 us (43%)
  Pallas kernels  42.1 us (26%)
  waiting for transfers between devices  40.3 us (25%)
  other arithmetic  4.23 us (3%)
  local copies, waits for them, and re-layouts  3.28 us (2%)
    ppermute x45, starting transfers between devices, send(): return lax.ppermute(value, axes, pairs)  65.2 us
    ppermute x45, waiting for transfers between devices, send(): return lax.ppermute(value, axes, pairs)  40.3 us
    pallas_call x1, Pallas kernels, hidden_rows(): pl.pallas_call(functools.partial(hidden_kernel, chunks, groups, late), gr...  21.6 us
    pallas_call x2, Pallas kernels, mix_rows(): pl.pallas_call(functools.partial(mix_kernel, order), grid=(experts // gro...  16.5 us
    all_to_all x1, starting transfers between devices, shards(): lax.all_to_all(choice, axes, split_axis=0, concat_axis=0, tiled=True)  4.03 us
    convert_element_type x15, other arithmetic, rounded_sum(): return total.astype(jnp.bfloat16)  3.2 us
  transfers between devices with their start and end apart: 46, of which 20 were waited for; matrix products, arithmetic and copies ran while one was open for 2% of the time, Pallas kernels for 7%

profile of v8, /device:TPU:8, one launch (start us, length us, event | category | flops | bytes accessed | tf_op | source)
XLA Modules:
  0.0 159.6 jit_solution(6671394325240507383)
XLA Ops:
  3.5 3.5 %collective-permute-start.1 = (bf16[128,1024]{1,0:T(8,128)(2,1)S(1)}, bf16[128,1024]{1,0:T(8,128)(2,1)S(1)}, u32[]{:S(2)}, u32[]{:S(2)}) collective-permute-start(bf16[128,1024]{1,0:T(8,128)(2,1)S(1)} %get-tuple-element.65.refs_0_), channel_id=1, source_target_pairs={{4,8},{5,9},{6,10},{7,11},{8,4},{9,5},{10,6},{11,7},{20,24},{21,25... | collective-permute-start | bytes 786440 | tf_op jit(solution)/shard_map/ppermute | solution.py:343
  7.7 2.3 %collective-permute-start.12 = (bf16[128,1024]{1,0:T(8,128)(2,1)S(1)}, bf16[128,1024]{1,0:T(8,128)(2,1)S(1)}, u32[]{:S(2)}, u32[]{:S(2)}) collective-permute-start(bf16[128,1024]{1,0:T(8,128)(2,1)S(1)} %get-tuple-element.82.refs_0_), channel_id=1, source_target_pairs={{4,8},{5,9},{6,10},{7,11},{8,4},{9,5},{10,6},{11,7},{20,24},{21,25... | collective-permute-start | bytes 786440 | tf_op jit(solution)/shard_map/ppermute | solution.py:343
  16.3 1.9 %collective-permute-start.4 = (bf16[128,1024]{1,0:T(8,128)(2,1)S(1)}, bf16[128,1024]{1,0:T(8,128)(2,1)S(1)}, u32[]{:S(2)}, u32[]{:S(2)}) collective-permute-start(bf16[128,1024]{1,0:T(8,128)(2,1)S(1)} %collective-permute-done.1), channel_id=1, source_target_pairs={{4,0},{5,1},{6,2},{7,3},{8,12},{9,13},{10,14},{11,15},{20,16},{21,... | collective-permute-start | bytes 786440 | tf_op jit(solution)/shard_map/ppermute | solution.py:343
  18.9 3.5 %collective-permute-start.3 = (bf16[128,1024]{1,0:T(8,128)(2,1)S(1)}, bf16[128,1024]{1,0:T(8,128)(2,1)S(1)}, u32[]{:S(2)}, u32[]{:S(2)}) collective-permute-start(bf16[128,1024]{1,0:T(8,128)(2,1)S(1)} %collective-permute-done.refs_1_), channel_id=1, source_target_pairs={{4,8},{5,9},{6,10},{7,11},{8,4},{9,5},{10,6},{11,7},{20,24},{21,25... | collective-permute-start | bytes 786440 | tf_op jit(solution)/shard_map/ppermute | solution.py:343
  22.4 4.0 %all-to-all-start = ((f32[16,16,128]{2,1,0:T(8,128)}), f32[16,16,128]{2,1,0:T(8,128)S(1)}, u32[]{:S(2)}, u32[]{:S(2)}) async-start(f32[16,16,128]{2,1,0:T(8,128)} %shard_map.74), calls=%async_computation | async-start | bytes 262144 | tf_op jit(solution)/shard_map/all_to_all | solution.py:439
  26.5 2.7 %collective-permute-start.15 = (bf16[128,1024]{1,0:T(8,128)(2,1)S(1)}, bf16[128,1024]{1,0:T(8,128)(2,1)}, u32[]{:S(2)}, u32[]{:S(2)}) collective-permute-start(bf16[128,1024]{1,0:T(8,128)(2,1)S(1)} %collective-permute-done.12), channel_id=1, source_target_pairs={{4,0},{5,1},{6,2},{7,3},{8,12},{9,13},{10,14},{11,15},{20,16},{21,... | collective-permute-start | bytes 786440 | tf_op jit(solution)/shard_map/ppermute | solution.py:343
  29.2 1.9 %collective-permute-start.16 = (bf16[128,1024]{1,0:T(8,128)(2,1)S(1)}, bf16[128,1024]{1,0:T(8,128)(2,1)S(1)}, u32[]{:S(2)}, u32[]{:S(2)}) collective-permute-start(bf16[128,1024]{1,0:T(8,128)(2,1)S(1)} %collective-permute-done.11.refs_1_), channel_id=1, source_target_pairs={{0,2},{2,0},{1,3},{3,1},{4,6},{6,4},{5,7},{7,5},{8,10},{10,8},{9,1... | collective-permute-start | bytes 786440 | tf_op jit(solution)/shard_map/ppermute | solution.py:343
  31.1 4.3 %collective-permute-start.14 = (bf16[128,1024]{1,0:T(8,128)(2,1)S(1)}, bf16[128,1024]{1,0:T(8,128)(2,1)S(1)}, u32[]{:S(2)}, u32[]{:S(2)}) collective-permute-start(bf16[128,1024]{1,0:T(8,128)(2,1)S(1)} %collective-permute-done.11.refs_1_), channel_id=1, source_target_pairs={{4,8},{5,9},{6,10},{7,11},{8,4},{9,5},{10,6},{11,7},{20,24},{21,25... | collective-permute-start | bytes 786440 | tf_op jit(solution)/shard_map/ppermute | solution.py:343
  37.9 3.5 %collective-permute-done.14 = bf16[128,1024]{1,0:T(8,128)(2,1)S(1)} collective-permute-done((bf16[128,1024]{1,0:T(8,128)(2,1)S(1)}, bf16[128,1024]{1,0:T(8,128)(2,1)S(1)}, u32[]{:S(2)}, u32[]{:S(2)}) %collective-permute-start.14) | collective-permute-done | bytes 262176 | tf_op jit(solution)/shard_map/ppermute | solution.py:343
  44.6 4.3 %collective-permute-done.18.refs_5_ = bf16[128,1024]{1,0:T(8,128)(2,1)S(1)} collective-permute-done((bf16[128,1024]{1,0:T(8,128)(2,1)S(1)}, bf16[128,1024]{1,0:T(8,128)(2,1)S(1)}, u32[]{:S(2)}, u32[]{:S(2)}) %collective-permute-start.18) | collective-permute-done | bytes 262176 | tf_op jit(solution)/shard_map/ppermute | solution.py:343
  53.8 7.0 %collective-permute-done.19.refs_9_ = bf16[128,1024]{1,0:T(8,128)(2,1)S(1)} collective-permute-done((bf16[128,1024]{1,0:T(8,128)(2,1)S(1)}, bf16[128,1024]{1,0:T(8,128)(2,1)S(1)}, u32[]{:S(2)}, u32[]{:S(2)}) %collective-permute-start.19) | collective-permute-done | bytes 262176 | tf_op jit(solution)/shard_map/ppermute | solution.py:343
  61.3 4.2 %collective-permute-done.9.refs_5_ = bf16[128,1024]{1,0:T(8,128)(2,1)S(1)} collective-permute-done((bf16[128,1024]{1,0:T(8,128)(2,1)S(1)}, bf16[128,1024]{1,0:T(8,128)(2,1)S(1)}, u32[]{:S(2)}, u32[]{:S(2)}) %collective-permute-start.9) | collective-permute-done | bytes 262176 | tf_op jit(solution)/shard_map/ppermute | solution.py:343
  67.0 21.6 %shard_map.78.hidden_ref = bf16[8,256,768]{2,1,0:T(8,128)(2,1)S(1)} custom-call(bf16[8,96,1024]{2,1,0:T(8,128)(2,1)S(1)} %bitcast.67, bf16[8,96,1024]{2,1,0:T(8,128)(2,1)S(1)} %bitcast.68, bf16[8,96,1024]{2,1,0:T(8,128)(2,1)S(1)} %bitcast.65, bf16[8,96,1024]{2,1,0:T(8,128)(2,1)S(1)} %bitcast.66, bf16[128,1024]{1,0:T(8,128)(2,1)S(1)} %broadcast_select_fusion.2.refs_4_, ...), custom_call_target="tpu_custom_call" | custom-call | flops 12884901888 | bytes 50331648 | tf_op jit(solution)/shard_map/pallas_call | solution.py:246
  88.7 8.2 %shard_map.79 = (bf16[8,128,1024]{2,1,0:T(8,128)(2,1)S(1)}, bf16[8,128,1024]{2,1,0:T(8,128)(2,1)S(1)}) custom-call(bf16[8,256,768]{2,1,0:T(8,128)(2,1)S(1)} %shard_map.78.hidden_ref, bf16[8,768,2048]{2,1,0:T(8,128)(2,1)} %down_ref.3, bf16[16,128,128]{2,1,0:T(8,128)(2,1)S(1)} %get-tuple-element.98.spread_ref), custom_call_target="tpu_custom_call" | custom-call | flops 3758096384 | bytes 19922944 | tf_op jit(solution)/shard_map/pallas_call | solution.py:299
  97.1 8.2 %shard_map.80 = (bf16[8,128,1024]{2,1,0:T(8,128)(2,1)S(1)}, bf16[8,128,1024]{2,1,0:T(8,128)(2,1)S(1)}) custom-call(bf16[8,256,768]{2,1,0:T(8,128)(2,1)S(1)} %shard_map.78.hidden_ref, bf16[8,768,2048]{2,1,0:T(8,128)(2,1)} %down_ref.3, bf16[16,128,128]{2,1,0:T(8,128)(2,1)S(1)} %get-tuple-element.98.spread_ref), custom_call_target="tpu_custom_call" | custom-call | flops 3758096384 | bytes 19922944 | tf_op jit(solution)/shard_map/pallas_call | solution.py:299
  119.5 2.1 %collective-permute-done.36 = bf16[128,1024]{1,0:T(8,128)(2,1)S(1)} collective-permute-done((bf16[128,1024]{1,0:T(8,128)(2,1)S(1)}, bf16[128,1024]{1,0:T(8,128)(2,1)S(1)}, u32[]{:S(2)}, u32[]{:S(2)}) %collective-permute-start.36) | collective-permute-done | bytes 262176 | tf_op jit(solution)/shard_map/ppermute | solution.py:343
  125.0 2.2 %collective-permute-done.28 = bf16[128,1024]{1,0:T(8,128)(2,1)S(1)} collective-permute-done((bf16[128,1024]{1,0:T(8,128)(2,1)S(1)}, bf16[128,1024]{1,0:T(8,128)(2,1)S(1)}, u32[]{:S(2)}, u32[]{:S(2)}) %collective-permute-start.28) | collective-permute-done | bytes 262176 | tf_op jit(solution)/shard_map/ppermute | solution.py:343
  127.3 4.5 %collective-permute-start.30 = (bf16[128,1024]{1,0:T(8,128)(2,1)S(1)}, bf16[128,1024]{1,0:T(8,128)(2,1)S(1)}, u32[]{:S(2)}, u32[]{:S(2)}) collective-permute-start(bf16[128,1024]{1,0:T(8,128)(2,1)S(1)} %add_convert_fusion.6), channel_id=1, source_target_pairs={{4,8},{5,9},{6,10},{7,11},{8,4},{9,5},{10,6},{11,7},{20,24},{21,25... | collective-permute-start | bytes 786440 | tf_op jit(solution)/shard_map/ppermute | solution.py:343
  134.7 2.0 %collective-permute-start.41 = (bf16[128,1024]{1,0:T(8,128)(2,1)S(1)}, bf16[128,1024]{1,0:T(8,128)(2,1)S(1)}, u32[]{:S(2)}, u32[]{:S(2)}) collective-permute-start(bf16[128,1024]{1,0:T(8,128)(2,1)S(1)} %add_convert_fusion.3), channel_id=1, source_target_pairs={{4,8},{5,9},{6,10},{7,11},{8,4},{9,5},{10,6},{11,7},{20,24},{21,25... | collective-permute-start | bytes 786440 | tf_op jit(solution)/shard_map/ppermute | solution.py:343
  140.2 2.4 %collective-permute-start.34 = (bf16[128,1024]{1,0:T(8,128)(2,1)S(1)}, bf16[128,1024]{1,0:T(8,128)(2,1)S(1)}, u32[]{:S(2)}, u32[]{:S(2)}) collective-permute-start(bf16[128,1024]{1,0:T(8,128)(2,1)S(1)} %fusion.7), channel_id=1, source_target_pairs={{0,4},{1,5},{2,6},{3,7},{4,0},{5,1},{6,2},{7,3},{8,12},{9,13},{10,... | collective-permute-start | bytes 786440 | tf_op jit(solution)/shard_map/ppermute | solution.py:343
  142.7 2.9 %collective-permute-start.33 = (bf16[128,1024]{1,0:T(8,128)(2,1)S(1)}, bf16[128,1024]{1,0:T(8,128)(2,1)S(1)}, u32[]{:S(2)}, u32[]{:S(2)}) collective-permute-start(bf16[128,1024]{1,0:T(8,128)(2,1)S(1)} %add_convert_fusion.5), channel_id=1, source_target_pairs={{4,8},{5,9},{6,10},{7,11},{8,4},{9,5},{10,6},{11,7},{20,24},{21,25... | collective-permute-start | bytes 786440 | tf_op jit(solution)/shard_map/ppermute | solution.py:343
  148.1 2.2 %collective-permute-start.44 = (bf16[128,1024]{1,0:T(8,128)(2,1)S(1)}, bf16[128,1024]{1,0:T(8,128)(2,1)S(1)}, u32[]{:S(2)}, u32[]{:S(2)}) collective-permute-start(bf16[128,1024]{1,0:T(8,128)(2,1)S(1)} %fusion), channel_id=1, source_target_pairs={{0,4},{1,5},{2,6},{3,7},{4,0},{5,1},{6,2},{7,3},{8,12},{9,13},{10,... | collective-permute-start | bytes 786440 | tf_op jit(solution)/shard_map/ppermute | solution.py:343
  150.3 2.9 %collective-permute-start.43 = (bf16[128,1024]{1,0:T(8,128)(2,1)S(1)}, bf16[128,1024]{1,0:T(8,128)(2,1)S(1)}, u32[]{:S(2)}, u32[]{:S(2)}) collective-permute-start(bf16[128,1024]{1,0:T(8,128)(2,1)S(1)} %add_convert_fusion.2), channel_id=1, source_target_pairs={{4,8},{5,9},{6,10},{7,11},{8,4},{9,5},{10,6},{11,7},{20,24},{21,25... | collective-permute-start | bytes 786440 | tf_op jit(solution)/shard_map/ppermute | solution.py:343
  153.8 3.2 %collective-permute-done.44 = bf16[128,1024]{1,0:T(8,128)(2,1)S(1)} collective-permute-done((bf16[128,1024]{1,0:T(8,128)(2,1)S(1)}, bf16[128,1024]{1,0:T(8,128)(2,1)S(1)}, u32[]{:S(2)}, u32[]{:S(2)}) %collective-permute-start.44) | collective-permute-done | bytes 262176 | tf_op jit(solution)/shard_map/ppermute | solution.py:343
  (107 shorter events, 53.6 us)
Async XLA Ops:
  3.5 11.1 %collective-permute-start.1 = (bf16[128,1024]{1,0:T(8,128)(2,1)S(1)}, bf16[128,1024]{1,0:T(8,128)(2,1)S(1)}, u32[]{:S(2)}, u32[]{:S(2)}) collective-permute-start(bf16[128,1024]{1,0:T(8,128)(2,1)S(1)} %get-tuple-element.65.refs_0_), channel_id=1, source_target_pairs={{4,8},{5,9},{6,10},{7,11},{8,4},{9,5},{10,6},{11,7},{20,24},{21,25... | collective-permute-start | bytes 786440 | tf_op jit(solution)/shard_map/ppermute | solution.py:343
  7.1 11.9 %collective-permute-start.13 = (bf16[128,1024]{1,0:T(8,128)(2,1)S(1)}, bf16[128,1024]{1,0:T(8,128)(2,1)S(1)}, u32[]{:S(2)}, u32[]{:S(2)}) collective-permute-start(bf16[128,1024]{1,0:T(8,128)(2,1)S(1)} %get-tuple-element.82.refs_0_), channel_id=1, source_target_pairs={{0,2},{2,0},{1,3},{3,1},{4,6},{6,4},{5,7},{7,5},{8,10},{10,8},{9,1... | collective-permute-start | bytes 786440 | tf_op jit(solution)/shard_map/ppermute | solution.py:343
  7.7 18.8 %collective-permute-start.12 = (bf16[128,1024]{1,0:T(8,128)(2,1)S(1)}, bf16[128,1024]{1,0:T(8,128)(2,1)S(1)}, u32[]{:S(2)}, u32[]{:S(2)}) collective-permute-start(bf16[128,1024]{1,0:T(8,128)(2,1)S(1)} %get-tuple-element.82.refs_0_), channel_id=1, source_target_pairs={{4,8},{5,9},{6,10},{7,11},{8,4},{9,5},{10,6},{11,7},{20,24},{21,25... | collective-permute-start | bytes 786440 | tf_op jit(solution)/shard_map/ppermute | solution.py:343
  11.1 15.4 %collective-permute-start.11 = (bf16[128,1024]{1,0:T(8,128)(2,1)S(1)}, bf16[128,1024]{1,0:T(8,128)(2,1)S(1)}, u32[]{:S(2)}, u32[]{:S(2)}) collective-permute-start(bf16[128,1024]{1,0:T(8,128)(2,1)S(1)} %get-tuple-element.82.refs_0_), channel_id=1, source_target_pairs={{0,4},{1,5},{2,6},{3,7},{4,0},{5,1},{6,2},{7,3},{8,12},{9,13},{10,... | collective-permute-start | bytes 786440 | tf_op jit(solution)/shard_map/ppermute | solution.py:343
  16.3 14.8 %collective-permute-start.4 = (bf16[128,1024]{1,0:T(8,128)(2,1)S(1)}, bf16[128,1024]{1,0:T(8,128)(2,1)S(1)}, u32[]{:S(2)}, u32[]{:S(2)}) collective-permute-start(bf16[128,1024]{1,0:T(8,128)(2,1)S(1)} %collective-permute-done.1), channel_id=1, source_target_pairs={{4,0},{5,1},{6,2},{7,3},{8,12},{9,13},{10,14},{11,15},{20,16},{21,... | collective-permute-start | bytes 786440 | tf_op jit(solution)/shard_map/ppermute | solution.py:343
  18.2 17.2 %collective-permute-start.5 = (bf16[128,1024]{1,0:T(8,128)(2,1)S(1)}, bf16[128,1024]{1,0:T(8,128)(2,1)S(1)}, u32[]{:S(2)}, u32[]{:S(2)}) collective-permute-start(bf16[128,1024]{1,0:T(8,128)(2,1)S(1)} %collective-permute-done.refs_1_), channel_id=1, source_target_pairs={{0,2},{2,0},{1,3},{3,1},{4,6},{6,4},{5,7},{7,5},{8,10},{10,8},{9,1... | collective-permute-start | bytes 786440 | tf_op jit(solution)/shard_map/ppermute | solution.py:343
  18.9 16.5 %collective-permute-start.3 = (bf16[128,1024]{1,0:T(8,128)(2,1)S(1)}, bf16[128,1024]{1,0:T(8,128)(2,1)S(1)}, u32[]{:S(2)}, u32[]{:S(2)}) collective-permute-start(bf16[128,1024]{1,0:T(8,128)(2,1)S(1)} %collective-permute-done.refs_1_), channel_id=1, source_target_pairs={{4,8},{5,9},{6,10},{7,11},{8,4},{9,5},{10,6},{11,7},{20,24},{21,25... | collective-permute-start | bytes 786440 | tf_op jit(solution)/shard_map/ppermute | solution.py:343
  22.4 13.0 %all-to-all-start = ((f32[16,16,128]{2,1,0:T(8,128)}), f32[16,16,128]{2,1,0:T(8,128)S(1)}, u32[]{:S(2)}, u32[]{:S(2)}) async-start(f32[16,16,128]{2,1,0:T(8,128)} %shard_map.74), calls=%async_computation | async-start | bytes 262144 | tf_op jit(solution)/shard_map/all_to_all | solution.py:439
  26.5 10.9 %collective-permute-start.15 = (bf16[128,1024]{1,0:T(8,128)(2,1)S(1)}, bf16[128,1024]{1,0:T(8,128)(2,1)}, u32[]{:S(2)}, u32[]{:S(2)}) collective-permute-start(bf16[128,1024]{1,0:T(8,128)(2,1)S(1)} %collective-permute-done.12), channel_id=1, source_target_pairs={{4,0},{5,1},{6,2},{7,3},{8,12},{9,13},{10,14},{11,15},{20,16},{21,... | collective-permute-start | bytes 786440 | tf_op jit(solution)/shard_map/ppermute | solution.py:343
  31.1 10.3 %collective-permute-start.14 = (bf16[128,1024]{1,0:T(8,128)(2,1)S(1)}, bf16[128,1024]{1,0:T(8,128)(2,1)S(1)}, u32[]{:S(2)}, u32[]{:S(2)}) collective-permute-start(bf16[128,1024]{1,0:T(8,128)(2,1)S(1)} %collective-permute-done.11.refs_1_), channel_id=1, source_target_pairs={{4,8},{5,9},{6,10},{7,11},{8,4},{9,5},{10,6},{11,7},{20,24},{21,25... | collective-permute-start | bytes 786440 | tf_op jit(solution)/shard_map/ppermute | solution.py:343
  35.5 13.5 %collective-permute-start.7 = (bf16[128,1024]{1,0:T(8,128)(2,1)S(1)}, bf16[128,1024]{1,0:T(8,128)(2,1)S(1)}, u32[]{:S(2)}, u32[]{:S(2)}) collective-permute-start(bf16[128,1024]{1,0:T(8,128)(2,1)S(1)} %broadcast_select_fusion.3.refs_2_), channel_id=1, source_target_pairs={{0,2},{2,0},{1,3},{3,1},{4,6},{6,4},{5,7},{7,5},{8,10},{10,8},{9,1... | collective-permute-start | bytes 786440 | tf_op jit(solution)/shard_map/ppermute | solution.py:343
  36.1 12.9 %collective-permute-start.6 = (bf16[128,1024]{1,0:T(8,128)(2,1)S(1)}, bf16[128,1024]{1,0:T(8,128)(2,1)S(1)}, u32[]{:S(2)}, u32[]{:S(2)}) collective-permute-start(bf16[128,1024]{1,0:T(8,128)(2,1)S(1)} %collective-permute-done.3), channel_id=1, source_target_pairs={{4,0},{5,1},{6,2},{7,3},{8,12},{9,13},{10,14},{11,15},{20,16},{21,... | collective-permute-start | bytes 786440 | tf_op jit(solution)/shard_map/ppermute | solution.py:343
  49.9 10.9 %collective-permute-start.20 = (bf16[8,6,16,1024]{3,2,1,0:T(8,128)(2,1)S(1)}, bf16[8,6,16,1024]{3,2,1,0:T(8,128)(2,1)S(1)}, u32[]{:S(2)}, u32[]{:S(2)}) collective-permute-start(bf16[8,6,16,1024]{3,2,1,0:T(8,128)(2,1)S(1)} %get-tuple-element.92), channel_id=1, source_target_pairs={{0,1},{1,0},{2,3},{3,2},{4,5},{5,4},{6,7},{7,6},{8,9},{9,8},{10,11... | collective-permute-start | bytes 4718600 | tf_op jit(solution)/shard_map/ppermute | solution.py:343
  51.0 14.5 %collective-permute-start.10 = (bf16[8,6,16,1024]{3,2,1,0:T(8,128)(2,1)S(1)}, bf16[8,6,16,1024]{3,2,1,0:T(8,128)(2,1)S(1)}, u32[]{:S(2)}, u32[]{:S(2)}) collective-permute-start(bf16[8,6,16,1024]{3,2,1,0:T(8,128)(2,1)S(1)} %get-tuple-element.80), channel_id=1, source_target_pairs={{0,1},{1,0},{2,3},{3,2},{4,5},{5,4},{6,7},{7,6},{8,9},{9,8},{10,11... | collective-permute-start | bytes 4718600 | tf_op jit(solution)/shard_map/ppermute | solution.py:343
  53.2 12.4 %collective-permute-start.9 = (bf16[128,1024]{1,0:T(8,128)(2,1)S(1)}, bf16[128,1024]{1,0:T(8,128)(2,1)S(1)}, u32[]{:S(2)}, u32[]{:S(2)}) collective-permute-start(bf16[128,1024]{1,0:T(8,128)(2,1)S(1)} %broadcast_select_fusion.2.refs_4_), channel_id=1, source_target_pairs={{0,2},{2,0},{1,3},{3,1},{4,6},{6,4},{5,7},{7,5},{8,10},{10,8},{9,1... | collective-permute-start | bytes 786440 | tf_op jit(solution)/shard_map/ppermute | solution.py:343
  53.8 11.7 %collective-permute-start.23 = (bf16[128,1024]{1,0:T(8,128)(2,1)S(1)}, bf16[128,1024]{1,0:T(8,128)(2,1)S(1)}, u32[]{:S(2)}, u32[]{:S(2)}) collective-permute-start(bf16[128,1024]{1,0:T(8,128)(2,1)S(1)} %broadcast_select_fusion.refs_8_), channel_id=1, source_target_pairs={{0,1},{1,0},{2,3},{3,2},{4,5},{5,4},{6,7},{7,6},{8,9},{9,8},{10,11... | collective-permute-start | bytes 786440 | tf_op jit(solution)/shard_map/ppermute | solution.py:343
  116.9 10.3 %collective-permute-start.28 = (bf16[128,1024]{1,0:T(8,128)(2,1)S(1)}, bf16[128,1024]{1,0:T(8,128)(2,1)S(1)}, u32[]{:S(2)}, u32[]{:S(2)}) collective-permute-start(bf16[128,1024]{1,0:T(8,128)(2,1)S(1)} %get-tuple-element.102), channel_id=1, source_target_pairs={{0,2},{2,0},{1,3},{3,1},{4,6},{6,4},{5,7},{7,5},{8,10},{10,8},{9,1... | collective-permute-start | bytes 786440 | tf_op jit(solution)/shard_map/ppermute | solution.py:343
  121.6 13.0 %collective-permute-start.38 = (bf16[128,1024]{1,0:T(8,128)(2,1)S(1)}, bf16[128,1024]{1,0:T(8,128)(2,1)S(1)}, u32[]{:S(2)}, u32[]{:S(2)}) collective-permute-start(bf16[128,1024]{1,0:T(8,128)(2,1)S(1)} %fusion.1), channel_id=1, source_target_pairs={{0,4},{1,5},{2,6},{3,7},{12,8},{13,9},{14,10},{15,11},{16,20},{17,... | collective-permute-start | bytes 786440 | tf_op jit(solution)/shard_map/ppermute | solution.py:343
  122.9 11.7 %collective-permute-start.39 = (bf16[128,1024]{1,0:T(8,128)(2,1)S(1)}, bf16[128,1024]{1,0:T(8,128)(2,1)S(1)}, u32[]{:S(2)}, u32[]{:S(2)}) collective-permute-start(bf16[128,1024]{1,0:T(8,128)(2,1)S(1)} %get-tuple-element.116), channel_id=1, source_target_pairs={{0,2},{2,0},{1,3},{3,1},{4,6},{6,4},{5,7},{7,5},{8,10},{10,8},{9,1... | collective-permute-start | bytes 786440 | tf_op jit(solution)/shard_map/ppermute | solution.py:343
  127.3 10.9 %collective-permute-start.30 = (bf16[128,1024]{1,0:T(8,128)(2,1)S(1)}, bf16[128,1024]{1,0:T(8,128)(2,1)S(1)}, u32[]{:S(2)}, u32[]{:S(2)}) collective-permute-start(bf16[128,1024]{1,0:T(8,128)(2,1)S(1)} %add_convert_fusion.6), channel_id=1, source_target_pairs={{4,8},{5,9},{6,10},{7,11},{8,4},{9,5},{10,6},{11,7},{20,24},{21,25... | collective-permute-start | bytes 786440 | tf_op jit(solution)/shard_map/ppermute | solution.py:343
  134.7 10.8 %collective-permute-start.41 = (bf16[128,1024]{1,0:T(8,128)(2,1)S(1)}, bf16[128,1024]{1,0:T(8,128)(2,1)S(1)}, u32[]{:S(2)}, u32[]{:S(2)}) collective-permute-start(bf16[128,1024]{1,0:T(8,128)(2,1)S(1)} %add_convert_fusion.3), channel_id=1, source_target_pairs={{4,8},{5,9},{6,10},{7,11},{8,4},{9,5},{10,6},{11,7},{20,24},{21,25... | collective-permute-start | bytes 786440 | tf_op jit(solution)/shard_map/ppermute | solution.py:343
  136.8 11.1 %collective-permute-start.40 = (bf16[128,1024]{1,0:T(8,128)(2,1)S(1)}, bf16[128,1024]{1,0:T(8,128)(2,1)S(1)}, u32[]{:S(2)}, u32[]{:S(2)}) collective-permute-start(bf16[128,1024]{1,0:T(8,128)(2,1)S(1)} %fusion.2), channel_id=1, source_target_pairs={{0,4},{1,5},{2,6},{3,7},{12,8},{13,9},{14,10},{15,11},{16,20},{17,... | collective-permute-start | bytes 786440 | tf_op jit(solution)/shard_map/ppermute | solution.py:343
  140.2 13.4 %collective-permute-start.34 = (bf16[128,1024]{1,0:T(8,128)(2,1)S(1)}, bf16[128,1024]{1,0:T(8,128)(2,1)S(1)}, u32[]{:S(2)}, u32[]{:S(2)}) collective-permute-start(bf16[128,1024]{1,0:T(8,128)(2,1)S(1)} %fusion.7), channel_id=1, source_target_pairs={{0,4},{1,5},{2,6},{3,7},{4,0},{5,1},{6,2},{7,3},{8,12},{9,13},{10,... | collective-permute-start | bytes 786440 | tf_op jit(solution)/shard_map/ppermute | solution.py:343
  142.7 10.9 %collective-permute-start.33 = (bf16[128,1024]{1,0:T(8,128)(2,1)S(1)}, bf16[128,1024]{1,0:T(8,128)(2,1)S(1)}, u32[]{:S(2)}, u32[]{:S(2)}) collective-permute-start(bf16[128,1024]{1,0:T(8,128)(2,1)S(1)} %add_convert_fusion.5), channel_id=1, source_target_pairs={{4,8},{5,9},{6,10},{7,11},{8,4},{9,5},{10,6},{11,7},{20,24},{21,25... | collective-permute-start | bytes 786440 | tf_op jit(solution)/shard_map/ppermute | solution.py:343
  (26 other events, 168.5 us)

commit v9 on v8

--- a/solution.py
+++ b/solution.py
@@ -137,7 +137,11 @@
             picker_refs[slot // early][slot % early] = picker.astype(jnp.bfloat16)
         else:
             picker_refs[2][slot - 2 * early] = picker.astype(jnp.bfloat16)
-        spread_ref[slot] = picker.T.astype(jnp.bfloat16)
+        spread = picker.T.astype(jnp.bfloat16)
+        blank = jnp.zeros_like(spread)
+        halves = (blank, spread) if slot % 2 else (spread, blank)
+        token_rows = pl.ds(slot % 2 * token_count, token_count)
+        spread_ref[slot // 2, token_rows] = jnp.concatenate(halves, axis=1)
 
 
 def tables(place, choices, experts):
@@ -147,7 +151,7 @@
     early = count // 2 - late
     shapes = [(early, rows, token_count), (early, rows, token_count), (2 * late, rows, token_count)]
     shapes = [jax.ShapeDtypeStruct(shape, jnp.bfloat16) for shape in shapes]
-    shapes.append(jax.ShapeDtypeStruct((count, token_count, rows), jnp.bfloat16))
+    shapes.append(jax.ShapeDtypeStruct((count // 2, 2 * token_count, 2 * rows), jnp.bfloat16))
     shapes.append(jax.ShapeDtypeStruct((experts, count * slots, 1), jnp.float32))
     return pl.pallas_call(
         table_kernel,
@@ -268,7 +272,7 @@
 def mix_kernel(order, hidden_ref, down_ref, spread_ref, first_ref, second_ref, made):
     step = pl.program_id(0)
     group = hidden_ref.shape[0]
-    sources = spread_ref.shape[0]
+    sources = made.shape[1]
     width = down_ref.shape[2]
     for one in range(group):
         made[step * group + one] = (
@@ -279,21 +283,23 @@
 
     @pl.when(step == pl.num_programs(0) - 1)
     def _():
-        for source in range(sources):
-            rows = made[:, source].reshape(spread_ref.shape[2], width)
+        local_rows, token_count = spread_ref.shape[2] // 2, spread_ref.shape[1] // 2
+        for pair in range(sources // 2):
+            rows = [made[:, 2 * pair + i].reshape(local_rows, width) for i in (0, 1)]
             mixed = jnp.dot(
-                spread_ref[source], rows, preferred_element_type=jnp.float32
+                spread_ref[pair], jnp.concatenate(rows, axis=0), preferred_element_type=jnp.float32
             ).astype(jnp.bfloat16)
-            if order[source] < sources // 2:
-                first_ref[order[source]] = mixed
-            else:
-                second_ref[order[source] - sources // 2] = mixed
+            for i in (0, 1):
+                to = order[2 * pair + i]
+                out_ref = first_ref if to < sources // 2 else second_ref
+                out_ref[to % (sources // 2)] = mixed[i * token_count : (i + 1) * token_count]
 
 
 def mix_rows(hidden, w_down, spread, order, chunk, chunks):
     experts, whole, hidden_dim = hidden.shape
     width = w_down.shape[2] // chunks
-    sources, token_count, local_rows = spread.shape
+    pairs, token_count, local_rows = spread.shape
+    sources, token_count, local_rows = 2 * pairs, token_count // 2, local_rows // 2
     group = 2 if experts % 2 == 0 else 1
     half = jax.ShapeDtypeStruct((sources // 2, token_count, width), jnp.bfloat16)
     return pl.pallas_call(
@@ -365,9 +371,8 @@
 
 def tree_rest(early, fourth, mine, theirs, experts):
     mine_rows, theirs_rows = pick_pair(early, mine, theirs, experts)
-    fourth_x, theirs_rows = together(send(fourth, swap_x), send(theirs_rows, swap_core))
-    late = [fourth, fourth_x]
-    return [mine_rows, theirs_rows], late + [send(block, swap_core) for block in late]
+    late = [fourth, send(fourth, swap_x)]
+    return [mine_rows, send(theirs_rows, swap_core)], late + [send(block, swap_core) for block in late]
 
 
 def chip_sums(mine, theirs):
@@ -470,7 +475,15 @@
         picker = match.astype(jnp.bfloat16).reshape(device_count, local_count * slots, token_count)
         scale = jnp.sum(jnp.where(match, named_weight[:, :, None, :], 0.0), axis=3)
         scale = scale.transpose(1, 0, 2).reshape(local_count, device_count * slots, 1)
-        spread = picker.transpose(0, 2, 1)
+        spread = picker.transpose(0, 2, 1).reshape(device_count // 2, 2, token_count, -1)
+        blank = jnp.zeros_like(spread[:, 0])
+        spread = jnp.concatenate(
+            [
+                jnp.concatenate([spread[:, 0], blank], axis=2),
+                jnp.concatenate([blank, spread[:, 1]], axis=2),
+            ],
+            axis=1,
+        )
         rows = [pick_rows(picker, lax.all_gather(part, axes), local_count) for part in parts]
         row_chunks = [[rows_of.reshape(local_count, -1, width)] for rows_of in rows]
         late_chunks, late_picker = [[]] * gather_chunks, None

time: 160 us -> 161 us (level)
  transfers between devices with their start and end apart: 46 -> 46, of which waited for: 20 -> 21; matrix products, arithmetic and copies ran while one was open for 2% -> 2% of each run, Pallas kernels for 7% -> 7%
where the time goes in v9:
time: 161 us; the launch traced here: 160 us
  starting transfers between devices  68.9 us (43%)
  Pallas kernels  42.2 us (26%)
  waiting for transfers between devices  41.1 us (26%)
  other arithmetic  4.22 us (3%)
  local copies, waits for them, and re-layouts  3.26 us (2%)
    ppermute x45, starting transfers between devices, send(): return lax.ppermute(value, axes, pairs)  64.9 us
    ppermute x45, waiting for transfers between devices, send(): return lax.ppermute(value, axes, pairs)  41.1 us
    pallas_call x1, Pallas kernels, hidden_rows(): pl.pallas_call(functools.partial(hidden_kernel, chunks, groups, late), gr...  21.6 us
    pallas_call x2, Pallas kernels, mix_rows(): pl.pallas_call(functools.partial(mix_kernel, order), grid=(experts // gro...  16.5 us
    all_to_all x1, starting transfers between devices, shards(): lax.all_to_all(choice, axes, split_axis=0, concat_axis=0, tiled=True)  4.03 us
  transfers between devices with their start and end apart: 46, of which 21 were waited for; matrix products, arithmetic and copies ran while one was open for 2% of the time, Pallas kernels for 7%

profile of v9, /device:TPU:8, one launch (start us, length us, event | category | flops | bytes accessed | tf_op | source)
XLA Modules:
  0.0 160.1 jit_solution(3181431913724610223)
XLA Ops:
  3.5 3.5 %collective-permute-start.1 = (bf16[128,1024]{1,0:T(8,128)(2,1)S(1)}, bf16[128,1024]{1,0:T(8,128)(2,1)S(1)}, u32[]{:S(2)}, u32[]{:S(2)}) collective-permute-start(bf16[128,1024]{1,0:T(8,128)(2,1)S(1)} %get-tuple-element.61.refs_0_), channel_id=1, source_target_pairs={{4,8},{5,9},{6,10},{7,11},{8,4},{9,5},{10,6},{11,7},{20,24},{21,25... | collective-permute-start | bytes 786440 | tf_op jit(solution)/shard_map/ppermute | solution.py:349
  7.7 2.3 %collective-permute-start.11 = (bf16[128,1024]{1,0:T(8,128)(2,1)S(1)}, bf16[128,1024]{1,0:T(8,128)(2,1)S(1)}, u32[]{:S(2)}, u32[]{:S(2)}) collective-permute-start(bf16[128,1024]{1,0:T(8,128)(2,1)S(1)} %get-tuple-element.76.refs_0_), channel_id=1, source_target_pairs={{4,8},{5,9},{6,10},{7,11},{8,4},{9,5},{10,6},{11,7},{20,24},{21,25... | collective-permute-start | bytes 786440 | tf_op jit(solution)/shard_map/ppermute | solution.py:349
  18.9 3.5 %collective-permute-start.3 = (bf16[128,1024]{1,0:T(8,128)(2,1)S(1)}, bf16[128,1024]{1,0:T(8,128)(2,1)S(1)}, u32[]{:S(2)}, u32[]{:S(2)}) collective-permute-start(bf16[128,1024]{1,0:T(8,128)(2,1)S(1)} %collective-permute-done.refs_1_), channel_id=1, source_target_pairs={{4,8},{5,9},{6,10},{7,11},{8,4},{9,5},{10,6},{11,7},{20,24},{21,25... | collective-permute-start | bytes 786440 | tf_op jit(solution)/shard_map/ppermute | solution.py:349
  22.4 4.0 %all-to-all-start = ((f32[16,16,128]{2,1,0:T(8,128)}), f32[16,16,128]{2,1,0:T(8,128)S(1)}, u32[]{:S(2)}, u32[]{:S(2)}) async-start(f32[16,16,128]{2,1,0:T(8,128)} %shard_map.74), calls=%async_computation | async-start | bytes 262144 | tf_op jit(solution)/shard_map/all_to_all | solution.py:444
  26.5 2.7 %collective-permute-start.14 = (bf16[128,1024]{1,0:T(8,128)(2,1)S(1)}, bf16[128,1024]{1,0:T(8,128)(2,1)}, u32[]{:S(2)}, u32[]{:S(2)}) collective-permute-start(bf16[128,1024]{1,0:T(8,128)(2,1)S(1)} %collective-permute-done.11), channel_id=1, source_target_pairs={{4,0},{5,1},{6,2},{7,3},{8,12},{9,13},{10,14},{11,15},{20,16},{21,... | collective-permute-start | bytes 786440 | tf_op jit(solution)/shard_map/ppermute | solution.py:349
  29.2 1.9 %collective-permute-start.15 = (bf16[128,1024]{1,0:T(8,128)(2,1)S(1)}, bf16[128,1024]{1,0:T(8,128)(2,1)S(1)}, u32[]{:S(2)}, u32[]{:S(2)}) collective-permute-start(bf16[128,1024]{1,0:T(8,128)(2,1)S(1)} %collective-permute-done.10.refs_1_), channel_id=1, source_target_pairs={{0,2},{2,0},{1,3},{3,1},{4,6},{6,4},{5,7},{7,5},{8,10},{10,8},{9,1... | collective-permute-start | bytes 786440 | tf_op jit(solution)/shard_map/ppermute | solution.py:349
  31.1 4.3 %collective-permute-start.13 = (bf16[128,1024]{1,0:T(8,128)(2,1)S(1)}, bf16[128,1024]{1,0:T(8,128)(2,1)S(1)}, u32[]{:S(2)}, u32[]{:S(2)}) collective-permute-start(bf16[128,1024]{1,0:T(8,128)(2,1)S(1)} %collective-permute-done.10.refs_1_), channel_id=1, source_target_pairs={{4,8},{5,9},{6,10},{7,11},{8,4},{9,5},{10,6},{11,7},{20,24},{21,25... | collective-permute-start | bytes 786440 | tf_op jit(solution)/shard_map/ppermute | solution.py:349
  37.9 3.5 %collective-permute-done.13 = bf16[128,1024]{1,0:T(8,128)(2,1)S(1)} collective-permute-done((bf16[128,1024]{1,0:T(8,128)(2,1)S(1)}, bf16[128,1024]{1,0:T(8,128)(2,1)S(1)}, u32[]{:S(2)}, u32[]{:S(2)}) %collective-permute-start.13) | collective-permute-done | bytes 262176 | tf_op jit(solution)/shard_map/ppermute | solution.py:349
  44.6 4.3 %collective-permute-done.17.refs_5_ = bf16[128,1024]{1,0:T(8,128)(2,1)S(1)} collective-permute-done((bf16[128,1024]{1,0:T(8,128)(2,1)S(1)}, bf16[128,1024]{1,0:T(8,128)(2,1)S(1)}, u32[]{:S(2)}, u32[]{:S(2)}) %collective-permute-start.17) | collective-permute-done | bytes 262176 | tf_op jit(solution)/shard_map/ppermute | solution.py:349
  53.9 2.2 %collective-permute-done.23.refs_10_ = bf16[128,1024]{1,0:T(8,128)(2,1)S(1)} collective-permute-done((bf16[128,1024]{1,0:T(8,128)(2,1)S(1)}, bf16[128,1024]{1,0:T(8,128)(2,1)S(1)}, u32[]{:S(2)}, u32[]{:S(2)}) %collective-permute-start.23) | collective-permute-done | bytes 262176 | tf_op jit(solution)/shard_map/ppermute | solution.py:349
  56.2 4.7 %collective-permute-done.22.refs_9_ = bf16[128,1024]{1,0:T(8,128)(2,1)S(1)} collective-permute-done((bf16[128,1024]{1,0:T(8,128)(2,1)S(1)}, bf16[128,1024]{1,0:T(8,128)(2,1)S(1)}, u32[]{:S(2)}, u32[]{:S(2)}) %collective-permute-start.22) | collective-permute-done | bytes 262176 | tf_op jit(solution)/shard_map/ppermute | solution.py:349
  60.8 5.2 %collective-permute-done.19.refs_5_ = bf16[128,1024]{1,0:T(8,128)(2,1)S(1)} collective-permute-done((bf16[128,1024]{1,0:T(8,128)(2,1)S(1)}, bf16[128,1024]{1,0:T(8,128)(2,1)S(1)}, u32[]{:S(2)}, u32[]{:S(2)}) %collective-permute-start.19) | collective-permute-done | bytes 262176 | tf_op jit(solution)/shard_map/ppermute | solution.py:349
  67.6 21.6 %shard_map.78.hidden_ref = bf16[8,256,768]{2,1,0:T(8,128)(2,1)S(1)} custom-call(bf16[8,96,1024]{2,1,0:T(8,128)(2,1)S(1)} %bitcast.67, bf16[8,96,1024]{2,1,0:T(8,128)(2,1)S(1)} %bitcast.68, bf16[8,96,1024]{2,1,0:T(8,128)(2,1)S(1)} %bitcast.65, bf16[8,96,1024]{2,1,0:T(8,128)(2,1)S(1)} %bitcast.66, bf16[128,1024]{1,0:T(8,128)(2,1)S(1)} %broadcast_select_fusion.1.refs_4_, ...), custom_call_target="tpu_custom_call" | custom-call | flops 12884901888 | bytes 50331648 | tf_op jit(solution)/shard_map/pallas_call | solution.py:250
  89.2 8.3 %shard_map.79 = (bf16[8,128,1024]{2,1,0:T(8,128)(2,1)S(1)}, bf16[8,128,1024]{2,1,0:T(8,128)(2,1)S(1)}) custom-call(bf16[8,256,768]{2,1,0:T(8,128)(2,1)S(1)} %shard_map.78.hidden_ref, bf16[8,768,2048]{2,1,0:T(8,128)(2,1)} %down_ref.3, bf16[8,256,256]{2,1,0:T(8,128)(2,1)S(1)} %get-tuple-element.90.spread_ref), custom_call_target="tpu_custom_call" | custom-call | flops 3758096384 | bytes 19922944 | tf_op jit(solution)/shard_map/pallas_call | solution.py:305
  97.6 8.2 %shard_map.80 = (bf16[8,128,1024]{2,1,0:T(8,128)(2,1)S(1)}, bf16[8,128,1024]{2,1,0:T(8,128)(2,1)S(1)}) custom-call(bf16[8,256,768]{2,1,0:T(8,128)(2,1)S(1)} %shard_map.78.hidden_ref, bf16[8,768,2048]{2,1,0:T(8,128)(2,1)} %down_ref.3, bf16[8,256,256]{2,1,0:T(8,128)(2,1)S(1)} %get-tuple-element.90.spread_ref), custom_call_target="tpu_custom_call" | custom-call | flops 3758096384 | bytes 19922944 | tf_op jit(solution)/shard_map/pallas_call | solution.py:305
  120.0 2.1 %collective-permute-done.36 = bf16[128,1024]{1,0:T(8,128)(2,1)S(1)} collective-permute-done((bf16[128,1024]{1,0:T(8,128)(2,1)S(1)}, bf16[128,1024]{1,0:T(8,128)(2,1)S(1)}, u32[]{:S(2)}, u32[]{:S(2)}) %collective-permute-start.36) | collective-permute-done | bytes 262176 | tf_op jit(solution)/shard_map/ppermute | solution.py:349
  125.5 2.2 %collective-permute-done.28 = bf16[128,1024]{1,0:T(8,128)(2,1)S(1)} collective-permute-done((bf16[128,1024]{1,0:T(8,128)(2,1)S(1)}, bf16[128,1024]{1,0:T(8,128)(2,1)S(1)}, u32[]{:S(2)}, u32[]{:S(2)}) %collective-permute-start.28) | collective-permute-done | bytes 262176 | tf_op jit(solution)/shard_map/ppermute | solution.py:349
  127.8 4.5 %collective-permute-start.30 = (bf16[128,1024]{1,0:T(8,128)(2,1)S(1)}, bf16[128,1024]{1,0:T(8,128)(2,1)S(1)}, u32[]{:S(2)}, u32[]{:S(2)}) collective-permute-start(bf16[128,1024]{1,0:T(8,128)(2,1)S(1)} %add_convert_fusion.6), channel_id=1, source_target_pairs={{4,8},{5,9},{6,10},{7,11},{8,4},{9,5},{10,6},{11,7},{20,24},{21,25... | collective-permute-start | bytes 786440 | tf_op jit(solution)/shard_map/ppermute | solution.py:349
  135.3 2.0 %collective-permute-start.41 = (bf16[128,1024]{1,0:T(8,128)(2,1)S(1)}, bf16[128,1024]{1,0:T(8,128)(2,1)S(1)}, u32[]{:S(2)}, u32[]{:S(2)}) collective-permute-start(bf16[128,1024]{1,0:T(8,128)(2,1)S(1)} %add_convert_fusion.3), channel_id=1, source_target_pairs={{4,8},{5,9},{6,10},{7,11},{8,4},{9,5},{10,6},{11,7},{20,24},{21,25... | collective-permute-start | bytes 786440 | tf_op jit(solution)/shard_map/ppermute | solution.py:349
  140.8 2.3 %collective-permute-start.34 = (bf16[128,1024]{1,0:T(8,128)(2,1)S(1)}, bf16[128,1024]{1,0:T(8,128)(2,1)S(1)}, u32[]{:S(2)}, u32[]{:S(2)}) collective-permute-start(bf16[128,1024]{1,0:T(8,128)(2,1)S(1)} %fusion.7), channel_id=1, source_target_pairs={{0,4},{1,5},{2,6},{3,7},{4,0},{5,1},{6,2},{7,3},{8,12},{9,13},{10,... | collective-permute-start | bytes 786440 | tf_op jit(solution)/shard_map/ppermute | solution.py:349
  143.1 2.9 %collective-permute-start.33 = (bf16[128,1024]{1,0:T(8,128)(2,1)S(1)}, bf16[128,1024]{1,0:T(8,128)(2,1)S(1)}, u32[]{:S(2)}, u32[]{:S(2)}) collective-permute-start(bf16[128,1024]{1,0:T(8,128)(2,1)S(1)} %add_convert_fusion.5), channel_id=1, source_target_pairs={{4,8},{5,9},{6,10},{7,11},{8,4},{9,5},{10,6},{11,7},{20,24},{21,25... | collective-permute-start | bytes 786440 | tf_op jit(solution)/shard_map/ppermute | solution.py:349
  148.7 2.2 %collective-permute-start.44 = (bf16[128,1024]{1,0:T(8,128)(2,1)S(1)}, bf16[128,1024]{1,0:T(8,128)(2,1)S(1)}, u32[]{:S(2)}, u32[]{:S(2)}) collective-permute-start(bf16[128,1024]{1,0:T(8,128)(2,1)S(1)} %fusion), channel_id=1, source_target_pairs={{0,4},{1,5},{2,6},{3,7},{4,0},{5,1},{6,2},{7,3},{8,12},{9,13},{10,... | collective-permute-start | bytes 786440 | tf_op jit(solution)/shard_map/ppermute | solution.py:349
  150.9 3.0 %collective-permute-start.43 = (bf16[128,1024]{1,0:T(8,128)(2,1)S(1)}, bf16[128,1024]{1,0:T(8,128)(2,1)S(1)}, u32[]{:S(2)}, u32[]{:S(2)}) collective-permute-start(bf16[128,1024]{1,0:T(8,128)(2,1)S(1)} %add_convert_fusion.2), channel_id=1, source_target_pairs={{4,8},{5,9},{6,10},{7,11},{8,4},{9,5},{10,6},{11,7},{20,24},{21,25... | collective-permute-start | bytes 786440 | tf_op jit(solution)/shard_map/ppermute | solution.py:349
  154.3 3.2 %collective-permute-done.44 = bf16[128,1024]{1,0:T(8,128)(2,1)S(1)} collective-permute-done((bf16[128,1024]{1,0:T(8,128)(2,1)S(1)}, bf16[128,1024]{1,0:T(8,128)(2,1)S(1)}, u32[]{:S(2)}, u32[]{:S(2)}) %collective-permute-start.44) | collective-permute-done | bytes 262176 | tf_op jit(solution)/shard_map/ppermute | solution.py:349
  (107 shorter events, 55.1 us)
Async XLA Ops:
  3.5 11.1 %collective-permute-start.1 = (bf16[128,1024]{1,0:T(8,128)(2,1)S(1)}, bf16[128,1024]{1,0:T(8,128)(2,1)S(1)}, u32[]{:S(2)}, u32[]{:S(2)}) collective-permute-start(bf16[128,1024]{1,0:T(8,128)(2,1)S(1)} %get-tuple-element.61.refs_0_), channel_id=1, source_target_pairs={{4,8},{5,9},{6,10},{7,11},{8,4},{9,5},{10,6},{11,7},{20,24},{21,25... | collective-permute-start | bytes 786440 | tf_op jit(solution)/shard_map/ppermute | solution.py:349
  7.1 11.9 %collective-permute-start.12 = (bf16[128,1024]{1,0:T(8,128)(2,1)S(1)}, bf16[128,1024]{1,0:T(8,128)(2,1)S(1)}, u32[]{:S(2)}, u32[]{:S(2)}) collective-permute-start(bf16[128,1024]{1,0:T(8,128)(2,1)S(1)} %get-tuple-element.76.refs_0_), channel_id=1, source_target_pairs={{0,2},{2,0},{1,3},{3,1},{4,6},{6,4},{5,7},{7,5},{8,10},{10,8},{9,1... | collective-permute-start | bytes 786440 | tf_op jit(solution)/shard_map/ppermute | solution.py:349
  7.7 18.8 %collective-permute-start.11 = (bf16[128,1024]{1,0:T(8,128)(2,1)S(1)}, bf16[128,1024]{1,0:T(8,128)(2,1)S(1)}, u32[]{:S(2)}, u32[]{:S(2)}) collective-permute-start(bf16[128,1024]{1,0:T(8,128)(2,1)S(1)} %get-tuple-element.76.refs_0_), channel_id=1, source_target_pairs={{4,8},{5,9},{6,10},{7,11},{8,4},{9,5},{10,6},{11,7},{20,24},{21,25... | collective-permute-start | bytes 786440 | tf_op jit(solution)/shard_map/ppermute | solution.py:349
  11.1 15.4 %collective-permute-start.10 = (bf16[128,1024]{1,0:T(8,128)(2,1)S(1)}, bf16[128,1024]{1,0:T(8,128)(2,1)S(1)}, u32[]{:S(2)}, u32[]{:S(2)}) collective-permute-start(bf16[128,1024]{1,0:T(8,128)(2,1)S(1)} %get-tuple-element.76.refs_0_), channel_id=1, source_target_pairs={{0,4},{1,5},{2,6},{3,7},{4,0},{5,1},{6,2},{7,3},{8,12},{9,13},{10,... | collective-permute-start | bytes 786440 | tf_op jit(solution)/shard_map/ppermute | solution.py:349
  16.3 14.8 %collective-permute-start.4 = (bf16[128,1024]{1,0:T(8,128)(2,1)S(1)}, bf16[128,1024]{1,0:T(8,128)(2,1)S(1)}, u32[]{:S(2)}, u32[]{:S(2)}) collective-permute-start(bf16[128,1024]{1,0:T(8,128)(2,1)S(1)} %collective-permute-done.1), channel_id=1, source_target_pairs={{4,0},{5,1},{6,2},{7,3},{8,12},{9,13},{10,14},{11,15},{20,16},{21,... | collective-permute-start | bytes 786440 | tf_op jit(solution)/shard_map/ppermute | solution.py:349
  18.2 17.2 %collective-permute-start.5 = (bf16[128,1024]{1,0:T(8,128)(2,1)S(1)}, bf16[128,1024]{1,0:T(8,128)(2,1)S(1)}, u32[]{:S(2)}, u32[]{:S(2)}) collective-permute-start(bf16[128,1024]{1,0:T(8,128)(2,1)S(1)} %collective-permute-done.refs_1_), channel_id=1, source_target_pairs={{0,2},{2,0},{1,3},{3,1},{4,6},{6,4},{5,7},{7,5},{8,10},{10,8},{9,1... | collective-permute-start | bytes 786440 | tf_op jit(solution)/shard_map/ppermute | solution.py:349
  18.9 16.5 %collective-permute-start.3 = (bf16[128,1024]{1,0:T(8,128)(2,1)S(1)}, bf16[128,1024]{1,0:T(8,128)(2,1)S(1)}, u32[]{:S(2)}, u32[]{:S(2)}) collective-permute-start(bf16[128,1024]{1,0:T(8,128)(2,1)S(1)} %collective-permute-done.refs_1_), channel_id=1, source_target_pairs={{4,8},{5,9},{6,10},{7,11},{8,4},{9,5},{10,6},{11,7},{20,24},{21,25... | collective-permute-start | bytes 786440 | tf_op jit(solution)/shard_map/ppermute | solution.py:349
  22.4 13.0 %all-to-all-start = ((f32[16,16,128]{2,1,0:T(8,128)}), f32[16,16,128]{2,1,0:T(8,128)S(1)}, u32[]{:S(2)}, u32[]{:S(2)}) async-start(f32[16,16,128]{2,1,0:T(8,128)} %shard_map.74), calls=%async_computation | async-start | bytes 262144 | tf_op jit(solution)/shard_map/all_to_all | solution.py:444
  26.5 10.9 %collective-permute-start.14 = (bf16[128,1024]{1,0:T(8,128)(2,1)S(1)}, bf16[128,1024]{1,0:T(8,128)(2,1)}, u32[]{:S(2)}, u32[]{:S(2)}) collective-permute-start(bf16[128,1024]{1,0:T(8,128)(2,1)S(1)} %collective-permute-done.11), channel_id=1, source_target_pairs={{4,0},{5,1},{6,2},{7,3},{8,12},{9,13},{10,14},{11,15},{20,16},{21,... | collective-permute-start | bytes 786440 | tf_op jit(solution)/shard_map/ppermute | solution.py:349
  31.1 10.3 %collective-permute-start.13 = (bf16[128,1024]{1,0:T(8,128)(2,1)S(1)}, bf16[128,1024]{1,0:T(8,128)(2,1)S(1)}, u32[]{:S(2)}, u32[]{:S(2)}) collective-permute-start(bf16[128,1024]{1,0:T(8,128)(2,1)S(1)} %collective-permute-done.10.refs_1_), channel_id=1, source_target_pairs={{4,8},{5,9},{6,10},{7,11},{8,4},{9,5},{10,6},{11,7},{20,24},{21,25... | collective-permute-start | bytes 786440 | tf_op jit(solution)/shard_map/ppermute | solution.py:349
  35.5 13.5 %collective-permute-start.7 = (bf16[128,1024]{1,0:T(8,128)(2,1)S(1)}, bf16[128,1024]{1,0:T(8,128)(2,1)S(1)}, u32[]{:S(2)}, u32[]{:S(2)}) collective-permute-start(bf16[128,1024]{1,0:T(8,128)(2,1)S(1)} %broadcast_select_fusion.3.refs_2_), channel_id=1, source_target_pairs={{0,2},{2,0},{1,3},{3,1},{4,6},{6,4},{5,7},{7,5},{8,10},{10,8},{9,1... | collective-permute-start | bytes 786440 | tf_op jit(solution)/shard_map/ppermute | solution.py:349
  36.1 12.9 %collective-permute-start.6 = (bf16[128,1024]{1,0:T(8,128)(2,1)S(1)}, bf16[128,1024]{1,0:T(8,128)(2,1)S(1)}, u32[]{:S(2)}, u32[]{:S(2)}) collective-permute-start(bf16[128,1024]{1,0:T(8,128)(2,1)S(1)} %collective-permute-done.3), channel_id=1, source_target_pairs={{4,0},{5,1},{6,2},{7,3},{8,12},{9,13},{10,14},{11,15},{20,16},{21,... | collective-permute-start | bytes 786440 | tf_op jit(solution)/shard_map/ppermute | solution.py:349
  49.9 17.6 %collective-permute-start.18 = (bf16[8,6,16,1024]{3,2,1,0:T(8,128)(2,1)S(1)}, bf16[8,6,16,1024]{3,2,1,0:T(8,128)(2,1)S(1)}, u32[]{:S(2)}, u32[]{:S(2)}) collective-permute-start(bf16[8,6,16,1024]{3,2,1,0:T(8,128)(2,1)S(1)} %get-tuple-element.85), channel_id=1, source_target_pairs={{0,1},{1,0},{2,3},{3,2},{4,5},{5,4},{6,7},{7,6},{8,9},{9,8},{10,11... | collective-permute-start | bytes 4718600 | tf_op jit(solution)/shard_map/ppermute | solution.py:349
  51.0 16.6 %collective-permute-start.9 = (bf16[8,6,16,1024]{3,2,1,0:T(8,128)(2,1)S(1)}, bf16[8,6,16,1024]{3,2,1,0:T(8,128)(2,1)S(1)}, u32[]{:S(2)}, u32[]{:S(2)}) collective-permute-start(bf16[8,6,16,1024]{3,2,1,0:T(8,128)(2,1)S(1)} %get-tuple-element.75), channel_id=1, source_target_pairs={{0,1},{1,0},{2,3},{3,2},{4,5},{5,4},{6,7},{7,6},{8,9},{9,8},{10,11... | collective-permute-start | bytes 4718600 | tf_op jit(solution)/shard_map/ppermute | solution.py:349
  53.2 12.8 %collective-permute-start.19 = (bf16[128,1024]{1,0:T(8,128)(2,1)S(1)}, bf16[128,1024]{1,0:T(8,128)(2,1)S(1)}, u32[]{:S(2)}, u32[]{:S(2)}) collective-permute-start(bf16[128,1024]{1,0:T(8,128)(2,1)S(1)} %broadcast_select_fusion.1.refs_4_), channel_id=1, source_target_pairs={{0,2},{2,0},{1,3},{3,1},{4,6},{6,4},{5,7},{7,5},{8,10},{10,8},{9,1... | collective-permute-start | bytes 786440 | tf_op jit(solution)/shard_map/ppermute | solution.py:349
  56.0 10.0 %collective-permute-start.20 = (bf16[128,1024]{1,0:T(8,128)(2,1)S(1)}, bf16[128,1024]{1,0:T(8,128)(2,1)S(1)}, u32[]{:S(2)}, u32[]{:S(2)}) collective-permute-start(bf16[128,1024]{1,0:T(8,128)(2,1)S(1)} %broadcast_select_fusion.1.refs_4_), channel_id=1, source_target_pairs={{0,1},{1,0},{2,3},{3,2},{4,5},{5,4},{6,7},{7,6},{8,9},{9,8},{10,11... | collective-permute-start | bytes 786440 | tf_op jit(solution)/shard_map/ppermute | solution.py:349
  117.5 10.3 %collective-permute-start.28 = (bf16[128,1024]{1,0:T(8,128)(2,1)S(1)}, bf16[128,1024]{1,0:T(8,128)(2,1)S(1)}, u32[]{:S(2)}, u32[]{:S(2)}) collective-permute-start(bf16[128,1024]{1,0:T(8,128)(2,1)S(1)} %get-tuple-element.94), channel_id=1, source_target_pairs={{0,2},{2,0},{1,3},{3,1},{4,6},{6,4},{5,7},{7,5},{8,10},{10,8},{9,1... | collective-permute-start | bytes 786440 | tf_op jit(solution)/shard_map/ppermute | solution.py:349
  122.2 13.0 %collective-permute-start.38 = (bf16[128,1024]{1,0:T(8,128)(2,1)S(1)}, bf16[128,1024]{1,0:T(8,128)(2,1)S(1)}, u32[]{:S(2)}, u32[]{:S(2)}) collective-permute-start(bf16[128,1024]{1,0:T(8,128)(2,1)S(1)} %fusion.1), channel_id=1, source_target_pairs={{0,4},{1,5},{2,6},{3,7},{12,8},{13,9},{14,10},{15,11},{16,20},{17,... | collective-permute-start | bytes 786440 | tf_op jit(solution)/shard_map/ppermute | solution.py:349
  123.5 11.7 %collective-permute-start.39 = (bf16[128,1024]{1,0:T(8,128)(2,1)S(1)}, bf16[128,1024]{1,0:T(8,128)(2,1)S(1)}, u32[]{:S(2)}, u32[]{:S(2)}) collective-permute-start(bf16[128,1024]{1,0:T(8,128)(2,1)S(1)} %get-tuple-element.108), channel_id=1, source_target_pairs={{0,2},{2,0},{1,3},{3,1},{4,6},{6,4},{5,7},{7,5},{8,10},{10,8},{9,1... | collective-permute-start | bytes 786440 | tf_op jit(solution)/shard_map/ppermute | solution.py:349
  127.8 10.9 %collective-permute-start.30 = (bf16[128,1024]{1,0:T(8,128)(2,1)S(1)}, bf16[128,1024]{1,0:T(8,128)(2,1)S(1)}, u32[]{:S(2)}, u32[]{:S(2)}) collective-permute-start(bf16[128,1024]{1,0:T(8,128)(2,1)S(1)} %add_convert_fusion.6), channel_id=1, source_target_pairs={{4,8},{5,9},{6,10},{7,11},{8,4},{9,5},{10,6},{11,7},{20,24},{21,25... | collective-permute-start | bytes 786440 | tf_op jit(solution)/shard_map/ppermute | solution.py:349
  135.3 10.8 %collective-permute-start.41 = (bf16[128,1024]{1,0:T(8,128)(2,1)S(1)}, bf16[128,1024]{1,0:T(8,128)(2,1)S(1)}, u32[]{:S(2)}, u32[]{:S(2)}) collective-permute-start(bf16[128,1024]{1,0:T(8,128)(2,1)S(1)} %add_convert_fusion.3), channel_id=1, source_target_pairs={{4,8},{5,9},{6,10},{7,11},{8,4},{9,5},{10,6},{11,7},{20,24},{21,25... | collective-permute-start | bytes 786440 | tf_op jit(solution)/shard_map/ppermute | solution.py:349
  137.4 11.1 %collective-permute-start.40 = (bf16[128,1024]{1,0:T(8,128)(2,1)S(1)}, bf16[128,1024]{1,0:T(8,128)(2,1)S(1)}, u32[]{:S(2)}, u32[]{:S(2)}) collective-permute-start(bf16[128,1024]{1,0:T(8,128)(2,1)S(1)} %fusion.2), channel_id=1, source_target_pairs={{0,4},{1,5},{2,6},{3,7},{12,8},{13,9},{14,10},{15,11},{16,20},{17,... | collective-permute-start | bytes 786440 | tf_op jit(solution)/shard_map/ppermute | solution.py:349
  140.8 13.3 %collective-permute-start.34 = (bf16[128,1024]{1,0:T(8,128)(2,1)S(1)}, bf16[128,1024]{1,0:T(8,128)(2,1)S(1)}, u32[]{:S(2)}, u32[]{:S(2)}) collective-permute-start(bf16[128,1024]{1,0:T(8,128)(2,1)S(1)} %fusion.7), channel_id=1, source_target_pairs={{0,4},{1,5},{2,6},{3,7},{4,0},{5,1},{6,2},{7,3},{8,12},{9,13},{10,... | collective-permute-start | bytes 786440 | tf_op jit(solution)/shard_map/ppermute | solution.py:349
  143.1 11.0 %collective-permute-start.33 = (bf16[128,1024]{1,0:T(8,128)(2,1)S(1)}, bf16[128,1024]{1,0:T(8,128)(2,1)S(1)}, u32[]{:S(2)}, u32[]{:S(2)}) collective-permute-start(bf16[128,1024]{1,0:T(8,128)(2,1)S(1)} %add_convert_fusion.5), channel_id=1, source_target_pairs={{4,8},{5,9},{6,10},{7,11},{8,4},{9,5},{10,6},{11,7},{20,24},{21,25... | collective-permute-start | bytes 786440 | tf_op jit(solution)/shard_map/ppermute | solution.py:349
  (26 other events, 168.7 us)

commit v10 on v8

--- a/solution.py
+++ b/solution.py
@@ -110,8 +110,8 @@
 def slot_sources(z, dp):
     low = z < 2
     column = z, z ^ 1, jnp.where(low, 2, 1), jnp.where(low, 3, 0)
-    early = [(column[i], side) for side in (0, 2) for i in range(3)]
-    late = [(column[3], side) for side in (0, 2)]
+    early = [(column[i], side) for side in (0, 2) for i in (0, 1)]
+    late = [(column[i], side) for side in (0, 2) for i in (2, 3)]
     return [
         from_z * 4 + (dp ^ (side + core))
         for group in (early, late)
@@ -143,7 +143,7 @@
 def tables(place, choices, experts):
     count, _, token_count = choices.shape
     rows = experts * slots
-    late = count // 8
+    late = count // 4
     early = count // 2 - late
     shapes = [(early, rows, token_count), (early, rows, token_count), (2 * late, rows, token_count)]
     shapes = [jax.ShapeDtypeStruct(shape, jnp.bfloat16) for shape in shapes]
@@ -363,11 +363,9 @@
     return third, third_x, jnp.where(edge, far, cross), *others
 
 
-def tree_rest(early, fourth, mine, theirs, experts):
-    mine_rows, theirs_rows = pick_pair(early, mine, theirs, experts)
-    fourth_x, theirs_rows = together(send(fourth, swap_x), send(theirs_rows, swap_core))
-    late = [fourth, fourth_x]
-    return [mine_rows, theirs_rows], late + [send(block, swap_core) for block in late]
+def late_blocks(third, fourth, third_x):
+    late = [third, fourth, third_x, send(fourth, swap_x)]
+    return late + [send(block, swap_core) for block in late]
 
 
 def chip_sums(mine, theirs):
@@ -375,7 +373,7 @@
 
 
 def tree_return(chip, near_by_z):
-    own, near, third, own_x, near_x, third_x, fourth, fourth_x = [chip[i] for i in range(8)]
+    own, near, own_x, near_x, third, fourth, third_x, fourth_x = [chip[i] for i in range(8)]
     if near_by_z:
         near_x = send(near_x, swap_z)
     fourth_in, third_x, near_x, own_x = together(send(fourth_x, swap_x), third_x, near_x, own_x)
@@ -448,22 +446,22 @@
             seconds.append((cross, outer, near_x))
         mine, theirs, late_picker, spread, scale = tables(place, choices, local_count)
         theirs = send(theirs, swap_core)
-        thirds = []
-        for (near, middle, own_x), (cross, outer, near_x) in zip(firsts, seconds):
-            if not thirds:
-                third, third_x, fourth, theirs = tree_third(cross, outer, middle, edge, theirs)
+        order = (0, 1, 2, 3, 8, 9, 10, 11, 4, 5, 6, 7, 12, 13, 14, 15)
+        row_chunks, late_chunks = [], []
+        for part, (near, middle, own_x), (cross, outer, near_x) in zip(parts, firsts, seconds):
+            mine_rows, theirs_rows = pick_pair(
+                (part, near, own_x, near_x), mine, theirs, local_count
+            )
+            theirs_rows = send(theirs_rows, swap_core)
+            if len(late_chunks) == gather_chunks - 1:
+                third, third_x, fourth, mine_rows = tree_third(
+                    cross, outer, middle, edge, mine_rows
+                )
             else:
                 third, third_x, fourth = tree_third(cross, outer, middle, edge)
-            thirds.append((third, third_x, fourth))
-        order = (0, 1, 2, 3, 4, 5, 8, 9, 10, 11, 12, 13, 6, 7, 14, 15)
-        row_chunks, late_chunks = [], []
-        for part, (near, middle, own_x), (cross, outer, near_x), (third, third_x, fourth) in zip(
-            parts, firsts, seconds, thirds
-        ):
-            early = part, near, third, own_x, near_x, third_x
-            rows, late = tree_rest(early, fourth, mine, theirs, local_count)
+            rows = mine_rows, theirs_rows
             row_chunks.append([rows_of.reshape(local_count, -1, width) for rows_of in rows])
-            late_chunks.append(late)
+            late_chunks.append(late_blocks(third, fourth, third_x))
     else:
         rank, named_weight = choices[:, :local_count], choices[:, local_count:]
         match = rank[:, :, None, :] == jnp.arange(slots, dtype=jnp.float32)[None, None, :, None]

time: 160 us -> 162 us (1.012)
  waiting for transfers between devices: 40.3 us -> 47.3 us
  starting transfers between devices: 69.2 us -> 64 us
    ppermute x45 -> x49, waiting for transfers between devices: 40.3 us -> 47.3 us  [send(): return lax.ppermute(value, axes, pairs)]
    ppermute x45 -> x49, starting transfers between devices: 65.2 us -> 59.3 us  [send(): return lax.ppermute(value, axes, pairs)]
  transfers between devices with their start and end apart: 46 -> 50, of which waited for: 20 -> 21; matrix products, arithmetic and copies ran while one was open for 2% -> 2% of each run, Pallas kernels for 7% -> 7%
where the time goes in v10:
time: 162 us; the launch traced here: 161 us
  starting transfers between devices  64 us (40%)
  waiting for transfers between devices  47.3 us (29%)
  Pallas kernels  42.1 us (26%)
  other arithmetic  4.26 us (3%)
  local copies, waits for them, and re-layouts  3.27 us (2%)
    ppermute x49, starting transfers between devices, send(): return lax.ppermute(value, axes, pairs)  59.3 us
    ppermute x49, waiting for transfers between devices, send(): return lax.ppermute(value, axes, pairs)  47.3 us
    pallas_call x1, Pallas kernels, hidden_rows(): pl.pallas_call(functools.partial(hidden_kernel, chunks, groups, late), gr...  22.2 us
    pallas_call x2, Pallas kernels, mix_rows(): pl.pallas_call(functools.partial(mix_kernel, order), grid=(experts // gro...  16.5 us
    all_to_all x1, starting transfers between devices, shards(): lax.all_to_all(choice, axes, split_axis=0, concat_axis=0, tiled=True)  4.68 us
  transfers between devices with their start and end apart: 50, of which 21 were waited for; matrix products, arithmetic and copies ran while one was open for 2% of the time, Pallas kernels for 7%

profile of v10, /device:TPU:8, one launch (start us, length us, event | category | flops | bytes accessed | tf_op | source)
XLA Modules:
  0.0 161.4 jit_solution(15039409495762901204)
XLA Ops:
  3.5 3.5 %collective-permute-start.1 = (bf16[128,1024]{1,0:T(8,128)(2,1)S(1)}, bf16[128,1024]{1,0:T(8,128)(2,1)S(1)}, u32[]{:S(2)}, u32[]{:S(2)}) collective-permute-start(bf16[128,1024]{1,0:T(8,128)(2,1)S(1)} %get-tuple-element.61.refs_0_), channel_id=1, source_target_pairs={{4,8},{5,9},{6,10},{7,11},{8,4},{9,5},{10,6},{11,7},{20,24},{21,25... | collective-permute-start | bytes 786440 | tf_op jit(solution)/shard_map/ppermute | solution.py:343
  7.7 2.3 %collective-permute-start.9 = (bf16[128,1024]{1,0:T(8,128)(2,1)S(1)}, bf16[128,1024]{1,0:T(8,128)(2,1)S(1)}, u32[]{:S(2)}, u32[]{:S(2)}) collective-permute-start(bf16[128,1024]{1,0:T(8,128)(2,1)S(1)} %get-tuple-element.72.refs_0_), channel_id=1, source_target_pairs={{4,8},{5,9},{6,10},{7,11},{8,4},{9,5},{10,6},{11,7},{20,24},{21,25... | collective-permute-start | bytes 786440 | tf_op jit(solution)/shard_map/ppermute | solution.py:343
  12.5 2.1 %collective-permute-done.1 = bf16[128,1024]{1,0:T(8,128)(2,1)S(1)} collective-permute-done((bf16[128,1024]{1,0:T(8,128)(2,1)S(1)}, bf16[128,1024]{1,0:T(8,128)(2,1)S(1)}, u32[]{:S(2)}, u32[]{:S(2)}) %collective-permute-start.1) | collective-permute-done | bytes 262176 | tf_op jit(solution)/shard_map/ppermute | solution.py:343
  15.5 2.2 %collective-permute-start.4 = (bf16[128,1024]{1,0:T(8,128)(2,1)S(1)}, bf16[128,1024]{1,0:T(8,128)(2,1)S(1)}, u32[]{:S(2)}, u32[]{:S(2)}) collective-permute-start(bf16[128,1024]{1,0:T(8,128)(2,1)S(1)} %collective-permute-done.1), channel_id=1, source_target_pairs={{4,0},{5,1},{6,2},{7,3},{8,12},{9,13},{10,14},{11,15},{20,16},{21,... | collective-permute-start | bytes 786440 | tf_op jit(solution)/shard_map/ppermute | solution.py:343
  17.8 3.5 %collective-permute-start.3 = (bf16[128,1024]{1,0:T(8,128)(2,1)S(1)}, bf16[128,1024]{1,0:T(8,128)(2,1)S(1)}, u32[]{:S(2)}, u32[]{:S(2)}) collective-permute-start(bf16[128,1024]{1,0:T(8,128)(2,1)S(1)} %collective-permute-done.refs_1_), channel_id=1, source_target_pairs={{4,8},{5,9},{6,10},{7,11},{8,4},{9,5},{10,6},{11,7},{20,24},{21,25... | collective-permute-start | bytes 786440 | tf_op jit(solution)/shard_map/ppermute | solution.py:343
  21.2 4.7 %all-to-all-start = ((f32[16,16,128]{2,1,0:T(8,128)}), f32[16,16,128]{2,1,0:T(8,128)S(1)}, u32[]{:S(2)}, u32[]{:S(2)}) async-start(f32[16,16,128]{2,1,0:T(8,128)} %shard_map.74), calls=%async_computation | async-start | bytes 262144 | tf_op jit(solution)/shard_map/all_to_all | solution.py:437
  27.5 3.4 %collective-permute-start.11 = (bf16[128,1024]{1,0:T(8,128)(2,1)S(1)}, bf16[128,1024]{1,0:T(8,128)(2,1)S(1)}, u32[]{:S(2)}, u32[]{:S(2)}) collective-permute-start(bf16[128,1024]{1,0:T(8,128)(2,1)S(1)} %collective-permute-done.8.refs_1_), channel_id=1, source_target_pairs={{4,8},{5,9},{6,10},{7,11},{8,4},{9,5},{10,6},{11,7},{20,24},{21,25... | collective-permute-start | bytes 786440 | tf_op jit(solution)/shard_map/ppermute | solution.py:343
  33.7 4.0 %collective-permute-done.12 = bf16[128,1024]{1,0:T(8,128)(2,1)} collective-permute-done((bf16[128,1024]{1,0:T(8,128)(2,1)S(1)}, bf16[128,1024]{1,0:T(8,128)(2,1)}, u32[]{:S(2)}, u32[]{:S(2)}) %collective-permute-start.12) | collective-permute-done | bytes 262176 | tf_op jit(solution)/shard_map/ppermute | solution.py:343
  37.7 4.5 %collective-permute-start.17 = (bf16[128,1024]{1,0:T(8,128)(2,1)S(1)}, bf16[128,1024]{1,0:T(8,128)(2,1)S(1)}, u32[]{:S(2)}, u32[]{:S(2)}) collective-permute-start(bf16[128,1024]{1,0:T(8,128)(2,1)S(1)} %collective-permute-done.3), channel_id=1, source_target_pairs={{4,0},{5,1},{6,2},{7,3},{8,12},{9,13},{10,14},{11,15},{20,16},{21,... | collective-permute-start | bytes 786440 | tf_op jit(solution)/shard_map/ppermute | solution.py:343
  48.6 3.6 %collective-permute-done.15.refs_14_ = bf16[128,1024]{1,0:T(8,128)(2,1)S(1)} collective-permute-done((bf16[128,1024]{1,0:T(8,128)(2,1)S(1)}, bf16[128,1024]{1,0:T(8,128)(2,1)S(1)}, u32[]{:S(2)}, u32[]{:S(2)}) %collective-permute-start.15) | collective-permute-done | bytes 262176 | tf_op jit(solution)/shard_map/ppermute | solution.py:343
  54.3 6.6 %collective-permute-done.19.refs_7_ = bf16[128,1024]{1,0:T(8,128)(2,1)S(1)} collective-permute-done((bf16[128,1024]{1,0:T(8,128)(2,1)S(1)}, bf16[128,1024]{1,0:T(8,128)(2,1)S(1)}, u32[]{:S(2)}, u32[]{:S(2)}) %collective-permute-start.19) | collective-permute-done | bytes 262176 | tf_op jit(solution)/shard_map/ppermute | solution.py:343
  62.0 6.5 %collective-permute-done.24.refs_15_ = bf16[128,1024]{1,0:T(8,128)(2,1)S(1)} collective-permute-done((bf16[128,1024]{1,0:T(8,128)(2,1)S(1)}, bf16[128,1024]{1,0:T(8,128)(2,1)S(1)}, u32[]{:S(2)}, u32[]{:S(2)}) %collective-permute-start.24) | collective-permute-done | bytes 262176 | tf_op jit(solution)/shard_map/ppermute | solution.py:343
  70.1 22.2 %shard_map.78.hidden_ref = bf16[8,256,768]{2,1,0:T(8,128)(2,1)S(1)} custom-call(bf16[8,64,1024]{2,1,0:T(8,128)(2,1)S(1)} %bitcast.66, bf16[8,64,1024]{2,1,0:T(8,128)(2,1)S(1)} %bitcast.67, bf16[8,64,1024]{2,1,0:T(8,128)(2,1)S(1)} %bitcast.65, bf16[8,64,1024]{2,1,0:T(8,128)(2,1)S(1)} %bitcast.68, bf16[128,1024]{1,0:T(8,128)(2,1)S(1)} %broadcast_select_fusion.2.refs_4_, ...), custom_call_target="tpu_custom_call" | custom-call | flops 12884901888 | bytes 50331648 | tf_op jit(solution)/shard_map/pallas_call | solution.py:246
  92.2 8.2 %shard_map.79 = (bf16[8,128,1024]{2,1,0:T(8,128)(2,1)S(1)}, bf16[8,128,1024]{2,1,0:T(8,128)(2,1)S(1)}) custom-call(bf16[8,256,768]{2,1,0:T(8,128)(2,1)S(1)} %shard_map.78.hidden_ref, bf16[8,768,2048]{2,1,0:T(8,128)(2,1)} %down_ref.3, bf16[16,128,128]{2,1,0:T(8,128)(2,1)S(1)} %get-tuple-element.90.spread_ref), custom_call_target="tpu_custom_call" | custom-call | flops 3758096384 | bytes 19922944 | tf_op jit(solution)/shard_map/pallas_call | solution.py:299
  100.7 8.2 %shard_map.80 = (bf16[8,128,1024]{2,1,0:T(8,128)(2,1)S(1)}, bf16[8,128,1024]{2,1,0:T(8,128)(2,1)S(1)}) custom-call(bf16[8,256,768]{2,1,0:T(8,128)(2,1)S(1)} %shard_map.78.hidden_ref, bf16[8,768,2048]{2,1,0:T(8,128)(2,1)} %down_ref.3, bf16[16,128,128]{2,1,0:T(8,128)(2,1)S(1)} %get-tuple-element.90.spread_ref), custom_call_target="tpu_custom_call" | custom-call | flops 3758096384 | bytes 19922944 | tf_op jit(solution)/shard_map/pallas_call | solution.py:299
  110.8 2.3 %collective-permute-done.39 = bf16[8,128,1024]{2,1,0:T(8,128)(2,1)S(1)} collective-permute-done((bf16[8,128,1024]{2,1,0:T(8,128)(2,1)S(1)}, bf16[8,128,1024]{2,1,0:T(8,128)(2,1)S(1)}, u32[]{:S(2)}, u32[]{:S(2)}) %collective-permute-start.39) | collective-permute-done | bytes 2097184 | tf_op jit(solution)/shard_map/ppermute | solution.py:343
  116.3 2.9 %collective-permute-done.30 = bf16[128,1024]{1,0:T(8,128)(2,1)S(1)} collective-permute-done((bf16[128,1024]{1,0:T(8,128)(2,1)S(1)}, bf16[128,1024]{1,0:T(8,128)(2,1)S(1)}, u32[]{:S(2)}, u32[]{:S(2)}) %collective-permute-start.30) | collective-permute-done | bytes 262176 | tf_op jit(solution)/shard_map/ppermute | solution.py:343
  120.8 2.3 %collective-permute-done.41 = bf16[128,1024]{1,0:T(8,128)(2,1)S(1)} collective-permute-done((bf16[128,1024]{1,0:T(8,128)(2,1)S(1)}, bf16[128,1024]{1,0:T(8,128)(2,1)S(1)}, u32[]{:S(2)}, u32[]{:S(2)}) %collective-permute-start.41) | collective-permute-done | bytes 262176 | tf_op jit(solution)/shard_map/ppermute | solution.py:343
  130.7 2.8 %collective-permute-start.34 = (bf16[128,1024]{1,0:T(8,128)(2,1)S(1)}, bf16[128,1024]{1,0:T(8,128)(2,1)S(1)}, u32[]{:S(2)}, u32[]{:S(2)}) collective-permute-start(bf16[128,1024]{1,0:T(8,128)(2,1)S(1)} %add_convert_fusion.6), channel_id=1, source_target_pairs={{4,8},{5,9},{6,10},{7,11},{8,4},{9,5},{10,6},{11,7},{20,24},{21,25... | collective-permute-start | bytes 786440 | tf_op jit(solution)/shard_map/ppermute | solution.py:343
  135.8 2.8 %collective-permute-start.45 = (bf16[128,1024]{1,0:T(8,128)(2,1)S(1)}, bf16[128,1024]{1,0:T(8,128)(2,1)S(1)}, u32[]{:S(2)}, u32[]{:S(2)}) collective-permute-start(bf16[128,1024]{1,0:T(8,128)(2,1)S(1)} %add_convert_fusion.3), channel_id=1, source_target_pairs={{4,8},{5,9},{6,10},{7,11},{8,4},{9,5},{10,6},{11,7},{20,24},{21,25... | collective-permute-start | bytes 786440 | tf_op jit(solution)/shard_map/ppermute | solution.py:343
  144.6 3.1 %collective-permute-start.37 = (bf16[128,1024]{1,0:T(8,128)(2,1)S(1)}, bf16[128,1024]{1,0:T(8,128)(2,1)S(1)}, u32[]{:S(2)}, u32[]{:S(2)}) collective-permute-start(bf16[128,1024]{1,0:T(8,128)(2,1)S(1)} %add_convert_fusion.5), channel_id=1, source_target_pairs={{4,8},{5,9},{6,10},{7,11},{8,4},{9,5},{10,6},{11,7},{20,24},{21,25... | collective-permute-start | bytes 786440 | tf_op jit(solution)/shard_map/ppermute | solution.py:343
  149.9 2.2 %collective-permute-start.48 = (bf16[128,1024]{1,0:T(8,128)(2,1)S(1)}, bf16[128,1024]{1,0:T(8,128)(2,1)S(1)}, u32[]{:S(2)}, u32[]{:S(2)}) collective-permute-start(bf16[128,1024]{1,0:T(8,128)(2,1)S(1)} %fusion), channel_id=1, source_target_pairs={{0,4},{1,5},{2,6},{3,7},{4,0},{5,1},{6,2},{7,3},{8,12},{9,13},{10,... | collective-permute-start | bytes 786440 | tf_op jit(solution)/shard_map/ppermute | solution.py:343
  152.1 3.1 %collective-permute-start.47 = (bf16[128,1024]{1,0:T(8,128)(2,1)S(1)}, bf16[128,1024]{1,0:T(8,128)(2,1)S(1)}, u32[]{:S(2)}, u32[]{:S(2)}) collective-permute-start(bf16[128,1024]{1,0:T(8,128)(2,1)S(1)} %add_convert_fusion.2), channel_id=1, source_target_pairs={{4,8},{5,9},{6,10},{7,11},{8,4},{9,5},{10,6},{11,7},{20,24},{21,25... | collective-permute-start | bytes 786440 | tf_op jit(solution)/shard_map/ppermute | solution.py:343
  155.6 3.7 %collective-permute-done.48 = bf16[128,1024]{1,0:T(8,128)(2,1)S(1)} collective-permute-done((bf16[128,1024]{1,0:T(8,128)(2,1)S(1)}, bf16[128,1024]{1,0:T(8,128)(2,1)S(1)}, u32[]{:S(2)}, u32[]{:S(2)}) %collective-permute-start.48) | collective-permute-done | bytes 262176 | tf_op jit(solution)/shard_map/ppermute | solution.py:343
  (115 shorter events, 50.3 us)
Async XLA Ops:
  2.0 10.3 %collective-permute-start.2 = (bf16[128,1024]{1,0:T(8,128)(2,1)S(1)}, bf16[128,1024]{1,0:T(8,128)(2,1)S(1)}, u32[]{:S(2)}, u32[]{:S(2)}) collective-permute-start(bf16[128,1024]{1,0:T(8,128)(2,1)S(1)} %get-tuple-element.61.refs_0_), channel_id=1, source_target_pairs={{0,2},{2,0},{1,3},{3,1},{4,6},{6,4},{5,7},{7,5},{8,10},{10,8},{9,1... | collective-permute-start | bytes 786440 | tf_op jit(solution)/shard_map/ppermute | solution.py:343
  3.5 11.1 %collective-permute-start.1 = (bf16[128,1024]{1,0:T(8,128)(2,1)S(1)}, bf16[128,1024]{1,0:T(8,128)(2,1)S(1)}, u32[]{:S(2)}, u32[]{:S(2)}) collective-permute-start(bf16[128,1024]{1,0:T(8,128)(2,1)S(1)} %get-tuple-element.61.refs_0_), channel_id=1, source_target_pairs={{4,8},{5,9},{6,10},{7,11},{8,4},{9,5},{10,6},{11,7},{20,24},{21,25... | collective-permute-start | bytes 786440 | tf_op jit(solution)/shard_map/ppermute | solution.py:343
  7.1 10.7 %collective-permute-start.10 = (bf16[128,1024]{1,0:T(8,128)(2,1)S(1)}, bf16[128,1024]{1,0:T(8,128)(2,1)S(1)}, u32[]{:S(2)}, u32[]{:S(2)}) collective-permute-start(bf16[128,1024]{1,0:T(8,128)(2,1)S(1)} %get-tuple-element.72.refs_0_), channel_id=1, source_target_pairs={{0,2},{2,0},{1,3},{3,1},{4,6},{6,4},{5,7},{7,5},{8,10},{10,8},{9,1... | collective-permute-start | bytes 786440 | tf_op jit(solution)/shard_map/ppermute | solution.py:343
  7.7 18.2 %collective-permute-start.9 = (bf16[128,1024]{1,0:T(8,128)(2,1)S(1)}, bf16[128,1024]{1,0:T(8,128)(2,1)S(1)}, u32[]{:S(2)}, u32[]{:S(2)}) collective-permute-start(bf16[128,1024]{1,0:T(8,128)(2,1)S(1)} %get-tuple-element.72.refs_0_), channel_id=1, source_target_pairs={{4,8},{5,9},{6,10},{7,11},{8,4},{9,5},{10,6},{11,7},{20,24},{21,25... | collective-permute-start | bytes 786440 | tf_op jit(solution)/shard_map/ppermute | solution.py:343
  12.2 13.7 %collective-permute-start.8 = (bf16[128,1024]{1,0:T(8,128)(2,1)S(1)}, bf16[128,1024]{1,0:T(8,128)(2,1)S(1)}, u32[]{:S(2)}, u32[]{:S(2)}) collective-permute-start(bf16[128,1024]{1,0:T(8,128)(2,1)S(1)} %get-tuple-element.72.refs_0_), channel_id=1, source_target_pairs={{0,4},{1,5},{2,6},{3,7},{4,0},{5,1},{6,2},{7,3},{8,12},{9,13},{10,... | collective-permute-start | bytes 786440 | tf_op jit(solution)/shard_map/ppermute | solution.py:343
  15.5 15.4 %collective-permute-start.4 = (bf16[128,1024]{1,0:T(8,128)(2,1)S(1)}, bf16[128,1024]{1,0:T(8,128)(2,1)S(1)}, u32[]{:S(2)}, u32[]{:S(2)}) collective-permute-start(bf16[128,1024]{1,0:T(8,128)(2,1)S(1)} %collective-permute-done.1), channel_id=1, source_target_pairs={{4,0},{5,1},{6,2},{7,3},{8,12},{9,13},{10,14},{11,15},{20,16},{21,... | collective-permute-start | bytes 786440 | tf_op jit(solution)/shard_map/ppermute | solution.py:343
  17.7 15.3 %collective-permute-start.5 = (bf16[128,1024]{1,0:T(8,128)(2,1)S(1)}, bf16[128,1024]{1,0:T(8,128)(2,1)S(1)}, u32[]{:S(2)}, u32[]{:S(2)}) collective-permute-start(bf16[128,1024]{1,0:T(8,128)(2,1)S(1)} %collective-permute-done.refs_1_), channel_id=1, source_target_pairs={{0,2},{2,0},{1,3},{3,1},{4,6},{6,4},{5,7},{7,5},{8,10},{10,8},{9,1... | collective-permute-start | bytes 786440 | tf_op jit(solution)/shard_map/ppermute | solution.py:343
  17.8 15.2 %collective-permute-start.3 = (bf16[128,1024]{1,0:T(8,128)(2,1)S(1)}, bf16[128,1024]{1,0:T(8,128)(2,1)S(1)}, u32[]{:S(2)}, u32[]{:S(2)}) collective-permute-start(bf16[128,1024]{1,0:T(8,128)(2,1)S(1)} %collective-permute-done.refs_1_), channel_id=1, source_target_pairs={{4,8},{5,9},{6,10},{7,11},{8,4},{9,5},{10,6},{11,7},{20,24},{21,25... | collective-permute-start | bytes 786440 | tf_op jit(solution)/shard_map/ppermute | solution.py:343
  21.2 11.7 %all-to-all-start = ((f32[16,16,128]{2,1,0:T(8,128)}), f32[16,16,128]{2,1,0:T(8,128)S(1)}, u32[]{:S(2)}, u32[]{:S(2)}) async-start(f32[16,16,128]{2,1,0:T(8,128)} %shard_map.74), calls=%async_computation | async-start | bytes 262144 | tf_op jit(solution)/shard_map/all_to_all | solution.py:437
  25.9 16.3 %collective-permute-start.13 = (bf16[128,1024]{1,0:T(8,128)(2,1)S(1)}, bf16[128,1024]{1,0:T(8,128)(2,1)S(1)}, u32[]{:S(2)}, u32[]{:S(2)}) collective-permute-start(bf16[128,1024]{1,0:T(8,128)(2,1)S(1)} %collective-permute-done.8.refs_1_), channel_id=1, source_target_pairs={{0,2},{2,0},{1,3},{3,1},{4,6},{6,4},{5,7},{7,5},{8,10},{10,8},{9,1... | collective-permute-start | bytes 786440 | tf_op jit(solution)/shard_map/ppermute | solution.py:343
  27.5 14.8 %collective-permute-start.11 = (bf16[128,1024]{1,0:T(8,128)(2,1)S(1)}, bf16[128,1024]{1,0:T(8,128)(2,1)S(1)}, u32[]{:S(2)}, u32[]{:S(2)}) collective-permute-start(bf16[128,1024]{1,0:T(8,128)(2,1)S(1)} %collective-permute-done.8.refs_1_), channel_id=1, source_target_pairs={{4,8},{5,9},{6,10},{7,11},{8,4},{9,5},{10,6},{11,7},{20,24},{21,25... | collective-permute-start | bytes 786440 | tf_op jit(solution)/shard_map/ppermute | solution.py:343
  33.0 15.5 %collective-permute-start.20 = (bf16[128,1024]{1,0:T(8,128)(2,1)S(1)}, bf16[128,1024]{1,0:T(8,128)(2,1)S(1)}, u32[]{:S(2)}, u32[]{:S(2)}) collective-permute-start(bf16[128,1024]{1,0:T(8,128)(2,1)S(1)} %broadcast_select_fusion.2.refs_4_), channel_id=1, source_target_pairs={{0,1},{1,0},{2,3},{3,2},{4,5},{5,4},{6,7},{7,6},{8,9},{9,8},{10,11... | collective-permute-start | bytes 786440 | tf_op jit(solution)/shard_map/ppermute | solution.py:343
  33.1 14.8 %collective-permute-start.18 = (bf16[128,1024]{1,0:T(8,128)(2,1)S(1)}, bf16[128,1024]{1,0:T(8,128)(2,1)S(1)}, u32[]{:S(2)}, u32[]{:S(2)}) collective-permute-start(bf16[128,1024]{1,0:T(8,128)(2,1)S(1)} %broadcast_select_fusion.2.refs_4_), channel_id=1, source_target_pairs={{0,2},{2,0},{1,3},{3,1},{4,6},{6,4},{5,7},{7,5},{8,10},{10,8},{9,1... | collective-permute-start | bytes 786440 | tf_op jit(solution)/shard_map/ppermute | solution.py:343
  37.7 10.3 %collective-permute-start.17 = (bf16[128,1024]{1,0:T(8,128)(2,1)S(1)}, bf16[128,1024]{1,0:T(8,128)(2,1)S(1)}, u32[]{:S(2)}, u32[]{:S(2)}) collective-permute-start(bf16[128,1024]{1,0:T(8,128)(2,1)S(1)} %collective-permute-done.3), channel_id=1, source_target_pairs={{4,0},{5,1},{6,2},{7,3},{8,12},{9,13},{10,14},{11,15},{20,16},{21,... | collective-permute-start | bytes 786440 | tf_op jit(solution)/shard_map/ppermute | solution.py:343
  47.9 22.1 %collective-permute-start.7 = (bf16[8,4,16,1024]{3,2,1,0:T(8,128)(2,1)S(1)}, bf16[8,4,16,1024]{3,2,1,0:T(8,128)(2,1)S(1)}, u32[]{:S(2)}, u32[]{:S(2)}) collective-permute-start(bf16[8,4,16,1024]{3,2,1,0:T(8,128)(2,1)S(1)} %get-tuple-element.71), channel_id=1, source_target_pairs={{0,1},{1,0},{2,3},{3,2},{4,5},{5,4},{6,7},{7,6},{8,9},{9,8},{10,11... | collective-permute-start | bytes 3145736 | tf_op jit(solution)/shard_map/ppermute | solution.py:343
  48.0 22.1 %collective-permute-start.16 = (bf16[8,4,16,1024]{3,2,1,0:T(8,128)(2,1)S(1)}, bf16[8,4,16,1024]{3,2,1,0:T(8,128)(2,1)S(1)}, u32[]{:S(2)}, u32[]{:S(2)}) collective-permute-start(bf16[8,4,16,1024]{3,2,1,0:T(8,128)(2,1)S(1)} %get-tuple-element.81), channel_id=1, source_target_pairs={{0,1},{1,0},{2,3},{3,2},{4,5},{5,4},{6,7},{7,6},{8,9},{9,8},{10,11... | collective-permute-start | bytes 3145736 | tf_op jit(solution)/shard_map/ppermute | solution.py:343
  120.6 10.0 %collective-permute-start.32 = (bf16[128,1024]{1,0:T(8,128)(2,1)S(1)}, bf16[128,1024]{1,0:T(8,128)(2,1)S(1)}, u32[]{:S(2)}, u32[]{:S(2)}) collective-permute-start(bf16[128,1024]{1,0:T(8,128)(2,1)S(1)} %get-tuple-element.94), channel_id=1, source_target_pairs={{0,2},{2,0},{1,3},{3,1},{4,6},{6,4},{5,7},{7,5},{8,10},{10,8},{9,1... | collective-permute-start | bytes 786440 | tf_op jit(solution)/shard_map/ppermute | solution.py:343
  125.1 10.3 %collective-permute-start.42 = (bf16[128,1024]{1,0:T(8,128)(2,1)S(1)}, bf16[128,1024]{1,0:T(8,128)(2,1)S(1)}, u32[]{:S(2)}, u32[]{:S(2)}) collective-permute-start(bf16[128,1024]{1,0:T(8,128)(2,1)S(1)} %fusion.1), channel_id=1, source_target_pairs={{0,4},{1,5},{2,6},{3,7},{12,8},{13,9},{14,10},{15,11},{16,20},{17,... | collective-permute-start | bytes 786440 | tf_op jit(solution)/shard_map/ppermute | solution.py:343
  135.8 11.9 %collective-permute-start.45 = (bf16[128,1024]{1,0:T(8,128)(2,1)S(1)}, bf16[128,1024]{1,0:T(8,128)(2,1)S(1)}, u32[]{:S(2)}, u32[]{:S(2)}) collective-permute-start(bf16[128,1024]{1,0:T(8,128)(2,1)S(1)} %add_convert_fusion.3), channel_id=1, source_target_pairs={{4,8},{5,9},{6,10},{7,11},{8,4},{9,5},{10,6},{11,7},{20,24},{21,25... | collective-permute-start | bytes 786440 | tf_op jit(solution)/shard_map/ppermute | solution.py:343
  138.7 11.1 %collective-permute-start.44 = (bf16[128,1024]{1,0:T(8,128)(2,1)S(1)}, bf16[128,1024]{1,0:T(8,128)(2,1)S(1)}, u32[]{:S(2)}, u32[]{:S(2)}) collective-permute-start(bf16[128,1024]{1,0:T(8,128)(2,1)S(1)} %fusion.2), channel_id=1, source_target_pairs={{0,4},{1,5},{2,6},{3,7},{12,8},{13,9},{14,10},{15,11},{16,20},{17,... | collective-permute-start | bytes 786440 | tf_op jit(solution)/shard_map/ppermute | solution.py:343
  140.0 9.8 %collective-permute-start.46 = (bf16[128,1024]{1,0:T(8,128)(2,1)S(1)}, bf16[128,1024]{1,0:T(8,128)(2,1)S(1)}, u32[]{:S(2)}, u32[]{:S(2)}) collective-permute-start(bf16[128,1024]{1,0:T(8,128)(2,1)S(1)} %add_convert_fusion.4), channel_id=1, source_target_pairs={{0,2},{2,0},{1,3},{3,1},{4,6},{6,4},{5,7},{7,5},{8,10},{10,8},{9,1... | collective-permute-start | bytes 786440 | tf_op jit(solution)/shard_map/ppermute | solution.py:343
  142.6 12.8 %collective-permute-start.38 = (bf16[128,1024]{1,0:T(8,128)(2,1)S(1)}, bf16[128,1024]{1,0:T(8,128)(2,1)S(1)}, u32[]{:S(2)}, u32[]{:S(2)}) collective-permute-start(bf16[128,1024]{1,0:T(8,128)(2,1)S(1)} %fusion.7), channel_id=1, source_target_pairs={{0,4},{1,5},{2,6},{3,7},{4,0},{5,1},{6,2},{7,3},{8,12},{9,13},{10,... | collective-permute-start | bytes 786440 | tf_op jit(solution)/shard_map/ppermute | solution.py:343
  144.6 10.8 %collective-permute-start.37 = (bf16[128,1024]{1,0:T(8,128)(2,1)S(1)}, bf16[128,1024]{1,0:T(8,128)(2,1)S(1)}, u32[]{:S(2)}, u32[]{:S(2)}) collective-permute-start(bf16[128,1024]{1,0:T(8,128)(2,1)S(1)} %add_convert_fusion.5), channel_id=1, source_target_pairs={{4,8},{5,9},{6,10},{7,11},{8,4},{9,5},{10,6},{11,7},{20,24},{21,25... | collective-permute-start | bytes 786440 | tf_op jit(solution)/shard_map/ppermute | solution.py:343
  149.9 9.4 %collective-permute-start.48 = (bf16[128,1024]{1,0:T(8,128)(2,1)S(1)}, bf16[128,1024]{1,0:T(8,128)(2,1)S(1)}, u32[]{:S(2)}, u32[]{:S(2)}) collective-permute-start(bf16[128,1024]{1,0:T(8,128)(2,1)S(1)} %fusion), channel_id=1, source_target_pairs={{0,4},{1,5},{2,6},{3,7},{4,0},{5,1},{6,2},{7,3},{8,12},{9,13},{10,... | collective-permute-start | bytes 786440 | tf_op jit(solution)/shard_map/ppermute | solution.py:343
  (30 other events, 190.6 us)
